TPU v7x, 768 devices: a whole 4x8x12 slice. The times are simulated.
768 devices in a mesh: row: 96 (over z, x, y_hi), col: 8 (over y_lo, core).
Axes of the slice: x: 4, y: 8 (y_hi: 2, y_lo: 4; y = y_hi * 4 + y_lo), z: 12, core: 2. Of those that a mesh axis runs over, the one named last changes fastest.
Arguments:
- x_band: float32 [288, 13, 128, 128], P('row', None, 'col'), may hold values from -0.48 to 0.48
- x_mask: int32 [288, 13], P('row'), may hold values 0 or 1
- sq_mask: int32 [288, 19], P('row'), may hold values 0 or 1
- cube_mask: int32 [288, 25], P('row'), may hold values 0 or 1
Outputs:
- purified: float32 [288, 25, 128, 128], P('row', None, 'col')
All inputs are finite; a program needn't handle non-finite values. No bound on the sum of `x_mask` or of `sq_mask` or of `cube_mask` on one device may be relied on, other than what follows from the above.
Results may differ from a plain program's by a relative error of at most 0.0001.
Values sent between devices are 32-bit elements; how exact they have to be, the bound alone decides.
No kernel may reach another device: no remote copies, remote signals or barrier semaphores. Data moves between devices by JAX's collectives and lax.ppermute only.
A program may use at most 32 MiB of HBM per device.

v0:
```python
import jax
import jax.numpy as jnp
from jax import lax
from jax.sharding import PartitionSpec as P


def from_behind(array, axis, by):
    devices = lax.axis_size(axis)
    return lax.ppermute(array, axis, [(i, (i + by) % devices) for i in range(devices)])


def band_apply(window, base_row, left_band, half_right, half_left, half_out):
    own_rows = left_band.shape[0]
    slab_cols = window.shape[2]
    full_cols = left_band.shape[3]
    summed = jnp.zeros((own_rows, 2 * half_out + 1, slab_cols, full_cols), jnp.float32)
    for offset_left in range(-half_left, half_left + 1):
        lowest = max(-half_out, offset_left - half_right)
        highest = min(half_out, offset_left + half_right)
        first_row = base_row + offset_left
        first_slot = lowest - offset_left + half_right
        right_slab = window[
            first_row : first_row + own_rows, first_slot : first_slot + highest - lowest + 1
        ]
        product = jnp.einsum(
            "gojk,gki->goji",
            right_slab,
            left_band[:, offset_left + half_left],
            precision=lax.Precision.HIGHEST,
        )
        summed = summed.at[:, lowest + half_out : highest + half_out + 1].add(product)
    return summed


def neighbour_rows(own_band, hop_count):
    below_list = []
    above_list = []
    for hop_index in range(1, hop_count + 1):
        for direction in (1, -1):
            arrived = from_behind(own_band, "row", direction * hop_index)
            if direction == 1:
                below_list.insert(0, arrived)
            else:
                above_list.append(arrived)
    return jnp.concatenate(below_list + [own_band] + above_list, axis=0)


def body(x_band, x_mask, sq_mask, cube_mask):
    own_rows = x_band.shape[0]
    half_x = (x_band.shape[1] - 1) // 2
    half_sq = (sq_mask.shape[1] - 1) // 2
    half_cube = (cube_mask.shape[1] - 1) // 2
    masked = x_band * x_mask[:, :, None, None].astype(jnp.float32)
    hop_count = -(-max(half_x, half_sq) // own_rows)
    window = neighbour_rows(masked, hop_count)
    base_row = hop_count * own_rows
    full_band = lax.all_gather(masked, "col", axis=2, tiled=True)
    square = band_apply(window, base_row, full_band, half_x, half_x, half_sq)
    square = square * sq_mask[:, :, None, None].astype(jnp.float32)
    full_square = lax.all_gather(square, "col", axis=2, tiled=True)
    cube = band_apply(window, base_row, full_square, half_x, half_sq, half_cube)
    widened = jnp.pad(square, ((0, 0), (half_cube - half_sq, half_cube - half_sq), (0, 0), (0, 0)))
    return (3.0 * widened - 2.0 * cube) * cube_mask[:, :, None, None].astype(jnp.float32)


def solution(mesh):
    return jax.shard_map(
        body,
        mesh=mesh,
        in_specs=(P("row", None, "col", None), P("row", None), P("row", None), P("row", None)),
        out_specs=P("row", None, "col", None),
        check_vma=False,
    )
```

profile of v0, /device:TPU:1, one launch (start us, length us, event | category | flops | bytes accessed | tf_op | source)
XLA Modules:
  0.0 184.6 jit_solution(10515828153357514300)
XLA Ops:
  6.5 0.7 convert_element_type.14
  7.3 1.8 copy_multiply_fusion
  9.2 9.2 %collective-permute-start.4 = (f32[3,13,16,128]{3,2,0,1:T(8,128)}, f32[3,13,16,128]{3,2,0,1:T(8,128)S(1)}, u32[]{:S(2)}, u32[]{:S(2)}) collective-permute-start(f32[3,13,16,128]{3,2,0,1:T(8,128)} %copy_multiply_fusion), channel_id=1, source_target_pairs={{0,24},{8,32},{16,40},{24,48},{32,56},{40,64},{48,72},{56,80},{64,... | collective-permute-start | bytes 958472 | tf_op jit(solution)/shard_map/ppermute | solution.py:9
  18.4 3.1 %collective-permute-start = (f32[3,13,16,128]{3,2,0,1:T(8,128)}, f32[3,13,16,128]{3,2,0,1:T(8,128)S(1)}, u32[]{:S(2)}, u32[]{:S(2)}) collective-permute-start(f32[3,13,16,128]{3,2,0,1:T(8,128)} %copy_multiply_fusion), channel_id=1, source_target_pairs={{0,16},{8,24},{16,32},{24,40},{32,48},{40,56},{48,64},{56,72},{64,... | collective-permute-start | bytes 958472 | tf_op jit(solution)/shard_map/ppermute | solution.py:9
  21.5 2.4 %collective-permute-start.1 = (f32[3,13,16,128]{3,2,0,1:T(8,128)}, f32[3,13,16,128]{3,2,0,1:T(8,128)S(1)}, u32[]{:S(2)}, u32[]{:S(2)}) collective-permute-start(f32[3,13,16,128]{3,2,0,1:T(8,128)} %copy_multiply_fusion), channel_id=1, source_target_pairs={{0,8},{8,16},{16,24},{24,32},{32,40},{40,48},{48,56},{56,64},{64,7... | collective-permute-start | bytes 958472 | tf_op jit(solution)/shard_map/ppermute | solution.py:9
  23.9 13.7 %collective-permute-start.2 = (f32[3,13,16,128]{3,2,0,1:T(8,128)}, f32[3,13,16,128]{3,2,0,1:T(8,128)S(1)}, u32[]{:S(2)}, u32[]{:S(2)}) collective-permute-start(f32[3,13,16,128]{3,2,0,1:T(8,128)} %copy_multiply_fusion), channel_id=1, source_target_pairs={{0,760},{8,0},{16,8},{24,16},{32,24},{40,32},{48,40},{56,48},{64,5... | collective-permute-start | bytes 958472 | tf_op jit(solution)/shard_map/ppermute | solution.py:9
  37.6 3.4 %collective-permute-start.3 = (f32[3,13,16,128]{3,2,0,1:T(8,128)}, f32[3,13,16,128]{3,2,0,1:T(8,128)S(1)}, u32[]{:S(2)}, u32[]{:S(2)}) collective-permute-start(f32[3,13,16,128]{3,2,0,1:T(8,128)} %copy_multiply_fusion), channel_id=1, source_target_pairs={{0,752},{8,760},{16,0},{24,8},{32,16},{40,24},{48,32},{56,40},{64,... | collective-permute-start | bytes 958472 | tf_op jit(solution)/shard_map/ppermute | solution.py:9
  40.9 0.7 convert_element_type.15
  41.6 3.8 %collective-permute-done.4 = f32[3,13,16,128]{3,2,0,1:T(8,128)S(1)} collective-permute-done((f32[3,13,16,128]{3,2,0,1:T(8,128)}, f32[3,13,16,128]{3,2,0,1:T(8,128)S(1)}, u32[]{:S(2)}, u32[]{:S(2)}) %collective-permute-start.4) | collective-permute-done | bytes 319520 | tf_op jit(solution)/shard_map/ppermute | solution.py:9
  45.5 2.8 %collective-permute-done = f32[3,13,16,128]{3,2,0,1:T(8,128)S(1)} collective-permute-done((f32[3,13,16,128]{3,2,0,1:T(8,128)}, f32[3,13,16,128]{3,2,0,1:T(8,128)S(1)}, u32[]{:S(2)}, u32[]{:S(2)}) %collective-permute-start) | collective-permute-done | bytes 319520 | tf_op jit(solution)/shard_map/ppermute | solution.py:9
  48.4 16.2 %collective-permute-done.1 = f32[3,13,16,128]{3,2,0,1:T(8,128)S(1)} collective-permute-done((f32[3,13,16,128]{3,2,0,1:T(8,128)}, f32[3,13,16,128]{3,2,0,1:T(8,128)S(1)}, u32[]{:S(2)}, u32[]{:S(2)}) %collective-permute-start.1) | collective-permute-done | bytes 319520 | tf_op jit(solution)/shard_map/ppermute | solution.py:9
  64.5 1.8 collective-permute-done.2
  66.4 1.3 pad_maximum_fusion
  67.7 0.7 copy-done.4
  68.5 0.8 constant_dynamic-update-slice_fusion.7
  69.3 18.4 %all-gather.3.cloned.1.call-done = f32[3,13,128,128]{3,2,0,1:T(8,128)} async-done(((f32[3,13,16,128]{3,2,0,1:T(8,128)}), f32[3,13,128,128]{3,2,0,1:T(8,128)}) %all-gather.3.cloned.1.call-update) | async-done | bytes 2555920 | tf_op jit(solution)/shard_map/all_gather | solution.py:57
  87.6 1.6 fusion.82
  89.3 1.4 add_dynamic-update-slice_fusion.1
  90.7 1.4 fusion.15
  92.1 1.4 fusion.13
  93.5 0.5 fusion.21
  94.1 0.5 fusion.12
  94.6 0.5 fusion.11
  95.2 0.5 fusion.10
  95.7 0.5 fusion.9
  97.9 0.9 broadcast_multiply_fusion
  98.8 17.1 %collective-permute-start.5 = (f32[3,13,16,128]{3,2,0,1:T(8,128)S(1)}, f32[3,13,16,128]{3,2,0,1:T(8,128)S(1)}, u32[]{:S(2)}, u32[]{:S(2)}) collective-permute-start(f32[3,13,16,128]{3,2,0,1:T(8,128)S(1)} %copy-done), channel_id=1, source_target_pairs={{0,744},{8,752},{16,760},{24,0},{32,8},{40,16},{48,24},{56,32},{64... | collective-permute-start | bytes 958472 | tf_op jit(solution)/shard_map/ppermute | solution.py:9
  115.9 0.9 fusion.89
  116.8 4.1 %collective-permute-done.5 = f32[3,13,16,128]{3,2,0,1:T(8,128)S(1)} collective-permute-done((f32[3,13,16,128]{3,2,0,1:T(8,128)S(1)}, f32[3,13,16,128]{3,2,0,1:T(8,128)S(1)}, u32[]{:S(2)}, u32[]{:S(2)}) %collective-permute-start.5) | collective-permute-done | bytes 319520 | tf_op jit(solution)/shard_map/ppermute | solution.py:9
  120.9 0.7 copy-done.16
  121.7 1.0 fusion.88
  122.7 40.3 %all-gather.5.cloned.1.call-done = f32[3,19,128,128]{3,2,1,0:T(8,128)} async-done(((f32[3,19,16,128]{3,2,1,0:T(8,128)}), f32[3,19,128,128]{3,2,1,0:T(8,128)}) %all-gather.5.cloned.1.call-update) | async-done | bytes 3735568 | tf_op jit(solution)/shard_map/all_gather | solution.py:60
  163.0 1.6 fusion.76
  164.6 1.5 add_dynamic-update-slice_fusion
  166.1 1.5 fusion.14
  167.6 1.5 fusion.8
  169.1 0.5 fusion.20
  169.6 0.5 fusion.7
  170.2 0.5 fusion.6
  170.7 0.5 fusion.19
  171.3 0.5 fusion.5
  171.8 0.5 fusion.4
  172.3 0.5 fusion.3
  172.9 0.5 fusion.2
  173.4 0.5 fusion.1
  174.0 0.5 fusion.18
  174.5 0.5 fusion
  176.7 1.0 subtract_multiply_fusion
  (57 shorter events, 3.7 us)
Async XLA Ops:
  6.5 81.1 %all-gather.3.cloned.1.call-start = ((), (), s32[]{:S(2)}) async-start(), calls=%async_computation | async-start | bytes 2875392 | tf_op jit(solution)/shard_map/all_gather | solution.py:57
  9.1 153.8 %all-gather.5.cloned.1.call-start = ((), (), s32[]{:S(2)}) async-start(), calls=%async_computation.1 | async-start | bytes 4202496 | tf_op jit(solution)/shard_map/all_gather | solution.py:60
  9.2 36.3 %collective-permute-start.4 = (f32[3,13,16,128]{3,2,0,1:T(8,128)}, f32[3,13,16,128]{3,2,0,1:T(8,128)S(1)}, u32[]{:S(2)}, u32[]{:S(2)}) collective-permute-start(f32[3,13,16,128]{3,2,0,1:T(8,128)} %copy_multiply_fusion), channel_id=1, source_target_pairs={{0,24},{8,32},{16,40},{24,48},{32,56},{40,64},{48,72},{56,80},{64,... | collective-permute-start | bytes 958472 | tf_op jit(solution)/shard_map/ppermute | solution.py:9
  18.4 29.9 %collective-permute-start = (f32[3,13,16,128]{3,2,0,1:T(8,128)}, f32[3,13,16,128]{3,2,0,1:T(8,128)S(1)}, u32[]{:S(2)}, u32[]{:S(2)}) collective-permute-start(f32[3,13,16,128]{3,2,0,1:T(8,128)} %copy_multiply_fusion), channel_id=1, source_target_pairs={{0,16},{8,24},{16,32},{24,40},{32,48},{40,56},{48,64},{56,72},{64,... | collective-permute-start | bytes 958472 | tf_op jit(solution)/shard_map/ppermute | solution.py:9
  21.5 43.0 %collective-permute-start.1 = (f32[3,13,16,128]{3,2,0,1:T(8,128)}, f32[3,13,16,128]{3,2,0,1:T(8,128)S(1)}, u32[]{:S(2)}, u32[]{:S(2)}) collective-permute-start(f32[3,13,16,128]{3,2,0,1:T(8,128)} %copy_multiply_fusion), channel_id=1, source_target_pairs={{0,8},{8,16},{16,24},{24,32},{32,40},{40,48},{48,56},{56,64},{64,7... | collective-permute-start | bytes 958472 | tf_op jit(solution)/shard_map/ppermute | solution.py:9
  23.9 42.5 %collective-permute-start.2 = (f32[3,13,16,128]{3,2,0,1:T(8,128)}, f32[3,13,16,128]{3,2,0,1:T(8,128)S(1)}, u32[]{:S(2)}, u32[]{:S(2)}) collective-permute-start(f32[3,13,16,128]{3,2,0,1:T(8,128)} %copy_multiply_fusion), channel_id=1, source_target_pairs={{0,760},{8,0},{16,8},{24,16},{32,24},{40,32},{48,40},{56,48},{64,5... | collective-permute-start | bytes 958472 | tf_op jit(solution)/shard_map/ppermute | solution.py:9
  37.6 30.1 %collective-permute-start.3 = (f32[3,13,16,128]{3,2,0,1:T(8,128)}, f32[3,13,16,128]{3,2,0,1:T(8,128)S(1)}, u32[]{:S(2)}, u32[]{:S(2)}) collective-permute-start(f32[3,13,16,128]{3,2,0,1:T(8,128)} %copy_multiply_fusion), channel_id=1, source_target_pairs={{0,752},{8,760},{16,0},{24,8},{32,16},{40,24},{48,32},{56,40},{64,... | collective-permute-start | bytes 958472 | tf_op jit(solution)/shard_map/ppermute | solution.py:9
  45.5 20.9 %copy-start.15 = (f32[3,13,16,128]{3,2,0,1:T(8,128)}, f32[3,13,16,128]{3,2,0,1:T(8,128)S(1)}, u32[]{:S(2)}) copy-start(f32[3,13,16,128]{3,2,0,1:T(8,128)S(1)} %collective-permute-done.4) | copy-start | bytes 958468
  48.3 18.1 %copy-start.7 = (f32[3,13,16,128]{3,2,0,1:T(8,128)}, f32[3,13,16,128]{3,2,0,1:T(8,128)S(1)}, u32[]{:S(2)}) copy-start(f32[3,13,16,128]{3,2,0,1:T(8,128)S(1)} %collective-permute-done) | copy-start | bytes 958468
  48.4 18.0 %copy-start.14 = (f32[6,13,16,128]{3,2,0,1:T(8,128)}, f32[6,13,16,128]{3,2,0,1:T(8,128)S(1)}, u32[]{:S(2)}) copy-start(f32[6,13,16,128]{3,2,0,1:T(8,128)S(1)} %get-tuple-element.399) | copy-start | bytes 1916932
  67.7 0.7 copy-start.4
  68.5 26.1 %copy-start = (f32[3,13,16,128]{3,2,0,1:T(8,128)S(1)}, f32[3,13,16,128]{3,2,0,1:T(8,128)}, u32[]{:S(2)}) copy-start(f32[3,13,16,128]{3,2,0,1:T(8,128)} %copy_multiply_fusion) | copy-start | bytes 958468
  87.6 5.9 %copy-start.3 = (f32[3,13,128,128]{3,2,0,1:T(8,128)S(1)}, f32[3,13,128,128]{3,2,0,1:T(8,128)}, u32[]{:S(2)}) copy-start(f32[3,13,128,128]{3,2,0,1:T(8,128)} %all-gather.3.cloned.1.call-done) | copy-start | bytes 7667716
  94.6 2.9 %copy-start.5 = (f32[3,13,16,128]{3,2,0,1:T(8,128)S(1)}, f32[3,13,16,128]{3,2,0,1:T(8,128)}, u32[]{:S(2)}) copy-start(f32[3,13,16,128]{3,2,0,1:T(8,128)} %copy-done.4) | copy-start | bytes 958468
  95.7 20.2 %copy-start.18 = (s32[3,25]{1,0:T(4,128)S(1)}, s32[3,25]{1,0:T(4,128)}, u32[]{:S(2)}) copy-start(s32[3,25]{1,0:T(4,128)} %param.71) | copy-start | bytes 904
  98.8 22.1 %collective-permute-start.5 = (f32[3,13,16,128]{3,2,0,1:T(8,128)S(1)}, f32[3,13,16,128]{3,2,0,1:T(8,128)S(1)}, u32[]{:S(2)}, u32[]{:S(2)}) collective-permute-start(f32[3,13,16,128]{3,2,0,1:T(8,128)S(1)} %copy-done), channel_id=1, source_target_pairs={{0,744},{8,752},{16,760},{24,0},{32,8},{40,16},{48,24},{56,32},{64... | collective-permute-start | bytes 958472 | tf_op jit(solution)/shard_map/ppermute | solution.py:9
  116.8 50.8 %copy-start.8 = (f32[3,13,16,128]{3,2,0,1:T(8,128)S(1)}, f32[3,13,16,128]{3,2,0,1:T(8,128)}, u32[]{:S(2)}) copy-start(f32[3,13,16,128]{3,2,0,1:T(8,128)} %copy-done.7) | copy-start | bytes 958468
  120.9 0.7 copy-start.16
  121.7 48.0 %copy-start.9 = (f32[3,13,16,128]{3,2,0,1:T(8,128)S(1)}, f32[3,13,16,128]{3,2,0,1:T(8,128)}, u32[]{:S(2)}) copy-start(f32[3,13,16,128]{3,2,0,1:T(8,128)} %get-tuple-element.391) | copy-start | bytes 958468
  122.7 46.4 %copy-start.10 = (f32[3,13,16,128]{3,2,0,1:T(8,128)S(1)}, f32[3,13,16,128]{3,2,0,1:T(8,128)}, u32[]{:S(2)}) copy-start(f32[3,13,16,128]{3,2,0,1:T(8,128)} %get-tuple-element.392) | copy-start | bytes 958468
  163.0 6.1 %copy-start.2 = (f32[3,19,128,128]{3,2,1,0:T(8,128)S(1)}, f32[3,19,128,128]{3,2,1,0:T(8,128)}, u32[]{:S(2)}) copy-start(f32[3,19,128,128]{3,2,1,0:T(8,128)} %all-gather.5.cloned.1.call-done) | copy-start | bytes 11206660
  170.7 3.2 %copy-start.12 = (f32[3,13,16,128]{3,2,0,1:T(8,128)S(1)}, f32[3,13,16,128]{3,2,0,1:T(8,128)}, u32[]{:S(2)}) copy-start(f32[3,13,16,128]{3,2,0,1:T(8,128)} %get-tuple-element.390) | copy-start | bytes 958468
  171.2 3.2 %copy-start.11 = (f32[3,13,16,128]{3,2,0,1:T(8,128)S(1)}, f32[3,13,16,128]{3,2,0,1:T(8,128)}, u32[]{:S(2)}) copy-start(f32[3,13,16,128]{3,2,0,1:T(8,128)} %get-tuple-element.389) | copy-start | bytes 958468
  171.8 3.2 %copy-start.6 = (f32[3,13,16,128]{3,2,0,1:T(8,128)S(1)}, f32[3,13,16,128]{3,2,0,1:T(8,128)}, u32[]{:S(2)}) copy-start(f32[3,13,16,128]{3,2,0,1:T(8,128)} %copy-done.4) | copy-start | bytes 958468
  172.3 3.2 %copy-start.13 = (f32[6,13,16,128]{3,2,0,1:T(8,128)S(1)}, f32[6,13,16,128]{3,2,0,1:T(8,128)}, u32[]{:S(2)}) copy-start(f32[6,13,16,128]{3,2,0,1:T(8,128)} %get-tuple-element.413) | copy-start | bytes 1916932
  173.4 2.9 %copy-start.17 = (f32[3,13,16,128]{3,2,0,1:T(8,128)S(1)}, f32[3,13,16,128]{3,2,0,1:T(8,128)}, u32[]{:S(2)}) copy-start(f32[3,13,16,128]{3,2,0,1:T(8,128)} %copy-done.16) | copy-start | bytes 958468
  173.9 2.8 %copy-start.1 = (f32[3,19,16,128]{3,2,1,0:T(8,128)S(1)}, f32[3,19,16,128]{3,2,1,0:T(8,128)}, u32[]{:S(2)}) copy-start(f32[3,19,16,128]{3,2,1,0:T(8,128)} %broadcast_multiply_fusion) | copy-start | bytes 1400836
Sparse Core Ops, SparseCore 0:
  9.7 77.8 all-gather.2
  99.0 63.9 all-gather.4
where the time goes:
time: 186 us; the launch traced here: 185 us
  waiting for transfers between devices  87.4 us (47%)
  starting transfers between devices  48.8 us (26%)
  matrix products  23.4 us (13%)
  between operations  14 us (8%)
  other arithmetic  6.38 us (3%)
  local copies, waits for them, and re-layouts  4.58 us (2%)
    ppermute x6, starting transfers between devices, from_behind(): lax.ppermute(array, axis, [(i, (i + by) % devices) for i in range(devices)])  48.8 us
    all_gather x1, waiting for transfers between devices, body(): full_square = lax.all_gather(square, 'col', axis=2, tiled=True)  40.3 us
    ppermute x6, waiting for transfers between devices, from_behind(): lax.ppermute(array, axis, [(i, (i + by) % devices) for i in range(devices)])  28.7 us
    dot_general x32, matrix products, band_apply(): jnp.einsum('gojk,gki->goji', right_slab, left_band[:, offset_left + half_...  23.4 us
    all_gather x1, waiting for transfers between devices, body(): full_band = lax.all_gather(masked, 'col', axis=2, tiled=True)  18.4 us
  transfers between devices with their start and end apart: 8, of which 7 were waited for; matrix products, arithmetic and copies ran while one was open for 3% of the time, Pallas kernels for 0%

commit v1 on v0

v1 whole, which is shorter than its diff:
```python
import jax
import jax.numpy as jnp
from jax import lax
from jax.experimental import pallas as pl
from jax.experimental.pallas import tpu as pltpu
from jax.sharding import PartitionSpec as P

Z, X, YH, YL, CORES = 12, 4, 2, 4, 2
CHAIN = Z * X
AXES = ("row", "col")
F32, BF16 = jnp.float32, jnp.bfloat16
VMEM_LIMIT = 48 * 1024 * 1024


def pairs(target):
    listed = []
    for c in range(CHAIN):
        for yh in range(YH):
            for yl in range(YL):
                for core in range(CORES):
                    to = target(c, yh, yl, core)
                    if to is not None:
                        tc, th, tl, tk = to
                        source = ((c * YH + yh) * YL + yl) * CORES + core
                        listed.append((source, (((tc % CHAIN) * YH + th) * YL + tl) * CORES + tk))
    return listed


UP = pairs(lambda c, h, l, k: (c + 1, h, l, k))
DOWN = pairs(lambda c, h, l, k: (c - 1, h, l, k))
ACROSS = pairs(lambda c, h, l, k: (c + 1 if h == 0 else c - 1, h, l, k))
AGAINST = pairs(lambda c, h, l, k: (c - 1 if h == 0 else c + 1, h, l, k))
FLIP = pairs(lambda c, h, l, k: (c, 1 - h, 3 - l, k))
MIRROR = pairs(lambda c, h, l, k: (c, h, 3 - l, k))
NEXT = pairs(lambda c, h, l, k: (c, h, l ^ 1, k))
SIBLING = pairs(lambda c, h, l, k: (c, h, l, 1 - k))


def send(array, which):
    return lax.ppermute(array, AXES, which)


def split(values):
    high = values.astype(BF16)
    return high, (values - high.astype(F32)).astype(BF16)


def mask_kernel(mask_ref, x_ref, out_ref):
    for g in range(x_ref.shape[0]):
        for d in range(x_ref.shape[1]):
            out_ref[g, d] = x_ref[g, d] * mask_ref[g, d].astype(F32)


def fill_window(place_ref, rows, first_place, high_ref, low_ref):
    for n, ref in enumerate(rows):
        base = place_ref[first_place + n] * 3
        for j in range(3):
            high, low = split(ref[j].reshape(high_ref.shape[1:]))
            high_ref[base + j] = high
            low_ref[base + j] = low


def fill_right(place_ref, slabs, first_place, pad, high_ref, low_ref):
    count = slabs[0].shape[1]
    blank = jnp.zeros((pad, 128, 128), BF16)
    for g in range(3):
        for ref in (high_ref, low_ref):
            ref[g, 0:pad] = blank
            ref[g, pad + count : 2 * pad + count] = blank
    for n, slab in enumerate(slabs):
        at = pl.ds(pl.multiple_of(place_ref[first_place + n] * 16, 16), 16)
        for g in range(3):
            high, low = split(slab[g])
            high_ref[g, pad : pad + count, at, :] = high
            low_ref[g, pad : pad + count, at, :] = low


def accumulate(window_rows, window_high, window_low, right_high, right_low, total_ref):
    total_ref[...] = jnp.zeros_like(total_ref)

    @pl.loop(0, window_rows)
    def _(r):
        left_high, left_low = window_high[r], window_low[r]
        highs = [right_high[g, r + 2 - g] for g in range(3)]
        lows = [right_low[g, r + 2 - g] for g in range(3)]
        wide_high = jnp.concatenate(highs, axis=1)
        wide_low = jnp.concatenate(lows, axis=1)
        product = jnp.dot(
            jnp.concatenate([left_high, left_low], axis=1),
            jnp.concatenate([wide_high, wide_high], axis=0),
            preferred_element_type=F32,
        ) + jnp.dot(left_high, wide_low, preferred_element_type=F32)
        product = product.reshape(13, 16, 384)
        for g in range(3):
            total_ref[g, pl.ds(r + 2 - g, 13)] += product[:, :, 128 * g : 128 * (g + 1)]


def square_kernel(place_ref, mask_ref, *refs):
    rows, slabs = refs[0:5], refs[5:13]
    out_ref, window_high, window_low, right_high, right_low, total_ref = refs[13:]
    fill_window(place_ref, rows, 0, window_high, window_low)
    fill_right(place_ref, slabs, 5, 2, right_high, right_low)
    accumulate(15, window_high, window_low, right_high, right_low, total_ref)
    for g in range(3):
        for e in range(19):
            out_ref[g, e] = total_ref[g, e + 5] * mask_ref[g, e].astype(F32)


def cube_kernel(place_ref, mask_ref, *refs):
    rows, slabs = refs[0:7], refs[7:15]
    out_ref, window_high, window_low, right_high, right_low, total_ref = refs[15:]
    own = slabs[0]
    fill_window(place_ref, rows, 0, window_high, window_low)
    fill_right(place_ref, slabs, 7, 2, right_high, right_low)
    accumulate(21, window_high, window_low, right_high, right_low, total_ref)
    for g in range(3):
        for f in range(25):
            value = -2.0 * total_ref[g, f + 5]
            if 3 <= f < 22:
                value = 3.0 * own[g, f - 3] + value
            out_ref[g, f] = value * mask_ref[g, f].astype(F32)


SMEM = pl.BlockSpec(memory_space=pltpu.SMEM)
VMEM = pl.BlockSpec(memory_space=pltpu.VMEM)


def banded(kernel, places, mask, arrays, window_rows, blocks_right, blocks_out, flops):
    return pl.pallas_call(
        kernel,
        out_shape=jax.ShapeDtypeStruct((3, mask.shape[1], 16, 128), F32),
        in_specs=[SMEM, SMEM] + [VMEM] * len(arrays),
        out_specs=VMEM,
        scratch_shapes=[
            pltpu.VMEM((window_rows, 13 * 16, 128), BF16),
            pltpu.VMEM((window_rows, 13 * 16, 128), BF16),
            pltpu.VMEM((3, blocks_right + 4, 128, 128), BF16),
            pltpu.VMEM((3, blocks_right + 4, 128, 128), BF16),
            pltpu.VMEM((3, blocks_out, 16, 128), F32),
        ],
        compiler_params=pltpu.CompilerParams(vmem_limit_bytes=VMEM_LIMIT),
        cost_estimate=pl.CostEstimate(
            flops=flops, bytes_accessed=4 * sum(a.size for a in arrays), transcendentals=0
        ),
    )(places, mask, *arrays)


def body(x_band, x_mask, sq_mask, cube_mask):
    high_y = lax.axis_index("row") % 2
    low_y, core = lax.axis_index("col") // 2, lax.axis_index("col") % 2

    own = pl.pallas_call(
        mask_kernel,
        out_shape=jax.ShapeDtypeStruct(x_band.shape, F32),
        in_specs=[SMEM, VMEM],
        out_specs=VMEM,
    )(x_mask, x_band)

    pair_m = send(own, FLIP)
    own_m = send(own, MIRROR)
    below_o, above_o = send(own, UP), send(own, DOWN)
    pair_o = send(pair_m, MIRROR)
    next_o, next_m = send(own, NEXT), send(own_m, NEXT)
    below_m, above_m = send(own_m, UP), send(own_m, DOWN)
    beside_m = send(pair_m, ACROSS)
    beside_o = send(pair_o, ACROSS)
    far_a = send(pair_o, AGAINST)
    far_b = send(beside_o, ACROSS)

    chips = jnp.stack([low_y, 3 - low_y, low_y ^ 1, (3 - low_y) ^ 1])
    orbitals = jnp.concatenate([2 * chips + core, 2 * chips + 1 - core])
    pair_at, beside_at = 3 - 2 * high_y, 1 + 2 * high_y
    square_rows = jnp.stack([jnp.int32(0), jnp.int32(4), jnp.int32(2), pair_at, beside_at])
    square_places = jnp.concatenate([square_rows, orbitals]).astype(jnp.int32)

    left = [own, own_m, next_o, next_m]
    left += [send(a, SIBLING) for a in left]
    square_flops = 2 * 3 * 45 * 208 * 128 * 128

    def square_of(rows):
        return banded(square_kernel, square_places, sq_mask, rows + left, 15, 13, 29, square_flops)

    square_m = square_of([below_m, above_m, own_m, pair_m, beside_m])
    square_o = square_of([below_o, above_o, own, pair_o, beside_o])

    right = [square_o, square_m, send(square_o, NEXT), send(square_m, NEXT)]
    right += [send(a, SIBLING) for a in right]
    cube_rows = [1, 5, 3, pair_at + 1, beside_at + 1, 6 - 6 * high_y, 6 * high_y]
    cube_places = jnp.concatenate([jnp.stack([jnp.int32(v) for v in cube_rows]), orbitals])
    cube_places = cube_places.astype(jnp.int32)
    rows = [below_o, above_o, own, pair_o, beside_o, far_a, far_b]
    return banded(
        cube_kernel, cube_places, cube_mask, rows + right, 21, 19, 35, 2 * 3 * 63 * 208 * 128 * 128
    )


def solution(mesh):
    return jax.shard_map(
        body,
        mesh=mesh,
        in_specs=(P("row", None, "col", None), P("row", None), P("row", None), P("row", None)),
        out_specs=P("row", None, "col", None),
        check_vma=False,
    )
```

time: 186 us -> 144 us (0.77)
  waiting for transfers between devices: 87.4 us -> 27.4 us
  starting transfers between devices: 48.8 us -> 86.9 us
  matrix products: 23.4 us -> 0 us
  Pallas kernels: 0 us -> 22.5 us
  between operations: 14 us -> 0.44 us
  other arithmetic: 6.38 us -> 0.08 us
    all_gather x2 -> x0, waiting for transfers between devices: 58.6 us -> none  [the longest x1 40.3 us: body(): full_square = lax.all_gather(square, 'col', axis=2, tiled=True)]
    ppermute x6 -> x23, starting transfers between devices: 48.8 us -> 86.9 us  [send(): return lax.ppermute(array, AXES, which)]
    dot_general x32 -> x0, matrix products: 23.4 us -> none  [band_apply(): jnp.einsum('gojk,gki->goji', right_slab, left_band[:, offset_left + half_...]
    pallas_call x0 -> x4, Pallas kernels: none -> 22.5 us  [the longest x3 20.8 us: banded(): pl.pallas_call(kernel, out_shape=jax.ShapeDtypeStruct((3, mask.shape[1],...]
    mul x3 -> x0, other arithmetic: 3.69 us -> none  [the longest x1 1.8 us: body(): masked = x_band * x_mask[:, :, None, None].astype(jnp.float32)]
    unnamed x40 -> x20, local copies, waits for them, and re-layouts: 2.39 us -> 5.36 us
    slice x2 -> x0, local copies, waits for them, and re-layouts: 1.92 us -> none  [band_apply(): window[first_row:first_row + own_rows, first_slot:first_slot + highest -...]
    ppermute x6 -> x23, waiting for transfers between devices: 28.7 us -> 27.4 us  [send(): return lax.ppermute(array, AXES, which)]
  transfers between devices with their start and end apart: 8 -> 23, of which waited for: 7 -> 2; matrix products, arithmetic and copies ran while one was open for 3% -> 0% of each run, Pallas kernels for 0% -> 8%
where the time goes in v1:
time: 144 us; the launch traced here: 143 us
  starting transfers between devices  86.9 us (60%)
  waiting for transfers between devices  27.4 us (19%)
  Pallas kernels  22.5 us (16%)
  local copies, waits for them, and re-layouts  5.53 us (4%)
    ppermute x23, starting transfers between devices, send(): return lax.ppermute(array, AXES, which)  86.9 us
    ppermute x23, waiting for transfers between devices, send(): return lax.ppermute(array, AXES, which)  27.4 us
    pallas_call x3, Pallas kernels, banded(): pl.pallas_call(kernel, out_shape=jax.ShapeDtypeStruct((3, mask.shape[1],...  20.8 us
    unnamed x20, local copies, waits for them, and re-layouts  5.36 us
  transfers between devices with their start and end apart: 23, of which 2 were waited for; matrix products, arithmetic and copies ran while one was open for 0% of the time, Pallas kernels for 8%

profile of v1, /device:TPU:1, one launch (start us, length us, event | category | flops | bytes accessed | tf_op | source)
XLA Modules:
  0.0 142.9 jit_solution(7430125093065538292)
XLA Ops:
  0.0 1.7 %shard_map.46.refs_2_.refs_5_ = f32[3,13,16,128]{3,2,1,0:T(8,128)} custom-call(s32[3,13]{1,0:T(4,128)} %mask_ref.4, f32[3,13,16,128]{3,2,1,0:T(8,128)} %x_ref.1), custom_call_target="tpu_custom_call" | custom-call | tf_op jit(solution)/shard_map/pallas_call | solution.py:152
  1.7 12.4 %collective-permute-start.10 = (f32[3,13,16,128]{3,2,1,0:T(8,128)}, f32[3,13,16,128]{3,2,1,0:T(8,128)S(1)}, u32[]{:S(2)}, u32[]{:S(2)}) collective-permute-start(f32[3,13,16,128]{3,2,1,0:T(8,128)} %shard_map.46.refs_2_.refs_5_), channel_id=1, source_target_pairs={{0,1},{1,0},{2,3},{3,2},{4,5},{5,4},{6,7},{7,6},{8,9},{9,8},{10,11... | collective-permute-start | bytes 958472 | tf_op jit(solution)/shard_map/ppermute | solution.py:40
  14.1 1.9 %collective-permute-start.8 = (f32[3,13,16,128]{3,2,1,0:T(8,128)}, f32[3,13,16,128]{3,2,1,0:T(8,128)S(1)}, u32[]{:S(2)}, u32[]{:S(2)}) collective-permute-start(f32[3,13,16,128]{3,2,1,0:T(8,128)} %shard_map.46.refs_2_.refs_5_), channel_id=1, source_target_pairs={{0,2},{1,3},{2,0},{3,1},{4,6},{5,7},{6,4},{7,5},{8,10},{9,11},{10,... | collective-permute-start | bytes 958472 | tf_op jit(solution)/shard_map/ppermute | solution.py:40
  16.1 1.9 %collective-permute-start.7 = (f32[3,13,16,128]{3,2,1,0:T(8,128)}, f32[3,13,16,128]{3,2,1,0:T(8,128)S(1)}, u32[]{:S(2)}, u32[]{:S(2)}) collective-permute-start(f32[3,13,16,128]{3,2,1,0:T(8,128)} %shard_map.46.refs_2_.refs_5_), channel_id=1, source_target_pairs={{0,6},{1,7},{2,4},{3,5},{4,2},{5,3},{6,0},{7,1},{8,14},{9,15},{10,... | collective-permute-start | bytes 958472 | tf_op jit(solution)/shard_map/ppermute | solution.py:40
  18.0 1.9 %collective-permute-start.2 = (f32[3,13,16,128]{3,2,1,0:T(8,128)}, f32[3,13,16,128]{3,2,1,0:T(8,128)}, u32[]{:S(2)}, u32[]{:S(2)}) collective-permute-start(f32[3,13,16,128]{3,2,1,0:T(8,128)} %shard_map.46.refs_2_.refs_5_), channel_id=1, source_target_pairs={{0,14},{1,15},{2,12},{3,13},{4,10},{5,11},{6,8},{7,9},{8,6},{9,7},... | collective-permute-start | bytes 958472 | tf_op jit(solution)/shard_map/ppermute | solution.py:40
  19.9 13.7 %collective-permute-start.1 = (f32[3,13,16,128]{3,2,1,0:T(8,128)}, f32[3,13,16,128]{3,2,1,0:T(8,128)S(1)}, u32[]{:S(2)}, u32[]{:S(2)}) collective-permute-start(f32[3,13,16,128]{3,2,1,0:T(8,128)} %shard_map.46.refs_2_.refs_5_), channel_id=1, source_target_pairs={{0,752},{1,753},{2,754},{3,755},{4,756},{5,757},{6,758},{7,759},{8... | collective-permute-start | bytes 958472 | tf_op jit(solution)/shard_map/ppermute | solution.py:40
  33.6 1.9 %collective-permute-start = (f32[3,13,16,128]{3,2,1,0:T(8,128)}, f32[3,13,16,128]{3,2,1,0:T(8,128)S(1)}, u32[]{:S(2)}, u32[]{:S(2)}) collective-permute-start(f32[3,13,16,128]{3,2,1,0:T(8,128)} %shard_map.46.refs_2_.refs_5_), channel_id=1, source_target_pairs={{0,16},{1,17},{2,18},{3,19},{4,20},{5,21},{6,22},{7,23},{8,24},{9,... | collective-permute-start | bytes 958472 | tf_op jit(solution)/shard_map/ppermute | solution.py:40
  35.6 3.0 %collective-permute-start.12 = (f32[3,13,16,128]{3,2,1,0:T(8,128)S(1)}, f32[3,13,16,128]{3,2,1,0:T(8,128)S(1)}, u32[]{:S(2)}, u32[]{:S(2)}) collective-permute-start(f32[3,13,16,128]{3,2,1,0:T(8,128)S(1)} %collective-permute-done.8.refs_7_), channel_id=1, source_target_pairs={{0,1},{1,0},{2,3},{3,2},{4,5},{5,4},{6,7},{7,6},{8,9},{9,8},{10,11... | collective-permute-start | bytes 958472 | tf_op jit(solution)/shard_map/ppermute | solution.py:40
  38.6 0.0 collective-permute-done.7.refs_6_.refs_2_
  38.6 1.9 %collective-permute-start.11 = (f32[3,13,16,128]{3,2,1,0:T(8,128)S(1)}, f32[3,13,16,128]{3,2,1,0:T(8,128)S(1)}, u32[]{:S(2)}, u32[]{:S(2)}) collective-permute-start(f32[3,13,16,128]{3,2,1,0:T(8,128)S(1)} %collective-permute-done.7.refs_6_.refs_2_), channel_id=1, source_target_pairs={{0,1},{1,0},{2,3},{3,2},{4,5},{5,4},{6,7},{7,6},{8,9},{9,8},{10,11... | collective-permute-start | bytes 958472 | tf_op jit(solution)/shard_map/ppermute | solution.py:40
  40.6 0.0 collective-permute-done.2.refs_3_
  40.6 3.0 %collective-permute-start.9 = (f32[3,13,16,128]{3,2,1,0:T(8,128)S(1)}, f32[3,13,16,128]{3,2,1,0:T(8,128)S(1)}, u32[]{:S(2)}, u32[]{:S(2)}) collective-permute-start(f32[3,13,16,128]{3,2,1,0:T(8,128)S(1)} %collective-permute-done.7.refs_6_.refs_2_), channel_id=1, source_target_pairs={{0,2},{1,3},{2,0},{3,1},{4,6},{5,7},{6,4},{7,5},{8,10},{9,11},{10,... | collective-permute-start | bytes 958472 | tf_op jit(solution)/shard_map/ppermute | solution.py:40
  43.5 0.0 collective-permute-done.1.refs_1_
  43.6 4.0 %collective-permute-start.3 = (f32[3,13,16,128]{3,2,1,0:T(8,128)}, f32[3,13,16,128]{3,2,1,0:T(8,128)S(1)}, u32[]{:S(2)}, u32[]{:S(2)}) collective-permute-start(f32[3,13,16,128]{3,2,1,0:T(8,128)} %collective-permute-done.2.refs_3_), channel_id=1, source_target_pairs={{0,6},{1,7},{2,4},{3,5},{4,2},{5,3},{6,0},{7,1},{8,14},{9,15},{10,... | collective-permute-start | bytes 958472 | tf_op jit(solution)/shard_map/ppermute | solution.py:40
  47.5 0.0 collective-permute-done.refs_0_
  47.6 9.7 %collective-permute-start.15 = (f32[3,13,16,128]{3,2,1,0:T(8,128)S(1)}, f32[3,13,16,128]{3,2,1,0:T(8,128)}, u32[]{:S(2)}, u32[]{:S(2)}) collective-permute-start(f32[3,13,16,128]{3,2,1,0:T(8,128)S(1)} %collective-permute-done.7.refs_6_.refs_2_), channel_id=1, source_target_pairs={{0,752},{1,753},{2,754},{3,755},{4,756},{5,757},{6,758},{7,759},{8... | collective-permute-start | bytes 958472 | tf_op jit(solution)/shard_map/ppermute | solution.py:40
  57.3 1.9 %collective-permute-start.14 = (f32[3,13,16,128]{3,2,1,0:T(8,128)S(1)}, f32[3,13,16,128]{3,2,1,0:T(8,128)}, u32[]{:S(2)}, u32[]{:S(2)}) collective-permute-start(f32[3,13,16,128]{3,2,1,0:T(8,128)S(1)} %collective-permute-done.7.refs_6_.refs_2_), channel_id=1, source_target_pairs={{0,16},{1,17},{2,18},{3,19},{4,20},{5,21},{6,22},{7,23},{8,24},{9,... | collective-permute-start | bytes 958472 | tf_op jit(solution)/shard_map/ppermute | solution.py:40
  59.2 1.9 %collective-permute-start.16 = (f32[3,13,16,128]{3,2,1,0:T(8,128)}, f32[3,13,16,128]{3,2,1,0:T(8,128)}, u32[]{:S(2)}, u32[]{:S(2)}) collective-permute-start(f32[3,13,16,128]{3,2,1,0:T(8,128)} %collective-permute-done.2.refs_3_), channel_id=1, source_target_pairs={{0,16},{1,17},{2,18},{3,19},{4,20},{5,21},{6,22},{7,23},{8,760},{9... | collective-permute-start | bytes 958472 | tf_op jit(solution)/shard_map/ppermute | solution.py:40
  61.2 3.5 %collective-permute-start.13 = (f32[3,13,16,128]{3,2,1,0:T(8,128)S(1)}, f32[3,13,16,128]{3,2,1,0:T(8,128)S(1)}, u32[]{:S(2)}, u32[]{:S(2)}) collective-permute-start(f32[3,13,16,128]{3,2,1,0:T(8,128)S(1)} %collective-permute-done.9.refs_8_), channel_id=1, source_target_pairs={{0,1},{1,0},{2,3},{3,2},{4,5},{5,4},{6,7},{7,6},{8,9},{9,8},{10,11... | collective-permute-start | bytes 958472 | tf_op jit(solution)/shard_map/ppermute | solution.py:40
  64.7 0.0 collective-permute-done.3.refs_3_
  64.8 1.9 %collective-permute-start.4 = (f32[3,13,16,128]{3,2,1,0:T(8,128)S(1)}, f32[3,13,16,128]{3,2,1,0:T(8,128)}, u32[]{:S(2)}, u32[]{:S(2)}) collective-permute-start(f32[3,13,16,128]{3,2,1,0:T(8,128)S(1)} %collective-permute-done.3.refs_3_), channel_id=1, source_target_pairs={{0,16},{1,17},{2,18},{3,19},{4,20},{5,21},{6,22},{7,23},{8,760},{9... | collective-permute-start | bytes 958472 | tf_op jit(solution)/shard_map/ppermute | solution.py:40
  66.7 0.1 add_subtract_fusion
  66.8 0.1 concatenate.10.place_ref
  66.9 0.7 copy-done.6
  67.6 16.1 %collective-permute-done.4.refs_4_ = f32[3,13,16,128]{3,2,1,0:T(8,128)} collective-permute-done((f32[3,13,16,128]{3,2,1,0:T(8,128)S(1)}, f32[3,13,16,128]{3,2,1,0:T(8,128)}, u32[]{:S(2)}, u32[]{:S(2)}) %collective-permute-start.4) | collective-permute-done | bytes 319520 | tf_op jit(solution)/shard_map/ppermute | solution.py:40
  83.7 1.0 copy-done
  84.7 1.0 copy-done.7
  85.7 5.7 %shard_map.47.refs_7_ = f32[3,19,16,128]{3,2,1,0:T(8,128)S(1)} custom-call(s32[13]{0:T(128)S(1)} %concatenate.10.place_ref, s32[3,19]{1,0:T(4,128)S(1)} %copy-done.8, f32[3,13,16,128]{3,2,1,0:T(8,128)S(1)} %collective-permute-done.refs_0_, f32[3,13,16,128]{3,2,1,0:T(8,128)S(1)} %collective-permute-done.1.refs_1_, f32[3,13,16,128]{3,2,1,0:T(8,128)S(1)} %copy-done, ...), custom_call_target="tpu_custom_call" | custom-call | flops 920125440 | bytes 4153344 | tf_op jit(solution)/shard_map/pallas_call | solution.py:129
  91.4 0.7 copy-done.2
  92.1 2.0 %collective-permute-start.17 = (f32[3,19,16,128]{3,2,1,0:T(8,128)S(1)}, f32[3,19,16,128]{3,2,1,0:T(8,128)}, u32[]{:S(2)}, u32[]{:S(2)}) collective-permute-start(f32[3,19,16,128]{3,2,1,0:T(8,128)S(1)} %shard_map.47.refs_7_), channel_id=1, source_target_pairs={{0,2},{1,3},{2,0},{3,1},{4,6},{5,7},{6,4},{7,5},{8,10},{9,11},{10,... | collective-permute-start | bytes 1400840 | tf_op jit(solution)/shard_map/ppermute | solution.py:40
  94.1 0.0 collective-permute-done.14.refs_0_
  94.2 0.0 collective-permute-done.16.refs_4_
  94.2 1.0 copy-done.3
  95.1 1.0 copy-done.5
  96.1 6.0 %shard_map.48.refs_8_ = f32[3,19,16,128]{3,2,1,0:T(8,128)S(1)} custom-call(s32[13]{0:T(128)S(1)} %concatenate.10.place_ref, s32[3,19]{1,0:T(4,128)S(1)} %copy-done.8, f32[3,13,16,128]{3,2,1,0:T(8,128)} %collective-permute-done.14.refs_0_, f32[3,13,16,128]{3,2,1,0:T(8,128)} %collective-permute-done.15.refs_1_, ...), custom_call_target="tpu_custom_call" | custom-call | flops 920125440 | bytes 4153344 | tf_op jit(solution)/shard_map/pallas_call | solution.py:129
  102.1 3.4 %collective-permute-start.18 = (f32[3,19,16,128]{3,2,1,0:T(8,128)S(1)}, f32[3,19,16,128]{3,2,1,0:T(8,128)S(1)}, u32[]{:S(2)}, u32[]{:S(2)}) collective-permute-start(f32[3,19,16,128]{3,2,1,0:T(8,128)S(1)} %shard_map.48.refs_8_), channel_id=1, source_target_pairs={{0,2},{1,3},{2,0},{3,1},{4,6},{5,7},{6,4},{7,5},{8,10},{9,11},{10,... | collective-permute-start | bytes 1400840 | tf_op jit(solution)/shard_map/ppermute | solution.py:40
  105.5 1.9 %collective-permute-start.5 = (f32[3,13,16,128]{3,2,1,0:T(8,128)S(1)}, f32[3,13,16,128]{3,2,1,0:T(8,128)S(1)}, u32[]{:S(2)}, u32[]{:S(2)}) collective-permute-start(f32[3,13,16,128]{3,2,1,0:T(8,128)S(1)} %collective-permute-done.3.refs_3_), channel_id=1, source_target_pairs={{0,752},{1,753},{2,754},{3,755},{4,756},{5,757},{6,758},{7,759},{8... | collective-permute-start | bytes 958472 | tf_op jit(solution)/shard_map/ppermute | solution.py:40
  107.4 5.0 %collective-permute-start.19 = (f32[3,19,16,128]{3,2,1,0:T(8,128)S(1)}, f32[3,19,16,128]{3,2,1,0:T(8,128)S(1)}, u32[]{:S(2)}, u32[]{:S(2)}) collective-permute-start(f32[3,19,16,128]{3,2,1,0:T(8,128)S(1)} %shard_map.47.refs_7_), channel_id=1, source_target_pairs={{0,1},{1,0},{2,3},{3,2},{4,5},{5,4},{6,7},{7,6},{8,9},{9,8},{10,11... | collective-permute-start | bytes 1400840 | tf_op jit(solution)/shard_map/ppermute | solution.py:40
  112.4 1.9 %collective-permute-start.20 = (f32[3,19,16,128]{3,2,1,0:T(8,128)S(1)}, f32[3,19,16,128]{3,2,1,0:T(8,128)}, u32[]{:S(2)}, u32[]{:S(2)}) collective-permute-start(f32[3,19,16,128]{3,2,1,0:T(8,128)S(1)} %shard_map.48.refs_8_), channel_id=1, source_target_pairs={{0,1},{1,0},{2,3},{3,2},{4,5},{5,4},{6,7},{7,6},{8,9},{9,8},{10,11... | collective-permute-start | bytes 1400840 | tf_op jit(solution)/shard_map/ppermute | solution.py:40
  114.4 0.0 collective-permute-done.17.refs_9_
  114.4 2.4 %collective-permute-start.21 = (f32[3,19,16,128]{3,2,1,0:T(8,128)}, f32[3,19,16,128]{3,2,1,0:T(8,128)}, u32[]{:S(2)}, u32[]{:S(2)}) collective-permute-start(f32[3,19,16,128]{3,2,1,0:T(8,128)} %collective-permute-done.17.refs_9_), channel_id=1, source_target_pairs={{0,1},{1,0},{2,3},{3,2},{4,5},{5,4},{6,7},{7,6},{8,9},{9,8},{10,11... | collective-permute-start | bytes 1400840 | tf_op jit(solution)/shard_map/ppermute | solution.py:40
  116.8 2.3 %collective-permute-start.22 = (f32[3,19,16,128]{3,2,1,0:T(8,128)S(1)}, f32[3,19,16,128]{3,2,1,0:T(8,128)}, u32[]{:S(2)}, u32[]{:S(2)}) collective-permute-start(f32[3,19,16,128]{3,2,1,0:T(8,128)S(1)} %collective-permute-done.18.refs_10_), channel_id=1, source_target_pairs={{0,1},{1,0},{2,3},{3,2},{4,5},{5,4},{6,7},{7,6},{8,9},{9,8},{10,11... | collective-permute-start | bytes 1400840 | tf_op jit(solution)/shard_map/ppermute | solution.py:40
  119.1 3.2 %collective-permute-start.6 = (f32[3,13,16,128]{3,2,1,0:T(8,128)}, f32[3,13,16,128]{3,2,1,0:T(8,128)}, u32[]{:S(2)}, u32[]{:S(2)}) collective-permute-start(f32[3,13,16,128]{3,2,1,0:T(8,128)} %collective-permute-done.4.refs_4_), channel_id=1, source_target_pairs={{0,16},{1,17},{2,18},{3,19},{4,20},{5,21},{6,22},{7,23},{8,760},{9... | collective-permute-start | bytes 958472 | tf_op jit(solution)/shard_map/ppermute | solution.py:40
  122.4 0.0 copy-start.9
  122.4 0.1 concatenate.9.place_ref
  122.5 11.3 %collective-permute-done.6.refs_6_ = f32[3,13,16,128]{3,2,1,0:T(8,128)} collective-permute-done((f32[3,13,16,128]{3,2,1,0:T(8,128)}, f32[3,13,16,128]{3,2,1,0:T(8,128)}, u32[]{:S(2)}, u32[]{:S(2)}) %collective-permute-start.6) | collective-permute-done | bytes 319520 | tf_op jit(solution)/shard_map/ppermute | solution.py:40
  133.8 0.0 collective-permute-done.19.refs_11_
  133.8 9.1 %shard_map.49 = f32[3,25,16,128]{3,2,1,0:T(8,128)} custom-call(s32[15]{0:T(128)S(1)} %concatenate.9.place_ref, s32[3,25]{1,0:T(4,128)S(1)} %copy-done.9, f32[3,13,16,128]{3,2,1,0:T(8,128)S(1)} %collective-permute-done.refs_0_, f32[3,13,16,128]{3,2,1,0:T(8,128)S(1)} %collective-permute-done.1.refs_1_, f32[3,13,16,128]{3,2,1,0:T(8,128)S(1)} %copy-done.1, ...), custom_call_target="tpu_custom_call" | custom-call | flops 1288175616 | bytes 5971968 | tf_op jit(solution)/shard_map/pallas_call | solution.py:129
  (26 shorter events, 0.1 us)
Async XLA Ops:
  1.7 31.9 %collective-permute-start.10 = (f32[3,13,16,128]{3,2,1,0:T(8,128)}, f32[3,13,16,128]{3,2,1,0:T(8,128)S(1)}, u32[]{:S(2)}, u32[]{:S(2)}) collective-permute-start(f32[3,13,16,128]{3,2,1,0:T(8,128)} %shard_map.46.refs_2_.refs_5_), channel_id=1, source_target_pairs={{0,1},{1,0},{2,3},{3,2},{4,5},{5,4},{6,7},{7,6},{8,9},{9,8},{10,11... | collective-permute-start | bytes 958472 | tf_op jit(solution)/shard_map/ppermute | solution.py:40
  14.1 21.4 %collective-permute-start.8 = (f32[3,13,16,128]{3,2,1,0:T(8,128)}, f32[3,13,16,128]{3,2,1,0:T(8,128)S(1)}, u32[]{:S(2)}, u32[]{:S(2)}) collective-permute-start(f32[3,13,16,128]{3,2,1,0:T(8,128)} %shard_map.46.refs_2_.refs_5_), channel_id=1, source_target_pairs={{0,2},{1,3},{2,0},{3,1},{4,6},{5,7},{6,4},{7,5},{8,10},{9,11},{10,... | collective-permute-start | bytes 958472 | tf_op jit(solution)/shard_map/ppermute | solution.py:40
  16.1 22.5 %collective-permute-start.7 = (f32[3,13,16,128]{3,2,1,0:T(8,128)}, f32[3,13,16,128]{3,2,1,0:T(8,128)S(1)}, u32[]{:S(2)}, u32[]{:S(2)}) collective-permute-start(f32[3,13,16,128]{3,2,1,0:T(8,128)} %shard_map.46.refs_2_.refs_5_), channel_id=1, source_target_pairs={{0,6},{1,7},{2,4},{3,5},{4,2},{5,3},{6,0},{7,1},{8,14},{9,15},{10,... | collective-permute-start | bytes 958472 | tf_op jit(solution)/shard_map/ppermute | solution.py:40
  18.0 22.6 %collective-permute-start.2 = (f32[3,13,16,128]{3,2,1,0:T(8,128)}, f32[3,13,16,128]{3,2,1,0:T(8,128)}, u32[]{:S(2)}, u32[]{:S(2)}) collective-permute-start(f32[3,13,16,128]{3,2,1,0:T(8,128)} %shard_map.46.refs_2_.refs_5_), channel_id=1, source_target_pairs={{0,14},{1,15},{2,12},{3,13},{4,10},{5,11},{6,8},{7,9},{8,6},{9,7},... | collective-permute-start | bytes 958472 | tf_op jit(solution)/shard_map/ppermute | solution.py:40
  19.9 23.6 %collective-permute-start.1 = (f32[3,13,16,128]{3,2,1,0:T(8,128)}, f32[3,13,16,128]{3,2,1,0:T(8,128)S(1)}, u32[]{:S(2)}, u32[]{:S(2)}) collective-permute-start(f32[3,13,16,128]{3,2,1,0:T(8,128)} %shard_map.46.refs_2_.refs_5_), channel_id=1, source_target_pairs={{0,752},{1,753},{2,754},{3,755},{4,756},{5,757},{6,758},{7,759},{8... | collective-permute-start | bytes 958472 | tf_op jit(solution)/shard_map/ppermute | solution.py:40
  33.6 13.9 %collective-permute-start = (f32[3,13,16,128]{3,2,1,0:T(8,128)}, f32[3,13,16,128]{3,2,1,0:T(8,128)S(1)}, u32[]{:S(2)}, u32[]{:S(2)}) collective-permute-start(f32[3,13,16,128]{3,2,1,0:T(8,128)} %shard_map.46.refs_2_.refs_5_), channel_id=1, source_target_pairs={{0,16},{1,17},{2,18},{3,19},{4,20},{5,21},{6,22},{7,23},{8,24},{9,... | collective-permute-start | bytes 958472 | tf_op jit(solution)/shard_map/ppermute | solution.py:40
  35.6 21.7 %collective-permute-start.12 = (f32[3,13,16,128]{3,2,1,0:T(8,128)S(1)}, f32[3,13,16,128]{3,2,1,0:T(8,128)S(1)}, u32[]{:S(2)}, u32[]{:S(2)}) collective-permute-start(f32[3,13,16,128]{3,2,1,0:T(8,128)S(1)} %collective-permute-done.8.refs_7_), channel_id=1, source_target_pairs={{0,1},{1,0},{2,3},{3,2},{4,5},{5,4},{6,7},{7,6},{8,9},{9,8},{10,11... | collective-permute-start | bytes 958472 | tf_op jit(solution)/shard_map/ppermute | solution.py:40
  38.6 20.6 %collective-permute-start.11 = (f32[3,13,16,128]{3,2,1,0:T(8,128)S(1)}, f32[3,13,16,128]{3,2,1,0:T(8,128)S(1)}, u32[]{:S(2)}, u32[]{:S(2)}) collective-permute-start(f32[3,13,16,128]{3,2,1,0:T(8,128)S(1)} %collective-permute-done.7.refs_6_.refs_2_), channel_id=1, source_target_pairs={{0,1},{1,0},{2,3},{3,2},{4,5},{5,4},{6,7},{7,6},{8,9},{9,8},{10,11... | collective-permute-start | bytes 958472 | tf_op jit(solution)/shard_map/ppermute | solution.py:40
  40.6 20.6 %collective-permute-start.9 = (f32[3,13,16,128]{3,2,1,0:T(8,128)S(1)}, f32[3,13,16,128]{3,2,1,0:T(8,128)S(1)}, u32[]{:S(2)}, u32[]{:S(2)}) collective-permute-start(f32[3,13,16,128]{3,2,1,0:T(8,128)S(1)} %collective-permute-done.7.refs_6_.refs_2_), channel_id=1, source_target_pairs={{0,2},{1,3},{2,0},{3,1},{4,6},{5,7},{6,4},{7,5},{8,10},{9,11},{10,... | collective-permute-start | bytes 958472 | tf_op jit(solution)/shard_map/ppermute | solution.py:40
  43.6 21.2 %collective-permute-start.3 = (f32[3,13,16,128]{3,2,1,0:T(8,128)}, f32[3,13,16,128]{3,2,1,0:T(8,128)S(1)}, u32[]{:S(2)}, u32[]{:S(2)}) collective-permute-start(f32[3,13,16,128]{3,2,1,0:T(8,128)} %collective-permute-done.2.refs_3_), channel_id=1, source_target_pairs={{0,6},{1,7},{2,4},{3,5},{4,2},{5,3},{6,0},{7,1},{8,14},{9,15},{10,... | collective-permute-start | bytes 958472 | tf_op jit(solution)/shard_map/ppermute | solution.py:40
  47.6 46.6 %collective-permute-start.15 = (f32[3,13,16,128]{3,2,1,0:T(8,128)S(1)}, f32[3,13,16,128]{3,2,1,0:T(8,128)}, u32[]{:S(2)}, u32[]{:S(2)}) collective-permute-start(f32[3,13,16,128]{3,2,1,0:T(8,128)S(1)} %collective-permute-done.7.refs_6_.refs_2_), channel_id=1, source_target_pairs={{0,752},{1,753},{2,754},{3,755},{4,756},{5,757},{6,758},{7,759},{8... | collective-permute-start | bytes 958472 | tf_op jit(solution)/shard_map/ppermute | solution.py:40
  57.3 36.8 %collective-permute-start.14 = (f32[3,13,16,128]{3,2,1,0:T(8,128)S(1)}, f32[3,13,16,128]{3,2,1,0:T(8,128)}, u32[]{:S(2)}, u32[]{:S(2)}) collective-permute-start(f32[3,13,16,128]{3,2,1,0:T(8,128)S(1)} %collective-permute-done.7.refs_6_.refs_2_), channel_id=1, source_target_pairs={{0,16},{1,17},{2,18},{3,19},{4,20},{5,21},{6,22},{7,23},{8,24},{9,... | collective-permute-start | bytes 958472 | tf_op jit(solution)/shard_map/ppermute | solution.py:40
  59.2 34.9 %collective-permute-start.16 = (f32[3,13,16,128]{3,2,1,0:T(8,128)}, f32[3,13,16,128]{3,2,1,0:T(8,128)}, u32[]{:S(2)}, u32[]{:S(2)}) collective-permute-start(f32[3,13,16,128]{3,2,1,0:T(8,128)} %collective-permute-done.2.refs_3_), channel_id=1, source_target_pairs={{0,16},{1,17},{2,18},{3,19},{4,20},{5,21},{6,22},{7,23},{8,760},{9... | collective-permute-start | bytes 958472 | tf_op jit(solution)/shard_map/ppermute | solution.py:40
  61.2 30.2 %copy-start.4 = (f32[3,13,16,128]{3,2,1,0:T(8,128)}, f32[3,13,16,128]{3,2,1,0:T(8,128)S(1)}, u32[]{:S(2)}) copy-start(f32[3,13,16,128]{3,2,1,0:T(8,128)S(1)} %collective-permute-done.9.refs_8_) | copy-start | bytes 958468
  61.2 5.7 %collective-permute-start.13 = (f32[3,13,16,128]{3,2,1,0:T(8,128)S(1)}, f32[3,13,16,128]{3,2,1,0:T(8,128)S(1)}, u32[]{:S(2)}, u32[]{:S(2)}) collective-permute-start(f32[3,13,16,128]{3,2,1,0:T(8,128)S(1)} %collective-permute-done.9.refs_8_), channel_id=1, source_target_pairs={{0,1},{1,0},{2,3},{3,2},{4,5},{5,4},{6,7},{7,6},{8,9},{9,8},{10,11... | collective-permute-start | bytes 958472 | tf_op jit(solution)/shard_map/ppermute | solution.py:40
  64.8 19.0 %collective-permute-start.4 = (f32[3,13,16,128]{3,2,1,0:T(8,128)S(1)}, f32[3,13,16,128]{3,2,1,0:T(8,128)}, u32[]{:S(2)}, u32[]{:S(2)}) collective-permute-start(f32[3,13,16,128]{3,2,1,0:T(8,128)S(1)} %collective-permute-done.3.refs_3_), channel_id=1, source_target_pairs={{0,16},{1,17},{2,18},{3,19},{4,20},{5,21},{6,22},{7,23},{8,760},{9... | collective-permute-start | bytes 958472 | tf_op jit(solution)/shard_map/ppermute | solution.py:40
  66.8 16.9 %copy-start.8 = (s32[3,19]{1,0:T(4,128)S(1)}, s32[3,19]{1,0:T(4,128)}, u32[]{:S(2)}) copy-start(s32[3,19]{1,0:T(4,128)} %mask_ref.6) | copy-start | bytes 688
  66.9 0.8 copy-start.6
  83.7 1.0 copy-start
  84.7 1.0 copy-start.7
  91.4 0.7 copy-start.2
  92.1 41.7 %copy-start.1 = (f32[3,13,16,128]{3,2,1,0:T(8,128)S(1)}, f32[3,13,16,128]{3,2,1,0:T(8,128)}, u32[]{:S(2)}) copy-start(f32[3,13,16,128]{3,2,1,0:T(8,128)} %shard_map.46.refs_2_.refs_5_) | copy-start | bytes 958468
  92.1 22.3 %collective-permute-start.17 = (f32[3,19,16,128]{3,2,1,0:T(8,128)S(1)}, f32[3,19,16,128]{3,2,1,0:T(8,128)}, u32[]{:S(2)}, u32[]{:S(2)}) collective-permute-start(f32[3,19,16,128]{3,2,1,0:T(8,128)S(1)} %shard_map.47.refs_7_), channel_id=1, source_target_pairs={{0,2},{1,3},{2,0},{3,1},{4,6},{5,7},{6,4},{7,5},{8,10},{9,11},{10,... | collective-permute-start | bytes 1400840 | tf_op jit(solution)/shard_map/ppermute | solution.py:40
  94.2 1.0 copy-start.3
  95.1 1.0 copy-start.5
  102.1 14.7 %collective-permute-start.18 = (f32[3,19,16,128]{3,2,1,0:T(8,128)S(1)}, f32[3,19,16,128]{3,2,1,0:T(8,128)S(1)}, u32[]{:S(2)}, u32[]{:S(2)}) collective-permute-start(f32[3,19,16,128]{3,2,1,0:T(8,128)S(1)} %shard_map.48.refs_8_), channel_id=1, source_target_pairs={{0,2},{1,3},{2,0},{3,1},{4,6},{5,7},{6,4},{7,5},{8,10},{9,11},{10,... | collective-permute-start | bytes 1400840 | tf_op jit(solution)/shard_map/ppermute | solution.py:40
  105.5 13.7 %collective-permute-start.5 = (f32[3,13,16,128]{3,2,1,0:T(8,128)S(1)}, f32[3,13,16,128]{3,2,1,0:T(8,128)S(1)}, u32[]{:S(2)}, u32[]{:S(2)}) collective-permute-start(f32[3,13,16,128]{3,2,1,0:T(8,128)S(1)} %collective-permute-done.3.refs_3_), channel_id=1, source_target_pairs={{0,752},{1,753},{2,754},{3,755},{4,756},{5,757},{6,758},{7,759},{8... | collective-permute-start | bytes 958472 | tf_op jit(solution)/shard_map/ppermute | solution.py:40
  107.4 26.4 %collective-permute-start.19 = (f32[3,19,16,128]{3,2,1,0:T(8,128)S(1)}, f32[3,19,16,128]{3,2,1,0:T(8,128)S(1)}, u32[]{:S(2)}, u32[]{:S(2)}) collective-permute-start(f32[3,19,16,128]{3,2,1,0:T(8,128)S(1)} %shard_map.47.refs_7_), channel_id=1, source_target_pairs={{0,1},{1,0},{2,3},{3,2},{4,5},{5,4},{6,7},{7,6},{8,9},{9,8},{10,11... | collective-permute-start | bytes 1400840 | tf_op jit(solution)/shard_map/ppermute | solution.py:40
  112.4 21.3 %collective-permute-start.20 = (f32[3,19,16,128]{3,2,1,0:T(8,128)S(1)}, f32[3,19,16,128]{3,2,1,0:T(8,128)}, u32[]{:S(2)}, u32[]{:S(2)}) collective-permute-start(f32[3,19,16,128]{3,2,1,0:T(8,128)S(1)} %shard_map.48.refs_8_), channel_id=1, source_target_pairs={{0,1},{1,0},{2,3},{3,2},{4,5},{5,4},{6,7},{7,6},{8,9},{9,8},{10,11... | collective-permute-start | bytes 1400840 | tf_op jit(solution)/shard_map/ppermute | solution.py:40
  114.4 19.4 %collective-permute-start.21 = (f32[3,19,16,128]{3,2,1,0:T(8,128)}, f32[3,19,16,128]{3,2,1,0:T(8,128)}, u32[]{:S(2)}, u32[]{:S(2)}) collective-permute-start(f32[3,19,16,128]{3,2,1,0:T(8,128)} %collective-permute-done.17.refs_9_), channel_id=1, source_target_pairs={{0,1},{1,0},{2,3},{3,2},{4,5},{5,4},{6,7},{7,6},{8,9},{9,8},{10,11... | collective-permute-start | bytes 1400840 | tf_op jit(solution)/shard_map/ppermute | solution.py:40
  116.8 17.0 %collective-permute-start.22 = (f32[3,19,16,128]{3,2,1,0:T(8,128)S(1)}, f32[3,19,16,128]{3,2,1,0:T(8,128)}, u32[]{:S(2)}, u32[]{:S(2)}) collective-permute-start(f32[3,19,16,128]{3,2,1,0:T(8,128)S(1)} %collective-permute-done.18.refs_10_), channel_id=1, source_target_pairs={{0,1},{1,0},{2,3},{3,2},{4,5},{5,4},{6,7},{7,6},{8,9},{9,8},{10,11... | collective-permute-start | bytes 1400840 | tf_op jit(solution)/shard_map/ppermute | solution.py:40
  119.1 14.6 %collective-permute-start.6 = (f32[3,13,16,128]{3,2,1,0:T(8,128)}, f32[3,13,16,128]{3,2,1,0:T(8,128)}, u32[]{:S(2)}, u32[]{:S(2)}) collective-permute-start(f32[3,13,16,128]{3,2,1,0:T(8,128)} %collective-permute-done.4.refs_4_), channel_id=1, source_target_pairs={{0,16},{1,17},{2,18},{3,19},{4,20},{5,21},{6,22},{7,23},{8,760},{9... | collective-permute-start | bytes 958472 | tf_op jit(solution)/shard_map/ppermute | solution.py:40
  122.4 11.4 %copy-start.9 = (s32[3,25]{1,0:T(4,128)S(1)}, s32[3,25]{1,0:T(4,128)}, u32[]{:S(2)}) copy-start(s32[3,25]{1,0:T(4,128)} %mask_ref.7) | copy-start | bytes 904

commit v2 on v1

v2 whole, which is shorter than its diff:
```python
import functools

import jax
import jax.numpy as jnp
from jax import lax
from jax.experimental import pallas as pl
from jax.experimental.pallas import tpu as pltpu
from jax.sharding import PartitionSpec as P

Z, X, YH, YL, CORES = 12, 4, 2, 4, 2
CHAIN = Z * X
AXES = ("row", "col")
F32, BF16 = jnp.float32, jnp.bfloat16


def pairs(target):
    listed = []
    for c in range(CHAIN):
        for yh in range(YH):
            for yl in range(YL):
                for core in range(CORES):
                    to = target(c, yh, yl, core)
                    if to is not None:
                        tc, th, tl, tk = to
                        source = ((c * YH + yh) * YL + yl) * CORES + core
                        listed.append((source, (((tc % CHAIN) * YH + th) * YL + tl) * CORES + tk))
    return listed


UP = pairs(lambda c, h, l, k: (c + 1, h, l, k))
DOWN = pairs(lambda c, h, l, k: (c - 1, h, l, k))
ACROSS = pairs(lambda c, h, l, k: (c + 1 if h == 0 else c - 1, h, l, k))
AGAINST = pairs(lambda c, h, l, k: (c - 1 if h == 0 else c + 1, h, l, k))
FLIP = pairs(lambda c, h, l, k: (c, 1 - h, 3 - l, k))
MIRROR = pairs(lambda c, h, l, k: (c, h, 3 - l, k))
NEXT = pairs(lambda c, h, l, k: (c, h, l ^ 1, k))
SIBLING = pairs(lambda c, h, l, k: (c, h, l, 1 - k))


def send(array, which):
    return lax.ppermute(array, AXES, which)


def together(*arrays):
    return lax.optimization_barrier(arrays)


def split(values):
    high = values.astype(BF16)
    return high, (values - high.astype(F32)).astype(BF16)


def mask_kernel(mask_ref, x_ref, out_ref):
    for g in range(x_ref.shape[0]):
        for d in range(x_ref.shape[1]):
            out_ref[g, d] = x_ref[g, d] * mask_ref[g, d].astype(F32)


def lanes(g):
    return slice(128 * g, 128 * (g + 1))


def blank_corners(right_ref, blocks):
    for g in range(3):
        for r in range(blocks + 2):
            if not 0 <= r - g < blocks:
                right_ref[r, :, lanes(g)] = jnp.zeros((right_ref.shape[1], 128), BF16)


def put_right(right_ref, at, slab):
    blocks = slab.shape[1]
    for g in range(3):
        high, low = split(slab[g])
        for first, is_high in at:
            spot = pl.ds(pl.multiple_of(first, 16), 16)
            right_ref[g : g + blocks, spot, lanes(g)] = high if is_high else low


def accumulate(window_ref, right_ref, total_ref):
    for r in range(window_ref.shape[0]):
        product = jnp.dot(window_ref[r], right_ref[r], preferred_element_type=F32)
        product = product.reshape(13, 16, 384)
        for g in range(3):
            total_ref[g, r + 2 - g : r + 15 - g] += product[:, :, lanes(g)]


def viewed(refs, views):
    return [refs[n] if part is None else refs[n].at[part] for n, part in views]


def square_kernel(views, arrays, place_ref, mask_ref, *refs):
    given = viewed(refs, views)
    rows, slabs = given[:5], given[5:]
    out_ref, window_ref, right_ref, total_ref = refs[arrays:]
    for n, ref in enumerate(rows):
        base = place_ref[n] * 3
        for j in range(3):
            high, low = split(ref[j].reshape(208, 128))
            for part, value in enumerate((high, low, high)):
                window_ref[base + j, :, lanes(part)] = value
    blank_corners(right_ref, 13)
    for n, slab in enumerate(slabs):
        at = place_ref[5 + n] * 16
        put_right(right_ref, ((at, True), (128 + at, True), (256 + at, False)), slab)
    total_ref[...] = jnp.zeros_like(total_ref)
    accumulate(window_ref, right_ref, total_ref)
    for g in range(3):
        for e in range(19):
            out_ref[g, e] = total_ref[g, e + 5] * mask_ref[g, e].astype(F32)


def fill_half(right_ref, chips, slabs, core):
    blank_corners(right_ref, 19)
    zero = jnp.zeros((21, 16, 384), BF16)
    for n, chip in enumerate(chips):
        other = lax.rem(chip + 2, 4)
        for k in range(2):
            right_ref[:, pl.ds(pl.multiple_of(128 + 32 * other + 16 * k, 16), 16), :] = zero
        for k, slab in ((core, slabs[n]), (1 - core, slabs[2 + n])):
            place = 32 * chip + 16 * k
            again = 32 * other + 16 * k
            put_right(right_ref, ((place, True), (again, True), (128 + place, False)), slab)


def cube_first_kernel(views, arrays, place_ref, *refs):
    given = viewed(refs, views)
    rows, slabs = given[:7], given[7:]
    total_ref, next_ref, window_ref, right_ref = refs[arrays:]
    low_y, core = place_ref[7], place_ref[8]
    chip = lax.broadcasted_iota(jnp.int32, (208, 128), 1) // 32
    mine = (chip == low_y) | (chip == 3 - low_y)
    for n, ref in enumerate(rows):
        base = place_ref[n] * 3
        for j in range(3):
            values = ref[j].reshape(208, 128)
            rounded = values.astype(BF16)
            high = rounded.astype(F32)
            low = pltpu.roll(values - high, 64, 1)
            window_ref[base + j, :, lanes(0)] = jnp.where(mine, high, low).astype(BF16)
            window_ref[base + j, :, lanes(1)] = rounded
            next_ref[base + j, :, lanes(0)] = jnp.where(mine, low, high).astype(BF16)
            next_ref[base + j, :, lanes(1)] = rounded
    fill_half(right_ref, (low_y, 3 - low_y), slabs, core)
    total_ref[...] = jnp.zeros_like(total_ref)
    accumulate(window_ref, right_ref, total_ref)


def cube_second_kernel(views, arrays, place_ref, mask_ref, *refs):
    given = viewed(refs, views)
    before_ref, window_ref, own_ref, slabs = given[0], given[1], given[2], given[3:]
    out_ref, right_ref, total_ref = refs[arrays:]
    low_y, core = place_ref[7], place_ref[8]
    fill_half(right_ref, (low_y ^ 1, (3 - low_y) ^ 1), slabs, core)
    total_ref[...] = before_ref[...]
    accumulate(window_ref, right_ref, total_ref)
    for g in range(3):
        for f in range(25):
            value = -2.0 * total_ref[g, f + 5]
            if 3 <= f < 22:
                value = 3.0 * own_ref[g, f - 3] + value
            out_ref[g, f] = value * mask_ref[g, f].astype(F32)


SMEM = pl.BlockSpec(memory_space=pltpu.SMEM)
VMEM = pl.BlockSpec(memory_space=pltpu.VMEM)
ANYWHERE = pl.BlockSpec(memory_space=pl.ANY)
MIB = 1024 * 1024


def call(kernel, scalars, given, out_shape, scratch, limit, micros, after=()):
    arrays, views = [], []
    for item in given:
        array, part = item if isinstance(item, tuple) else (item, None)
        held = [n for n, known in enumerate(arrays) if known is array]
        if not held:
            arrays.append(array)
        views.append((held[0] if held else len(arrays) - 1, part))
    operands = arrays + list(after)
    return pl.pallas_call(
        functools.partial(kernel, tuple(views), len(operands)),
        out_shape=out_shape,
        in_specs=[SMEM] * len(scalars) + [VMEM] * len(arrays) + [ANYWHERE] * len(after),
        out_specs=jax.tree.map(lambda _: VMEM, out_shape),
        scratch_shapes=scratch,
        compiler_params=pltpu.CompilerParams(vmem_limit_bytes=limit),
        cost_estimate=pl.CostEstimate(
            flops=int(micros * 1.15e9), bytes_accessed=4 * MIB, transcendentals=0
        ),
    )(*scalars, *operands)


def body(x_band, x_mask, sq_mask, cube_mask):
    high_y = lax.axis_index("row") % 2
    low_y, core = lax.axis_index("col") // 2, lax.axis_index("col") % 2

    own = pl.pallas_call(
        mask_kernel,
        out_shape=jax.ShapeDtypeStruct(x_band.shape, F32),
        in_specs=[SMEM, VMEM],
        out_specs=VMEM,
    )(x_mask, x_band)

    own_m, pair_m = together(send(own, MIRROR), send(own, FLIP))
    both = jnp.stack([own, own_m])
    after = send(both, NEXT)
    pair_o = send(pair_m, MIRROR)
    below, above = send(both, UP), send(both, DOWN)
    twin = send(both, SIBLING)
    beside_m = send(pair_m, ACROSS)
    twin_after = send(after, SIBLING)
    beside_o = send(pair_o, ACROSS)
    far_a = send(pair_o, AGAINST)
    far_b = send(beside_o, ACROSS)

    chips = jnp.stack([low_y, 3 - low_y, low_y ^ 1, (3 - low_y) ^ 1])
    orbitals = jnp.concatenate([2 * chips + core, 2 * chips + 1 - core])
    pair_at, beside_at = 3 - 2 * high_y, 1 + 2 * high_y
    square_rows = jnp.stack([jnp.int32(0), jnp.int32(4), jnp.int32(2), pair_at, beside_at])
    square_places = jnp.concatenate([square_rows, orbitals]).astype(jnp.int32)
    cube_places = [1, 5, 3, pair_at + 1, beside_at + 1, 6 - 6 * high_y, 6 * high_y, low_y, core]
    cube_places = jnp.stack([jnp.int32(v) for v in cube_places])

    left = [(array, part) for array in (both, after, twin, twin_after) for part in (0, 1)]

    def square_of(part, pair, beside, behind):
        return call(
            square_kernel,
            (square_places, sq_mask),
            [(below, part), (above, part), (both, part), pair, beside] + left,
            jax.ShapeDtypeStruct((3, 19, 16, 128), F32),
            [
                pltpu.VMEM((15, 208, 384), BF16),
                pltpu.VMEM((15, 384, 384), BF16),
                pltpu.VMEM((3, 29, 16, 128), F32),
            ],
            20 * MIB,
            4.5,
            behind,
        )

    square_m = square_of(1, pair_m, beside_m, (beside_o,))
    twin_m, next_m = send(square_m, SIBLING), send(square_m, NEXT)
    square_o = square_of(0, pair_o, beside_o, (twin_m, far_a))
    twin_o, next_o = send(square_o, SIBLING), send(square_o, NEXT)
    total, window = call(
        cube_first_kernel,
        (cube_places,),
        [(below, 0), (above, 0), (both, 0), pair_o, beside_o, far_a, far_b]
        + [square_o, square_m, twin_o, twin_m],
        (
            jax.ShapeDtypeStruct((3, 35, 16, 128), F32),
            jax.ShapeDtypeStruct((21, 208, 256), BF16),
        ),
        [pltpu.VMEM((21, 208, 256), BF16), pltpu.VMEM((21, 256, 384), BF16)],
        24 * MIB,
        5,
    )
    return call(
        cube_second_kernel,
        (cube_places, cube_mask),
        [total, window, square_o, next_o, next_m, send(next_o, SIBLING), send(next_m, SIBLING)],
        jax.ShapeDtypeStruct((3, 25, 16, 128), F32),
        [pltpu.VMEM((21, 256, 384), BF16), pltpu.VMEM((3, 35, 16, 128), F32)],
        20 * MIB,
        4,
    )


def solution(mesh):
    return jax.shard_map(
        body,
        mesh=mesh,
        in_specs=(P("row", None, "col", None), P("row", None), P("row", None), P("row", None)),
        out_specs=P("row", None, "col", None),
        check_vma=False,
    )
```

time: 144 us -> 137 us (0.951)
  starting transfers between devices: 86.9 us -> 64.8 us
  waiting for transfers between devices: 27.4 us -> 47.6 us
  local copies, waits for them, and re-layouts: 5.53 us -> 2.86 us
  Pallas kernels: 22.5 us -> 20 us
    ppermute x23 -> x18, starting transfers between devices: 86.9 us -> 64.8 us  [send(): return lax.ppermute(array, AXES, which)]
    ppermute x23 -> x18, waiting for transfers between devices: 27.4 us -> 47.6 us  [send(): return lax.ppermute(array, AXES, which)]
    unnamed x20 -> x12, local copies, waits for them, and re-layouts: 5.36 us -> 2.69 us
    pallas_call x3 -> x4, Pallas kernels: 20.8 us -> 18.3 us  [call(): pl.pallas_call(functools.partial(kernel, tuple(views), len(operands)), ou...]
  transfers between devices with their start and end apart: 23 -> 18, of which waited for: 2 -> 7; matrix products, arithmetic and copies ran while one was open for 0% -> 0% of each run, Pallas kernels for 8% -> 7%
where the time goes in v2:
time: 137 us
  starting transfers between devices  64.8 us (47%)
  waiting for transfers between devices  47.6 us (35%)
  Pallas kernels  20 us (15%)
  local copies, waits for them, and re-layouts  2.86 us (2%)
    ppermute x18, starting transfers between devices, send(): return lax.ppermute(array, AXES, which)  64.8 us
    ppermute x18, waiting for transfers between devices, send(): return lax.ppermute(array, AXES, which)  47.6 us
    pallas_call x4, Pallas kernels, call(): pl.pallas_call(functools.partial(kernel, tuple(views), len(operands)), ou...  18.3 us
  transfers between devices with their start and end apart: 18, of which 7 were waited for; matrix products, arithmetic and copies ran while one was open for 0% of the time, Pallas kernels for 7%

profile of v2, /device:TPU:1, one launch (start us, length us, event | category | flops | bytes accessed | tf_op | source)
XLA Modules:
  0.0 136.5 jit_solution(12591886981388545331)
XLA Ops:
  0.0 1.7 %shard_map.46 = f32[3,13,16,128]{3,2,1,0:T(8,128)} custom-call(s32[3,13]{1,0:T(4,128)} %mask_ref.4, f32[3,13,16,128]{3,2,1,0:T(8,128)} %x_ref.1), custom_call_target="tpu_custom_call" | custom-call | tf_op jit(solution)/shard_map/pallas_call | solution.py:196
  1.7 6.0 %collective-permute-start = (f32[3,13,16,128]{3,2,1,0:T(8,128)}, f32[3,13,16,128]{3,2,1,0:T(8,128)S(1)}, u32[]{:S(2)}, u32[]{:S(2)}) collective-permute-start(f32[3,13,16,128]{3,2,1,0:T(8,128)} %shard_map.46), channel_id=1, source_target_pairs={{0,6},{1,7},{2,4},{3,5},{4,2},{5,3},{6,0},{7,1},{8,14},{9,15},{10,... | collective-permute-start | bytes 958472 | tf_op jit(solution)/shard_map/ppermute | solution.py:41
  7.8 4.4 %collective-permute-start.1 = (f32[3,13,16,128]{3,2,1,0:T(8,128)}, f32[3,13,16,128]{3,2,1,0:T(8,128)}, u32[]{:S(2)}, u32[]{:S(2)}) collective-permute-start(f32[3,13,16,128]{3,2,1,0:T(8,128)} %shard_map.46), channel_id=1, source_target_pairs={{0,14},{1,15},{2,12},{3,13},{4,10},{5,11},{6,8},{7,9},{8,6},{9,7},... | collective-permute-start | bytes 958472 | tf_op jit(solution)/shard_map/ppermute | solution.py:41
  12.2 0.3 collective-permute-done
  12.5 14.0 %collective-permute-done.1.refs_3_ = f32[3,13,16,128]{3,2,1,0:T(8,128)} collective-permute-done((f32[3,13,16,128]{3,2,1,0:T(8,128)}, f32[3,13,16,128]{3,2,1,0:T(8,128)}, u32[]{:S(2)}, u32[]{:S(2)}) %collective-permute-start.1) | collective-permute-done | bytes 319520 | tf_op jit(solution)/shard_map/ppermute | solution.py:41
  26.5 1.0 pad_maximum_fusion.refs_2_
  27.5 2.5 %collective-permute-start.8 = (f32[2,3,13,16,128]{4,3,2,1,0:T(8,128)S(1)}, f32[2,3,13,16,128]{4,3,2,1,0:T(8,128)S(1)}, u32[]{:S(2)}, u32[]{:S(2)}) collective-permute-start(f32[2,3,13,16,128]{4,3,2,1,0:T(8,128)S(1)} %pad_maximum_fusion.refs_2_), channel_id=1, source_target_pairs={{0,2},{1,3},{2,0},{3,1},{4,6},{5,7},{6,4},{7,5},{8,10},{9,11},{10,... | collective-permute-start | bytes 1916936 | tf_op jit(solution)/shard_map/ppermute | solution.py:41
  30.0 2.1 %collective-permute-start.4 = (f32[3,13,16,128]{3,2,1,0:T(8,128)}, f32[3,13,16,128]{3,2,1,0:T(8,128)S(1)}, u32[]{:S(2)}, u32[]{:S(2)}) collective-permute-start(f32[3,13,16,128]{3,2,1,0:T(8,128)} %collective-permute-done.1.refs_3_), channel_id=1, source_target_pairs={{0,6},{1,7},{2,4},{3,5},{4,2},{5,3},{6,0},{7,1},{8,14},{9,15},{10,... | collective-permute-start | bytes 958472 | tf_op jit(solution)/shard_map/ppermute | solution.py:41
  32.1 5.2 %collective-permute-start.11 = (f32[3,13,16,128]{3,2,1,0:T(8,128)}, f32[3,13,16,128]{3,2,1,0:T(8,128)}, u32[]{:S(2)}, u32[]{:S(2)}) collective-permute-start(f32[3,13,16,128]{3,2,1,0:T(8,128)} %collective-permute-done.1.refs_3_), channel_id=1, source_target_pairs={{0,16},{1,17},{2,18},{3,19},{4,20},{5,21},{6,22},{7,23},{8,760},{9... | collective-permute-start | bytes 958472 | tf_op jit(solution)/shard_map/ppermute | solution.py:41
  37.3 3.1 %collective-permute-start.2 = (f32[2,3,13,16,128]{4,3,2,1,0:T(8,128)S(1)}, f32[2,3,13,16,128]{4,3,2,1,0:T(8,128)S(1)}, u32[]{:S(2)}, u32[]{:S(2)}) collective-permute-start(f32[2,3,13,16,128]{4,3,2,1,0:T(8,128)S(1)} %pad_maximum_fusion.refs_2_), channel_id=1, source_target_pairs={{0,16},{1,17},{2,18},{3,19},{4,20},{5,21},{6,22},{7,23},{8,24},{9,... | collective-permute-start | bytes 1916936 | tf_op jit(solution)/shard_map/ppermute | solution.py:41
  40.4 14.1 %collective-permute-start.3 = (f32[2,3,13,16,128]{4,3,2,1,0:T(8,128)S(1)}, f32[2,3,13,16,128]{4,3,2,1,0:T(8,128)S(1)}, u32[]{:S(2)}, u32[]{:S(2)}) collective-permute-start(f32[2,3,13,16,128]{4,3,2,1,0:T(8,128)S(1)} %pad_maximum_fusion.refs_2_), channel_id=1, source_target_pairs={{0,752},{1,753},{2,754},{3,755},{4,756},{5,757},{6,758},{7,759},{8... | collective-permute-start | bytes 1916936 | tf_op jit(solution)/shard_map/ppermute | solution.py:41
  54.5 0.0 collective-permute-done.4.refs_3_
  54.5 3.3 %collective-permute-start.9 = (f32[2,3,13,16,128]{4,3,2,1,0:T(8,128)S(1)}, f32[2,3,13,16,128]{4,3,2,1,0:T(8,128)S(1)}, u32[]{:S(2)}, u32[]{:S(2)}) collective-permute-start(f32[2,3,13,16,128]{4,3,2,1,0:T(8,128)S(1)} %pad_maximum_fusion.refs_2_), channel_id=1, source_target_pairs={{0,1},{1,0},{2,3},{3,2},{4,5},{5,4},{6,7},{7,6},{8,9},{9,8},{10,11... | collective-permute-start | bytes 1916936 | tf_op jit(solution)/shard_map/ppermute | solution.py:41
  57.8 0.0 collective-permute-done.8.refs_5_
  57.8 1.9 %collective-permute-start.10 = (f32[2,3,13,16,128]{4,3,2,1,0:T(8,128)S(1)}, f32[2,3,13,16,128]{4,3,2,1,0:T(8,128)}, u32[]{:S(2)}, u32[]{:S(2)}) collective-permute-start(f32[2,3,13,16,128]{4,3,2,1,0:T(8,128)S(1)} %collective-permute-done.8.refs_5_), channel_id=1, source_target_pairs={{0,1},{1,0},{2,3},{3,2},{4,5},{5,4},{6,7},{7,6},{8,9},{9,8},{10,11... | collective-permute-start | bytes 1916936 | tf_op jit(solution)/shard_map/ppermute | solution.py:41
  59.8 0.0 collective-permute-done.11.refs_4_
  59.8 1.9 %collective-permute-start.5 = (f32[3,13,16,128]{3,2,1,0:T(8,128)S(1)}, f32[3,13,16,128]{3,2,1,0:T(8,128)}, u32[]{:S(2)}, u32[]{:S(2)}) collective-permute-start(f32[3,13,16,128]{3,2,1,0:T(8,128)S(1)} %collective-permute-done.4.refs_3_), channel_id=1, source_target_pairs={{0,16},{1,17},{2,18},{3,19},{4,20},{5,21},{6,22},{7,23},{8,760},{9... | collective-permute-start | bytes 958472 | tf_op jit(solution)/shard_map/ppermute | solution.py:41
  61.7 0.1 add_subtract_fusion
  61.8 0.1 concatenate.3.place_ref
  61.9 9.4 %collective-permute-done.2.refs_0_ = f32[2,3,13,16,128]{4,3,2,1,0:T(8,128)S(1)} collective-permute-done((f32[2,3,13,16,128]{4,3,2,1,0:T(8,128)S(1)}, f32[2,3,13,16,128]{4,3,2,1,0:T(8,128)S(1)}, u32[]{:S(2)}, u32[]{:S(2)}) %collective-permute-start.2) | collective-permute-done | bytes 639008 | tf_op jit(solution)/shard_map/ppermute | solution.py:41
  71.3 0.0 collective-permute-done.3.refs_1_
  71.3 0.0 collective-permute-done.9.refs_6_
  71.3 11.0 %collective-permute-done.5.refs_8_.refs_4_ = f32[3,13,16,128]{3,2,1,0:T(8,128)} collective-permute-done((f32[3,13,16,128]{3,2,1,0:T(8,128)S(1)}, f32[3,13,16,128]{3,2,1,0:T(8,128)}, u32[]{:S(2)}, u32[]{:S(2)}) %collective-permute-start.5) | collective-permute-done | bytes 319520 | tf_op jit(solution)/shard_map/ppermute | solution.py:41
  82.3 0.0 collective-permute-done.10.refs_7_
  82.4 0.7 copy-done.4
  83.0 4.8 %shard_map.47.refs_8_ = f32[3,19,16,128]{3,2,1,0:T(8,128)} custom-call(s32[13]{0:T(128)S(1)} %concatenate.3.place_ref, s32[3,19]{1,0:T(4,128)S(1)} %copy-done.4, f32[2,3,13,16,128]{4,3,2,1,0:T(8,128)S(1)} %collective-permute-done.2.refs_0_, f32[2,3,13,16,128]{4,3,2,1,0:T(8,128)S(1)} %collective-permute-done.3.refs_1_, ...), custom_call_target="tpu_custom_call" | custom-call | flops 5175000064 | bytes 4194304 | tf_op jit(solution)/shard_map/pallas_call | solution.py:179
  87.9 2.9 %collective-permute-start.12 = (f32[3,19,16,128]{3,2,1,0:T(8,128)}, f32[3,19,16,128]{3,2,1,0:T(8,128)S(1)}, u32[]{:S(2)}, u32[]{:S(2)}) collective-permute-start(f32[3,19,16,128]{3,2,1,0:T(8,128)} %shard_map.47.refs_8_), channel_id=1, source_target_pairs={{0,1},{1,0},{2,3},{3,2},{4,5},{5,4},{6,7},{7,6},{8,9},{9,8},{10,11... | collective-permute-start | bytes 1400840 | tf_op jit(solution)/shard_map/ppermute | solution.py:41
  90.8 3.4 %collective-permute-start.6 = (f32[3,13,16,128]{3,2,1,0:T(8,128)S(1)}, f32[3,13,16,128]{3,2,1,0:T(8,128)S(1)}, u32[]{:S(2)}, u32[]{:S(2)}) collective-permute-start(f32[3,13,16,128]{3,2,1,0:T(8,128)S(1)} %collective-permute-done.4.refs_3_), channel_id=1, source_target_pairs={{0,752},{1,753},{2,754},{3,755},{4,756},{5,757},{6,758},{7,759},{8... | collective-permute-start | bytes 958472 | tf_op jit(solution)/shard_map/ppermute | solution.py:41
  94.2 1.9 %collective-permute-start.15 = (f32[3,19,16,128]{3,2,1,0:T(8,128)}, f32[3,19,16,128]{3,2,1,0:T(8,128)}, u32[]{:S(2)}, u32[]{:S(2)}) collective-permute-start(f32[3,19,16,128]{3,2,1,0:T(8,128)} %shard_map.47.refs_8_), channel_id=1, source_target_pairs={{0,2},{1,3},{2,0},{3,1},{4,6},{5,7},{6,4},{7,5},{8,10},{9,11},{10,... | collective-permute-start | bytes 1400840 | tf_op jit(solution)/shard_map/ppermute | solution.py:41
  96.1 5.9 %collective-permute-done.6.refs_9_.refs_5_ = f32[3,13,16,128]{3,2,1,0:T(8,128)S(1)} collective-permute-done((f32[3,13,16,128]{3,2,1,0:T(8,128)S(1)}, f32[3,13,16,128]{3,2,1,0:T(8,128)S(1)}, u32[]{:S(2)}, u32[]{:S(2)}) %collective-permute-start.6) | collective-permute-done | bytes 319520 | tf_op jit(solution)/shard_map/ppermute | solution.py:41
  101.9 0.0 collective-permute-done.12.refs_8_.refs_10_
  101.9 5.0 %shard_map.48.refs_7_.refs_2_ = f32[3,19,16,128]{3,2,1,0:T(8,128)} custom-call(s32[13]{0:T(128)S(1)} %concatenate.3.place_ref, s32[3,19]{1,0:T(4,128)S(1)} %copy-done.4, f32[2,3,13,16,128]{4,3,2,1,0:T(8,128)S(1)} %collective-permute-done.2.refs_0_, f32[2,3,13,16,128]{4,3,2,1,0:T(8,128)S(1)} %collective-permute-done.3.refs_1_, ...), custom_call_target="tpu_custom_call" | custom-call | flops 5175000064 | bytes 4194304 | tf_op jit(solution)/shard_map/pallas_call | solution.py:179
  107.0 1.9 %collective-permute-start.14 = (f32[3,19,16,128]{3,2,1,0:T(8,128)}, f32[3,19,16,128]{3,2,1,0:T(8,128)S(1)}, u32[]{:S(2)}, u32[]{:S(2)}) collective-permute-start(f32[3,19,16,128]{3,2,1,0:T(8,128)} %shard_map.48.refs_7_.refs_2_), channel_id=1, source_target_pairs={{0,2},{1,3},{2,0},{3,1},{4,6},{5,7},{6,4},{7,5},{8,10},{9,11},{10,... | collective-permute-start | bytes 1400840 | tf_op jit(solution)/shard_map/ppermute | solution.py:41
  108.9 2.6 %collective-permute-start.13 = (f32[3,19,16,128]{3,2,1,0:T(8,128)}, f32[3,19,16,128]{3,2,1,0:T(8,128)S(1)}, u32[]{:S(2)}, u32[]{:S(2)}) collective-permute-start(f32[3,19,16,128]{3,2,1,0:T(8,128)} %shard_map.48.refs_7_.refs_2_), channel_id=1, source_target_pairs={{0,1},{1,0},{2,3},{3,2},{4,5},{5,4},{6,7},{7,6},{8,9},{9,8},{10,11... | collective-permute-start | bytes 1400840 | tf_op jit(solution)/shard_map/ppermute | solution.py:41
  111.5 1.9 %collective-permute-start.7 = (f32[3,13,16,128]{3,2,1,0:T(8,128)}, f32[3,13,16,128]{3,2,1,0:T(8,128)S(1)}, u32[]{:S(2)}, u32[]{:S(2)}) collective-permute-start(f32[3,13,16,128]{3,2,1,0:T(8,128)} %collective-permute-done.5.refs_8_.refs_4_), channel_id=1, source_target_pairs={{0,16},{1,17},{2,18},{3,19},{4,20},{5,21},{6,22},{7,23},{8,760},{9... | collective-permute-start | bytes 958472 | tf_op jit(solution)/shard_map/ppermute | solution.py:41
  113.4 0.0 copy-start.5
  113.4 0.1 stack.55.place_ref
  113.5 0.0 collective-permute-done.15.refs_4_
  113.5 1.9 %collective-permute-start.17 = (f32[3,19,16,128]{3,2,1,0:T(8,128)}, f32[3,19,16,128]{3,2,1,0:T(8,128)S(1)}, u32[]{:S(2)}, u32[]{:S(2)}) collective-permute-start(f32[3,19,16,128]{3,2,1,0:T(8,128)} %collective-permute-done.15.refs_4_), channel_id=1, source_target_pairs={{0,1},{1,0},{2,3},{3,2},{4,5},{5,4},{6,7},{7,6},{8,9},{9,8},{10,11... | collective-permute-start | bytes 1400840 | tf_op jit(solution)/shard_map/ppermute | solution.py:41
  115.5 5.2 %collective-permute-done.14.refs_3_ = f32[3,19,16,128]{3,2,1,0:T(8,128)S(1)} collective-permute-done((f32[3,19,16,128]{3,2,1,0:T(8,128)}, f32[3,19,16,128]{3,2,1,0:T(8,128)S(1)}, u32[]{:S(2)}, u32[]{:S(2)}) %collective-permute-start.14) | collective-permute-done | bytes 466976 | tf_op jit(solution)/shard_map/ppermute | solution.py:41
  120.6 3.6 %collective-permute-start.16 = (f32[3,19,16,128]{3,2,1,0:T(8,128)S(1)}, f32[3,19,16,128]{3,2,1,0:T(8,128)S(1)}, u32[]{:S(2)}, u32[]{:S(2)}) collective-permute-start(f32[3,19,16,128]{3,2,1,0:T(8,128)S(1)} %collective-permute-done.14.refs_3_), channel_id=1, source_target_pairs={{0,1},{1,0},{2,3},{3,2},{4,5},{5,4},{6,7},{7,6},{8,9},{9,8},{10,11... | collective-permute-start | bytes 1400840 | tf_op jit(solution)/shard_map/ppermute | solution.py:41
  124.3 1.8 %collective-permute-done.7.refs_6_ = f32[3,13,16,128]{3,2,1,0:T(8,128)S(1)} collective-permute-done((f32[3,13,16,128]{3,2,1,0:T(8,128)}, f32[3,13,16,128]{3,2,1,0:T(8,128)S(1)}, u32[]{:S(2)}, u32[]{:S(2)}) %collective-permute-start.7) | collective-permute-done | bytes 319520 | tf_op jit(solution)/shard_map/ppermute | solution.py:41
  126.1 0.0 collective-permute-done.13.refs_9_
  126.1 1.0 copy-done.1
  127.1 1.0 copy-done.3
  128.1 4.4 %shard_map.49 = (f32[3,35,16,128]{3,2,1,0:T(8,128)S(1)}, bf16[21,208,256]{2,1,0:T(8,128)(2,1)S(1)}) custom-call(s32[9]{0:T(128)S(1)} %stack.55.place_ref, f32[2,3,13,16,128]{4,3,2,1,0:T(8,128)S(1)} %collective-permute-done.2.refs_0_, f32[2,3,13,16,128]{4,3,2,1,0:T(8,128)S(1)} %collective-permute-done.3.refs_1_, ...), custom_call_target="tpu_custom_call" | custom-call | flops 5750000128 | bytes 4194304 | tf_op jit(solution)/shard_map/pallas_call | solution.py:179
  132.5 0.0 collective-permute-done.16.refs_5_
  132.5 4.1 %shard_map.50 = f32[3,25,16,128]{3,2,1,0:T(8,128)} custom-call(s32[9]{0:T(128)S(1)} %stack.55.place_ref, s32[3,25]{1,0:T(4,128)S(1)} %copy-done.5, f32[3,35,16,128]{3,2,1,0:T(8,128)S(1)} %get-tuple-element.11.refs_0_, bf16[21,208,256]{2,1,0:T(8,128)(2,1)S(1)} %get-tuple-element.12.refs_1_, f32[3,19,16,128]{3,2,1,0:T(8,128)} %shard_map.48.refs_7_.refs_2_, ...), custom_call_target="tpu_custom_call" | custom-call | flops 4600000000 | bytes 4194304 | tf_op jit(solution)/shard_map/pallas_call | solution.py:179
  (10 shorter events, 0.0 us)
Async XLA Ops:
  1.7 10.7 %collective-permute-start = (f32[3,13,16,128]{3,2,1,0:T(8,128)}, f32[3,13,16,128]{3,2,1,0:T(8,128)S(1)}, u32[]{:S(2)}, u32[]{:S(2)}) collective-permute-start(f32[3,13,16,128]{3,2,1,0:T(8,128)} %shard_map.46), channel_id=1, source_target_pairs={{0,6},{1,7},{2,4},{3,5},{4,2},{5,3},{6,0},{7,1},{8,14},{9,15},{10,... | collective-permute-start | bytes 958472 | tf_op jit(solution)/shard_map/ppermute | solution.py:41
  7.8 18.7 %collective-permute-start.1 = (f32[3,13,16,128]{3,2,1,0:T(8,128)}, f32[3,13,16,128]{3,2,1,0:T(8,128)}, u32[]{:S(2)}, u32[]{:S(2)}) collective-permute-start(f32[3,13,16,128]{3,2,1,0:T(8,128)} %shard_map.46), channel_id=1, source_target_pairs={{0,14},{1,15},{2,12},{3,13},{4,10},{5,11},{6,8},{7,9},{8,6},{9,7},... | collective-permute-start | bytes 958472 | tf_op jit(solution)/shard_map/ppermute | solution.py:41
  27.5 30.3 %collective-permute-start.8 = (f32[2,3,13,16,128]{4,3,2,1,0:T(8,128)S(1)}, f32[2,3,13,16,128]{4,3,2,1,0:T(8,128)S(1)}, u32[]{:S(2)}, u32[]{:S(2)}) collective-permute-start(f32[2,3,13,16,128]{4,3,2,1,0:T(8,128)S(1)} %pad_maximum_fusion.refs_2_), channel_id=1, source_target_pairs={{0,2},{1,3},{2,0},{3,1},{4,6},{5,7},{6,4},{7,5},{8,10},{9,11},{10,... | collective-permute-start | bytes 1916936 | tf_op jit(solution)/shard_map/ppermute | solution.py:41
  30.0 24.5 %collective-permute-start.4 = (f32[3,13,16,128]{3,2,1,0:T(8,128)}, f32[3,13,16,128]{3,2,1,0:T(8,128)S(1)}, u32[]{:S(2)}, u32[]{:S(2)}) collective-permute-start(f32[3,13,16,128]{3,2,1,0:T(8,128)} %collective-permute-done.1.refs_3_), channel_id=1, source_target_pairs={{0,6},{1,7},{2,4},{3,5},{4,2},{5,3},{6,0},{7,1},{8,14},{9,15},{10,... | collective-permute-start | bytes 958472 | tf_op jit(solution)/shard_map/ppermute | solution.py:41
  32.1 27.7 %collective-permute-start.11 = (f32[3,13,16,128]{3,2,1,0:T(8,128)}, f32[3,13,16,128]{3,2,1,0:T(8,128)}, u32[]{:S(2)}, u32[]{:S(2)}) collective-permute-start(f32[3,13,16,128]{3,2,1,0:T(8,128)} %collective-permute-done.1.refs_3_), channel_id=1, source_target_pairs={{0,16},{1,17},{2,18},{3,19},{4,20},{5,21},{6,22},{7,23},{8,760},{9... | collective-permute-start | bytes 958472 | tf_op jit(solution)/shard_map/ppermute | solution.py:41
  37.3 34.0 %collective-permute-start.2 = (f32[2,3,13,16,128]{4,3,2,1,0:T(8,128)S(1)}, f32[2,3,13,16,128]{4,3,2,1,0:T(8,128)S(1)}, u32[]{:S(2)}, u32[]{:S(2)}) collective-permute-start(f32[2,3,13,16,128]{4,3,2,1,0:T(8,128)S(1)} %pad_maximum_fusion.refs_2_), channel_id=1, source_target_pairs={{0,16},{1,17},{2,18},{3,19},{4,20},{5,21},{6,22},{7,23},{8,24},{9,... | collective-permute-start | bytes 1916936 | tf_op jit(solution)/shard_map/ppermute | solution.py:41
  40.4 30.9 %collective-permute-start.3 = (f32[2,3,13,16,128]{4,3,2,1,0:T(8,128)S(1)}, f32[2,3,13,16,128]{4,3,2,1,0:T(8,128)S(1)}, u32[]{:S(2)}, u32[]{:S(2)}) collective-permute-start(f32[2,3,13,16,128]{4,3,2,1,0:T(8,128)S(1)} %pad_maximum_fusion.refs_2_), channel_id=1, source_target_pairs={{0,752},{1,753},{2,754},{3,755},{4,756},{5,757},{6,758},{7,759},{8... | collective-permute-start | bytes 1916936 | tf_op jit(solution)/shard_map/ppermute | solution.py:41
  54.5 16.8 %collective-permute-start.9 = (f32[2,3,13,16,128]{4,3,2,1,0:T(8,128)S(1)}, f32[2,3,13,16,128]{4,3,2,1,0:T(8,128)S(1)}, u32[]{:S(2)}, u32[]{:S(2)}) collective-permute-start(f32[2,3,13,16,128]{4,3,2,1,0:T(8,128)S(1)} %pad_maximum_fusion.refs_2_), channel_id=1, source_target_pairs={{0,1},{1,0},{2,3},{3,2},{4,5},{5,4},{6,7},{7,6},{8,9},{9,8},{10,11... | collective-permute-start | bytes 1916936 | tf_op jit(solution)/shard_map/ppermute | solution.py:41
  57.8 24.5 %collective-permute-start.10 = (f32[2,3,13,16,128]{4,3,2,1,0:T(8,128)S(1)}, f32[2,3,13,16,128]{4,3,2,1,0:T(8,128)}, u32[]{:S(2)}, u32[]{:S(2)}) collective-permute-start(f32[2,3,13,16,128]{4,3,2,1,0:T(8,128)S(1)} %collective-permute-done.8.refs_5_), channel_id=1, source_target_pairs={{0,1},{1,0},{2,3},{3,2},{4,5},{5,4},{6,7},{7,6},{8,9},{9,8},{10,11... | collective-permute-start | bytes 1916936 | tf_op jit(solution)/shard_map/ppermute | solution.py:41
  59.8 22.5 %collective-permute-start.5 = (f32[3,13,16,128]{3,2,1,0:T(8,128)S(1)}, f32[3,13,16,128]{3,2,1,0:T(8,128)}, u32[]{:S(2)}, u32[]{:S(2)}) collective-permute-start(f32[3,13,16,128]{3,2,1,0:T(8,128)S(1)} %collective-permute-done.4.refs_3_), channel_id=1, source_target_pairs={{0,16},{1,17},{2,18},{3,19},{4,20},{5,21},{6,22},{7,23},{8,760},{9... | collective-permute-start | bytes 958472 | tf_op jit(solution)/shard_map/ppermute | solution.py:41
  82.4 0.7 copy-start.4
  87.9 14.1 %collective-permute-start.12 = (f32[3,19,16,128]{3,2,1,0:T(8,128)}, f32[3,19,16,128]{3,2,1,0:T(8,128)S(1)}, u32[]{:S(2)}, u32[]{:S(2)}) collective-permute-start(f32[3,19,16,128]{3,2,1,0:T(8,128)} %shard_map.47.refs_8_), channel_id=1, source_target_pairs={{0,1},{1,0},{2,3},{3,2},{4,5},{5,4},{6,7},{7,6},{8,9},{9,8},{10,11... | collective-permute-start | bytes 1400840 | tf_op jit(solution)/shard_map/ppermute | solution.py:41
  90.8 11.2 %collective-permute-start.6 = (f32[3,13,16,128]{3,2,1,0:T(8,128)S(1)}, f32[3,13,16,128]{3,2,1,0:T(8,128)S(1)}, u32[]{:S(2)}, u32[]{:S(2)}) collective-permute-start(f32[3,13,16,128]{3,2,1,0:T(8,128)S(1)} %collective-permute-done.4.refs_3_), channel_id=1, source_target_pairs={{0,752},{1,753},{2,754},{3,755},{4,756},{5,757},{6,758},{7,759},{8... | collective-permute-start | bytes 958472 | tf_op jit(solution)/shard_map/ppermute | solution.py:41
  94.2 19.4 %collective-permute-start.15 = (f32[3,19,16,128]{3,2,1,0:T(8,128)}, f32[3,19,16,128]{3,2,1,0:T(8,128)}, u32[]{:S(2)}, u32[]{:S(2)}) collective-permute-start(f32[3,19,16,128]{3,2,1,0:T(8,128)} %shard_map.47.refs_8_), channel_id=1, source_target_pairs={{0,2},{1,3},{2,0},{3,1},{4,6},{5,7},{6,4},{7,5},{8,10},{9,11},{10,... | collective-permute-start | bytes 1400840 | tf_op jit(solution)/shard_map/ppermute | solution.py:41
  101.9 5.0 %copy-start.2 = (f32[3,13,16,128]{3,2,1,0:T(8,128)}, f32[3,13,16,128]{3,2,1,0:T(8,128)S(1)}, u32[]{:S(2)}) copy-start(f32[3,13,16,128]{3,2,1,0:T(8,128)S(1)} %collective-permute-done.6.refs_9_.refs_5_) | copy-start | bytes 958468
  101.9 5.0 %copy-start = (f32[3,19,16,128]{3,2,1,0:T(8,128)}, f32[3,19,16,128]{3,2,1,0:T(8,128)S(1)}, u32[]{:S(2)}) copy-start(f32[3,19,16,128]{3,2,1,0:T(8,128)S(1)} %collective-permute-done.12.refs_8_.refs_10_) | copy-start | bytes 1400836
  107.0 13.7 %collective-permute-start.14 = (f32[3,19,16,128]{3,2,1,0:T(8,128)}, f32[3,19,16,128]{3,2,1,0:T(8,128)S(1)}, u32[]{:S(2)}, u32[]{:S(2)}) collective-permute-start(f32[3,19,16,128]{3,2,1,0:T(8,128)} %shard_map.48.refs_7_.refs_2_), channel_id=1, source_target_pairs={{0,2},{1,3},{2,0},{3,1},{4,6},{5,7},{6,4},{7,5},{8,10},{9,11},{10,... | collective-permute-start | bytes 1400840 | tf_op jit(solution)/shard_map/ppermute | solution.py:41
  108.9 17.2 %collective-permute-start.13 = (f32[3,19,16,128]{3,2,1,0:T(8,128)}, f32[3,19,16,128]{3,2,1,0:T(8,128)S(1)}, u32[]{:S(2)}, u32[]{:S(2)}) collective-permute-start(f32[3,19,16,128]{3,2,1,0:T(8,128)} %shard_map.48.refs_7_.refs_2_), channel_id=1, source_target_pairs={{0,1},{1,0},{2,3},{3,2},{4,5},{5,4},{6,7},{7,6},{8,9},{9,8},{10,11... | collective-permute-start | bytes 1400840 | tf_op jit(solution)/shard_map/ppermute | solution.py:41
  111.5 14.6 %collective-permute-start.7 = (f32[3,13,16,128]{3,2,1,0:T(8,128)}, f32[3,13,16,128]{3,2,1,0:T(8,128)S(1)}, u32[]{:S(2)}, u32[]{:S(2)}) collective-permute-start(f32[3,13,16,128]{3,2,1,0:T(8,128)} %collective-permute-done.5.refs_8_.refs_4_), channel_id=1, source_target_pairs={{0,16},{1,17},{2,18},{3,19},{4,20},{5,21},{6,22},{7,23},{8,760},{9... | collective-permute-start | bytes 958472 | tf_op jit(solution)/shard_map/ppermute | solution.py:41
  113.4 19.1 %copy-start.5 = (s32[3,25]{1,0:T(4,128)S(1)}, s32[3,25]{1,0:T(4,128)}, u32[]{:S(2)}) copy-start(s32[3,25]{1,0:T(4,128)} %mask_ref.7) | copy-start | bytes 904
  113.5 18.9 %collective-permute-start.17 = (f32[3,19,16,128]{3,2,1,0:T(8,128)}, f32[3,19,16,128]{3,2,1,0:T(8,128)S(1)}, u32[]{:S(2)}, u32[]{:S(2)}) collective-permute-start(f32[3,19,16,128]{3,2,1,0:T(8,128)} %collective-permute-done.15.refs_4_), channel_id=1, source_target_pairs={{0,1},{1,0},{2,3},{3,2},{4,5},{5,4},{6,7},{7,6},{8,9},{9,8},{10,11... | collective-permute-start | bytes 1400840 | tf_op jit(solution)/shard_map/ppermute | solution.py:41
  120.6 11.8 %collective-permute-start.16 = (f32[3,19,16,128]{3,2,1,0:T(8,128)S(1)}, f32[3,19,16,128]{3,2,1,0:T(8,128)S(1)}, u32[]{:S(2)}, u32[]{:S(2)}) collective-permute-start(f32[3,19,16,128]{3,2,1,0:T(8,128)S(1)} %collective-permute-done.14.refs_3_), channel_id=1, source_target_pairs={{0,1},{1,0},{2,3},{3,2},{4,5},{5,4},{6,7},{7,6},{8,9},{9,8},{10,11... | collective-permute-start | bytes 1400840 | tf_op jit(solution)/shard_map/ppermute | solution.py:41
  126.1 1.0 copy-start.1
  127.1 1.0 copy-start.3

commit v3 on v2

--- a/solution.py
+++ b/solution.py
@@ -200,16 +200,16 @@
         out_specs=VMEM,
     )(x_mask, x_band)
 
-    own_m, pair_m = together(send(own, MIRROR), send(own, FLIP))
+    own_m, pair_m, below_o, above_o = together(
+        send(own, MIRROR), send(own, FLIP), send(own, UP), send(own, DOWN)
+    )
     both = jnp.stack([own, own_m])
-    after = send(both, NEXT)
-    pair_o = send(pair_m, MIRROR)
-    below, above = send(both, UP), send(both, DOWN)
-    twin = send(both, SIBLING)
-    beside_m = send(pair_m, ACROSS)
+    after, twin = send(both, NEXT), send(both, SIBLING)
+    pair_o, below_m, above_m, beside_m = together(
+        send(pair_m, MIRROR), send(own_m, UP), send(own_m, DOWN), send(pair_m, ACROSS)
+    )
+    beside_o, far_a = together(send(pair_o, ACROSS), send(pair_o, AGAINST))
     twin_after = send(after, SIBLING)
-    beside_o = send(pair_o, ACROSS)
-    far_a = send(pair_o, AGAINST)
     far_b = send(beside_o, ACROSS)
 
     chips = jnp.stack([low_y, 3 - low_y, low_y ^ 1, (3 - low_y) ^ 1])
@@ -222,37 +222,37 @@
 
     left = [(array, part) for array in (both, after, twin, twin_after) for part in (0, 1)]
 
-    def square_of(part, pair, beside, behind):
+    def square_of(rows, behind):
         return call(
             square_kernel,
             (square_places, sq_mask),
-            [(below, part), (above, part), (both, part), pair, beside] + left,
+            rows + left,
             jax.ShapeDtypeStruct((3, 19, 16, 128), F32),
             [
                 pltpu.VMEM((15, 208, 384), BF16),
                 pltpu.VMEM((15, 384, 384), BF16),
                 pltpu.VMEM((3, 29, 16, 128), F32),
             ],
-            20 * MIB,
-            4.5,
+            14 * MIB,
+            0.2,
             behind,
         )
 
-    square_m = square_of(1, pair_m, beside_m, (beside_o,))
+    square_m = square_of([below_m, above_m, (both, 1), pair_m, beside_m], (beside_o,))
     twin_m, next_m = send(square_m, SIBLING), send(square_m, NEXT)
-    square_o = square_of(0, pair_o, beside_o, (twin_m, far_a))
+    square_o = square_of([below_o, above_o, (both, 0), pair_o, beside_o], (twin_m,))
     twin_o, next_o = send(square_o, SIBLING), send(square_o, NEXT)
     total, window = call(
         cube_first_kernel,
         (cube_places,),
-        [(below, 0), (above, 0), (both, 0), pair_o, beside_o, far_a, far_b]
+        [below_o, above_o, (both, 0), pair_o, beside_o, far_a, far_b]
         + [square_o, square_m, twin_o, twin_m],
         (
             jax.ShapeDtypeStruct((3, 35, 16, 128), F32),
             jax.ShapeDtypeStruct((21, 208, 256), BF16),
         ),
         [pltpu.VMEM((21, 208, 256), BF16), pltpu.VMEM((21, 256, 384), BF16)],
-        24 * MIB,
+        17 * MIB,
         5,
     )
     return call(
@@ -261,7 +261,7 @@
         [total, window, square_o, next_o, next_m, send(next_o, SIBLING), send(next_m, SIBLING)],
         jax.ShapeDtypeStruct((3, 25, 16, 128), F32),
         [pltpu.VMEM((21, 256, 384), BF16), pltpu.VMEM((3, 35, 16, 128), F32)],
-        20 * MIB,
+        14 * MIB,
         4,
     )
 

time: 137 us -> 138 us (level)
  the two profiles are of different devices: /device:TPU:1 before, /device:TPU:57 now
where the time goes in v3:
time: 138 us; the launch traced here: 137 us
  starting transfers between devices  81.7 us (59%)
  waiting for transfers between devices  25.1 us (18%)
  Pallas kernels  18 us (13%)
  local copies, waits for them, and re-layouts  10.3 us (7%)
    ppermute x20, starting transfers between devices, send(): return lax.ppermute(array, AXES, which)  81.7 us
    ppermute x20, waiting for transfers between devices, send(): return lax.ppermute(array, AXES, which)  25.1 us
    pallas_call x4, Pallas kernels, call(): pl.pallas_call(functools.partial(kernel, tuple(views), len(operands)), ou...  16.2 us
    unnamed x34, local copies, waits for them, and re-layouts  10.2 us
  transfers between devices with their start and end apart: 20, of which 7 were waited for; matrix products, arithmetic and copies ran while one was open for 0% of the time, Pallas kernels for 6%

profile of v3, /device:TPU:57, one launch (start us, length us, event | category | flops | bytes accessed | tf_op | source)
XLA Modules:
  0.0 136.7 jit_solution(395476034701617678)
XLA Ops:
  0.0 1.7 %shard_map.46 = f32[3,13,16,128]{3,2,1,0:T(8,128)} custom-call(s32[3,13]{1,0:T(4,128)} %mask_ref.4, f32[3,13,16,128]{3,2,1,0:T(8,128)} %x_ref.1), custom_call_target="tpu_custom_call" | custom-call | tf_op jit(solution)/shard_map/pallas_call | solution.py:196
  1.7 4.5 %collective-permute-start = (f32[3,13,16,128]{3,2,1,0:T(8,128)}, f32[3,13,16,128]{3,2,1,0:T(8,128)}, u32[]{:S(2)}, u32[]{:S(2)}) collective-permute-start(f32[3,13,16,128]{3,2,1,0:T(8,128)} %shard_map.46), channel_id=1, source_target_pairs={{0,6},{1,7},{2,4},{3,5},{4,2},{5,3},{6,0},{7,1},{8,14},{9,15},{10,... | collective-permute-start | bytes 958472 | tf_op jit(solution)/shard_map/ppermute | solution.py:41
  6.3 2.1 %collective-permute-start.1 = (f32[3,13,16,128]{3,2,1,0:T(8,128)}, f32[3,13,16,128]{3,2,1,0:T(8,128)S(1)}, u32[]{:S(2)}, u32[]{:S(2)}) collective-permute-start(f32[3,13,16,128]{3,2,1,0:T(8,128)} %shard_map.46), channel_id=1, source_target_pairs={{0,14},{1,15},{2,12},{3,13},{4,10},{5,11},{6,8},{7,9},{8,6},{9,7},... | collective-permute-start | bytes 958472 | tf_op jit(solution)/shard_map/ppermute | solution.py:41
  8.4 3.1 %collective-permute-start.2 = (f32[3,13,16,128]{3,2,1,0:T(8,128)}, f32[3,13,16,128]{3,2,1,0:T(8,128)S(1)}, u32[]{:S(2)}, u32[]{:S(2)}) collective-permute-start(f32[3,13,16,128]{3,2,1,0:T(8,128)} %shard_map.46), channel_id=1, source_target_pairs={{0,16},{1,17},{2,18},{3,19},{4,20},{5,21},{6,22},{7,23},{8,24},{9,... | collective-permute-start | bytes 958472 | tf_op jit(solution)/shard_map/ppermute | solution.py:41
  11.5 15.3 %collective-permute-start.3 = (f32[3,13,16,128]{3,2,1,0:T(8,128)}, f32[3,13,16,128]{3,2,1,0:T(8,128)S(1)}, u32[]{:S(2)}, u32[]{:S(2)}) collective-permute-start(f32[3,13,16,128]{3,2,1,0:T(8,128)} %shard_map.46), channel_id=1, source_target_pairs={{0,752},{1,753},{2,754},{3,755},{4,756},{5,757},{6,758},{7,759},{8... | collective-permute-start | bytes 958472 | tf_op jit(solution)/shard_map/ppermute | solution.py:41
  26.8 4.9 %collective-permute-done.2.refs_0_ = f32[3,13,16,128]{3,2,1,0:T(8,128)S(1)} collective-permute-done((f32[3,13,16,128]{3,2,1,0:T(8,128)}, f32[3,13,16,128]{3,2,1,0:T(8,128)S(1)}, u32[]{:S(2)}, u32[]{:S(2)}) %collective-permute-start.2) | collective-permute-done | bytes 319520 | tf_op jit(solution)/shard_map/ppermute | solution.py:41
  31.7 0.7 copy-done.2
  32.4 0.3 collective-permute-done.3.refs_1_
  32.7 0.7 copy-done.5
  33.4 1.1 pad_maximum_fusion.refs_2_
  34.5 2.1 %collective-permute-start.11 = (f32[2,3,13,16,128]{4,3,2,1,0:T(8,128)S(1)}, f32[2,3,13,16,128]{4,3,2,1,0:T(8,128)S(1)}, u32[]{:S(2)}, u32[]{:S(2)}) collective-permute-start(f32[2,3,13,16,128]{4,3,2,1,0:T(8,128)S(1)} %pad_maximum_fusion.refs_2_), channel_id=1, source_target_pairs={{0,2},{1,3},{2,0},{3,1},{4,6},{5,7},{6,4},{7,5},{8,10},{9,11},{10,... | collective-permute-start | bytes 1916936 | tf_op jit(solution)/shard_map/ppermute | solution.py:41
  36.6 3.0 %collective-permute-start.4 = (f32[3,13,16,128]{3,2,1,0:T(8,128)S(1)}, f32[3,13,16,128]{3,2,1,0:T(8,128)S(1)}, u32[]{:S(2)}, u32[]{:S(2)}) collective-permute-start(f32[3,13,16,128]{3,2,1,0:T(8,128)S(1)} %collective-permute-done.1.refs_3_), channel_id=1, source_target_pairs={{0,6},{1,7},{2,4},{3,5},{4,2},{5,3},{6,0},{7,1},{8,14},{9,15},{10,... | collective-permute-start | bytes 958472 | tf_op jit(solution)/shard_map/ppermute | solution.py:41
  39.6 1.9 %collective-permute-start.5 = (f32[3,13,16,128]{3,2,1,0:T(8,128)}, f32[3,13,16,128]{3,2,1,0:T(8,128)S(1)}, u32[]{:S(2)}, u32[]{:S(2)}) collective-permute-start(f32[3,13,16,128]{3,2,1,0:T(8,128)} %collective-permute-done), channel_id=1, source_target_pairs={{0,16},{1,17},{2,18},{3,19},{4,20},{5,21},{6,22},{7,23},{8,24},{9,... | collective-permute-start | bytes 958472 | tf_op jit(solution)/shard_map/ppermute | solution.py:41
  41.5 9.1 %collective-permute-start.6 = (f32[3,13,16,128]{3,2,1,0:T(8,128)}, f32[3,13,16,128]{3,2,1,0:T(8,128)}, u32[]{:S(2)}, u32[]{:S(2)}) collective-permute-start(f32[3,13,16,128]{3,2,1,0:T(8,128)} %collective-permute-done), channel_id=1, source_target_pairs={{0,752},{1,753},{2,754},{3,755},{4,756},{5,757},{6,758},{7,759},{8... | collective-permute-start | bytes 958472 | tf_op jit(solution)/shard_map/ppermute | solution.py:41
  50.6 3.4 %collective-permute-start.7 = (f32[3,13,16,128]{3,2,1,0:T(8,128)S(1)}, f32[3,13,16,128]{3,2,1,0:T(8,128)}, u32[]{:S(2)}, u32[]{:S(2)}) collective-permute-start(f32[3,13,16,128]{3,2,1,0:T(8,128)S(1)} %collective-permute-done.1.refs_3_), channel_id=1, source_target_pairs={{0,16},{1,17},{2,18},{3,19},{4,20},{5,21},{6,22},{7,23},{8,760},{9... | collective-permute-start | bytes 958472 | tf_op jit(solution)/shard_map/ppermute | solution.py:41
  54.0 0.7 copy-done.11
  54.7 2.0 %collective-permute-done.4.refs_3_ = f32[3,13,16,128]{3,2,1,0:T(8,128)S(1)} collective-permute-done((f32[3,13,16,128]{3,2,1,0:T(8,128)S(1)}, f32[3,13,16,128]{3,2,1,0:T(8,128)S(1)}, u32[]{:S(2)}, u32[]{:S(2)}) %collective-permute-start.4) | collective-permute-done | bytes 319520 | tf_op jit(solution)/shard_map/ppermute | solution.py:41
  56.8 5.1 %collective-permute-start.12 = (f32[2,3,13,16,128]{4,3,2,1,0:T(8,128)S(1)}, f32[2,3,13,16,128]{4,3,2,1,0:T(8,128)S(1)}, u32[]{:S(2)}, u32[]{:S(2)}) collective-permute-start(f32[2,3,13,16,128]{4,3,2,1,0:T(8,128)S(1)} %pad_maximum_fusion.refs_2_), channel_id=1, source_target_pairs={{0,1},{1,0},{2,3},{3,2},{4,5},{5,4},{6,7},{7,6},{8,9},{9,8},{10,11... | collective-permute-start | bytes 1916936 | tf_op jit(solution)/shard_map/ppermute | solution.py:41
  61.9 1.9 %collective-permute-start.13 = (f32[2,3,13,16,128]{4,3,2,1,0:T(8,128)S(1)}, f32[2,3,13,16,128]{4,3,2,1,0:T(8,128)S(1)}, u32[]{:S(2)}, u32[]{:S(2)}) collective-permute-start(f32[2,3,13,16,128]{4,3,2,1,0:T(8,128)S(1)} %collective-permute-done.11.refs_5_), channel_id=1, source_target_pairs={{0,1},{1,0},{2,3},{3,2},{4,5},{5,4},{6,7},{7,6},{8,9},{9,8},{10,11... | collective-permute-start | bytes 1916936 | tf_op jit(solution)/shard_map/ppermute | solution.py:41
  63.8 0.7 copy-done.13
  64.6 9.1 %collective-permute-start.8 = (f32[3,13,16,128]{3,2,1,0:T(8,128)S(1)}, f32[3,13,16,128]{3,2,1,0:T(8,128)S(1)}, u32[]{:S(2)}, u32[]{:S(2)}) collective-permute-start(f32[3,13,16,128]{3,2,1,0:T(8,128)S(1)} %collective-permute-done.4.refs_3_), channel_id=1, source_target_pairs={{0,16},{1,17},{2,18},{3,19},{4,20},{5,21},{6,22},{7,23},{8,760},{9... | collective-permute-start | bytes 958472 | tf_op jit(solution)/shard_map/ppermute | solution.py:41
  73.7 1.9 %collective-permute-start.9 = (f32[3,13,16,128]{3,2,1,0:T(8,128)S(1)}, f32[3,13,16,128]{3,2,1,0:T(8,128)}, u32[]{:S(2)}, u32[]{:S(2)}) collective-permute-start(f32[3,13,16,128]{3,2,1,0:T(8,128)S(1)} %collective-permute-done.4.refs_3_), channel_id=1, source_target_pairs={{0,752},{1,753},{2,754},{3,755},{4,756},{5,757},{6,758},{7,759},{8... | collective-permute-start | bytes 958472 | tf_op jit(solution)/shard_map/ppermute | solution.py:41
  75.6 0.7 copy-done.8
  76.3 0.1 add_subtract_fusion
  76.4 0.1 concatenate.3.place_ref
  76.5 3.5 %collective-permute-done.8.refs_8_.refs_4_ = f32[3,13,16,128]{3,2,1,0:T(8,128)S(1)} collective-permute-done((f32[3,13,16,128]{3,2,1,0:T(8,128)S(1)}, f32[3,13,16,128]{3,2,1,0:T(8,128)S(1)}, u32[]{:S(2)}, u32[]{:S(2)}) %collective-permute-start.8) | collective-permute-done | bytes 319520 | tf_op jit(solution)/shard_map/ppermute | solution.py:41
  80.0 7.2 %collective-permute-done.9.refs_5_ = f32[3,13,16,128]{3,2,1,0:T(8,128)} collective-permute-done((f32[3,13,16,128]{3,2,1,0:T(8,128)S(1)}, f32[3,13,16,128]{3,2,1,0:T(8,128)}, u32[]{:S(2)}, u32[]{:S(2)}) %collective-permute-start.9) | collective-permute-done | bytes 319520 | tf_op jit(solution)/shard_map/ppermute | solution.py:41
  87.3 1.0 copy-done.12
  88.2 1.0 copy-done.14
  89.2 0.7 copy-done.15
  89.9 3.8 %shard_map.47.refs_8_ = f32[3,19,16,128]{3,2,1,0:T(8,128)S(1)} custom-call(s32[13]{0:T(128)S(1)} %concatenate.3.place_ref, s32[3,19]{1,0:T(4,128)S(1)} %copy-done.15, f32[3,13,16,128]{3,2,1,0:T(8,128)S(1)} %copy-done.14, f32[3,13,16,128]{3,2,1,0:T(8,128)} %collective-permute-done.6.refs_1_, f32[2,3,13,16,128]{4,3,2,1,0:T(8,128)S(1)} %pad_maximum_fusion.refs_2_, ...), custom_call_target="tpu_custom_call" | custom-call | flops 230000000 | bytes 4194304 | tf_op jit(solution)/shard_map/pallas_call | solution.py:179
  93.7 3.6 %collective-permute-start.14 = (f32[3,19,16,128]{3,2,1,0:T(8,128)S(1)}, f32[3,19,16,128]{3,2,1,0:T(8,128)S(1)}, u32[]{:S(2)}, u32[]{:S(2)}) collective-permute-start(f32[3,19,16,128]{3,2,1,0:T(8,128)S(1)} %shard_map.47.refs_8_), channel_id=1, source_target_pairs={{0,1},{1,0},{2,3},{3,2},{4,5},{5,4},{6,7},{7,6},{8,9},{9,8},{10,11... | collective-permute-start | bytes 1400840 | tf_op jit(solution)/shard_map/ppermute | solution.py:41
  97.3 1.9 %collective-permute-start.17 = (f32[3,19,16,128]{3,2,1,0:T(8,128)S(1)}, f32[3,19,16,128]{3,2,1,0:T(8,128)}, u32[]{:S(2)}, u32[]{:S(2)}) collective-permute-start(f32[3,19,16,128]{3,2,1,0:T(8,128)S(1)} %shard_map.47.refs_8_), channel_id=1, source_target_pairs={{0,2},{1,3},{2,0},{3,1},{4,6},{5,7},{6,4},{7,5},{8,10},{9,11},{10,... | collective-permute-start | bytes 1400840 | tf_op jit(solution)/shard_map/ppermute | solution.py:41
  99.3 4.2 %shard_map.48.refs_7_.refs_2_ = f32[3,19,16,128]{3,2,1,0:T(8,128)} custom-call(s32[13]{0:T(128)S(1)} %concatenate.3.place_ref, s32[3,19]{1,0:T(4,128)S(1)} %copy-done.15, f32[3,13,16,128]{3,2,1,0:T(8,128)S(1)} %copy-done.3, f32[3,13,16,128]{3,2,1,0:T(8,128)S(1)} %copy-done.6, f32[2,3,13,16,128]{4,3,2,1,0:T(8,128)S(1)} %pad_maximum_fusion.refs_2_, ...), custom_call_target="tpu_custom_call" | custom-call | flops 230000000 | bytes 4194304 | tf_op jit(solution)/shard_map/pallas_call | solution.py:179
  103.5 3.3 %collective-permute-start.16 = (f32[3,19,16,128]{3,2,1,0:T(8,128)}, f32[3,19,16,128]{3,2,1,0:T(8,128)S(1)}, u32[]{:S(2)}, u32[]{:S(2)}) collective-permute-start(f32[3,19,16,128]{3,2,1,0:T(8,128)} %shard_map.48.refs_7_.refs_2_), channel_id=1, source_target_pairs={{0,2},{1,3},{2,0},{3,1},{4,6},{5,7},{6,4},{7,5},{8,10},{9,11},{10,... | collective-permute-start | bytes 1400840 | tf_op jit(solution)/shard_map/ppermute | solution.py:41
  106.8 2.5 %collective-permute-start.15 = (f32[3,19,16,128]{3,2,1,0:T(8,128)}, f32[3,19,16,128]{3,2,1,0:T(8,128)S(1)}, u32[]{:S(2)}, u32[]{:S(2)}) collective-permute-start(f32[3,19,16,128]{3,2,1,0:T(8,128)} %shard_map.48.refs_7_.refs_2_), channel_id=1, source_target_pairs={{0,1},{1,0},{2,3},{3,2},{4,5},{5,4},{6,7},{7,6},{8,9},{9,8},{10,11... | collective-permute-start | bytes 1400840 | tf_op jit(solution)/shard_map/ppermute | solution.py:41
  109.3 1.9 %collective-permute-start.10 = (f32[3,13,16,128]{3,2,1,0:T(8,128)S(1)}, f32[3,13,16,128]{3,2,1,0:T(8,128)S(1)}, u32[]{:S(2)}, u32[]{:S(2)}) collective-permute-start(f32[3,13,16,128]{3,2,1,0:T(8,128)S(1)} %collective-permute-done.8.refs_8_.refs_4_), channel_id=1, source_target_pairs={{0,16},{1,17},{2,18},{3,19},{4,20},{5,21},{6,22},{7,23},{8,760},{9... | collective-permute-start | bytes 958472 | tf_op jit(solution)/shard_map/ppermute | solution.py:41
  111.2 0.1 stack.55.place_ref
  111.3 0.3 collective-permute-done.17.refs_4_
  111.6 3.1 %collective-permute-start.19 = (f32[3,19,16,128]{3,2,1,0:T(8,128)}, f32[3,19,16,128]{3,2,1,0:T(8,128)S(1)}, u32[]{:S(2)}, u32[]{:S(2)}) collective-permute-start(f32[3,19,16,128]{3,2,1,0:T(8,128)} %collective-permute-done.17.refs_4_), channel_id=1, source_target_pairs={{0,1},{1,0},{2,3},{3,2},{4,5},{5,4},{6,7},{7,6},{8,9},{9,8},{10,11... | collective-permute-start | bytes 1400840 | tf_op jit(solution)/shard_map/ppermute | solution.py:41
  114.7 6.8 %collective-permute-done.16.refs_3_ = f32[3,19,16,128]{3,2,1,0:T(8,128)S(1)} collective-permute-done((f32[3,19,16,128]{3,2,1,0:T(8,128)}, f32[3,19,16,128]{3,2,1,0:T(8,128)S(1)}, u32[]{:S(2)}, u32[]{:S(2)}) %collective-permute-start.16) | collective-permute-done | bytes 466976 | tf_op jit(solution)/shard_map/ppermute | solution.py:41
  121.5 2.9 %collective-permute-start.18 = (f32[3,19,16,128]{3,2,1,0:T(8,128)S(1)}, f32[3,19,16,128]{3,2,1,0:T(8,128)S(1)}, u32[]{:S(2)}, u32[]{:S(2)}) collective-permute-start(f32[3,19,16,128]{3,2,1,0:T(8,128)S(1)} %collective-permute-done.16.refs_3_), channel_id=1, source_target_pairs={{0,1},{1,0},{2,3},{3,2},{4,5},{5,4},{6,7},{7,6},{8,9},{9,8},{10,11... | collective-permute-start | bytes 1400840 | tf_op jit(solution)/shard_map/ppermute | solution.py:41
  124.5 1.0 copy-done.1
  125.5 1.0 copy-done.4
  126.4 1.0 copy-done.7
  127.4 1.0 copy-done.10
  128.4 4.2 %shard_map.49 = (f32[3,35,16,128]{3,2,1,0:T(8,128)S(1)}, bf16[21,208,256]{2,1,0:T(8,128)(2,1)S(1)}) custom-call(s32[9]{0:T(128)S(1)} %stack.55.place_ref, f32[3,13,16,128]{3,2,1,0:T(8,128)S(1)} %copy-done.4, f32[3,13,16,128]{3,2,1,0:T(8,128)S(1)} %copy-done.7, f32[2,3,13,16,128]{4,3,2,1,0:T(8,128)S(1)} %pad_maximum_fusion.refs_2_, ...), custom_call_target="tpu_custom_call" | custom-call | flops 5750000128 | bytes 4194304 | tf_op jit(solution)/shard_map/pallas_call | solution.py:179
  132.6 4.0 %shard_map.50 = f32[3,25,16,128]{3,2,1,0:T(8,128)} custom-call(s32[9]{0:T(128)S(1)} %stack.55.place_ref, s32[3,25]{1,0:T(4,128)S(1)} %copy-done.16, f32[3,35,16,128]{3,2,1,0:T(8,128)S(1)} %get-tuple-element.27.refs_0_, bf16[21,208,256]{2,1,0:T(8,128)(2,1)S(1)} %get-tuple-element.28.refs_1_, f32[3,19,16,128]{3,2,1,0:T(8,128)} %shard_map.48.refs_7_.refs_2_, ...), custom_call_target="tpu_custom_call" | custom-call | flops 4600000000 | bytes 4194304 | tf_op jit(solution)/shard_map/pallas_call | solution.py:179
  (36 shorter events, 0.1 us)
Async XLA Ops:
  1.7 25.1 %collective-permute-start = (f32[3,13,16,128]{3,2,1,0:T(8,128)}, f32[3,13,16,128]{3,2,1,0:T(8,128)}, u32[]{:S(2)}, u32[]{:S(2)}) collective-permute-start(f32[3,13,16,128]{3,2,1,0:T(8,128)} %shard_map.46), channel_id=1, source_target_pairs={{0,6},{1,7},{2,4},{3,5},{4,2},{5,3},{6,0},{7,1},{8,14},{9,15},{10,... | collective-permute-start | bytes 958472 | tf_op jit(solution)/shard_map/ppermute | solution.py:41
  6.3 20.5 %collective-permute-start.1 = (f32[3,13,16,128]{3,2,1,0:T(8,128)}, f32[3,13,16,128]{3,2,1,0:T(8,128)S(1)}, u32[]{:S(2)}, u32[]{:S(2)}) collective-permute-start(f32[3,13,16,128]{3,2,1,0:T(8,128)} %shard_map.46), channel_id=1, source_target_pairs={{0,14},{1,15},{2,12},{3,13},{4,10},{5,11},{6,8},{7,9},{8,6},{9,7},... | collective-permute-start | bytes 958472 | tf_op jit(solution)/shard_map/ppermute | solution.py:41
  8.4 23.3 %collective-permute-start.2 = (f32[3,13,16,128]{3,2,1,0:T(8,128)}, f32[3,13,16,128]{3,2,1,0:T(8,128)S(1)}, u32[]{:S(2)}, u32[]{:S(2)}) collective-permute-start(f32[3,13,16,128]{3,2,1,0:T(8,128)} %shard_map.46), channel_id=1, source_target_pairs={{0,16},{1,17},{2,18},{3,19},{4,20},{5,21},{6,22},{7,23},{8,24},{9,... | collective-permute-start | bytes 958472 | tf_op jit(solution)/shard_map/ppermute | solution.py:41
  11.5 21.2 %collective-permute-start.3 = (f32[3,13,16,128]{3,2,1,0:T(8,128)}, f32[3,13,16,128]{3,2,1,0:T(8,128)S(1)}, u32[]{:S(2)}, u32[]{:S(2)}) collective-permute-start(f32[3,13,16,128]{3,2,1,0:T(8,128)} %shard_map.46), channel_id=1, source_target_pairs={{0,752},{1,753},{2,754},{3,755},{4,756},{5,757},{6,758},{7,759},{8... | collective-permute-start | bytes 958472 | tf_op jit(solution)/shard_map/ppermute | solution.py:41
  31.7 0.7 copy-start.2
  32.7 0.7 copy-start.5
  34.5 27.3 %collective-permute-start.11 = (f32[2,3,13,16,128]{4,3,2,1,0:T(8,128)S(1)}, f32[2,3,13,16,128]{4,3,2,1,0:T(8,128)S(1)}, u32[]{:S(2)}, u32[]{:S(2)}) collective-permute-start(f32[2,3,13,16,128]{4,3,2,1,0:T(8,128)S(1)} %pad_maximum_fusion.refs_2_), channel_id=1, source_target_pairs={{0,2},{1,3},{2,0},{3,1},{4,6},{5,7},{6,4},{7,5},{8,10},{9,11},{10,... | collective-permute-start | bytes 1916936 | tf_op jit(solution)/shard_map/ppermute | solution.py:41
  36.6 20.1 %collective-permute-start.4 = (f32[3,13,16,128]{3,2,1,0:T(8,128)S(1)}, f32[3,13,16,128]{3,2,1,0:T(8,128)S(1)}, u32[]{:S(2)}, u32[]{:S(2)}) collective-permute-start(f32[3,13,16,128]{3,2,1,0:T(8,128)S(1)} %collective-permute-done.1.refs_3_), channel_id=1, source_target_pairs={{0,6},{1,7},{2,4},{3,5},{4,2},{5,3},{6,0},{7,1},{8,14},{9,15},{10,... | collective-permute-start | bytes 958472 | tf_op jit(solution)/shard_map/ppermute | solution.py:41
  39.6 24.2 %collective-permute-start.5 = (f32[3,13,16,128]{3,2,1,0:T(8,128)}, f32[3,13,16,128]{3,2,1,0:T(8,128)S(1)}, u32[]{:S(2)}, u32[]{:S(2)}) collective-permute-start(f32[3,13,16,128]{3,2,1,0:T(8,128)} %collective-permute-done), channel_id=1, source_target_pairs={{0,16},{1,17},{2,18},{3,19},{4,20},{5,21},{6,22},{7,23},{8,24},{9,... | collective-permute-start | bytes 958472 | tf_op jit(solution)/shard_map/ppermute | solution.py:41
  41.5 23.0 %collective-permute-start.6 = (f32[3,13,16,128]{3,2,1,0:T(8,128)}, f32[3,13,16,128]{3,2,1,0:T(8,128)}, u32[]{:S(2)}, u32[]{:S(2)}) collective-permute-start(f32[3,13,16,128]{3,2,1,0:T(8,128)} %collective-permute-done), channel_id=1, source_target_pairs={{0,752},{1,753},{2,754},{3,755},{4,756},{5,757},{6,758},{7,759},{8... | collective-permute-start | bytes 958472 | tf_op jit(solution)/shard_map/ppermute | solution.py:41
  50.6 13.9 %collective-permute-start.7 = (f32[3,13,16,128]{3,2,1,0:T(8,128)S(1)}, f32[3,13,16,128]{3,2,1,0:T(8,128)}, u32[]{:S(2)}, u32[]{:S(2)}) collective-permute-start(f32[3,13,16,128]{3,2,1,0:T(8,128)S(1)} %collective-permute-done.1.refs_3_), channel_id=1, source_target_pairs={{0,16},{1,17},{2,18},{3,19},{4,20},{5,21},{6,22},{7,23},{8,760},{9... | collective-permute-start | bytes 958472 | tf_op jit(solution)/shard_map/ppermute | solution.py:41
  54.0 0.7 copy-start.11
  56.8 30.5 %collective-permute-start.12 = (f32[2,3,13,16,128]{4,3,2,1,0:T(8,128)S(1)}, f32[2,3,13,16,128]{4,3,2,1,0:T(8,128)S(1)}, u32[]{:S(2)}, u32[]{:S(2)}) collective-permute-start(f32[2,3,13,16,128]{4,3,2,1,0:T(8,128)S(1)} %pad_maximum_fusion.refs_2_), channel_id=1, source_target_pairs={{0,1},{1,0},{2,3},{3,2},{4,5},{5,4},{6,7},{7,6},{8,9},{9,8},{10,11... | collective-permute-start | bytes 1916936 | tf_op jit(solution)/shard_map/ppermute | solution.py:41
  61.9 25.4 %collective-permute-start.13 = (f32[2,3,13,16,128]{4,3,2,1,0:T(8,128)S(1)}, f32[2,3,13,16,128]{4,3,2,1,0:T(8,128)S(1)}, u32[]{:S(2)}, u32[]{:S(2)}) collective-permute-start(f32[2,3,13,16,128]{4,3,2,1,0:T(8,128)S(1)} %collective-permute-done.11.refs_5_), channel_id=1, source_target_pairs={{0,1},{1,0},{2,3},{3,2},{4,5},{5,4},{6,7},{7,6},{8,9},{9,8},{10,11... | collective-permute-start | bytes 1916936 | tf_op jit(solution)/shard_map/ppermute | solution.py:41
  63.8 0.7 copy-start.13
  64.6 15.5 %collective-permute-start.8 = (f32[3,13,16,128]{3,2,1,0:T(8,128)S(1)}, f32[3,13,16,128]{3,2,1,0:T(8,128)S(1)}, u32[]{:S(2)}, u32[]{:S(2)}) collective-permute-start(f32[3,13,16,128]{3,2,1,0:T(8,128)S(1)} %collective-permute-done.4.refs_3_), channel_id=1, source_target_pairs={{0,16},{1,17},{2,18},{3,19},{4,20},{5,21},{6,22},{7,23},{8,760},{9... | collective-permute-start | bytes 958472 | tf_op jit(solution)/shard_map/ppermute | solution.py:41
  73.7 13.6 %collective-permute-start.9 = (f32[3,13,16,128]{3,2,1,0:T(8,128)S(1)}, f32[3,13,16,128]{3,2,1,0:T(8,128)}, u32[]{:S(2)}, u32[]{:S(2)}) collective-permute-start(f32[3,13,16,128]{3,2,1,0:T(8,128)S(1)} %collective-permute-done.4.refs_3_), channel_id=1, source_target_pairs={{0,752},{1,753},{2,754},{3,755},{4,756},{5,757},{6,758},{7,759},{8... | collective-permute-start | bytes 958472 | tf_op jit(solution)/shard_map/ppermute | solution.py:41
  75.6 0.7 copy-start.8
  76.5 22.8 %copy-start.3 = (f32[3,13,16,128]{3,2,1,0:T(8,128)S(1)}, f32[3,13,16,128]{3,2,1,0:T(8,128)}, u32[]{:S(2)}) copy-start(f32[3,13,16,128]{3,2,1,0:T(8,128)} %copy-done.2) | copy-start | bytes 958468
  76.5 22.8 %copy-start.6 = (f32[3,13,16,128]{3,2,1,0:T(8,128)S(1)}, f32[3,13,16,128]{3,2,1,0:T(8,128)}, u32[]{:S(2)}) copy-start(f32[3,13,16,128]{3,2,1,0:T(8,128)} %copy-done.5) | copy-start | bytes 958468
  76.5 22.8 %copy-start.9 = (f32[3,13,16,128]{3,2,1,0:T(8,128)S(1)}, f32[3,13,16,128]{3,2,1,0:T(8,128)}, u32[]{:S(2)}) copy-start(f32[3,13,16,128]{3,2,1,0:T(8,128)} %copy-done.8) | copy-start | bytes 958468
  87.3 1.0 copy-start.12
  88.2 1.0 copy-start.14
  89.2 0.7 copy-start.15
  93.7 5.5 %collective-permute-start.14 = (f32[3,19,16,128]{3,2,1,0:T(8,128)S(1)}, f32[3,19,16,128]{3,2,1,0:T(8,128)S(1)}, u32[]{:S(2)}, u32[]{:S(2)}) collective-permute-start(f32[3,19,16,128]{3,2,1,0:T(8,128)S(1)} %shard_map.47.refs_8_), channel_id=1, source_target_pairs={{0,1},{1,0},{2,3},{3,2},{4,5},{5,4},{6,7},{7,6},{8,9},{9,8},{10,11... | collective-permute-start | bytes 1400840 | tf_op jit(solution)/shard_map/ppermute | solution.py:41
  97.3 14.3 %collective-permute-start.17 = (f32[3,19,16,128]{3,2,1,0:T(8,128)S(1)}, f32[3,19,16,128]{3,2,1,0:T(8,128)}, u32[]{:S(2)}, u32[]{:S(2)}) collective-permute-start(f32[3,19,16,128]{3,2,1,0:T(8,128)S(1)} %shard_map.47.refs_8_), channel_id=1, source_target_pairs={{0,2},{1,3},{2,0},{3,1},{4,6},{5,7},{6,4},{7,5},{8,10},{9,11},{10,... | collective-permute-start | bytes 1400840 | tf_op jit(solution)/shard_map/ppermute | solution.py:41
  99.3 4.2 %copy-start = (f32[3,19,16,128]{3,2,1,0:T(8,128)}, f32[3,19,16,128]{3,2,1,0:T(8,128)S(1)}, u32[]{:S(2)}) copy-start(f32[3,19,16,128]{3,2,1,0:T(8,128)S(1)} %collective-permute-done.14.refs_8_.refs_10_) | copy-start | bytes 1400836
  103.5 18.1 %collective-permute-start.16 = (f32[3,19,16,128]{3,2,1,0:T(8,128)}, f32[3,19,16,128]{3,2,1,0:T(8,128)S(1)}, u32[]{:S(2)}, u32[]{:S(2)}) collective-permute-start(f32[3,19,16,128]{3,2,1,0:T(8,128)} %shard_map.48.refs_7_.refs_2_), channel_id=1, source_target_pairs={{0,2},{1,3},{2,0},{3,1},{4,6},{5,7},{6,4},{7,5},{8,10},{9,11},{10,... | collective-permute-start | bytes 1400840 | tf_op jit(solution)/shard_map/ppermute | solution.py:41
  106.8 17.6 %collective-permute-start.15 = (f32[3,19,16,128]{3,2,1,0:T(8,128)}, f32[3,19,16,128]{3,2,1,0:T(8,128)S(1)}, u32[]{:S(2)}, u32[]{:S(2)}) collective-permute-start(f32[3,19,16,128]{3,2,1,0:T(8,128)} %shard_map.48.refs_7_.refs_2_), channel_id=1, source_target_pairs={{0,1},{1,0},{2,3},{3,2},{4,5},{5,4},{6,7},{7,6},{8,9},{9,8},{10,11... | collective-permute-start | bytes 1400840 | tf_op jit(solution)/shard_map/ppermute | solution.py:41
  109.3 15.1 %collective-permute-start.10 = (f32[3,13,16,128]{3,2,1,0:T(8,128)S(1)}, f32[3,13,16,128]{3,2,1,0:T(8,128)S(1)}, u32[]{:S(2)}, u32[]{:S(2)}) collective-permute-start(f32[3,13,16,128]{3,2,1,0:T(8,128)S(1)} %collective-permute-done.8.refs_8_.refs_4_), channel_id=1, source_target_pairs={{0,16},{1,17},{2,18},{3,19},{4,20},{5,21},{6,22},{7,23},{8,760},{9... | collective-permute-start | bytes 958472 | tf_op jit(solution)/shard_map/ppermute | solution.py:41
  111.2 21.4 %copy-start.16 = (s32[3,25]{1,0:T(4,128)S(1)}, s32[3,25]{1,0:T(4,128)}, u32[]{:S(2)}) copy-start(s32[3,25]{1,0:T(4,128)} %mask_ref.7) | copy-start | bytes 904
  111.6 21.0 %collective-permute-start.19 = (f32[3,19,16,128]{3,2,1,0:T(8,128)}, f32[3,19,16,128]{3,2,1,0:T(8,128)S(1)}, u32[]{:S(2)}, u32[]{:S(2)}) collective-permute-start(f32[3,19,16,128]{3,2,1,0:T(8,128)} %collective-permute-done.17.refs_4_), channel_id=1, source_target_pairs={{0,1},{1,0},{2,3},{3,2},{4,5},{5,4},{6,7},{7,6},{8,9},{9,8},{10,11... | collective-permute-start | bytes 1400840 | tf_op jit(solution)/shard_map/ppermute | solution.py:41
  121.5 11.1 %collective-permute-start.18 = (f32[3,19,16,128]{3,2,1,0:T(8,128)S(1)}, f32[3,19,16,128]{3,2,1,0:T(8,128)S(1)}, u32[]{:S(2)}, u32[]{:S(2)}) collective-permute-start(f32[3,19,16,128]{3,2,1,0:T(8,128)S(1)} %collective-permute-done.16.refs_3_), channel_id=1, source_target_pairs={{0,1},{1,0},{2,3},{3,2},{4,5},{5,4},{6,7},{7,6},{8,9},{9,8},{10,11... | collective-permute-start | bytes 1400840 | tf_op jit(solution)/shard_map/ppermute | solution.py:41
  124.4 1.0 copy-start.1
  125.5 1.0 copy-start.4
  126.4 1.0 copy-start.7
  127.4 1.0 copy-start.10

commit v4 on v3

v4 whole, which is shorter than its diff:
```python
import functools

import jax
import jax.numpy as jnp
from jax import lax
from jax.experimental import pallas as pl
from jax.experimental.pallas import tpu as pltpu
from jax.sharding import PartitionSpec as P

Z, X, YH, YL, CORES = 12, 4, 2, 4, 2
CHAIN = Z * X
AXES = ("row", "col")
F32, BF16 = jnp.float32, jnp.bfloat16


def pairs(target):
    listed = []
    for c in range(CHAIN):
        for yh in range(YH):
            for yl in range(YL):
                for core in range(CORES):
                    to = target(c, yh, yl, core)
                    if to is not None:
                        tc, th, tl, tk = to
                        source = ((c * YH + yh) * YL + yl) * CORES + core
                        listed.append((source, (((tc % CHAIN) * YH + th) * YL + tl) * CORES + tk))
    return listed


UP = pairs(lambda c, h, l, k: (c + 1, h, l, k))
DOWN = pairs(lambda c, h, l, k: (c - 1, h, l, k))
ACROSS = pairs(lambda c, h, l, k: (c + 1 if h == 0 else c - 1, h, l, k))
AGAINST = pairs(lambda c, h, l, k: (c - 1 if h == 0 else c + 1, h, l, k))
FLIP = pairs(lambda c, h, l, k: (c, 1 - h, 3 - l, k))
MIRROR = pairs(lambda c, h, l, k: (c, h, 3 - l, k))
NEXT = pairs(lambda c, h, l, k: (c, h, l ^ 1, k))
SIBLING = pairs(lambda c, h, l, k: (c, h, l, 1 - k))


def send(array, which):
    return lax.ppermute(array, AXES, which)


def together(*arrays):
    return lax.optimization_barrier(arrays)


def split(values):
    high = values.astype(BF16)
    return high, (values - high.astype(F32)).astype(BF16)


def mask_kernel(mask_ref, x_ref, out_ref):
    for g in range(x_ref.shape[0]):
        for d in range(x_ref.shape[1]):
            out_ref[g, d] = x_ref[g, d] * mask_ref[g, d].astype(F32)


def lanes(g):
    return slice(128 * g, 128 * (g + 1))


def blank_corners(right_ref, blocks):
    for g in range(3):
        for r in range(blocks + 2):
            if not 0 <= r - g < blocks:
                right_ref[r, :, lanes(g)] = jnp.zeros((right_ref.shape[1], 128), BF16)


def put_right(right_ref, at, slab):
    blocks = slab.shape[1]
    for g in range(3):
        high, low = split(slab[g])
        for first, is_high in at:
            spot = pl.ds(pl.multiple_of(first, 16), 16)
            right_ref[g : g + blocks, spot, lanes(g)] = high if is_high else low


def accumulate(window_ref, right_ref, total_ref):
    rows = window_ref.shape[2]
    for r in range(window_ref.shape[0]):
        left = window_ref[r].reshape(13 * rows, window_ref.shape[3])
        product = jnp.dot(left, right_ref[r], preferred_element_type=F32)
        product = product.reshape(13, rows, 384)
        for g in range(3):
            total_ref[g, r + 2 - g : r + 15 - g] += product[:, :, lanes(g)]


def fetched(given, scratch, semaphores):
    copies = [
        pltpu.make_async_copy(ref, held, semaphores.at[n])
        for n, (ref, held) in enumerate(zip(given, scratch))
    ]
    for copy in copies:
        copy.start()

    def arrived(copy, held):
        def wait():
            copy.wait()
            return held

        return wait

    return [arrived(copy, held) for copy, held in zip(copies, scratch)]


def square_kernel(place_ref, mask_ref, given, out_ref, window_ref, right_ref, total_ref):
    rows, slabs = given[:10], given[10:]
    blank_corners(right_ref, 13)
    total_ref[...] = jnp.zeros_like(total_ref)
    for n, wait in enumerate(slabs):
        at = place_ref[5 + n] * 16
        put_right(right_ref, ((at, True), (128 + at, True), (256 + at, False)), wait())
    for n in range(5):
        base = place_ref[n] * 3
        for side in range(2):
            ref = rows[2 * n + side]()
            for j in range(3):
                high, low = split(ref[j])
                for part, value in enumerate((high, low, high)):
                    window_ref[base + j, :, 16 * side : 16 * side + 16, lanes(part)] = value
    accumulate(window_ref, right_ref, total_ref)
    for g in range(3):
        for e in range(19):
            kept = mask_ref[g, e].astype(F32)
            for side in range(2):
                out_ref[side, g, e] = total_ref[g, e + 5, 16 * side : 16 * side + 16] * kept


def fill_half(right_ref, chips, slabs, core):
    blank_corners(right_ref, 19)
    zero = jnp.zeros((21, 16, 384), BF16)
    for n, chip in enumerate(chips):
        other = lax.rem(chip + 2, 4)
        for k in range(2):
            right_ref[:, pl.ds(pl.multiple_of(128 + 32 * other + 16 * k, 16), 16), :] = zero
        for k, slab in ((core, slabs[n]), (1 - core, slabs[2 + n])):
            place = 32 * chip + 16 * k
            again = 32 * other + 16 * k
            put_right(right_ref, ((place, True), (again, True), (128 + place, False)), slab())


def cube_first_kernel(place_ref, given, total_ref, next_ref, window_ref, right_ref):
    rows, slabs = given[:7], given[7:]
    low_y, core = place_ref[7], place_ref[8]
    fill_half(right_ref, (low_y, 3 - low_y), slabs, core)
    chip = lax.broadcasted_iota(jnp.int32, (208, 128), 1) // 32
    mine = (chip == low_y) | (chip == 3 - low_y)
    blocks = window_ref.shape[1:3] + (128,)
    for n, wait in enumerate(rows):
        base = place_ref[n] * 3
        ref = wait()
        for j in range(3):
            values = ref[j].reshape(208, 128)
            rounded = values.astype(BF16)
            high = rounded.astype(F32)
            low = pltpu.roll(values - high, 64, 1)
            first = jnp.where(mine, high, low).astype(BF16)
            second = jnp.where(mine, low, high).astype(BF16)
            window_ref[base + j, :, :, lanes(0)] = first.reshape(blocks)
            window_ref[base + j, :, :, lanes(1)] = rounded.reshape(blocks)
            next_ref[base + j, :, :, lanes(0)] = second.reshape(blocks)
            next_ref[base + j, :, :, lanes(1)] = rounded.reshape(blocks)
    total_ref[...] = jnp.zeros_like(total_ref)
    accumulate(window_ref, right_ref, total_ref)


def cube_second_kernel(place_ref, mask_ref, given, out_ref, right_ref):
    before, window, own, slabs = given[0], given[1], given[2], given[3:]
    low_y, core = place_ref[7], place_ref[8]
    fill_half(right_ref, (low_y ^ 1, (3 - low_y) ^ 1), slabs, core)
    total_ref, window_ref, own_ref = before(), window(), own()
    accumulate(window_ref, right_ref, total_ref)
    for g in range(3):
        for f in range(25):
            value = -2.0 * total_ref[g, f + 5]
            if 3 <= f < 22:
                value = 3.0 * own_ref[g, f - 3] + value
            out_ref[g, f] = value * mask_ref[g, f].astype(F32)


SMEM = pl.BlockSpec(memory_space=pltpu.SMEM)
VMEM = pl.BlockSpec(memory_space=pltpu.VMEM)
IN_HBM = pl.BlockSpec(memory_space=pltpu.HBM)
MIB = 1024 * 1024
LIMIT = 60


def call(kernel, scalars, given, out_shape, scratch, micros):
    arrays, views, held = [], [], []
    for item in given:
        array, part = item if isinstance(item, tuple) else (item, None)
        known = [n for n, other in enumerate(arrays) if other is array]
        if not known:
            arrays.append(array)
        views.append((known[0] if known else len(arrays) - 1, part))
        held.append(pltpu.VMEM(array.shape if part is None else array.shape[1:], array.dtype))
    first = len(scalars)
    last = first + len(arrays)
    outs = len(jax.tree.leaves(out_shape))

    def whole(*refs):
        parts = [refs[first + n] if p is None else refs[first + n].at[p] for n, p in views]
        own, brought = refs[last : len(refs) - len(held) - 1], refs[len(refs) - len(held) - 1 : -1]
        kernel(*refs[:first], fetched(parts, brought, refs[-1]), *own)

    return pl.pallas_call(
        whole,
        out_shape=out_shape,
        in_specs=[SMEM] * first + [IN_HBM] * len(arrays),
        out_specs=jax.tree.map(lambda _: VMEM, out_shape),
        scratch_shapes=scratch + held + [pltpu.SemaphoreType.DMA((len(held),))],
        compiler_params=pltpu.CompilerParams(vmem_limit_bytes=LIMIT * MIB),
        cost_estimate=pl.CostEstimate(
            flops=int(micros * 1.15e9), bytes_accessed=int(micros * MIB), transcendentals=0
        ),
    )(*scalars, *arrays)


def body(x_band, x_mask, sq_mask, cube_mask):
    high_y = lax.axis_index("row") % 2
    low_y, core = lax.axis_index("col") // 2, lax.axis_index("col") % 2

    own = pl.pallas_call(
        mask_kernel,
        out_shape=jax.ShapeDtypeStruct(x_band.shape, F32),
        in_specs=[SMEM, VMEM],
        out_specs=VMEM,
    )(x_mask, x_band)

    own_m, pair_m, below_o, above_o = together(
        send(own, MIRROR), send(own, FLIP), send(own, UP), send(own, DOWN)
    )
    both = jnp.stack([own, own_m])
    after, twin = send(both, NEXT), send(both, SIBLING)
    pair_o, below_m, above_m = together(
        send(pair_m, MIRROR), send(own_m, UP), send(own_m, DOWN)
    )
    pair = jnp.stack([pair_o, pair_m])
    beside, twin_after = send(pair, ACROSS), send(after, SIBLING)

    chips = jnp.stack([low_y, 3 - low_y, low_y ^ 1, (3 - low_y) ^ 1])
    orbitals = jnp.concatenate([2 * chips + core, 2 * chips + 1 - core])
    pair_at, beside_at = 3 - 2 * high_y, 1 + 2 * high_y
    square_rows = jnp.stack([jnp.int32(0), jnp.int32(4), jnp.int32(2), pair_at, beside_at])
    square_places = jnp.concatenate([square_rows, orbitals]).astype(jnp.int32)
    cube_places = [1, 5, 3, pair_at + 1, beside_at + 1, 6 - 6 * high_y, 6 * high_y, low_y, core]
    cube_places = jnp.stack([jnp.int32(v) for v in cube_places])

    left = [(array, part) for array in (both, after, twin, twin_after) for part in (0, 1)]

    square = call(
        square_kernel,
        (square_places, sq_mask),
        [below_o, below_m, above_o, above_m, (both, 0), (both, 1)]
        + [(pair, 0), (pair, 1), (beside, 0), (beside, 1)]
        + left,
        jax.ShapeDtypeStruct((2, 3, 19, 16, 128), F32),
        [
            pltpu.VMEM((15, 13, 32, 384), BF16),
            pltpu.VMEM((15, 384, 384), BF16),
            pltpu.VMEM((3, 29, 32, 128), F32),
        ],
        0.01,
    )
    square_after = send(square, NEXT)
    square_twin, pair_late, beside_late = together(send(square, SIBLING), pair_o, beside)
    far_a, far_b = send(pair_late, AGAINST), send(beside_late, ACROSS)
    total, window = call(
        cube_first_kernel,
        (cube_places,),
        [below_o, above_o, (both, 0), (pair, 0), (beside, 0), far_a, (far_b, 0)]
        + [(square, 0), (square, 1), (square_twin, 0), (square_twin, 1)],
        (
            jax.ShapeDtypeStruct((3, 35, 16, 128), F32),
            jax.ShapeDtypeStruct((21, 13, 16, 256), BF16),
        ),
        [pltpu.VMEM((21, 13, 16, 256), BF16), pltpu.VMEM((21, 256, 384), BF16)],
        0.01,
    )
    total, square_after = together(total, square_after)
    after_twin = send(square_after, SIBLING)
    return call(
        cube_second_kernel,
        (cube_places, cube_mask),
        [total, window, (square, 0), (square_after, 0), (square_after, 1)]
        + [(after_twin, 0), (after_twin, 1)],
        jax.ShapeDtypeStruct((3, 25, 16, 128), F32),
        [pltpu.VMEM((21, 256, 384), BF16)],
        4,
    )


def solution(mesh):
    return jax.shard_map(
        body,
        mesh=mesh,
        in_specs=(P("row", None, "col", None), P("row", None), P("row", None), P("row", None)),
        out_specs=P("row", None, "col", None),
        check_vma=False,
    )
```

time: 138 us -> 144 us (1.043)
  the two profiles are of different devices: /device:TPU:57 before, /device:TPU:1 now
where the time goes in v4:
time: 144 us; the launch traced here: 143 us
  starting transfers between devices  79.7 us (55%)
  waiting for transfers between devices  35 us (24%)
  Pallas kernels  22.2 us (15%)
  local copies, waits for them, and re-layouts  3.81 us (3%)
  other arithmetic  2.25 us (2%)
    ppermute x16, starting transfers between devices, send(): return lax.ppermute(array, AXES, which)  79.7 us
    ppermute x16, waiting for transfers between devices, send(): return lax.ppermute(array, AXES, which)  35 us
    pallas_call x3, Pallas kernels, call(): pl.pallas_call(whole, out_shape=out_shape, in_specs=[SMEM] * first + [IN_...  20.5 us
  transfers between devices with their start and end apart: 16, of which 7 were waited for; matrix products, arithmetic and copies ran while one was open for 2% of the time, Pallas kernels for 4%

profile of v4, /device:TPU:1, one launch (start us, length us, event | category | flops | bytes accessed | tf_op | source)
XLA Modules:
  0.0 143.3 jit_solution(12484486378984950645)
XLA Ops:
  0.0 1.7 %shard_map.46 = f32[3,13,16,128]{3,2,1,0:T(8,128)} custom-call(s32[3,13]{1,0:T(4,128)} %mask_ref.1, f32[3,13,16,128]{3,2,1,0:T(8,128)} %x_ref.1), custom_call_target="tpu_custom_call" | custom-call | tf_op jit(solution)/shard_map/pallas_call | solution.py:224
  1.7 6.0 %collective-permute-start = (f32[3,13,16,128]{3,2,1,0:T(8,128)}, f32[3,13,16,128]{3,2,1,0:T(8,128)S(1)}, u32[]{:S(2)}, u32[]{:S(2)}) collective-permute-start(f32[3,13,16,128]{3,2,1,0:T(8,128)} %shard_map.46), channel_id=1, source_target_pairs={{0,6},{1,7},{2,4},{3,5},{4,2},{5,3},{6,0},{7,1},{8,14},{9,15},{10,... | collective-permute-start | bytes 958472 | tf_op jit(solution)/shard_map/ppermute | solution.py:41
  7.8 4.4 %collective-permute-start.1 = (f32[3,13,16,128]{3,2,1,0:T(8,128)}, f32[3,13,16,128]{3,2,1,0:T(8,128)S(1)}, u32[]{:S(2)}, u32[]{:S(2)}) collective-permute-start(f32[3,13,16,128]{3,2,1,0:T(8,128)} %shard_map.46), channel_id=1, source_target_pairs={{0,14},{1,15},{2,12},{3,13},{4,10},{5,11},{6,8},{7,9},{8,6},{9,7},... | collective-permute-start | bytes 958472 | tf_op jit(solution)/shard_map/ppermute | solution.py:41
  12.2 3.1 %collective-permute-start.2 = (f32[3,13,16,128]{3,2,1,0:T(8,128)}, f32[3,13,16,128]{3,2,1,0:T(8,128)S(1)}, u32[]{:S(2)}, u32[]{:S(2)}) collective-permute-start(f32[3,13,16,128]{3,2,1,0:T(8,128)} %shard_map.46), channel_id=1, source_target_pairs={{0,16},{1,17},{2,18},{3,19},{4,20},{5,21},{6,22},{7,23},{8,24},{9,... | collective-permute-start | bytes 958472 | tf_op jit(solution)/shard_map/ppermute | solution.py:41
  15.3 15.3 %collective-permute-start.3 = (f32[3,13,16,128]{3,2,1,0:T(8,128)}, f32[3,13,16,128]{3,2,1,0:T(8,128)S(1)}, u32[]{:S(2)}, u32[]{:S(2)}) collective-permute-start(f32[3,13,16,128]{3,2,1,0:T(8,128)} %shard_map.46), channel_id=1, source_target_pairs={{0,752},{1,753},{2,754},{3,755},{4,756},{5,757},{6,758},{7,759},{8... | collective-permute-start | bytes 958472 | tf_op jit(solution)/shard_map/ppermute | solution.py:41
  30.6 0.0 collective-permute-done
  30.6 0.0 collective-permute-done.1
  30.7 4.9 %collective-permute-done.2.refs_2_.refs_1_ = f32[3,13,16,128]{3,2,1,0:T(8,128)S(1)} collective-permute-done((f32[3,13,16,128]{3,2,1,0:T(8,128)}, f32[3,13,16,128]{3,2,1,0:T(8,128)S(1)}, u32[]{:S(2)}, u32[]{:S(2)}) %collective-permute-start.2) | collective-permute-done | bytes 319520 | tf_op jit(solution)/shard_map/ppermute | solution.py:41
  35.5 1.0 collective-permute-done.3.refs_4_.refs_2_
  36.5 1.1 pad_maximum_fusion.refs_6_.refs_3_
  37.7 2.3 %collective-permute-start.8 = (f32[2,3,13,16,128]{4,3,2,1,0:T(8,128)S(1)}, f32[2,3,13,16,128]{4,3,2,1,0:T(8,128)S(1)}, u32[]{:S(2)}, u32[]{:S(2)}) collective-permute-start(f32[2,3,13,16,128]{4,3,2,1,0:T(8,128)S(1)} %pad_maximum_fusion.refs_6_.refs_3_), channel_id=1, source_target_pairs={{0,2},{1,3},{2,0},{3,1},{4,6},{5,7},{6,4},{7,5},{8,10},{9,11},{10,... | collective-permute-start | bytes 1916936 | tf_op jit(solution)/shard_map/ppermute | solution.py:41
  40.0 1.9 %collective-permute-start.5 = (f32[3,13,16,128]{3,2,1,0:T(8,128)S(1)}, f32[3,13,16,128]{3,2,1,0:T(8,128)S(1)}, u32[]{:S(2)}, u32[]{:S(2)}) collective-permute-start(f32[3,13,16,128]{3,2,1,0:T(8,128)S(1)} %collective-permute-done), channel_id=1, source_target_pairs={{0,16},{1,17},{2,18},{3,19},{4,20},{5,21},{6,22},{7,23},{8,24},{9,... | collective-permute-start | bytes 958472 | tf_op jit(solution)/shard_map/ppermute | solution.py:41
  41.9 7.3 %collective-permute-start.6 = (f32[3,13,16,128]{3,2,1,0:T(8,128)S(1)}, f32[3,13,16,128]{3,2,1,0:T(8,128)S(1)}, u32[]{:S(2)}, u32[]{:S(2)}) collective-permute-start(f32[3,13,16,128]{3,2,1,0:T(8,128)S(1)} %collective-permute-done), channel_id=1, source_target_pairs={{0,752},{1,753},{2,754},{3,755},{4,756},{5,757},{6,758},{7,759},{8... | collective-permute-start | bytes 958472 | tf_op jit(solution)/shard_map/ppermute | solution.py:41
  49.2 3.5 %collective-permute-start.4 = (f32[3,13,16,128]{3,2,1,0:T(8,128)S(1)}, f32[3,13,16,128]{3,2,1,0:T(8,128)}, u32[]{:S(2)}, u32[]{:S(2)}) collective-permute-start(f32[3,13,16,128]{3,2,1,0:T(8,128)S(1)} %collective-permute-done.1), channel_id=1, source_target_pairs={{0,6},{1,7},{2,4},{3,5},{4,2},{5,3},{6,0},{7,1},{8,14},{9,15},{10,... | collective-permute-start | bytes 958472 | tf_op jit(solution)/shard_map/ppermute | solution.py:41
  52.8 4.6 %collective-permute-start.9 = (f32[2,3,13,16,128]{4,3,2,1,0:T(8,128)S(1)}, f32[2,3,13,16,128]{4,3,2,1,0:T(8,128)}, u32[]{:S(2)}, u32[]{:S(2)}) collective-permute-start(f32[2,3,13,16,128]{4,3,2,1,0:T(8,128)S(1)} %pad_maximum_fusion.refs_6_.refs_3_), channel_id=1, source_target_pairs={{0,1},{1,0},{2,3},{3,2},{4,5},{5,4},{6,7},{7,6},{8,9},{9,8},{10,11... | collective-permute-start | bytes 1916936 | tf_op jit(solution)/shard_map/ppermute | solution.py:41
  57.4 0.0 collective-permute-done.5.refs_3_
  57.4 0.0 copy-start.8
  57.4 0.0 collective-permute-done.6.refs_5_
  57.4 0.0 copy-start.9
  57.4 3.1 %collective-permute-done.4 = f32[3,13,16,128]{3,2,1,0:T(8,128)} collective-permute-done((f32[3,13,16,128]{3,2,1,0:T(8,128)S(1)}, f32[3,13,16,128]{3,2,1,0:T(8,128)}, u32[]{:S(2)}, u32[]{:S(2)}) %collective-permute-start.4) | collective-permute-done | bytes 319520 | tf_op jit(solution)/shard_map/ppermute | solution.py:41
  60.5 0.0 copy-done.9
  60.5 1.0 pad_maximum_fusion.1.refs_7_.refs_4_
  61.6 1.9 %collective-permute-start.7 = (f32[2,3,13,16,128]{4,3,2,1,0:T(8,128)S(1)}, f32[2,3,13,16,128]{4,3,2,1,0:T(8,128)S(1)}, u32[]{:S(2)}, u32[]{:S(2)}) collective-permute-start(f32[2,3,13,16,128]{4,3,2,1,0:T(8,128)S(1)} %pad_maximum_fusion.1.refs_7_.refs_4_), channel_id=1, source_target_pairs={{0,16},{1,17},{2,18},{3,19},{4,20},{5,21},{6,22},{7,23},{8,760},{9... | collective-permute-start | bytes 1916936 | tf_op jit(solution)/shard_map/ppermute | solution.py:41
  63.5 0.0 collective-permute-done.8.refs_9_
  63.5 5.0 %collective-permute-start.10 = (f32[2,3,13,16,128]{4,3,2,1,0:T(8,128)S(1)}, f32[2,3,13,16,128]{4,3,2,1,0:T(8,128)}, u32[]{:S(2)}, u32[]{:S(2)}) collective-permute-start(f32[2,3,13,16,128]{4,3,2,1,0:T(8,128)S(1)} %collective-permute-done.8.refs_9_), channel_id=1, source_target_pairs={{0,1},{1,0},{2,3},{3,2},{4,5},{5,4},{6,7},{7,6},{8,9},{9,8},{10,11... | collective-permute-start | bytes 1916936 | tf_op jit(solution)/shard_map/ppermute | solution.py:41
  68.6 0.1 add_subtract_fusion
  68.7 0.6 concatenate.3.refs_0_
  69.3 0.0 collective-permute-done.9.refs_10_
  69.3 12.0 %collective-permute-done.7.refs_8_.refs_5_ = f32[2,3,13,16,128]{4,3,2,1,0:T(8,128)S(1)} collective-permute-done((f32[2,3,13,16,128]{4,3,2,1,0:T(8,128)S(1)}, f32[2,3,13,16,128]{4,3,2,1,0:T(8,128)S(1)}, u32[]{:S(2)}, u32[]{:S(2)}) %collective-permute-start.7) | collective-permute-done | bytes 639008 | tf_op jit(solution)/shard_map/ppermute | solution.py:41
  81.3 0.0 collective-permute-done.10.refs_11_
  81.3 0.0 copy-done.3
  81.4 0.8 copy-done.2
  82.1 8.5 %shard_map.47.refs_8_.refs_4_ = f32[2,3,19,16,128]{4,3,2,1,0:T(8,128)} custom-call(s32[13]{0:T(128)} %concatenate.3.refs_0_, s32[3,19]{1,0:T(4,128)} %refs_1_.2, f32[3,13,16,128]{3,2,1,0:T(8,128)} %copy-done.3, f32[3,13,16,128]{3,2,1,0:T(8,128)} %copy-done.8, f32[3,13,16,128]{3,2,1,0:T(8,128)} %copy-done.4, f32[3,13,16,128]{3,2,1,0:T(8,128)} %copy-done.9, ...), custom_call_target="tpu_custom_call" | custom-call | flops 11500000 | bytes 10485 | tf_op jit(solution)/shard_map/pallas_call | solution.py:207
  90.7 5.4 %collective-permute-start.11 = (f32[2,3,19,16,128]{4,3,2,1,0:T(8,128)}, f32[2,3,19,16,128]{4,3,2,1,0:T(8,128)S(1)}, u32[]{:S(2)}, u32[]{:S(2)}) collective-permute-start(f32[2,3,19,16,128]{4,3,2,1,0:T(8,128)} %shard_map.47.refs_8_.refs_4_), channel_id=1, source_target_pairs={{0,1},{1,0},{2,3},{3,2},{4,5},{5,4},{6,7},{7,6},{8,9},{9,8},{10,11... | collective-permute-start | bytes 2801672 | tf_op jit(solution)/shard_map/ppermute | solution.py:41
  96.1 7.2 %collective-permute-start.14 = (f32[2,3,19,16,128]{4,3,2,1,0:T(8,128)}, f32[2,3,19,16,128]{4,3,2,1,0:T(8,128)S(1)}, u32[]{:S(2)}, u32[]{:S(2)}) collective-permute-start(f32[2,3,19,16,128]{4,3,2,1,0:T(8,128)} %shard_map.47.refs_8_.refs_4_), channel_id=1, source_target_pairs={{0,2},{1,3},{2,0},{3,1},{4,6},{5,7},{6,4},{7,5},{8,10},{9,11},{10,... | collective-permute-start | bytes 2801672 | tf_op jit(solution)/shard_map/ppermute | solution.py:41
  103.2 0.0 collective-permute-done.11.refs_9_
  103.2 1.9 %collective-permute-start.13 = (f32[2,3,13,16,128]{4,3,2,1,0:T(8,128)}, f32[2,3,13,16,128]{4,3,2,1,0:T(8,128)S(1)}, u32[]{:S(2)}, u32[]{:S(2)}) collective-permute-start(f32[2,3,13,16,128]{4,3,2,1,0:T(8,128)} %copy-done.2), channel_id=1, source_target_pairs={{0,16},{1,17},{2,18},{3,19},{4,20},{5,21},{6,22},{7,23},{8,760},{9... | collective-permute-start | bytes 1916936 | tf_op jit(solution)/shard_map/ppermute | solution.py:41
  105.2 6.7 %collective-permute-start.12 = (f32[3,13,16,128]{3,2,1,0:T(8,128)}, f32[3,13,16,128]{3,2,1,0:T(8,128)S(1)}, u32[]{:S(2)}, u32[]{:S(2)}) collective-permute-start(f32[3,13,16,128]{3,2,1,0:T(8,128)} %collective-permute-done.4), channel_id=1, source_target_pairs={{0,752},{1,753},{2,754},{3,755},{4,756},{5,757},{6,758},{7,759},{8... | collective-permute-start | bytes 958472 | tf_op jit(solution)/shard_map/ppermute | solution.py:41
  111.9 0.6 stack.64.refs_0_
  112.5 6.0 %collective-permute-done.12.refs_6_ = f32[3,13,16,128]{3,2,1,0:T(8,128)S(1)} collective-permute-done((f32[3,13,16,128]{3,2,1,0:T(8,128)}, f32[3,13,16,128]{3,2,1,0:T(8,128)S(1)}, u32[]{:S(2)}, u32[]{:S(2)}) %collective-permute-start.12) | collective-permute-done | bytes 319520 | tf_op jit(solution)/shard_map/ppermute | solution.py:41
  118.5 5.9 %collective-permute-done.13.refs_7_ = f32[2,3,13,16,128]{4,3,2,1,0:T(8,128)S(1)} collective-permute-done((f32[2,3,13,16,128]{4,3,2,1,0:T(8,128)}, f32[2,3,13,16,128]{4,3,2,1,0:T(8,128)S(1)}, u32[]{:S(2)}, u32[]{:S(2)}) %collective-permute-start.13) | collective-permute-done | bytes 639008 | tf_op jit(solution)/shard_map/ppermute | solution.py:41
  124.4 0.8 copy-done.7
  125.2 6.3 %shard_map.48 = (f32[3,35,16,128]{3,2,1,0:T(8,128)}, bf16[21,13,16,256]{3,2,1,0:T(8,128)(2,1)}) custom-call(s32[9]{0:T(128)} %stack.64.refs_0_, f32[3,13,16,128]{3,2,1,0:T(8,128)} %copy-done.3, f32[3,13,16,128]{3,2,1,0:T(8,128)} %copy-done.4, f32[2,3,13,16,128]{4,3,2,1,0:T(8,128)} %copy-done, f32[2,3,13,16,128]{4,3,2,1,0:T(8,128)} %copy-done.1, ...), custom_call_target="tpu_custom_call" | custom-call | flops 11500000 | bytes 10485 | tf_op jit(solution)/shard_map/pallas_call | solution.py:207
  131.5 0.0 collective-permute-done.14.refs_5_
  131.5 3.0 %collective-permute-start.15 = (f32[2,3,19,16,128]{4,3,2,1,0:T(8,128)S(1)}, f32[2,3,19,16,128]{4,3,2,1,0:T(8,128)S(1)}, u32[]{:S(2)}, u32[]{:S(2)}) collective-permute-start(f32[2,3,19,16,128]{4,3,2,1,0:T(8,128)S(1)} %collective-permute-done.14.refs_5_), channel_id=1, source_target_pairs={{0,1},{1,0},{2,3},{3,2},{4,5},{5,4},{6,7},{7,6},{8,9},{9,8},{10,11... | collective-permute-start | bytes 2801672 | tf_op jit(solution)/shard_map/ppermute | solution.py:41
  134.6 2.1 %collective-permute-done.15.refs_6_ = f32[2,3,19,16,128]{4,3,2,1,0:T(8,128)S(1)} collective-permute-done((f32[2,3,19,16,128]{4,3,2,1,0:T(8,128)S(1)}, f32[2,3,19,16,128]{4,3,2,1,0:T(8,128)S(1)}, u32[]{:S(2)}, u32[]{:S(2)}) %collective-permute-start.15) | collective-permute-done | bytes 933920 | tf_op jit(solution)/shard_map/ppermute | solution.py:41
  136.7 0.9 copy-done.12
  137.6 5.7 %shard_map.49 = f32[3,25,16,128]{3,2,1,0:T(8,128)} custom-call(s32[9]{0:T(128)} %stack.64.refs_0_, s32[3,25]{1,0:T(4,128)} %refs_1_.3, f32[3,35,16,128]{3,2,1,0:T(8,128)} %get-tuple-element.30.refs_2_, bf16[21,13,16,256]{3,2,1,0:T(8,128)(2,1)} %get-tuple-element.31.refs_3_, f32[2,3,19,16,128]{4,3,2,1,0:T(8,128)} %shard_map.47.refs_8_.refs_4_, ...), custom_call_target="tpu_custom_call" | custom-call | flops 4600000000 | bytes 4194304 | tf_op jit(solution)/shard_map/pallas_call | solution.py:207
  (20 shorter events, 0.0 us)
Async XLA Ops:
  1.7 28.9 %collective-permute-start = (f32[3,13,16,128]{3,2,1,0:T(8,128)}, f32[3,13,16,128]{3,2,1,0:T(8,128)S(1)}, u32[]{:S(2)}, u32[]{:S(2)}) collective-permute-start(f32[3,13,16,128]{3,2,1,0:T(8,128)} %shard_map.46), channel_id=1, source_target_pairs={{0,6},{1,7},{2,4},{3,5},{4,2},{5,3},{6,0},{7,1},{8,14},{9,15},{10,... | collective-permute-start | bytes 958472 | tf_op jit(solution)/shard_map/ppermute | solution.py:41
  7.8 22.9 %collective-permute-start.1 = (f32[3,13,16,128]{3,2,1,0:T(8,128)}, f32[3,13,16,128]{3,2,1,0:T(8,128)S(1)}, u32[]{:S(2)}, u32[]{:S(2)}) collective-permute-start(f32[3,13,16,128]{3,2,1,0:T(8,128)} %shard_map.46), channel_id=1, source_target_pairs={{0,14},{1,15},{2,12},{3,13},{4,10},{5,11},{6,8},{7,9},{8,6},{9,7},... | collective-permute-start | bytes 958472 | tf_op jit(solution)/shard_map/ppermute | solution.py:41
  12.2 23.3 %collective-permute-start.2 = (f32[3,13,16,128]{3,2,1,0:T(8,128)}, f32[3,13,16,128]{3,2,1,0:T(8,128)S(1)}, u32[]{:S(2)}, u32[]{:S(2)}) collective-permute-start(f32[3,13,16,128]{3,2,1,0:T(8,128)} %shard_map.46), channel_id=1, source_target_pairs={{0,16},{1,17},{2,18},{3,19},{4,20},{5,21},{6,22},{7,23},{8,24},{9,... | collective-permute-start | bytes 958472 | tf_op jit(solution)/shard_map/ppermute | solution.py:41
  15.3 21.2 %collective-permute-start.3 = (f32[3,13,16,128]{3,2,1,0:T(8,128)}, f32[3,13,16,128]{3,2,1,0:T(8,128)S(1)}, u32[]{:S(2)}, u32[]{:S(2)}) collective-permute-start(f32[3,13,16,128]{3,2,1,0:T(8,128)} %shard_map.46), channel_id=1, source_target_pairs={{0,752},{1,753},{2,754},{3,755},{4,756},{5,757},{6,758},{7,759},{8... | collective-permute-start | bytes 958472 | tf_op jit(solution)/shard_map/ppermute | solution.py:41
  35.5 45.8 %copy-start.3 = (f32[3,13,16,128]{3,2,1,0:T(8,128)}, f32[3,13,16,128]{3,2,1,0:T(8,128)S(1)}, u32[]{:S(2)}) copy-start(f32[3,13,16,128]{3,2,1,0:T(8,128)S(1)} %collective-permute-done.2.refs_2_.refs_1_) | copy-start | bytes 958468
  36.5 44.8 %copy-start.4 = (f32[3,13,16,128]{3,2,1,0:T(8,128)}, f32[3,13,16,128]{3,2,1,0:T(8,128)S(1)}, u32[]{:S(2)}) copy-start(f32[3,13,16,128]{3,2,1,0:T(8,128)S(1)} %collective-permute-done.3.refs_4_.refs_2_) | copy-start | bytes 958468
  37.7 43.7 %copy-start = (f32[2,3,13,16,128]{4,3,2,1,0:T(8,128)}, f32[2,3,13,16,128]{4,3,2,1,0:T(8,128)S(1)}, u32[]{:S(2)}) copy-start(f32[2,3,13,16,128]{4,3,2,1,0:T(8,128)S(1)} %pad_maximum_fusion.refs_6_.refs_3_) | copy-start | bytes 1916932
  37.7 25.8 %collective-permute-start.8 = (f32[2,3,13,16,128]{4,3,2,1,0:T(8,128)S(1)}, f32[2,3,13,16,128]{4,3,2,1,0:T(8,128)S(1)}, u32[]{:S(2)}, u32[]{:S(2)}) collective-permute-start(f32[2,3,13,16,128]{4,3,2,1,0:T(8,128)S(1)} %pad_maximum_fusion.refs_6_.refs_3_), channel_id=1, source_target_pairs={{0,2},{1,3},{2,0},{3,1},{4,6},{5,7},{6,4},{7,5},{8,10},{9,11},{10,... | collective-permute-start | bytes 1916936 | tf_op jit(solution)/shard_map/ppermute | solution.py:41
  40.0 17.4 %collective-permute-start.5 = (f32[3,13,16,128]{3,2,1,0:T(8,128)S(1)}, f32[3,13,16,128]{3,2,1,0:T(8,128)S(1)}, u32[]{:S(2)}, u32[]{:S(2)}) collective-permute-start(f32[3,13,16,128]{3,2,1,0:T(8,128)S(1)} %collective-permute-done), channel_id=1, source_target_pairs={{0,16},{1,17},{2,18},{3,19},{4,20},{5,21},{6,22},{7,23},{8,24},{9,... | collective-permute-start | bytes 958472 | tf_op jit(solution)/shard_map/ppermute | solution.py:41
  41.9 15.5 %collective-permute-start.6 = (f32[3,13,16,128]{3,2,1,0:T(8,128)S(1)}, f32[3,13,16,128]{3,2,1,0:T(8,128)S(1)}, u32[]{:S(2)}, u32[]{:S(2)}) collective-permute-start(f32[3,13,16,128]{3,2,1,0:T(8,128)S(1)} %collective-permute-done), channel_id=1, source_target_pairs={{0,752},{1,753},{2,754},{3,755},{4,756},{5,757},{6,758},{7,759},{8... | collective-permute-start | bytes 958472 | tf_op jit(solution)/shard_map/ppermute | solution.py:41
  49.2 11.3 %collective-permute-start.4 = (f32[3,13,16,128]{3,2,1,0:T(8,128)S(1)}, f32[3,13,16,128]{3,2,1,0:T(8,128)}, u32[]{:S(2)}, u32[]{:S(2)}) collective-permute-start(f32[3,13,16,128]{3,2,1,0:T(8,128)S(1)} %collective-permute-done.1), channel_id=1, source_target_pairs={{0,6},{1,7},{2,4},{3,5},{4,2},{5,3},{6,0},{7,1},{8,14},{9,15},{10,... | collective-permute-start | bytes 958472 | tf_op jit(solution)/shard_map/ppermute | solution.py:41
  52.8 16.6 %collective-permute-start.9 = (f32[2,3,13,16,128]{4,3,2,1,0:T(8,128)S(1)}, f32[2,3,13,16,128]{4,3,2,1,0:T(8,128)}, u32[]{:S(2)}, u32[]{:S(2)}) collective-permute-start(f32[2,3,13,16,128]{4,3,2,1,0:T(8,128)S(1)} %pad_maximum_fusion.refs_6_.refs_3_), channel_id=1, source_target_pairs={{0,1},{1,0},{2,3},{3,2},{4,5},{5,4},{6,7},{7,6},{8,9},{9,8},{10,11... | collective-permute-start | bytes 1916936 | tf_op jit(solution)/shard_map/ppermute | solution.py:41
  57.4 23.9 %copy-start.8 = (f32[3,13,16,128]{3,2,1,0:T(8,128)}, f32[3,13,16,128]{3,2,1,0:T(8,128)S(1)}, u32[]{:S(2)}) copy-start(f32[3,13,16,128]{3,2,1,0:T(8,128)S(1)} %collective-permute-done.5.refs_3_) | copy-start | bytes 958468
  57.4 3.1 %copy-start.9 = (f32[3,13,16,128]{3,2,1,0:T(8,128)}, f32[3,13,16,128]{3,2,1,0:T(8,128)S(1)}, u32[]{:S(2)}) copy-start(f32[3,13,16,128]{3,2,1,0:T(8,128)S(1)} %collective-permute-done.6.refs_5_) | copy-start | bytes 958468
  61.6 19.8 %copy-start.1 = (f32[2,3,13,16,128]{4,3,2,1,0:T(8,128)}, f32[2,3,13,16,128]{4,3,2,1,0:T(8,128)S(1)}, u32[]{:S(2)}) copy-start(f32[2,3,13,16,128]{4,3,2,1,0:T(8,128)S(1)} %pad_maximum_fusion.1.refs_7_.refs_4_) | copy-start | bytes 1916932
  61.6 19.7 %collective-permute-start.7 = (f32[2,3,13,16,128]{4,3,2,1,0:T(8,128)S(1)}, f32[2,3,13,16,128]{4,3,2,1,0:T(8,128)S(1)}, u32[]{:S(2)}, u32[]{:S(2)}) collective-permute-start(f32[2,3,13,16,128]{4,3,2,1,0:T(8,128)S(1)} %pad_maximum_fusion.1.refs_7_.refs_4_), channel_id=1, source_target_pairs={{0,16},{1,17},{2,18},{3,19},{4,20},{5,21},{6,22},{7,23},{8,760},{9... | collective-permute-start | bytes 1916936 | tf_op jit(solution)/shard_map/ppermute | solution.py:41
  63.5 17.8 %copy-start.6 = (f32[2,3,13,16,128]{4,3,2,1,0:T(8,128)}, f32[2,3,13,16,128]{4,3,2,1,0:T(8,128)S(1)}, u32[]{:S(2)}) copy-start(f32[2,3,13,16,128]{4,3,2,1,0:T(8,128)S(1)} %collective-permute-done.8.refs_9_) | copy-start | bytes 1916932
  63.5 17.8 %collective-permute-start.10 = (f32[2,3,13,16,128]{4,3,2,1,0:T(8,128)S(1)}, f32[2,3,13,16,128]{4,3,2,1,0:T(8,128)}, u32[]{:S(2)}, u32[]{:S(2)}) collective-permute-start(f32[2,3,13,16,128]{4,3,2,1,0:T(8,128)S(1)} %collective-permute-done.8.refs_9_), channel_id=1, source_target_pairs={{0,1},{1,0},{2,3},{3,2},{4,5},{5,4},{6,7},{7,6},{8,9},{9,8},{10,11... | collective-permute-start | bytes 1916936 | tf_op jit(solution)/shard_map/ppermute | solution.py:41
  81.3 0.8 copy-start.2
  90.7 12.6 %collective-permute-start.11 = (f32[2,3,19,16,128]{4,3,2,1,0:T(8,128)}, f32[2,3,19,16,128]{4,3,2,1,0:T(8,128)S(1)}, u32[]{:S(2)}, u32[]{:S(2)}) collective-permute-start(f32[2,3,19,16,128]{4,3,2,1,0:T(8,128)} %shard_map.47.refs_8_.refs_4_), channel_id=1, source_target_pairs={{0,1},{1,0},{2,3},{3,2},{4,5},{5,4},{6,7},{7,6},{8,9},{9,8},{10,11... | collective-permute-start | bytes 2801672 | tf_op jit(solution)/shard_map/ppermute | solution.py:41
  96.1 35.4 %collective-permute-start.14 = (f32[2,3,19,16,128]{4,3,2,1,0:T(8,128)}, f32[2,3,19,16,128]{4,3,2,1,0:T(8,128)S(1)}, u32[]{:S(2)}, u32[]{:S(2)}) collective-permute-start(f32[2,3,19,16,128]{4,3,2,1,0:T(8,128)} %shard_map.47.refs_8_.refs_4_), channel_id=1, source_target_pairs={{0,2},{1,3},{2,0},{3,1},{4,6},{5,7},{6,4},{7,5},{8,10},{9,11},{10,... | collective-permute-start | bytes 2801672 | tf_op jit(solution)/shard_map/ppermute | solution.py:41
  103.2 21.1 %copy-start.5 = (f32[2,3,19,16,128]{4,3,2,1,0:T(8,128)}, f32[2,3,19,16,128]{4,3,2,1,0:T(8,128)S(1)}, u32[]{:S(2)}) copy-start(f32[2,3,19,16,128]{4,3,2,1,0:T(8,128)S(1)} %collective-permute-done.11.refs_9_) | copy-start | bytes 2801668
  103.2 21.1 %collective-permute-start.13 = (f32[2,3,13,16,128]{4,3,2,1,0:T(8,128)}, f32[2,3,13,16,128]{4,3,2,1,0:T(8,128)S(1)}, u32[]{:S(2)}, u32[]{:S(2)}) collective-permute-start(f32[2,3,13,16,128]{4,3,2,1,0:T(8,128)} %copy-done.2), channel_id=1, source_target_pairs={{0,16},{1,17},{2,18},{3,19},{4,20},{5,21},{6,22},{7,23},{8,760},{9... | collective-permute-start | bytes 1916936 | tf_op jit(solution)/shard_map/ppermute | solution.py:41
  105.2 13.3 %collective-permute-start.12 = (f32[3,13,16,128]{3,2,1,0:T(8,128)}, f32[3,13,16,128]{3,2,1,0:T(8,128)S(1)}, u32[]{:S(2)}, u32[]{:S(2)}) collective-permute-start(f32[3,13,16,128]{3,2,1,0:T(8,128)} %collective-permute-done.4), channel_id=1, source_target_pairs={{0,752},{1,753},{2,754},{3,755},{4,756},{5,757},{6,758},{7,759},{8... | collective-permute-start | bytes 958472 | tf_op jit(solution)/shard_map/ppermute | solution.py:41
  118.5 5.9 %copy-start.10 = (f32[3,13,16,128]{3,2,1,0:T(8,128)}, f32[3,13,16,128]{3,2,1,0:T(8,128)S(1)}, u32[]{:S(2)}) copy-start(f32[3,13,16,128]{3,2,1,0:T(8,128)S(1)} %collective-permute-done.12.refs_6_) | copy-start | bytes 958468
  124.4 0.9 copy-start.7
  131.5 5.2 %copy-start.11 = (f32[2,3,19,16,128]{4,3,2,1,0:T(8,128)}, f32[2,3,19,16,128]{4,3,2,1,0:T(8,128)S(1)}, u32[]{:S(2)}) copy-start(f32[2,3,19,16,128]{4,3,2,1,0:T(8,128)S(1)} %collective-permute-done.14.refs_5_) | copy-start | bytes 2801668
  131.5 5.1 %collective-permute-start.15 = (f32[2,3,19,16,128]{4,3,2,1,0:T(8,128)S(1)}, f32[2,3,19,16,128]{4,3,2,1,0:T(8,128)S(1)}, u32[]{:S(2)}, u32[]{:S(2)}) collective-permute-start(f32[2,3,19,16,128]{4,3,2,1,0:T(8,128)S(1)} %collective-permute-done.14.refs_5_), channel_id=1, source_target_pairs={{0,1},{1,0},{2,3},{3,2},{4,5},{5,4},{6,7},{7,6},{8,9},{9,8},{10,11... | collective-permute-start | bytes 2801672 | tf_op jit(solution)/shard_map/ppermute | solution.py:41
  136.7 0.9 copy-start.12

commit v5 on v4

--- a/solution.py
+++ b/solution.py
@@ -76,14 +76,17 @@
             right_ref[g : g + blocks, spot, lanes(g)] = high if is_high else low
 
 
-def accumulate(window_ref, right_ref, total_ref):
-    rows = window_ref.shape[2]
-    for r in range(window_ref.shape[0]):
-        left = window_ref[r].reshape(13 * rows, window_ref.shape[3])
-        product = jnp.dot(left, right_ref[r], preferred_element_type=F32)
-        product = product.reshape(13, rows, 384)
+def accumulate(pieces, total_ref, rows, firsts):
+    for (left, right), r in zip(pieces, firsts):
+        product = jnp.dot(left, right, preferred_element_type=F32).reshape(13, rows, 384)
         for g in range(3):
-            total_ref[g, r + 2 - g : r + 15 - g] += product[:, :, lanes(g)]
+            total_ref[g, pl.ds(r + 2 - g, 13)] += product[:, :, lanes(g)]
+
+
+def all_rows(window_ref, right_ref, total_ref):
+    count, _, rows, depth = window_ref.shape
+    pieces = ((window_ref[r].reshape(13 * rows, depth), right_ref[r]) for r in range(count))
+    accumulate(pieces, total_ref, rows, range(count))
 
 
 def fetched(given, scratch, semaphores):
@@ -104,22 +107,48 @@
     return [arrived(copy, held) for copy, held in zip(copies, scratch)]
 
 
-def square_kernel(place_ref, mask_ref, given, out_ref, window_ref, right_ref, total_ref):
-    rows, slabs = given[:10], given[10:]
+def here(ref):
+    return lambda: ref
+
+
+def put_left(window_ref, base, side, ref):
+    for j in range(3):
+        high, low = split(ref[j])
+        for part, value in enumerate((high, low, high)):
+            window_ref[base + j, :, 16 * side : 16 * side + 16, lanes(part)] = value
+
+
+def square_first_kernel(
+    place_ref, given, total_ref, rest_ref, window_ref, right_ref
+):
+    rows, slabs = given[:8], given[8:]
     blank_corners(right_ref, 13)
     total_ref[...] = jnp.zeros_like(total_ref)
     for n, wait in enumerate(slabs):
         at = place_ref[5 + n] * 16
         put_right(right_ref, ((at, True), (128 + at, True), (256 + at, False)), wait())
-    for n in range(5):
-        base = place_ref[n] * 3
+    for n in range(4):
         for side in range(2):
-            ref = rows[2 * n + side]()
-            for j in range(3):
-                high, low = split(ref[j])
-                for part, value in enumerate((high, low, high)):
-                    window_ref[base + j, :, 16 * side : 16 * side + 16, lanes(part)] = value
-    accumulate(window_ref, right_ref, total_ref)
+            put_left(window_ref, 3 * n, side, rows[2 * n + side]())
+    for j in range(3):
+        rest_ref[j] = right_ref[place_ref[4] * 3 + j]
+    firsts = [place_ref[n] * 3 + j for n in range(4) for j in range(3)]
+    pieces = (
+        (window_ref[n].reshape(13 * 32, 384), right_ref[r]) for n, r in enumerate(firsts)
+    )
+    accumulate(pieces, total_ref, 32, firsts)
+
+
+def square_second_kernel(place_ref, mask_ref, given, out_ref, sent_ref, window_ref):
+    before, rest, beside_o, beside_m = given
+    kept_o = beside_o()
+    put_left(window_ref, 0, 0, kept_o)
+    put_left(window_ref, 0, 1, beside_m())
+    sent_ref[...] = kept_o[...]
+    total_ref, right_ref = before(), rest()
+    firsts = [place_ref[4] * 3 + j for j in range(3)]
+    pieces = ((window_ref[j].reshape(13 * 32, 384), right_ref[j]) for j in range(3))
+    accumulate(pieces, total_ref, 32, firsts)
     for g in range(3):
         for e in range(19):
             kept = mask_ref[g, e].astype(F32)
@@ -162,15 +191,16 @@
             next_ref[base + j, :, :, lanes(0)] = second.reshape(blocks)
             next_ref[base + j, :, :, lanes(1)] = rounded.reshape(blocks)
     total_ref[...] = jnp.zeros_like(total_ref)
-    accumulate(window_ref, right_ref, total_ref)
-
-
-def cube_second_kernel(place_ref, mask_ref, given, out_ref, right_ref):
+    all_rows(window_ref, right_ref, total_ref)
+
+
+def cube_second_kernel(place_ref, mask_ref, given, out_ref, right_ref, total_ref):
     before, window, own, slabs = given[0], given[1], given[2], given[3:]
     low_y, core = place_ref[7], place_ref[8]
     fill_half(right_ref, (low_y ^ 1, (3 - low_y) ^ 1), slabs, core)
-    total_ref, window_ref, own_ref = before(), window(), own()
-    accumulate(window_ref, right_ref, total_ref)
+    total_ref[...] = before()[...]
+    window_ref, own_ref = window(), own()
+    all_rows(window_ref, right_ref, total_ref)
     for g in range(3):
         for f in range(25):
             value = -2.0 * total_ref[g, f + 5]
@@ -183,10 +213,10 @@
 VMEM = pl.BlockSpec(memory_space=pltpu.VMEM)
 IN_HBM = pl.BlockSpec(memory_space=pltpu.HBM)
 MIB = 1024 * 1024
-LIMIT = 60
-
-
-def call(kernel, scalars, given, out_shape, scratch, micros):
+LARGE, SMALL = 60, 24
+
+
+def call(kernel, scalars, given, out_shape, scratch, limit, fetch):
     arrays, views, held = [], [], []
     for item in given:
         array, part = item if isinstance(item, tuple) else (item, None)
@@ -197,23 +227,22 @@
         held.append(pltpu.VMEM(array.shape if part is None else array.shape[1:], array.dtype))
     first = len(scalars)
     last = first + len(arrays)
-    outs = len(jax.tree.leaves(out_shape))
+    extra = held + [pltpu.SemaphoreType.DMA((len(held),))] if fetch else []
 
     def whole(*refs):
         parts = [refs[first + n] if p is None else refs[first + n].at[p] for n, p in views]
-        own, brought = refs[last : len(refs) - len(held) - 1], refs[len(refs) - len(held) - 1 : -1]
-        kernel(*refs[:first], fetched(parts, brought, refs[-1]), *own)
+        end = len(refs) - len(extra)
+        waits = fetched(parts, refs[end:-1], refs[-1]) if fetch else [here(p) for p in parts]
+        kernel(*refs[:first], waits, *refs[last:end])
 
     return pl.pallas_call(
         whole,
         out_shape=out_shape,
-        in_specs=[SMEM] * first + [IN_HBM] * len(arrays),
+        in_specs=[SMEM] * first + [IN_HBM if fetch else VMEM] * len(arrays),
         out_specs=jax.tree.map(lambda _: VMEM, out_shape),
-        scratch_shapes=scratch + held + [pltpu.SemaphoreType.DMA((len(held),))],
-        compiler_params=pltpu.CompilerParams(vmem_limit_bytes=LIMIT * MIB),
-        cost_estimate=pl.CostEstimate(
-            flops=int(micros * 1.15e9), bytes_accessed=int(micros * MIB), transcendentals=0
-        ),
+        scratch_shapes=scratch + extra,
+        compiler_params=pltpu.CompilerParams(vmem_limit_bytes=limit * MIB),
+        cost_estimate=pl.CostEstimate(flops=1000000, bytes_accessed=1000, transcendentals=0),
     )(*scalars, *arrays)
 
 
@@ -233,9 +262,8 @@
     )
     both = jnp.stack([own, own_m])
     after, twin = send(both, NEXT), send(both, SIBLING)
-    pair_o, below_m, above_m = together(
-        send(pair_m, MIRROR), send(own_m, UP), send(own_m, DOWN)
-    )
+    pair_o = send(pair_m, MIRROR)
+    after, below_m, above_m = together(after, send(own_m, UP), send(own_m, DOWN))
     pair = jnp.stack([pair_o, pair_m])
     beside, twin_after = send(pair, ACROSS), send(after, SIBLING)
 
@@ -249,34 +277,45 @@
 
     left = [(array, part) for array in (both, after, twin, twin_after) for part in (0, 1)]
 
-    square = call(
-        square_kernel,
+    partial, rest = call(
+        square_first_kernel,
+        (square_places,),
+        [below_o, below_m, above_o, above_m, (both, 0), (both, 1), (pair, 0), (pair, 1)] + left,
+        (
+            jax.ShapeDtypeStruct((3, 29, 32, 128), F32),
+            jax.ShapeDtypeStruct((3, 384, 384), BF16),
+        ),
+        [pltpu.VMEM((12, 13, 32, 384), BF16), pltpu.VMEM((15, 384, 384), BF16)],
+        LARGE,
+        True,
+    )
+    square, beside_o = call(
+        square_second_kernel,
         (square_places, sq_mask),
-        [below_o, below_m, above_o, above_m, (both, 0), (both, 1)]
-        + [(pair, 0), (pair, 1), (beside, 0), (beside, 1)]
-        + left,
-        jax.ShapeDtypeStruct((2, 3, 19, 16, 128), F32),
-        [
-            pltpu.VMEM((15, 13, 32, 384), BF16),
-            pltpu.VMEM((15, 384, 384), BF16),
-            pltpu.VMEM((3, 29, 32, 128), F32),
-        ],
-        0.01,
+        [partial, rest, (beside, 0), (beside, 1)],
+        (
+            jax.ShapeDtypeStruct((2, 3, 19, 16, 128), F32),
+            jax.ShapeDtypeStruct((3, 13, 16, 128), F32),
+        ),
+        [pltpu.VMEM((3, 13, 32, 384), BF16)],
+        LARGE,
+        True,
     )
     square_after = send(square, NEXT)
-    square_twin, pair_late, beside_late = together(send(square, SIBLING), pair_o, beside)
+    square_twin, pair_late, beside_late = together(send(square, SIBLING), pair_o, beside_o)
     far_a, far_b = send(pair_late, AGAINST), send(beside_late, ACROSS)
     total, window = call(
         cube_first_kernel,
         (cube_places,),
-        [below_o, above_o, (both, 0), (pair, 0), (beside, 0), far_a, (far_b, 0)]
+        [below_o, above_o, (both, 0), (pair, 0), beside_o, far_a, far_b]
         + [(square, 0), (square, 1), (square_twin, 0), (square_twin, 1)],
         (
             jax.ShapeDtypeStruct((3, 35, 16, 128), F32),
             jax.ShapeDtypeStruct((21, 13, 16, 256), BF16),
         ),
         [pltpu.VMEM((21, 13, 16, 256), BF16), pltpu.VMEM((21, 256, 384), BF16)],
-        0.01,
+        SMALL,
+        False,
     )
     total, square_after = together(total, square_after)
     after_twin = send(square_after, SIBLING)
@@ -286,8 +325,9 @@
         [total, window, (square, 0), (square_after, 0), (square_after, 1)]
         + [(after_twin, 0), (after_twin, 1)],
         jax.ShapeDtypeStruct((3, 25, 16, 128), F32),
-        [pltpu.VMEM((21, 256, 384), BF16)],
-        4,
+        [pltpu.VMEM((21, 256, 384), BF16), pltpu.VMEM((3, 35, 16, 128), F32)],
+        SMALL,
+        False,
     )
 
 

time: 144 us -> 132 us (0.917)
  waiting for transfers between devices: 35 us -> 26.8 us
  starting transfers between devices: 79.7 us -> 73.2 us
  local copies, waits for them, and re-layouts: 3.81 us -> 5.34 us
    ppermute x16, waiting for transfers between devices: 35 us -> 26.8 us  [send(): return lax.ppermute(array, AXES, which)]
    ppermute x16, starting transfers between devices: 79.7 us -> 73.2 us  [send(): return lax.ppermute(array, AXES, which)]
    unnamed x26 -> x30, local copies, waits for them, and re-layouts: 2.6 us -> 4.56 us
    pallas_call x3 -> x4, Pallas kernels: 20.5 us -> 20.2 us  [call(): pl.pallas_call(whole, out_shape=out_shape, in_specs=[SMEM] * first + [IN_...]
  transfers between devices with their start and end apart: 16 -> 16, of which waited for: 7 -> 7; matrix products, arithmetic and copies ran while one was open for 2% -> 2% of each run, Pallas kernels for 4% -> 10%
where the time goes in v5:
time: 132 us; the launch traced here: 131 us
  starting transfers between devices  73.2 us (55%)
  waiting for transfers between devices  26.8 us (20%)
  Pallas kernels  21.9 us (17%)
  local copies, waits for them, and re-layouts  5.34 us (4%)
  other arithmetic  3.08 us (2%)
    ppermute x16, starting transfers between devices, send(): return lax.ppermute(array, AXES, which)  73.2 us
    ppermute x16, waiting for transfers between devices, send(): return lax.ppermute(array, AXES, which)  26.8 us
    pallas_call x4, Pallas kernels, call(): pl.pallas_call(whole, out_shape=out_shape, in_specs=[SMEM] * first + [IN_...  20.2 us
    unnamed x30, local copies, waits for them, and re-layouts  4.56 us
  transfers between devices with their start and end apart: 16, of which 7 were waited for; matrix products, arithmetic and copies ran while one was open for 2% of the time, Pallas kernels for 10%

profile of v5, /device:TPU:1, one launch (start us, length us, event | category | flops | bytes accessed | tf_op | source)
XLA Modules:
  0.0 130.7 jit_solution(9276442795148954130)
XLA Ops:
  0.0 1.7 %shard_map.46 = f32[3,13,16,128]{3,2,1,0:T(8,128)} custom-call(s32[3,13]{1,0:T(4,128)} %mask_ref.1, f32[3,13,16,128]{3,2,1,0:T(8,128)} %x_ref.1), custom_call_target="tpu_custom_call" | custom-call | tf_op jit(solution)/shard_map/pallas_call | solution.py:253
  1.7 6.0 %collective-permute-start = (f32[3,13,16,128]{3,2,1,0:T(8,128)}, f32[3,13,16,128]{3,2,1,0:T(8,128)S(1)}, u32[]{:S(2)}, u32[]{:S(2)}) collective-permute-start(f32[3,13,16,128]{3,2,1,0:T(8,128)} %shard_map.46), channel_id=1, source_target_pairs={{0,6},{1,7},{2,4},{3,5},{4,2},{5,3},{6,0},{7,1},{8,14},{9,15},{10,... | collective-permute-start | bytes 958472 | tf_op jit(solution)/shard_map/ppermute | solution.py:41
  7.8 4.4 %collective-permute-start.1 = (f32[3,13,16,128]{3,2,1,0:T(8,128)}, f32[3,13,16,128]{3,2,1,0:T(8,128)S(1)}, u32[]{:S(2)}, u32[]{:S(2)}) collective-permute-start(f32[3,13,16,128]{3,2,1,0:T(8,128)} %shard_map.46), channel_id=1, source_target_pairs={{0,14},{1,15},{2,12},{3,13},{4,10},{5,11},{6,8},{7,9},{8,6},{9,7},... | collective-permute-start | bytes 958472 | tf_op jit(solution)/shard_map/ppermute | solution.py:41
  12.2 3.1 %collective-permute-start.2 = (f32[3,13,16,128]{3,2,1,0:T(8,128)}, f32[3,13,16,128]{3,2,1,0:T(8,128)S(1)}, u32[]{:S(2)}, u32[]{:S(2)}) collective-permute-start(f32[3,13,16,128]{3,2,1,0:T(8,128)} %shard_map.46), channel_id=1, source_target_pairs={{0,16},{1,17},{2,18},{3,19},{4,20},{5,21},{6,22},{7,23},{8,24},{9,... | collective-permute-start | bytes 958472 | tf_op jit(solution)/shard_map/ppermute | solution.py:41
  15.3 15.3 %collective-permute-start.3 = (f32[3,13,16,128]{3,2,1,0:T(8,128)}, f32[3,13,16,128]{3,2,1,0:T(8,128)S(1)}, u32[]{:S(2)}, u32[]{:S(2)}) collective-permute-start(f32[3,13,16,128]{3,2,1,0:T(8,128)} %shard_map.46), channel_id=1, source_target_pairs={{0,752},{1,753},{2,754},{3,755},{4,756},{5,757},{6,758},{7,759},{8... | collective-permute-start | bytes 958472 | tf_op jit(solution)/shard_map/ppermute | solution.py:41
  30.6 0.0 collective-permute-done
  30.6 0.0 collective-permute-done.1
  30.7 4.9 %collective-permute-done.2.refs_1_ = f32[3,13,16,128]{3,2,1,0:T(8,128)S(1)} collective-permute-done((f32[3,13,16,128]{3,2,1,0:T(8,128)}, f32[3,13,16,128]{3,2,1,0:T(8,128)S(1)}, u32[]{:S(2)}, u32[]{:S(2)}) %collective-permute-start.2) | collective-permute-done | bytes 319520 | tf_op jit(solution)/shard_map/ppermute | solution.py:41
  35.5 1.0 collective-permute-done.3.refs_3_.refs_2_
  36.5 1.1 pad_maximum_fusion.refs_5_.refs_3_
  37.7 2.3 %collective-permute-start.5 = (f32[2,3,13,16,128]{4,3,2,1,0:T(8,128)S(1)}, f32[2,3,13,16,128]{4,3,2,1,0:T(8,128)S(1)}, u32[]{:S(2)}, u32[]{:S(2)}) collective-permute-start(f32[2,3,13,16,128]{4,3,2,1,0:T(8,128)S(1)} %pad_maximum_fusion.refs_5_.refs_3_), channel_id=1, source_target_pairs={{0,2},{1,3},{2,0},{3,1},{4,6},{5,7},{6,4},{7,5},{8,10},{9,11},{10,... | collective-permute-start | bytes 1916936 | tf_op jit(solution)/shard_map/ppermute | solution.py:41
  40.0 1.9 %collective-permute-start.6 = (f32[3,13,16,128]{3,2,1,0:T(8,128)S(1)}, f32[3,13,16,128]{3,2,1,0:T(8,128)S(1)}, u32[]{:S(2)}, u32[]{:S(2)}) collective-permute-start(f32[3,13,16,128]{3,2,1,0:T(8,128)S(1)} %collective-permute-done), channel_id=1, source_target_pairs={{0,16},{1,17},{2,18},{3,19},{4,20},{5,21},{6,22},{7,23},{8,24},{9,... | collective-permute-start | bytes 958472 | tf_op jit(solution)/shard_map/ppermute | solution.py:41
  41.9 7.3 %collective-permute-start.7 = (f32[3,13,16,128]{3,2,1,0:T(8,128)S(1)}, f32[3,13,16,128]{3,2,1,0:T(8,128)S(1)}, u32[]{:S(2)}, u32[]{:S(2)}) collective-permute-start(f32[3,13,16,128]{3,2,1,0:T(8,128)S(1)} %collective-permute-done), channel_id=1, source_target_pairs={{0,752},{1,753},{2,754},{3,755},{4,756},{5,757},{6,758},{7,759},{8... | collective-permute-start | bytes 958472 | tf_op jit(solution)/shard_map/ppermute | solution.py:41
  49.3 3.5 %collective-permute-start.4 = (f32[3,13,16,128]{3,2,1,0:T(8,128)S(1)}, f32[3,13,16,128]{3,2,1,0:T(8,128)}, u32[]{:S(2)}, u32[]{:S(2)}) collective-permute-start(f32[3,13,16,128]{3,2,1,0:T(8,128)S(1)} %collective-permute-done.1), channel_id=1, source_target_pairs={{0,6},{1,7},{2,4},{3,5},{4,2},{5,3},{6,0},{7,1},{8,14},{9,15},{10,... | collective-permute-start | bytes 958472 | tf_op jit(solution)/shard_map/ppermute | solution.py:41
  52.8 4.6 %collective-permute-start.8 = (f32[2,3,13,16,128]{4,3,2,1,0:T(8,128)S(1)}, f32[2,3,13,16,128]{4,3,2,1,0:T(8,128)S(1)}, u32[]{:S(2)}, u32[]{:S(2)}) collective-permute-start(f32[2,3,13,16,128]{4,3,2,1,0:T(8,128)S(1)} %pad_maximum_fusion.refs_5_.refs_3_), channel_id=1, source_target_pairs={{0,1},{1,0},{2,3},{3,2},{4,5},{5,4},{6,7},{7,6},{8,9},{9,8},{10,11... | collective-permute-start | bytes 1916936 | tf_op jit(solution)/shard_map/ppermute | solution.py:41
  57.4 0.0 collective-permute-done.6.refs_2_
  57.4 0.0 copy-start.13
  57.4 0.0 collective-permute-done.7.refs_4_
  57.4 0.7 copy-done.14
  58.2 0.0 collective-permute-done.5.refs_7_
  58.2 1.9 %collective-permute-start.9 = (f32[2,3,13,16,128]{4,3,2,1,0:T(8,128)S(1)}, f32[2,3,13,16,128]{4,3,2,1,0:T(8,128)S(1)}, u32[]{:S(2)}, u32[]{:S(2)}) collective-permute-start(f32[2,3,13,16,128]{4,3,2,1,0:T(8,128)S(1)} %collective-permute-done.5.refs_7_), channel_id=1, source_target_pairs={{0,1},{1,0},{2,3},{3,2},{4,5},{5,4},{6,7},{7,6},{8,9},{9,8},{10,11... | collective-permute-start | bytes 1916936 | tf_op jit(solution)/shard_map/ppermute | solution.py:41
  60.1 0.4 collective-permute-done.4
  60.5 1.8 %pad_maximum_fusion.1.refs_6_.refs_4_ = f32[2,3,13,16,128]{4,3,2,1,0:T(8,128)} fusion(f32[1,3,13,16,128]{4,3,2,1,0:T(8,128)S(1)} %bitcast.16, f32[1,3,13,16,128]{4,3,2,1,0:T(8,128)} %bitcast.8), kind=kLoop, calls=%fused_computation.1 | loop fusion | flops 159744 | bytes 1277952 | tf_op jit(solution)/shard_map/stack | solution.py:267
  62.4 1.9 %collective-permute-start.10 = (f32[2,3,13,16,128]{4,3,2,1,0:T(8,128)}, f32[2,3,13,16,128]{4,3,2,1,0:T(8,128)}, u32[]{:S(2)}, u32[]{:S(2)}) collective-permute-start(f32[2,3,13,16,128]{4,3,2,1,0:T(8,128)} %pad_maximum_fusion.1.refs_6_.refs_4_), channel_id=1, source_target_pairs={{0,16},{1,17},{2,18},{3,19},{4,20},{5,21},{6,22},{7,23},{8,760},{9... | collective-permute-start | bytes 1916936 | tf_op jit(solution)/shard_map/ppermute | solution.py:41
  64.4 0.1 add_subtract_fusion
  64.4 0.7 concatenate.3.refs_0_
  65.1 0.0 collective-permute-done.8.refs_8_
  65.1 0.0 collective-permute-done.9.refs_9_
  65.2 0.8 copy-done.11
  66.0 0.8 copy-done.12
  66.8 8.1 %shard_map.47 = (f32[3,29,32,128]{3,2,1,0:T(8,128)}, bf16[3,384,384]{2,1,0:T(8,128)(2,1)}) custom-call(s32[13]{0:T(128)} %concatenate.3.refs_0_, f32[3,13,16,128]{3,2,1,0:T(8,128)} %copy-done.4, f32[3,13,16,128]{3,2,1,0:T(8,128)} %copy-done.13, f32[3,13,16,128]{3,2,1,0:T(8,128)} %copy-done.6, f32[3,13,16,128]{3,2,1,0:T(8,128)} %copy-done.14, ...), custom_call_target="tpu_custom_call" | custom-call | flops 1000000 | bytes 1000 | tf_op jit(solution)/shard_map/pallas_call | solution.py:238
  75.0 7.5 %collective-permute-done.10.refs_4_ = f32[2,3,13,16,128]{4,3,2,1,0:T(8,128)} collective-permute-done((f32[2,3,13,16,128]{4,3,2,1,0:T(8,128)}, f32[2,3,13,16,128]{4,3,2,1,0:T(8,128)}, u32[]{:S(2)}, u32[]{:S(2)}) %collective-permute-start.10) | collective-permute-done | bytes 639008 | tf_op jit(solution)/shard_map/ppermute | solution.py:41
  82.4 4.3 %shard_map.48 = (f32[2,3,19,16,128]{4,3,2,1,0:T(8,128)}, f32[3,13,16,128]{3,2,1,0:T(8,128)}) custom-call(s32[13]{0:T(128)} %concatenate.3.refs_0_, s32[3,19]{1,0:T(4,128)} %refs_1_.2, f32[3,29,32,128]{3,2,1,0:T(8,128)} %get-tuple-element.30.refs_2_, bf16[3,384,384]{2,1,0:T(8,128)(2,1)} %get-tuple-element.31.refs_3_, ...), custom_call_target="tpu_custom_call" | custom-call | flops 1000000 | bytes 1000 | tf_op jit(solution)/shard_map/pallas_call | solution.py:238
  86.8 5.4 %collective-permute-start.11 = (f32[2,3,19,16,128]{4,3,2,1,0:T(8,128)}, f32[2,3,19,16,128]{4,3,2,1,0:T(8,128)S(1)}, u32[]{:S(2)}, u32[]{:S(2)}) collective-permute-start(f32[2,3,19,16,128]{4,3,2,1,0:T(8,128)} %get-tuple-element.33.refs_8_.refs_4_), channel_id=1, source_target_pairs={{0,1},{1,0},{2,3},{3,2},{4,5},{5,4},{6,7},{7,6},{8,9},{9,8},{10,11... | collective-permute-start | bytes 2801672 | tf_op jit(solution)/shard_map/ppermute | solution.py:41
  92.2 7.2 %collective-permute-start.14 = (f32[2,3,19,16,128]{4,3,2,1,0:T(8,128)}, f32[2,3,19,16,128]{4,3,2,1,0:T(8,128)S(1)}, u32[]{:S(2)}, u32[]{:S(2)}) collective-permute-start(f32[2,3,19,16,128]{4,3,2,1,0:T(8,128)} %get-tuple-element.33.refs_8_.refs_4_), channel_id=1, source_target_pairs={{0,2},{1,3},{2,0},{3,1},{4,6},{5,7},{6,4},{7,5},{8,10},{9,11},{10,... | collective-permute-start | bytes 2801672 | tf_op jit(solution)/shard_map/ppermute | solution.py:41
  99.4 0.0 collective-permute-done.11.refs_9_
  99.4 1.9 %collective-permute-start.12 = (f32[3,13,16,128]{3,2,1,0:T(8,128)}, f32[3,13,16,128]{3,2,1,0:T(8,128)S(1)}, u32[]{:S(2)}, u32[]{:S(2)}) collective-permute-start(f32[3,13,16,128]{3,2,1,0:T(8,128)} %collective-permute-done.4), channel_id=1, source_target_pairs={{0,752},{1,753},{2,754},{3,755},{4,756},{5,757},{6,758},{7,759},{8... | collective-permute-start | bytes 958472 | tf_op jit(solution)/shard_map/ppermute | solution.py:41
  101.3 3.4 %collective-permute-start.13 = (f32[3,13,16,128]{3,2,1,0:T(8,128)}, f32[3,13,16,128]{3,2,1,0:T(8,128)}, u32[]{:S(2)}, u32[]{:S(2)}) collective-permute-start(f32[3,13,16,128]{3,2,1,0:T(8,128)} %get-tuple-element.35.refs_5_), channel_id=1, source_target_pairs={{0,16},{1,17},{2,18},{3,19},{4,20},{5,21},{6,22},{7,23},{8,760},{9... | collective-permute-start | bytes 958472 | tf_op jit(solution)/shard_map/ppermute | solution.py:41
  104.7 0.0 copy-start.9
  104.7 0.1 stack.64.refs_0_
  104.8 5.6 %collective-permute-done.12.refs_6_ = f32[3,13,16,128]{3,2,1,0:T(8,128)S(1)} collective-permute-done((f32[3,13,16,128]{3,2,1,0:T(8,128)}, f32[3,13,16,128]{3,2,1,0:T(8,128)S(1)}, u32[]{:S(2)}, u32[]{:S(2)}) %collective-permute-start.12) | collective-permute-done | bytes 319520 | tf_op jit(solution)/shard_map/ppermute | solution.py:41
  110.4 5.2 %collective-permute-done.13.refs_7_ = f32[3,13,16,128]{3,2,1,0:T(8,128)} collective-permute-done((f32[3,13,16,128]{3,2,1,0:T(8,128)}, f32[3,13,16,128]{3,2,1,0:T(8,128)}, u32[]{:S(2)}, u32[]{:S(2)}) %collective-permute-start.13) | collective-permute-done | bytes 319520 | tf_op jit(solution)/shard_map/ppermute | solution.py:41
  115.7 1.2 copy-done.2
  116.9 1.0 copy-done.8
  117.8 4.3 %shard_map.49 = (f32[3,35,16,128]{3,2,1,0:T(8,128)S(1)}, bf16[21,13,16,256]{3,2,1,0:T(8,128)(2,1)S(1)}) custom-call(s32[9]{0:T(128)S(1)} %stack.64.refs_0_, f32[3,13,16,128]{3,2,1,0:T(8,128)S(1)} %copy-done.5, f32[3,13,16,128]{3,2,1,0:T(8,128)S(1)} %copy-done.7, f32[2,3,13,16,128]{4,3,2,1,0:T(8,128)S(1)} %copy-done.1, ...), custom_call_target="tpu_custom_call" | custom-call | flops 1000000 | bytes 1000 | tf_op jit(solution)/shard_map/pallas_call | solution.py:238
  122.2 3.0 %collective-permute-start.15 = (f32[2,3,19,16,128]{4,3,2,1,0:T(8,128)S(1)}, f32[2,3,19,16,128]{4,3,2,1,0:T(8,128)S(1)}, u32[]{:S(2)}, u32[]{:S(2)}) collective-permute-start(f32[2,3,19,16,128]{4,3,2,1,0:T(8,128)S(1)} %collective-permute-done.14.refs_5_), channel_id=1, source_target_pairs={{0,1},{1,0},{2,3},{3,2},{4,5},{5,4},{6,7},{7,6},{8,9},{9,8},{10,11... | collective-permute-start | bytes 2801672 | tf_op jit(solution)/shard_map/ppermute | solution.py:41
  125.2 2.1 %collective-permute-done.15.refs_6_ = f32[2,3,19,16,128]{4,3,2,1,0:T(8,128)S(1)} collective-permute-done((f32[2,3,19,16,128]{4,3,2,1,0:T(8,128)S(1)}, f32[2,3,19,16,128]{4,3,2,1,0:T(8,128)S(1)}, u32[]{:S(2)}, u32[]{:S(2)}) %collective-permute-start.15) | collective-permute-done | bytes 933920 | tf_op jit(solution)/shard_map/ppermute | solution.py:41
  127.3 3.4 %shard_map.50 = f32[3,25,16,128]{3,2,1,0:T(8,128)} custom-call(s32[9]{0:T(128)S(1)} %stack.64.refs_0_, s32[3,25]{1,0:T(4,128)S(1)} %copy-done.9, f32[3,35,16,128]{3,2,1,0:T(8,128)S(1)} %get-tuple-element.38.refs_2_, bf16[21,13,16,256]{3,2,1,0:T(8,128)(2,1)S(1)} %get-tuple-element.39.refs_3_, f32[2,3,19,16,128]{4,3,2,1,0:T(8,128)S(1)} %copy-done.3, ...), custom_call_target="tpu_custom_call" | custom-call | flops 1000000 | bytes 1000 | tf_op jit(solution)/shard_map/pallas_call | solution.py:238
  (25 shorter events, 0.1 us)
Async XLA Ops:
  1.7 28.9 %collective-permute-start = (f32[3,13,16,128]{3,2,1,0:T(8,128)}, f32[3,13,16,128]{3,2,1,0:T(8,128)S(1)}, u32[]{:S(2)}, u32[]{:S(2)}) collective-permute-start(f32[3,13,16,128]{3,2,1,0:T(8,128)} %shard_map.46), channel_id=1, source_target_pairs={{0,6},{1,7},{2,4},{3,5},{4,2},{5,3},{6,0},{7,1},{8,14},{9,15},{10,... | collective-permute-start | bytes 958472 | tf_op jit(solution)/shard_map/ppermute | solution.py:41
  7.8 22.9 %collective-permute-start.1 = (f32[3,13,16,128]{3,2,1,0:T(8,128)}, f32[3,13,16,128]{3,2,1,0:T(8,128)S(1)}, u32[]{:S(2)}, u32[]{:S(2)}) collective-permute-start(f32[3,13,16,128]{3,2,1,0:T(8,128)} %shard_map.46), channel_id=1, source_target_pairs={{0,14},{1,15},{2,12},{3,13},{4,10},{5,11},{6,8},{7,9},{8,6},{9,7},... | collective-permute-start | bytes 958472 | tf_op jit(solution)/shard_map/ppermute | solution.py:41
  12.2 23.3 %collective-permute-start.2 = (f32[3,13,16,128]{3,2,1,0:T(8,128)}, f32[3,13,16,128]{3,2,1,0:T(8,128)S(1)}, u32[]{:S(2)}, u32[]{:S(2)}) collective-permute-start(f32[3,13,16,128]{3,2,1,0:T(8,128)} %shard_map.46), channel_id=1, source_target_pairs={{0,16},{1,17},{2,18},{3,19},{4,20},{5,21},{6,22},{7,23},{8,24},{9,... | collective-permute-start | bytes 958472 | tf_op jit(solution)/shard_map/ppermute | solution.py:41
  15.3 21.2 %collective-permute-start.3 = (f32[3,13,16,128]{3,2,1,0:T(8,128)}, f32[3,13,16,128]{3,2,1,0:T(8,128)S(1)}, u32[]{:S(2)}, u32[]{:S(2)}) collective-permute-start(f32[3,13,16,128]{3,2,1,0:T(8,128)} %shard_map.46), channel_id=1, source_target_pairs={{0,752},{1,753},{2,754},{3,755},{4,756},{5,757},{6,758},{7,759},{8... | collective-permute-start | bytes 958472 | tf_op jit(solution)/shard_map/ppermute | solution.py:41
  35.5 29.6 %copy-start.4 = (f32[3,13,16,128]{3,2,1,0:T(8,128)}, f32[3,13,16,128]{3,2,1,0:T(8,128)S(1)}, u32[]{:S(2)}) copy-start(f32[3,13,16,128]{3,2,1,0:T(8,128)S(1)} %collective-permute-done.2.refs_1_) | copy-start | bytes 958468
  36.5 28.6 %copy-start.6 = (f32[3,13,16,128]{3,2,1,0:T(8,128)}, f32[3,13,16,128]{3,2,1,0:T(8,128)S(1)}, u32[]{:S(2)}) copy-start(f32[3,13,16,128]{3,2,1,0:T(8,128)S(1)} %collective-permute-done.3.refs_3_.refs_2_) | copy-start | bytes 958468
  37.7 27.5 %copy-start = (f32[2,3,13,16,128]{4,3,2,1,0:T(8,128)}, f32[2,3,13,16,128]{4,3,2,1,0:T(8,128)S(1)}, u32[]{:S(2)}) copy-start(f32[2,3,13,16,128]{4,3,2,1,0:T(8,128)S(1)} %pad_maximum_fusion.refs_5_.refs_3_) | copy-start | bytes 1916932
  37.7 20.5 %collective-permute-start.5 = (f32[2,3,13,16,128]{4,3,2,1,0:T(8,128)S(1)}, f32[2,3,13,16,128]{4,3,2,1,0:T(8,128)S(1)}, u32[]{:S(2)}, u32[]{:S(2)}) collective-permute-start(f32[2,3,13,16,128]{4,3,2,1,0:T(8,128)S(1)} %pad_maximum_fusion.refs_5_.refs_3_), channel_id=1, source_target_pairs={{0,2},{1,3},{2,0},{3,1},{4,6},{5,7},{6,4},{7,5},{8,10},{9,11},{10,... | collective-permute-start | bytes 1916936 | tf_op jit(solution)/shard_map/ppermute | solution.py:41
  40.0 17.4 %collective-permute-start.6 = (f32[3,13,16,128]{3,2,1,0:T(8,128)S(1)}, f32[3,13,16,128]{3,2,1,0:T(8,128)S(1)}, u32[]{:S(2)}, u32[]{:S(2)}) collective-permute-start(f32[3,13,16,128]{3,2,1,0:T(8,128)S(1)} %collective-permute-done), channel_id=1, source_target_pairs={{0,16},{1,17},{2,18},{3,19},{4,20},{5,21},{6,22},{7,23},{8,24},{9,... | collective-permute-start | bytes 958472 | tf_op jit(solution)/shard_map/ppermute | solution.py:41
  41.9 15.5 %collective-permute-start.7 = (f32[3,13,16,128]{3,2,1,0:T(8,128)S(1)}, f32[3,13,16,128]{3,2,1,0:T(8,128)S(1)}, u32[]{:S(2)}, u32[]{:S(2)}) collective-permute-start(f32[3,13,16,128]{3,2,1,0:T(8,128)S(1)} %collective-permute-done), channel_id=1, source_target_pairs={{0,752},{1,753},{2,754},{3,755},{4,756},{5,757},{6,758},{7,759},{8... | collective-permute-start | bytes 958472 | tf_op jit(solution)/shard_map/ppermute | solution.py:41
  49.3 11.3 %collective-permute-start.4 = (f32[3,13,16,128]{3,2,1,0:T(8,128)S(1)}, f32[3,13,16,128]{3,2,1,0:T(8,128)}, u32[]{:S(2)}, u32[]{:S(2)}) collective-permute-start(f32[3,13,16,128]{3,2,1,0:T(8,128)S(1)} %collective-permute-done.1), channel_id=1, source_target_pairs={{0,6},{1,7},{2,4},{3,5},{4,2},{5,3},{6,0},{7,1},{8,14},{9,15},{10,... | collective-permute-start | bytes 958472 | tf_op jit(solution)/shard_map/ppermute | solution.py:41
  52.8 12.4 %collective-permute-start.8 = (f32[2,3,13,16,128]{4,3,2,1,0:T(8,128)S(1)}, f32[2,3,13,16,128]{4,3,2,1,0:T(8,128)S(1)}, u32[]{:S(2)}, u32[]{:S(2)}) collective-permute-start(f32[2,3,13,16,128]{4,3,2,1,0:T(8,128)S(1)} %pad_maximum_fusion.refs_5_.refs_3_), channel_id=1, source_target_pairs={{0,1},{1,0},{2,3},{3,2},{4,5},{5,4},{6,7},{7,6},{8,9},{9,8},{10,11... | collective-permute-start | bytes 1916936 | tf_op jit(solution)/shard_map/ppermute | solution.py:41
  57.4 7.8 %copy-start.13 = (f32[3,13,16,128]{3,2,1,0:T(8,128)}, f32[3,13,16,128]{3,2,1,0:T(8,128)S(1)}, u32[]{:S(2)}) copy-start(f32[3,13,16,128]{3,2,1,0:T(8,128)S(1)} %collective-permute-done.6.refs_2_) | copy-start | bytes 958468
  57.4 0.8 copy-start.14
  58.2 7.0 %copy-start.10 = (f32[2,3,13,16,128]{4,3,2,1,0:T(8,128)}, f32[2,3,13,16,128]{4,3,2,1,0:T(8,128)S(1)}, u32[]{:S(2)}) copy-start(f32[2,3,13,16,128]{4,3,2,1,0:T(8,128)S(1)} %collective-permute-done.5.refs_7_) | copy-start | bytes 1916932
  58.2 6.9 %collective-permute-start.9 = (f32[2,3,13,16,128]{4,3,2,1,0:T(8,128)S(1)}, f32[2,3,13,16,128]{4,3,2,1,0:T(8,128)S(1)}, u32[]{:S(2)}, u32[]{:S(2)}) collective-permute-start(f32[2,3,13,16,128]{4,3,2,1,0:T(8,128)S(1)} %collective-permute-done.5.refs_7_), channel_id=1, source_target_pairs={{0,1},{1,0},{2,3},{3,2},{4,5},{5,4},{6,7},{7,6},{8,9},{9,8},{10,11... | collective-permute-start | bytes 1916936 | tf_op jit(solution)/shard_map/ppermute | solution.py:41
  62.4 20.0 %collective-permute-start.10 = (f32[2,3,13,16,128]{4,3,2,1,0:T(8,128)}, f32[2,3,13,16,128]{4,3,2,1,0:T(8,128)}, u32[]{:S(2)}, u32[]{:S(2)}) collective-permute-start(f32[2,3,13,16,128]{4,3,2,1,0:T(8,128)} %pad_maximum_fusion.1.refs_6_.refs_4_), channel_id=1, source_target_pairs={{0,16},{1,17},{2,18},{3,19},{4,20},{5,21},{6,22},{7,23},{8,760},{9... | collective-permute-start | bytes 1916936 | tf_op jit(solution)/shard_map/ppermute | solution.py:41
  65.1 0.9 copy-start.11
  66.0 0.8 copy-start.12
  74.9 40.7 %copy-start.1 = (f32[2,3,13,16,128]{4,3,2,1,0:T(8,128)S(1)}, f32[2,3,13,16,128]{4,3,2,1,0:T(8,128)}, u32[]{:S(2)}) copy-start(f32[2,3,13,16,128]{4,3,2,1,0:T(8,128)} %copy-done) | copy-start | bytes 1916932
  74.9 40.7 %copy-start.5 = (f32[3,13,16,128]{3,2,1,0:T(8,128)S(1)}, f32[3,13,16,128]{3,2,1,0:T(8,128)}, u32[]{:S(2)}) copy-start(f32[3,13,16,128]{3,2,1,0:T(8,128)} %copy-done.4) | copy-start | bytes 958468
  74.9 40.7 %copy-start.7 = (f32[3,13,16,128]{3,2,1,0:T(8,128)S(1)}, f32[3,13,16,128]{3,2,1,0:T(8,128)}, u32[]{:S(2)}) copy-start(f32[3,13,16,128]{3,2,1,0:T(8,128)} %copy-done.6) | copy-start | bytes 958468
  86.8 12.6 %collective-permute-start.11 = (f32[2,3,19,16,128]{4,3,2,1,0:T(8,128)}, f32[2,3,19,16,128]{4,3,2,1,0:T(8,128)S(1)}, u32[]{:S(2)}, u32[]{:S(2)}) collective-permute-start(f32[2,3,19,16,128]{4,3,2,1,0:T(8,128)} %get-tuple-element.33.refs_8_.refs_4_), channel_id=1, source_target_pairs={{0,1},{1,0},{2,3},{3,2},{4,5},{5,4},{6,7},{7,6},{8,9},{9,8},{10,11... | collective-permute-start | bytes 2801672 | tf_op jit(solution)/shard_map/ppermute | solution.py:41
  92.2 30.0 %collective-permute-start.14 = (f32[2,3,19,16,128]{4,3,2,1,0:T(8,128)}, f32[2,3,19,16,128]{4,3,2,1,0:T(8,128)S(1)}, u32[]{:S(2)}, u32[]{:S(2)}) collective-permute-start(f32[2,3,19,16,128]{4,3,2,1,0:T(8,128)} %get-tuple-element.33.refs_8_.refs_4_), channel_id=1, source_target_pairs={{0,2},{1,3},{2,0},{3,1},{4,6},{5,7},{6,4},{7,5},{8,10},{9,11},{10,... | collective-permute-start | bytes 2801672 | tf_op jit(solution)/shard_map/ppermute | solution.py:41
  99.4 11.0 %collective-permute-start.12 = (f32[3,13,16,128]{3,2,1,0:T(8,128)}, f32[3,13,16,128]{3,2,1,0:T(8,128)S(1)}, u32[]{:S(2)}, u32[]{:S(2)}) collective-permute-start(f32[3,13,16,128]{3,2,1,0:T(8,128)} %collective-permute-done.4), channel_id=1, source_target_pairs={{0,752},{1,753},{2,754},{3,755},{4,756},{5,757},{6,758},{7,759},{8... | collective-permute-start | bytes 958472 | tf_op jit(solution)/shard_map/ppermute | solution.py:41
  101.3 14.4 %collective-permute-start.13 = (f32[3,13,16,128]{3,2,1,0:T(8,128)}, f32[3,13,16,128]{3,2,1,0:T(8,128)}, u32[]{:S(2)}, u32[]{:S(2)}) collective-permute-start(f32[3,13,16,128]{3,2,1,0:T(8,128)} %get-tuple-element.35.refs_5_), channel_id=1, source_target_pairs={{0,16},{1,17},{2,18},{3,19},{4,20},{5,21},{6,22},{7,23},{8,760},{9... | collective-permute-start | bytes 958472 | tf_op jit(solution)/shard_map/ppermute | solution.py:41
  104.7 22.7 %copy-start.9 = (s32[3,25]{1,0:T(4,128)S(1)}, s32[3,25]{1,0:T(4,128)}, u32[]{:S(2)}) copy-start(s32[3,25]{1,0:T(4,128)} %refs_1_.3) | copy-start | bytes 904
  115.7 1.2 copy-start.2
  116.9 1.0 copy-start.8
  117.8 9.5 %copy-start.3 = (f32[2,3,19,16,128]{4,3,2,1,0:T(8,128)S(1)}, f32[2,3,19,16,128]{4,3,2,1,0:T(8,128)}, u32[]{:S(2)}) copy-start(f32[2,3,19,16,128]{4,3,2,1,0:T(8,128)} %get-tuple-element.33.refs_8_.refs_4_) | copy-start | bytes 2801668
  122.2 5.1 %collective-permute-start.15 = (f32[2,3,19,16,128]{4,3,2,1,0:T(8,128)S(1)}, f32[2,3,19,16,128]{4,3,2,1,0:T(8,128)S(1)}, u32[]{:S(2)}, u32[]{:S(2)}) collective-permute-start(f32[2,3,19,16,128]{4,3,2,1,0:T(8,128)S(1)} %collective-permute-done.14.refs_5_), channel_id=1, source_target_pairs={{0,1},{1,0},{2,3},{3,2},{4,5},{5,4},{6,7},{7,6},{8,9},{9,8},{10,11... | collective-permute-start | bytes 2801672 | tf_op jit(solution)/shard_map/ppermute | solution.py:41

commit v6 on v5

--- a/solution.py
+++ b/solution.py
@@ -261,11 +261,12 @@
         send(own, MIRROR), send(own, FLIP), send(own, UP), send(own, DOWN)
     )
     both = jnp.stack([own, own_m])
+    pair_o = send(own_m, FLIP)
     after, twin = send(both, NEXT), send(both, SIBLING)
-    pair_o = send(pair_m, MIRROR)
-    after, below_m, above_m = together(after, send(own_m, UP), send(own_m, DOWN))
-    pair = jnp.stack([pair_o, pair_m])
-    beside, twin_after = send(pair, ACROSS), send(after, SIBLING)
+    pair_o, below_m, above_m, beside_m = together(
+        pair_o, send(own_m, UP), send(own_m, DOWN), send(pair_m, ACROSS)
+    )
+    beside_o, twin_after = send(pair_o, ACROSS), send(after, SIBLING)
 
     chips = jnp.stack([low_y, 3 - low_y, low_y ^ 1, (3 - low_y) ^ 1])
     orbitals = jnp.concatenate([2 * chips + core, 2 * chips + 1 - core])
@@ -280,7 +281,7 @@
     partial, rest = call(
         square_first_kernel,
         (square_places,),
-        [below_o, below_m, above_o, above_m, (both, 0), (both, 1), (pair, 0), (pair, 1)] + left,
+        [below_o, below_m, above_o, above_m, (both, 0), (both, 1), pair_o, pair_m] + left,
         (
             jax.ShapeDtypeStruct((3, 29, 32, 128), F32),
             jax.ShapeDtypeStruct((3, 384, 384), BF16),
@@ -289,10 +290,10 @@
         LARGE,
         True,
     )
-    square, beside_o = call(
+    square, beside_late = call(
         square_second_kernel,
         (square_places, sq_mask),
-        [partial, rest, (beside, 0), (beside, 1)],
+        [partial, rest, beside_o, beside_m],
         (
             jax.ShapeDtypeStruct((2, 3, 19, 16, 128), F32),
             jax.ShapeDtypeStruct((3, 13, 16, 128), F32),
@@ -307,7 +308,7 @@
     total, window = call(
         cube_first_kernel,
         (cube_places,),
-        [below_o, above_o, (both, 0), (pair, 0), beside_o, far_a, far_b]
+        [below_o, above_o, (both, 0), pair_o, beside_o, far_a, far_b]
         + [(square, 0), (square, 1), (square_twin, 0), (square_twin, 1)],
         (
             jax.ShapeDtypeStruct((3, 35, 16, 128), F32),

time: 132 us -> 129 us (0.977)
  waiting for transfers between devices: 26.8 us -> 22.6 us
  starting transfers between devices: 73.2 us -> 77 us
  other arithmetic: 3.08 us -> 1.31 us
    ppermute x16 -> x17, waiting for transfers between devices: 26.8 us -> 22.6 us  [send(): return lax.ppermute(array, AXES, which)]
    ppermute x16 -> x17, starting transfers between devices: 73.2 us -> 77 us  [send(): return lax.ppermute(array, AXES, which)]
    another operation x1 -> x0, other arithmetic: 1.85 us -> none  [body(): pair = jnp.stack([pair_o, pair_m])]
    unnamed x30 -> x32, local copies, waits for them, and re-layouts: 4.56 us -> 4.46 us
  transfers between devices with their start and end apart: 16 -> 17, of which waited for: 7 -> 6; matrix products, arithmetic and copies ran while one was open for 2% -> 1% of each run, Pallas kernels for 10% -> 10%
where the time goes in v6:
time: 129 us; the launch traced here: 128 us
  starting transfers between devices  77 us (60%)
  waiting for transfers between devices  22.6 us (18%)
  Pallas kernels  21.8 us (17%)
  local copies, waits for them, and re-layouts  5.16 us (4%)
  other arithmetic  1.31 us (1%)
    ppermute x17, starting transfers between devices, send(): return lax.ppermute(array, AXES, which)  77 us
    ppermute x17, waiting for transfers between devices, send(): return lax.ppermute(array, AXES, which)  22.6 us
    pallas_call x4, Pallas kernels, call(): pl.pallas_call(whole, out_shape=out_shape, in_specs=[SMEM] * first + [IN_...  20 us
    unnamed x32, local copies, waits for them, and re-layouts  4.46 us
  transfers between devices with their start and end apart: 17, of which 6 were waited for; matrix products, arithmetic and copies ran while one was open for 1% of the time, Pallas kernels for 10%

profile of v6, /device:TPU:1, one launch (start us, length us, event | category | flops | bytes accessed | tf_op | source)
XLA Modules:
  0.0 128.2 jit_solution(12778182985517873078)
XLA Ops:
  0.0 1.7 %shard_map.46 = f32[3,13,16,128]{3,2,1,0:T(8,128)} custom-call(s32[3,13]{1,0:T(4,128)} %mask_ref.1, f32[3,13,16,128]{3,2,1,0:T(8,128)} %x_ref.1), custom_call_target="tpu_custom_call" | custom-call | tf_op jit(solution)/shard_map/pallas_call | solution.py:253
  1.7 6.0 %collective-permute-start = (f32[3,13,16,128]{3,2,1,0:T(8,128)}, f32[3,13,16,128]{3,2,1,0:T(8,128)}, u32[]{:S(2)}, u32[]{:S(2)}) collective-permute-start(f32[3,13,16,128]{3,2,1,0:T(8,128)} %shard_map.46), channel_id=1, source_target_pairs={{0,6},{1,7},{2,4},{3,5},{4,2},{5,3},{6,0},{7,1},{8,14},{9,15},{10,... | collective-permute-start | bytes 958472 | tf_op jit(solution)/shard_map/ppermute | solution.py:41
  7.8 4.4 %collective-permute-start.1 = (f32[3,13,16,128]{3,2,1,0:T(8,128)}, f32[3,13,16,128]{3,2,1,0:T(8,128)S(1)}, u32[]{:S(2)}, u32[]{:S(2)}) collective-permute-start(f32[3,13,16,128]{3,2,1,0:T(8,128)} %shard_map.46), channel_id=1, source_target_pairs={{0,14},{1,15},{2,12},{3,13},{4,10},{5,11},{6,8},{7,9},{8,6},{9,7},... | collective-permute-start | bytes 958472 | tf_op jit(solution)/shard_map/ppermute | solution.py:41
  12.2 3.1 %collective-permute-start.2 = (f32[3,13,16,128]{3,2,1,0:T(8,128)}, f32[3,13,16,128]{3,2,1,0:T(8,128)S(1)}, u32[]{:S(2)}, u32[]{:S(2)}) collective-permute-start(f32[3,13,16,128]{3,2,1,0:T(8,128)} %shard_map.46), channel_id=1, source_target_pairs={{0,16},{1,17},{2,18},{3,19},{4,20},{5,21},{6,22},{7,23},{8,24},{9,... | collective-permute-start | bytes 958472 | tf_op jit(solution)/shard_map/ppermute | solution.py:41
  15.3 15.3 %collective-permute-start.3 = (f32[3,13,16,128]{3,2,1,0:T(8,128)}, f32[3,13,16,128]{3,2,1,0:T(8,128)S(1)}, u32[]{:S(2)}, u32[]{:S(2)}) collective-permute-start(f32[3,13,16,128]{3,2,1,0:T(8,128)} %shard_map.46), channel_id=1, source_target_pairs={{0,752},{1,753},{2,754},{3,755},{4,756},{5,757},{6,758},{7,759},{8... | collective-permute-start | bytes 958472 | tf_op jit(solution)/shard_map/ppermute | solution.py:41
  30.6 0.0 collective-permute-done
  30.7 0.0 collective-permute-done.1.refs_7_
  30.7 4.9 %collective-permute-done.2.refs_1_ = f32[3,13,16,128]{3,2,1,0:T(8,128)S(1)} collective-permute-done((f32[3,13,16,128]{3,2,1,0:T(8,128)}, f32[3,13,16,128]{3,2,1,0:T(8,128)S(1)}, u32[]{:S(2)}, u32[]{:S(2)}) %collective-permute-start.2) | collective-permute-done | bytes 319520 | tf_op jit(solution)/shard_map/ppermute | solution.py:41
  35.5 1.0 collective-permute-done.3.refs_3_.refs_2_
  36.5 1.2 pad_maximum_fusion.refs_5_.refs_3_
  37.8 2.3 %collective-permute-start.9 = (f32[2,3,13,16,128]{4,3,2,1,0:T(8,128)S(1)}, f32[2,3,13,16,128]{4,3,2,1,0:T(8,128)S(1)}, u32[]{:S(2)}, u32[]{:S(2)}) collective-permute-start(f32[2,3,13,16,128]{4,3,2,1,0:T(8,128)S(1)} %pad_maximum_fusion.refs_5_.refs_3_), channel_id=1, source_target_pairs={{0,2},{1,3},{2,0},{3,1},{4,6},{5,7},{6,4},{7,5},{8,10},{9,11},{10,... | collective-permute-start | bytes 1916936 | tf_op jit(solution)/shard_map/ppermute | solution.py:41
  40.1 1.9 %collective-permute-start.4 = (f32[3,13,16,128]{3,2,1,0:T(8,128)}, f32[3,13,16,128]{3,2,1,0:T(8,128)}, u32[]{:S(2)}, u32[]{:S(2)}) collective-permute-start(f32[3,13,16,128]{3,2,1,0:T(8,128)} %collective-permute-done), channel_id=1, source_target_pairs={{0,14},{1,15},{2,12},{3,13},{4,10},{5,11},{6,8},{7,9},{8,6},{9,7},... | collective-permute-start | bytes 958472 | tf_op jit(solution)/shard_map/ppermute | solution.py:41
  42.0 1.9 %collective-permute-start.5 = (f32[3,13,16,128]{3,2,1,0:T(8,128)}, f32[3,13,16,128]{3,2,1,0:T(8,128)S(1)}, u32[]{:S(2)}, u32[]{:S(2)}) collective-permute-start(f32[3,13,16,128]{3,2,1,0:T(8,128)} %collective-permute-done), channel_id=1, source_target_pairs={{0,16},{1,17},{2,18},{3,19},{4,20},{5,21},{6,22},{7,23},{8,24},{9,... | collective-permute-start | bytes 958472 | tf_op jit(solution)/shard_map/ppermute | solution.py:41
  43.9 8.5 %collective-permute-start.6 = (f32[3,13,16,128]{3,2,1,0:T(8,128)}, f32[3,13,16,128]{3,2,1,0:T(8,128)S(1)}, u32[]{:S(2)}, u32[]{:S(2)}) collective-permute-start(f32[3,13,16,128]{3,2,1,0:T(8,128)} %collective-permute-done), channel_id=1, source_target_pairs={{0,752},{1,753},{2,754},{3,755},{4,756},{5,757},{6,758},{7,759},{8... | collective-permute-start | bytes 958472 | tf_op jit(solution)/shard_map/ppermute | solution.py:41
  52.5 1.9 %collective-permute-start.7 = (f32[3,13,16,128]{3,2,1,0:T(8,128)S(1)}, f32[3,13,16,128]{3,2,1,0:T(8,128)}, u32[]{:S(2)}, u32[]{:S(2)}) collective-permute-start(f32[3,13,16,128]{3,2,1,0:T(8,128)S(1)} %collective-permute-done.1.refs_7_), channel_id=1, source_target_pairs={{0,16},{1,17},{2,18},{3,19},{4,20},{5,21},{6,22},{7,23},{8,760},{9... | collective-permute-start | bytes 958472 | tf_op jit(solution)/shard_map/ppermute | solution.py:41
  54.4 0.0 collective-permute-done.4.refs_6_.refs_4_
  54.4 4.2 %collective-permute-start.10 = (f32[2,3,13,16,128]{4,3,2,1,0:T(8,128)S(1)}, f32[2,3,13,16,128]{4,3,2,1,0:T(8,128)S(1)}, u32[]{:S(2)}, u32[]{:S(2)}) collective-permute-start(f32[2,3,13,16,128]{4,3,2,1,0:T(8,128)S(1)} %pad_maximum_fusion.refs_5_.refs_3_), channel_id=1, source_target_pairs={{0,1},{1,0},{2,3},{3,2},{4,5},{5,4},{6,7},{7,6},{8,9},{9,8},{10,11... | collective-permute-start | bytes 1916936 | tf_op jit(solution)/shard_map/ppermute | solution.py:41
  58.6 0.0 collective-permute-done.9.refs_8_
  58.6 2.4 %collective-permute-start.11 = (f32[2,3,13,16,128]{4,3,2,1,0:T(8,128)S(1)}, f32[2,3,13,16,128]{4,3,2,1,0:T(8,128)}, u32[]{:S(2)}, u32[]{:S(2)}) collective-permute-start(f32[2,3,13,16,128]{4,3,2,1,0:T(8,128)S(1)} %collective-permute-done.9.refs_8_), channel_id=1, source_target_pairs={{0,1},{1,0},{2,3},{3,2},{4,5},{5,4},{6,7},{7,6},{8,9},{9,8},{10,11... | collective-permute-start | bytes 1916936 | tf_op jit(solution)/shard_map/ppermute | solution.py:41
  61.1 0.0 copy-start.14
  61.1 0.0 collective-permute-done.6.refs_4_
  61.1 0.8 copy-done.15
  61.9 2.6 %collective-permute-done.7.refs_5_ = f32[3,13,16,128]{3,2,1,0:T(8,128)} collective-permute-done((f32[3,13,16,128]{3,2,1,0:T(8,128)S(1)}, f32[3,13,16,128]{3,2,1,0:T(8,128)}, u32[]{:S(2)}, u32[]{:S(2)}) %collective-permute-start.7) | collective-permute-done | bytes 319520 | tf_op jit(solution)/shard_map/ppermute | solution.py:41
  64.5 1.9 %collective-permute-start.8 = (f32[3,13,16,128]{3,2,1,0:T(8,128)}, f32[3,13,16,128]{3,2,1,0:T(8,128)S(1)}, u32[]{:S(2)}, u32[]{:S(2)}) collective-permute-start(f32[3,13,16,128]{3,2,1,0:T(8,128)} %collective-permute-done.4.refs_6_.refs_4_), channel_id=1, source_target_pairs={{0,16},{1,17},{2,18},{3,19},{4,20},{5,21},{6,22},{7,23},{8,760},{9... | collective-permute-start | bytes 958472 | tf_op jit(solution)/shard_map/ppermute | solution.py:41
  66.4 0.1 add_subtract_fusion
  66.5 0.6 concatenate.3.refs_0_
  67.1 0.0 collective-permute-done.10.refs_9_
  67.1 0.0 collective-permute-done.11.refs_10_
  67.2 0.8 copy-done.12
  68.0 8.0 %shard_map.47 = (f32[3,29,32,128]{3,2,1,0:T(8,128)}, bf16[3,384,384]{2,1,0:T(8,128)(2,1)}) custom-call(s32[13]{0:T(128)} %concatenate.3.refs_0_, f32[3,13,16,128]{3,2,1,0:T(8,128)} %copy-done.4, f32[3,13,16,128]{3,2,1,0:T(8,128)} %copy-done.14, f32[3,13,16,128]{3,2,1,0:T(8,128)} %copy-done.6, f32[3,13,16,128]{3,2,1,0:T(8,128)} %copy-done.15, ...), custom_call_target="tpu_custom_call" | custom-call | flops 1000000 | bytes 1000 | tf_op jit(solution)/shard_map/pallas_call | solution.py:238
  76.1 0.0 copy-start.8
  76.1 0.7 copy-done.8
  76.8 4.4 %shard_map.48 = (f32[2,3,19,16,128]{4,3,2,1,0:T(8,128)}, f32[3,13,16,128]{3,2,1,0:T(8,128)}) custom-call(s32[13]{0:T(128)} %concatenate.3.refs_0_, s32[3,19]{1,0:T(4,128)} %refs_1_.2, f32[3,29,32,128]{3,2,1,0:T(8,128)} %get-tuple-element.30.refs_2_, bf16[3,384,384]{2,1,0:T(8,128)(2,1)} %get-tuple-element.31.refs_3_, f32[3,13,16,128]{3,2,1,0:T(8,128)} %copy-done.8, ...), custom_call_target="tpu_custom_call" | custom-call | flops 1000000 | bytes 1000 | tf_op jit(solution)/shard_map/pallas_call | solution.py:238
  81.2 0.0 copy-start.10
  81.2 6.0 %collective-permute-start.12 = (f32[2,3,19,16,128]{4,3,2,1,0:T(8,128)}, f32[2,3,19,16,128]{4,3,2,1,0:T(8,128)S(1)}, u32[]{:S(2)}, u32[]{:S(2)}) collective-permute-start(f32[2,3,19,16,128]{4,3,2,1,0:T(8,128)} %get-tuple-element.33.refs_8_.refs_4_), channel_id=1, source_target_pairs={{0,1},{1,0},{2,3},{3,2},{4,5},{5,4},{6,7},{7,6},{8,9},{9,8},{10,11... | collective-permute-start | bytes 2801672 | tf_op jit(solution)/shard_map/ppermute | solution.py:41
  87.1 8.4 %collective-permute-start.15 = (f32[2,3,19,16,128]{4,3,2,1,0:T(8,128)}, f32[2,3,19,16,128]{4,3,2,1,0:T(8,128)S(1)}, u32[]{:S(2)}, u32[]{:S(2)}) collective-permute-start(f32[2,3,19,16,128]{4,3,2,1,0:T(8,128)} %get-tuple-element.33.refs_8_.refs_4_), channel_id=1, source_target_pairs={{0,2},{1,3},{2,0},{3,1},{4,6},{5,7},{6,4},{7,5},{8,10},{9,11},{10,... | collective-permute-start | bytes 2801672 | tf_op jit(solution)/shard_map/ppermute | solution.py:41
  95.5 3.4 %collective-permute-start.13 = (f32[3,13,16,128]{3,2,1,0:T(8,128)}, f32[3,13,16,128]{3,2,1,0:T(8,128)S(1)}, u32[]{:S(2)}, u32[]{:S(2)}) collective-permute-start(f32[3,13,16,128]{3,2,1,0:T(8,128)} %collective-permute-done.4.refs_6_.refs_4_), channel_id=1, source_target_pairs={{0,752},{1,753},{2,754},{3,755},{4,756},{5,757},{6,758},{7,759},{8... | collective-permute-start | bytes 958472 | tf_op jit(solution)/shard_map/ppermute | solution.py:41
  98.9 1.9 %collective-permute-start.14 = (f32[3,13,16,128]{3,2,1,0:T(8,128)}, f32[3,13,16,128]{3,2,1,0:T(8,128)}, u32[]{:S(2)}, u32[]{:S(2)}) collective-permute-start(f32[3,13,16,128]{3,2,1,0:T(8,128)} %copy-done.8), channel_id=1, source_target_pairs={{0,16},{1,17},{2,18},{3,19},{4,20},{5,21},{6,22},{7,23},{8,760},{9... | collective-permute-start | bytes 958472 | tf_op jit(solution)/shard_map/ppermute | solution.py:41
  100.8 0.1 stack.55.refs_0_
  100.9 5.5 %collective-permute-done.13.refs_6_ = f32[3,13,16,128]{3,2,1,0:T(8,128)S(1)} collective-permute-done((f32[3,13,16,128]{3,2,1,0:T(8,128)}, f32[3,13,16,128]{3,2,1,0:T(8,128)S(1)}, u32[]{:S(2)}, u32[]{:S(2)}) %collective-permute-start.13) | collective-permute-done | bytes 319520 | tf_op jit(solution)/shard_map/ppermute | solution.py:41
  106.5 6.5 %collective-permute-done.14.refs_7_ = f32[3,13,16,128]{3,2,1,0:T(8,128)} collective-permute-done((f32[3,13,16,128]{3,2,1,0:T(8,128)}, f32[3,13,16,128]{3,2,1,0:T(8,128)}, u32[]{:S(2)}, u32[]{:S(2)}) %collective-permute-start.14) | collective-permute-done | bytes 319520 | tf_op jit(solution)/shard_map/ppermute | solution.py:41
  113.0 1.2 copy-done.2
  114.2 1.0 copy-done.9
  115.1 4.2 %shard_map.49 = (f32[3,35,16,128]{3,2,1,0:T(8,128)S(1)}, bf16[21,13,16,256]{3,2,1,0:T(8,128)(2,1)S(1)}) custom-call(s32[9]{0:T(128)S(1)} %stack.55.refs_0_, f32[3,13,16,128]{3,2,1,0:T(8,128)S(1)} %copy-done.5, f32[3,13,16,128]{3,2,1,0:T(8,128)S(1)} %copy-done.7, f32[2,3,13,16,128]{4,3,2,1,0:T(8,128)S(1)} %copy-done.1, ...), custom_call_target="tpu_custom_call" | custom-call | flops 1000000 | bytes 1000 | tf_op jit(solution)/shard_map/pallas_call | solution.py:238
  119.4 0.0 collective-permute-done.15.refs_5_
  119.4 3.3 %collective-permute-start.16 = (f32[2,3,19,16,128]{4,3,2,1,0:T(8,128)S(1)}, f32[2,3,19,16,128]{4,3,2,1,0:T(8,128)S(1)}, u32[]{:S(2)}, u32[]{:S(2)}) collective-permute-start(f32[2,3,19,16,128]{4,3,2,1,0:T(8,128)S(1)} %collective-permute-done.15.refs_5_), channel_id=1, source_target_pairs={{0,1},{1,0},{2,3},{3,2},{4,5},{5,4},{6,7},{7,6},{8,9},{9,8},{10,11... | collective-permute-start | bytes 2801672 | tf_op jit(solution)/shard_map/ppermute | solution.py:41
  122.7 2.1 %collective-permute-done.16.refs_6_ = f32[2,3,19,16,128]{4,3,2,1,0:T(8,128)S(1)} collective-permute-done((f32[2,3,19,16,128]{4,3,2,1,0:T(8,128)S(1)}, f32[2,3,19,16,128]{4,3,2,1,0:T(8,128)S(1)}, u32[]{:S(2)}, u32[]{:S(2)}) %collective-permute-start.16) | collective-permute-done | bytes 933920 | tf_op jit(solution)/shard_map/ppermute | solution.py:41
  124.8 3.4 %shard_map.50 = f32[3,25,16,128]{3,2,1,0:T(8,128)} custom-call(s32[9]{0:T(128)S(1)} %stack.55.refs_0_, s32[3,25]{1,0:T(4,128)S(1)} %copy-done.10, f32[3,35,16,128]{3,2,1,0:T(8,128)S(1)} %get-tuple-element.38.refs_2_, bf16[21,13,16,256]{3,2,1,0:T(8,128)(2,1)S(1)} %get-tuple-element.39.refs_3_, f32[2,3,19,16,128]{4,3,2,1,0:T(8,128)S(1)} %copy-done.3, ...), custom_call_target="tpu_custom_call" | custom-call | flops 1000000 | bytes 1000 | tf_op jit(solution)/shard_map/pallas_call | solution.py:238
  (28 shorter events, 0.1 us)
Async XLA Ops:
  1.7 28.9 %collective-permute-start = (f32[3,13,16,128]{3,2,1,0:T(8,128)}, f32[3,13,16,128]{3,2,1,0:T(8,128)}, u32[]{:S(2)}, u32[]{:S(2)}) collective-permute-start(f32[3,13,16,128]{3,2,1,0:T(8,128)} %shard_map.46), channel_id=1, source_target_pairs={{0,6},{1,7},{2,4},{3,5},{4,2},{5,3},{6,0},{7,1},{8,14},{9,15},{10,... | collective-permute-start | bytes 958472 | tf_op jit(solution)/shard_map/ppermute | solution.py:41
  7.8 22.9 %collective-permute-start.1 = (f32[3,13,16,128]{3,2,1,0:T(8,128)}, f32[3,13,16,128]{3,2,1,0:T(8,128)S(1)}, u32[]{:S(2)}, u32[]{:S(2)}) collective-permute-start(f32[3,13,16,128]{3,2,1,0:T(8,128)} %shard_map.46), channel_id=1, source_target_pairs={{0,14},{1,15},{2,12},{3,13},{4,10},{5,11},{6,8},{7,9},{8,6},{9,7},... | collective-permute-start | bytes 958472 | tf_op jit(solution)/shard_map/ppermute | solution.py:41
  12.2 23.3 %collective-permute-start.2 = (f32[3,13,16,128]{3,2,1,0:T(8,128)}, f32[3,13,16,128]{3,2,1,0:T(8,128)S(1)}, u32[]{:S(2)}, u32[]{:S(2)}) collective-permute-start(f32[3,13,16,128]{3,2,1,0:T(8,128)} %shard_map.46), channel_id=1, source_target_pairs={{0,16},{1,17},{2,18},{3,19},{4,20},{5,21},{6,22},{7,23},{8,24},{9,... | collective-permute-start | bytes 958472 | tf_op jit(solution)/shard_map/ppermute | solution.py:41
  15.3 21.2 %collective-permute-start.3 = (f32[3,13,16,128]{3,2,1,0:T(8,128)}, f32[3,13,16,128]{3,2,1,0:T(8,128)S(1)}, u32[]{:S(2)}, u32[]{:S(2)}) collective-permute-start(f32[3,13,16,128]{3,2,1,0:T(8,128)} %shard_map.46), channel_id=1, source_target_pairs={{0,752},{1,753},{2,754},{3,755},{4,756},{5,757},{6,758},{7,759},{8... | collective-permute-start | bytes 958472 | tf_op jit(solution)/shard_map/ppermute | solution.py:41
  30.7 36.5 %copy-start.13 = (f32[3,13,16,128]{3,2,1,0:T(8,128)}, f32[3,13,16,128]{3,2,1,0:T(8,128)S(1)}, u32[]{:S(2)}) copy-start(f32[3,13,16,128]{3,2,1,0:T(8,128)S(1)} %collective-permute-done.1.refs_7_) | copy-start | bytes 958468
  35.5 31.6 %copy-start.4 = (f32[3,13,16,128]{3,2,1,0:T(8,128)}, f32[3,13,16,128]{3,2,1,0:T(8,128)S(1)}, u32[]{:S(2)}) copy-start(f32[3,13,16,128]{3,2,1,0:T(8,128)S(1)} %collective-permute-done.2.refs_1_) | copy-start | bytes 958468
  36.5 30.7 %copy-start.6 = (f32[3,13,16,128]{3,2,1,0:T(8,128)}, f32[3,13,16,128]{3,2,1,0:T(8,128)S(1)}, u32[]{:S(2)}) copy-start(f32[3,13,16,128]{3,2,1,0:T(8,128)S(1)} %collective-permute-done.3.refs_3_.refs_2_) | copy-start | bytes 958468
  37.8 29.4 %copy-start = (f32[2,3,13,16,128]{4,3,2,1,0:T(8,128)}, f32[2,3,13,16,128]{4,3,2,1,0:T(8,128)S(1)}, u32[]{:S(2)}) copy-start(f32[2,3,13,16,128]{4,3,2,1,0:T(8,128)S(1)} %pad_maximum_fusion.refs_5_.refs_3_) | copy-start | bytes 1916932
  37.8 20.8 %collective-permute-start.9 = (f32[2,3,13,16,128]{4,3,2,1,0:T(8,128)S(1)}, f32[2,3,13,16,128]{4,3,2,1,0:T(8,128)S(1)}, u32[]{:S(2)}, u32[]{:S(2)}) collective-permute-start(f32[2,3,13,16,128]{4,3,2,1,0:T(8,128)S(1)} %pad_maximum_fusion.refs_5_.refs_3_), channel_id=1, source_target_pairs={{0,2},{1,3},{2,0},{3,1},{4,6},{5,7},{6,4},{7,5},{8,10},{9,11},{10,... | collective-permute-start | bytes 1916936 | tf_op jit(solution)/shard_map/ppermute | solution.py:41
  40.1 14.3 %collective-permute-start.4 = (f32[3,13,16,128]{3,2,1,0:T(8,128)}, f32[3,13,16,128]{3,2,1,0:T(8,128)}, u32[]{:S(2)}, u32[]{:S(2)}) collective-permute-start(f32[3,13,16,128]{3,2,1,0:T(8,128)} %collective-permute-done), channel_id=1, source_target_pairs={{0,14},{1,15},{2,12},{3,13},{4,10},{5,11},{6,8},{7,9},{8,6},{9,7},... | collective-permute-start | bytes 958472 | tf_op jit(solution)/shard_map/ppermute | solution.py:41
  42.0 19.1 %collective-permute-start.5 = (f32[3,13,16,128]{3,2,1,0:T(8,128)}, f32[3,13,16,128]{3,2,1,0:T(8,128)S(1)}, u32[]{:S(2)}, u32[]{:S(2)}) collective-permute-start(f32[3,13,16,128]{3,2,1,0:T(8,128)} %collective-permute-done), channel_id=1, source_target_pairs={{0,16},{1,17},{2,18},{3,19},{4,20},{5,21},{6,22},{7,23},{8,24},{9,... | collective-permute-start | bytes 958472 | tf_op jit(solution)/shard_map/ppermute | solution.py:41
  43.9 17.2 %collective-permute-start.6 = (f32[3,13,16,128]{3,2,1,0:T(8,128)}, f32[3,13,16,128]{3,2,1,0:T(8,128)S(1)}, u32[]{:S(2)}, u32[]{:S(2)}) collective-permute-start(f32[3,13,16,128]{3,2,1,0:T(8,128)} %collective-permute-done), channel_id=1, source_target_pairs={{0,752},{1,753},{2,754},{3,755},{4,756},{5,757},{6,758},{7,759},{8... | collective-permute-start | bytes 958472 | tf_op jit(solution)/shard_map/ppermute | solution.py:41
  52.5 12.1 %collective-permute-start.7 = (f32[3,13,16,128]{3,2,1,0:T(8,128)S(1)}, f32[3,13,16,128]{3,2,1,0:T(8,128)}, u32[]{:S(2)}, u32[]{:S(2)}) collective-permute-start(f32[3,13,16,128]{3,2,1,0:T(8,128)S(1)} %collective-permute-done.1.refs_7_), channel_id=1, source_target_pairs={{0,16},{1,17},{2,18},{3,19},{4,20},{5,21},{6,22},{7,23},{8,760},{9... | collective-permute-start | bytes 958472 | tf_op jit(solution)/shard_map/ppermute | solution.py:41
  54.4 12.8 %collective-permute-start.10 = (f32[2,3,13,16,128]{4,3,2,1,0:T(8,128)S(1)}, f32[2,3,13,16,128]{4,3,2,1,0:T(8,128)S(1)}, u32[]{:S(2)}, u32[]{:S(2)}) collective-permute-start(f32[2,3,13,16,128]{4,3,2,1,0:T(8,128)S(1)} %pad_maximum_fusion.refs_5_.refs_3_), channel_id=1, source_target_pairs={{0,1},{1,0},{2,3},{3,2},{4,5},{5,4},{6,7},{7,6},{8,9},{9,8},{10,11... | collective-permute-start | bytes 1916936 | tf_op jit(solution)/shard_map/ppermute | solution.py:41
  58.6 8.6 %copy-start.11 = (f32[2,3,13,16,128]{4,3,2,1,0:T(8,128)}, f32[2,3,13,16,128]{4,3,2,1,0:T(8,128)S(1)}, u32[]{:S(2)}) copy-start(f32[2,3,13,16,128]{4,3,2,1,0:T(8,128)S(1)} %collective-permute-done.9.refs_8_) | copy-start | bytes 1916932
  58.6 8.5 %collective-permute-start.11 = (f32[2,3,13,16,128]{4,3,2,1,0:T(8,128)S(1)}, f32[2,3,13,16,128]{4,3,2,1,0:T(8,128)}, u32[]{:S(2)}, u32[]{:S(2)}) collective-permute-start(f32[2,3,13,16,128]{4,3,2,1,0:T(8,128)S(1)} %collective-permute-done.9.refs_8_), channel_id=1, source_target_pairs={{0,1},{1,0},{2,3},{3,2},{4,5},{5,4},{6,7},{7,6},{8,9},{9,8},{10,11... | collective-permute-start | bytes 1916936 | tf_op jit(solution)/shard_map/ppermute | solution.py:41
  61.1 6.1 %copy-start.14 = (f32[3,13,16,128]{3,2,1,0:T(8,128)}, f32[3,13,16,128]{3,2,1,0:T(8,128)S(1)}, u32[]{:S(2)}) copy-start(f32[3,13,16,128]{3,2,1,0:T(8,128)S(1)} %collective-permute-done.5.refs_2_) | copy-start | bytes 958468
  61.1 0.8 copy-start.15
  64.5 11.5 %collective-permute-start.8 = (f32[3,13,16,128]{3,2,1,0:T(8,128)}, f32[3,13,16,128]{3,2,1,0:T(8,128)S(1)}, u32[]{:S(2)}, u32[]{:S(2)}) collective-permute-start(f32[3,13,16,128]{3,2,1,0:T(8,128)} %collective-permute-done.4.refs_6_.refs_4_), channel_id=1, source_target_pairs={{0,16},{1,17},{2,18},{3,19},{4,20},{5,21},{6,22},{7,23},{8,760},{9... | collective-permute-start | bytes 958472 | tf_op jit(solution)/shard_map/ppermute | solution.py:41
  67.1 0.8 copy-start.12
  76.0 36.9 %copy-start.1 = (f32[2,3,13,16,128]{4,3,2,1,0:T(8,128)S(1)}, f32[2,3,13,16,128]{4,3,2,1,0:T(8,128)}, u32[]{:S(2)}) copy-start(f32[2,3,13,16,128]{4,3,2,1,0:T(8,128)} %copy-done) | copy-start | bytes 1916932
  76.0 36.9 %copy-start.5 = (f32[3,13,16,128]{3,2,1,0:T(8,128)S(1)}, f32[3,13,16,128]{3,2,1,0:T(8,128)}, u32[]{:S(2)}) copy-start(f32[3,13,16,128]{3,2,1,0:T(8,128)} %copy-done.4) | copy-start | bytes 958468
  76.0 36.9 %copy-start.7 = (f32[3,13,16,128]{3,2,1,0:T(8,128)S(1)}, f32[3,13,16,128]{3,2,1,0:T(8,128)}, u32[]{:S(2)}) copy-start(f32[3,13,16,128]{3,2,1,0:T(8,128)} %copy-done.6) | copy-start | bytes 958468
  76.1 0.7 copy-start.8
  81.2 43.7 %copy-start.10 = (s32[3,25]{1,0:T(4,128)S(1)}, s32[3,25]{1,0:T(4,128)}, u32[]{:S(2)}) copy-start(s32[3,25]{1,0:T(4,128)} %refs_1_.3) | copy-start | bytes 904
  81.2 14.4 %collective-permute-start.12 = (f32[2,3,19,16,128]{4,3,2,1,0:T(8,128)}, f32[2,3,19,16,128]{4,3,2,1,0:T(8,128)S(1)}, u32[]{:S(2)}, u32[]{:S(2)}) collective-permute-start(f32[2,3,19,16,128]{4,3,2,1,0:T(8,128)} %get-tuple-element.33.refs_8_.refs_4_), channel_id=1, source_target_pairs={{0,1},{1,0},{2,3},{3,2},{4,5},{5,4},{6,7},{7,6},{8,9},{9,8},{10,11... | collective-permute-start | bytes 2801672 | tf_op jit(solution)/shard_map/ppermute | solution.py:41
  87.1 32.2 %collective-permute-start.15 = (f32[2,3,19,16,128]{4,3,2,1,0:T(8,128)}, f32[2,3,19,16,128]{4,3,2,1,0:T(8,128)S(1)}, u32[]{:S(2)}, u32[]{:S(2)}) collective-permute-start(f32[2,3,19,16,128]{4,3,2,1,0:T(8,128)} %get-tuple-element.33.refs_8_.refs_4_), channel_id=1, source_target_pairs={{0,2},{1,3},{2,0},{3,1},{4,6},{5,7},{6,4},{7,5},{8,10},{9,11},{10,... | collective-permute-start | bytes 2801672 | tf_op jit(solution)/shard_map/ppermute | solution.py:41
  95.5 10.9 %collective-permute-start.13 = (f32[3,13,16,128]{3,2,1,0:T(8,128)}, f32[3,13,16,128]{3,2,1,0:T(8,128)S(1)}, u32[]{:S(2)}, u32[]{:S(2)}) collective-permute-start(f32[3,13,16,128]{3,2,1,0:T(8,128)} %collective-permute-done.4.refs_6_.refs_4_), channel_id=1, source_target_pairs={{0,752},{1,753},{2,754},{3,755},{4,756},{5,757},{6,758},{7,759},{8... | collective-permute-start | bytes 958472 | tf_op jit(solution)/shard_map/ppermute | solution.py:41
  98.9 14.0 %collective-permute-start.14 = (f32[3,13,16,128]{3,2,1,0:T(8,128)}, f32[3,13,16,128]{3,2,1,0:T(8,128)}, u32[]{:S(2)}, u32[]{:S(2)}) collective-permute-start(f32[3,13,16,128]{3,2,1,0:T(8,128)} %copy-done.8), channel_id=1, source_target_pairs={{0,16},{1,17},{2,18},{3,19},{4,20},{5,21},{6,22},{7,23},{8,760},{9... | collective-permute-start | bytes 958472 | tf_op jit(solution)/shard_map/ppermute | solution.py:41
  113.0 1.2 copy-start.2
  114.2 1.0 copy-start.9
  115.1 9.7 %copy-start.3 = (f32[2,3,19,16,128]{4,3,2,1,0:T(8,128)S(1)}, f32[2,3,19,16,128]{4,3,2,1,0:T(8,128)}, u32[]{:S(2)}) copy-start(f32[2,3,19,16,128]{4,3,2,1,0:T(8,128)} %get-tuple-element.33.refs_8_.refs_4_) | copy-start | bytes 2801668
  119.4 5.5 %collective-permute-start.16 = (f32[2,3,19,16,128]{4,3,2,1,0:T(8,128)S(1)}, f32[2,3,19,16,128]{4,3,2,1,0:T(8,128)S(1)}, u32[]{:S(2)}, u32[]{:S(2)}) collective-permute-start(f32[2,3,19,16,128]{4,3,2,1,0:T(8,128)S(1)} %collective-permute-done.15.refs_5_), channel_id=1, source_target_pairs={{0,1},{1,0},{2,3},{3,2},{4,5},{5,4},{6,7},{7,6},{8,9},{9,8},{10,11... | collective-permute-start | bytes 2801672 | tf_op jit(solution)/shard_map/ppermute | solution.py:41

commit v7 on v6

--- a/solution.py
+++ b/solution.py
@@ -76,17 +76,18 @@
             right_ref[g : g + blocks, spot, lanes(g)] = high if is_high else low
 
 
-def accumulate(pieces, total_ref, rows, firsts):
-    for (left, right), r in zip(pieces, firsts):
-        product = jnp.dot(left, right, preferred_element_type=F32).reshape(13, rows, 384)
-        for g in range(3):
-            total_ref[g, pl.ds(r + 2 - g, 13)] += product[:, :, lanes(g)]
+def add_row(left, right, total_ref, r, strip):
+    rows = strip.stop - strip.start
+    product = jnp.dot(left, right, preferred_element_type=F32).reshape(13, rows, 384)
+    for g in range(3):
+        total_ref[g, pl.ds(r + 2 - g, 13), strip] += product[:, :, lanes(g)]
 
 
 def all_rows(window_ref, right_ref, total_ref):
     count, _, rows, depth = window_ref.shape
-    pieces = ((window_ref[r].reshape(13 * rows, depth), right_ref[r]) for r in range(count))
-    accumulate(pieces, total_ref, rows, range(count))
+    for r in range(count):
+        left = window_ref[r].reshape(13 * rows, depth)
+        add_row(left, right_ref[r], total_ref, r, slice(0, rows))
 
 
 def fetched(given, scratch, semaphores):
@@ -118,10 +119,17 @@
             window_ref[base + j, :, 16 * side : 16 * side + 16, lanes(part)] = value
 
 
+def kept_square(out_ref, total_ref, mask_ref, strip):
+    for g in range(3):
+        for e in range(19):
+            out_ref[g, e] = total_ref[g, e + 5, strip] * mask_ref[g, e].astype(F32)
+
+
 def square_first_kernel(
-    place_ref, given, total_ref, rest_ref, window_ref, right_ref
+    place_ref, mask_ref, given, out_ref, partial_ref, rest_ref,
+    window_ref, narrow_ref, right_ref, total_ref,
 ):
-    rows, slabs = given[:8], given[8:]
+    slabs, rows, last = given[:8], given[8:16], given[16]
     blank_corners(right_ref, 13)
     total_ref[...] = jnp.zeros_like(total_ref)
     for n, wait in enumerate(slabs):
@@ -130,30 +138,28 @@
     for n in range(4):
         for side in range(2):
             put_left(window_ref, 3 * n, side, rows[2 * n + side]())
+        for j in range(3):
+            r = place_ref[n] * 3 + j
+            left = window_ref[3 * n + j].reshape(13 * 32, 384)
+            add_row(left, right_ref[r], total_ref, r, slice(0, 32))
+    put_left(narrow_ref, 0, 0, last())
     for j in range(3):
-        rest_ref[j] = right_ref[place_ref[4] * 3 + j]
-    firsts = [place_ref[n] * 3 + j for n in range(4) for j in range(3)]
-    pieces = (
-        (window_ref[n].reshape(13 * 32, 384), right_ref[r]) for n, r in enumerate(firsts)
-    )
-    accumulate(pieces, total_ref, 32, firsts)
-
-
-def square_second_kernel(place_ref, mask_ref, given, out_ref, sent_ref, window_ref):
-    before, rest, beside_o, beside_m = given
-    kept_o = beside_o()
-    put_left(window_ref, 0, 0, kept_o)
-    put_left(window_ref, 0, 1, beside_m())
-    sent_ref[...] = kept_o[...]
-    total_ref, right_ref = before(), rest()
-    firsts = [place_ref[4] * 3 + j for j in range(3)]
-    pieces = ((window_ref[j].reshape(13 * 32, 384), right_ref[j]) for j in range(3))
-    accumulate(pieces, total_ref, 32, firsts)
-    for g in range(3):
-        for e in range(19):
-            kept = mask_ref[g, e].astype(F32)
-            for side in range(2):
-                out_ref[side, g, e] = total_ref[g, e + 5, 16 * side : 16 * side + 16] * kept
+        r = place_ref[4] * 3 + j
+        rest_ref[j] = right_ref[r]
+        left = narrow_ref[j].reshape(13 * 16, 384)
+        add_row(left, right_ref[r], total_ref, r, slice(16, 32))
+    partial_ref[...] = total_ref[:, :, 0:16]
+    kept_square(out_ref, total_ref, mask_ref, slice(16, 32))
+
+
+def square_second_kernel(place_ref, mask_ref, given, out_ref, narrow_ref):
+    last, rest, before = given
+    put_left(narrow_ref, 0, 0, last())
+    right_ref, total_ref = rest(), before()
+    for j in range(3):
+        left = narrow_ref[j].reshape(13 * 16, 384)
+        add_row(left, right_ref[j], total_ref, place_ref[4] * 3 + j, slice(0, 16))
+    kept_square(out_ref, total_ref, mask_ref, slice(0, 16))
 
 
 def fill_half(right_ref, chips, slabs, core):
@@ -263,10 +269,10 @@
     both = jnp.stack([own, own_m])
     pair_o = send(own_m, FLIP)
     after, twin = send(both, NEXT), send(both, SIBLING)
-    pair_o, below_m, above_m, beside_m = together(
-        pair_o, send(own_m, UP), send(own_m, DOWN), send(pair_m, ACROSS)
-    )
-    beside_o, twin_after = send(pair_o, ACROSS), send(after, SIBLING)
+    pair_o, below_m, above_m = together(pair_o, send(own_m, UP), send(own_m, DOWN))
+    after, beside_m = together(after, send(pair_m, ACROSS))
+    beside_o, beside_m = together(send(pair_o, ACROSS), beside_m)
+    twin_after = send(after, SIBLING)
 
     chips = jnp.stack([low_y, 3 - low_y, low_y ^ 1, (3 - low_y) ^ 1])
     orbitals = jnp.concatenate([2 * chips + core, 2 * chips + 1 - core])
@@ -278,38 +284,44 @@
 
     left = [(array, part) for array in (both, after, twin, twin_after) for part in (0, 1)]
 
-    partial, rest = call(
+    square_shape = jax.ShapeDtypeStruct((3, 19, 16, 128), F32)
+    square_m, partial, rest = call(
         square_first_kernel,
-        (square_places,),
-        [below_o, below_m, above_o, above_m, (both, 0), (both, 1), pair_o, pair_m] + left,
+        (square_places, sq_mask),
+        left
+        + [below_o, below_m, above_o, above_m, (both, 0), (both, 1), pair_o, pair_m, beside_m],
         (
-            jax.ShapeDtypeStruct((3, 29, 32, 128), F32),
+            square_shape,
+            jax.ShapeDtypeStruct((3, 29, 16, 128), F32),
             jax.ShapeDtypeStruct((3, 384, 384), BF16),
         ),
-        [pltpu.VMEM((12, 13, 32, 384), BF16), pltpu.VMEM((15, 384, 384), BF16)],
+        [
+            pltpu.VMEM((12, 13, 32, 384), BF16),
+            pltpu.VMEM((3, 13, 16, 384), BF16),
+            pltpu.VMEM((15, 384, 384), BF16),
+            pltpu.VMEM((3, 29, 32, 128), F32),
+        ],
         LARGE,
         True,
     )
-    square, beside_late = call(
+    next_m = send(square_m, NEXT)
+    twin_m, beside_o = together(send(square_m, SIBLING), beside_o)
+    square_o = call(
         square_second_kernel,
         (square_places, sq_mask),
-        [partial, rest, beside_o, beside_m],
-        (
-            jax.ShapeDtypeStruct((2, 3, 19, 16, 128), F32),
-            jax.ShapeDtypeStruct((3, 13, 16, 128), F32),
-        ),
-        [pltpu.VMEM((3, 13, 32, 384), BF16)],
+        [beside_o, rest, partial],
+        square_shape,
+        [pltpu.VMEM((3, 13, 16, 384), BF16)],
         LARGE,
         True,
     )
-    square_after = send(square, NEXT)
-    square_twin, pair_late, beside_late = together(send(square, SIBLING), pair_o, beside_o)
-    far_a, far_b = send(pair_late, AGAINST), send(beside_late, ACROSS)
+    twin_o, next_o = send(square_o, SIBLING), send(square_o, NEXT)
+    far_a, far_b = send(pair_o, AGAINST), send(beside_o, ACROSS)
     total, window = call(
         cube_first_kernel,
         (cube_places,),
         [below_o, above_o, (both, 0), pair_o, beside_o, far_a, far_b]
-        + [(square, 0), (square, 1), (square_twin, 0), (square_twin, 1)],
+        + [square_o, square_m, twin_o, twin_m],
         (
             jax.ShapeDtypeStruct((3, 35, 16, 128), F32),
             jax.ShapeDtypeStruct((21, 13, 16, 256), BF16),
@@ -318,13 +330,11 @@
         SMALL,
         False,
     )
-    total, square_after = together(total, square_after)
-    after_twin = send(square_after, SIBLING)
+    total, next_o = together(total, next_o)
     return call(
         cube_second_kernel,
         (cube_places, cube_mask),
-        [total, window, (square, 0), (square_after, 0), (square_after, 1)]
-        + [(after_twin, 0), (after_twin, 1)],
+        [total, window, square_o, next_o, next_m, send(next_o, SIBLING), send(next_m, SIBLING)],
         jax.ShapeDtypeStruct((3, 25, 16, 128), F32),
         [pltpu.VMEM((21, 256, 384), BF16), pltpu.VMEM((3, 35, 16, 128), F32)],
         SMALL,

time: 129 us -> 136 us (1.054)
  starting transfers between devices: 77 us -> 82.9 us
  waiting for transfers between devices: 22.6 us -> 25.4 us
    ppermute x17 -> x20, starting transfers between devices: 77 us -> 82.9 us  [send(): return lax.ppermute(array, AXES, which)]
    ppermute x17 -> x20, waiting for transfers between devices: 22.6 us -> 25.4 us  [send(): return lax.ppermute(array, AXES, which)]
    unnamed x32 -> x38, local copies, waits for them, and re-layouts: 4.46 us -> 3.66 us
  transfers between devices with their start and end apart: 17 -> 20, of which waited for: 6 -> 6; matrix products, arithmetic and copies ran while one was open for 1% -> 1% of each run, Pallas kernels for 10% -> 6%
where the time goes in v7:
time: 136 us
  starting transfers between devices  82.9 us (61%)
  waiting for transfers between devices  25.4 us (19%)
  Pallas kernels  21 us (15%)
  local copies, waits for them, and re-layouts  4.41 us (3%)
    ppermute x20, starting transfers between devices, send(): return lax.ppermute(array, AXES, which)  82.9 us
    ppermute x20, waiting for transfers between devices, send(): return lax.ppermute(array, AXES, which)  25.4 us
    pallas_call x4, Pallas kernels, call(): pl.pallas_call(whole, out_shape=out_shape, in_specs=[SMEM] * first + [IN_...  19.3 us
    unnamed x38, local copies, waits for them, and re-layouts  3.66 us
  transfers between devices with their start and end apart: 20, of which 6 were waited for; matrix products, arithmetic and copies ran while one was open for 1% of the time, Pallas kernels for 6%

profile of v7, /device:TPU:1, one launch (start us, length us, event | category | flops | bytes accessed | tf_op | source)
XLA Modules:
  0.0 135.6 jit_solution(865933378773723811)
XLA Ops:
  0.0 1.7 %shard_map.46 = f32[3,13,16,128]{3,2,1,0:T(8,128)} custom-call(s32[3,13]{1,0:T(4,128)} %mask_ref.1, f32[3,13,16,128]{3,2,1,0:T(8,128)} %x_ref.1), custom_call_target="tpu_custom_call" | custom-call | tf_op jit(solution)/shard_map/pallas_call | solution.py:259
  1.7 6.0 %collective-permute-start = (f32[3,13,16,128]{3,2,1,0:T(8,128)}, f32[3,13,16,128]{3,2,1,0:T(8,128)}, u32[]{:S(2)}, u32[]{:S(2)}) collective-permute-start(f32[3,13,16,128]{3,2,1,0:T(8,128)} %shard_map.46), channel_id=1, source_target_pairs={{0,6},{1,7},{2,4},{3,5},{4,2},{5,3},{6,0},{7,1},{8,14},{9,15},{10,... | collective-permute-start | bytes 958472 | tf_op jit(solution)/shard_map/ppermute | solution.py:41
  7.8 4.4 %collective-permute-start.1 = (f32[3,13,16,128]{3,2,1,0:T(8,128)}, f32[3,13,16,128]{3,2,1,0:T(8,128)S(1)}, u32[]{:S(2)}, u32[]{:S(2)}) collective-permute-start(f32[3,13,16,128]{3,2,1,0:T(8,128)} %shard_map.46), channel_id=1, source_target_pairs={{0,14},{1,15},{2,12},{3,13},{4,10},{5,11},{6,8},{7,9},{8,6},{9,7},... | collective-permute-start | bytes 958472 | tf_op jit(solution)/shard_map/ppermute | solution.py:41
  12.2 3.1 %collective-permute-start.2 = (f32[3,13,16,128]{3,2,1,0:T(8,128)}, f32[3,13,16,128]{3,2,1,0:T(8,128)S(1)}, u32[]{:S(2)}, u32[]{:S(2)}) collective-permute-start(f32[3,13,16,128]{3,2,1,0:T(8,128)} %shard_map.46), channel_id=1, source_target_pairs={{0,16},{1,17},{2,18},{3,19},{4,20},{5,21},{6,22},{7,23},{8,24},{9,... | collective-permute-start | bytes 958472 | tf_op jit(solution)/shard_map/ppermute | solution.py:41
  15.3 15.3 %collective-permute-start.3 = (f32[3,13,16,128]{3,2,1,0:T(8,128)}, f32[3,13,16,128]{3,2,1,0:T(8,128)S(1)}, u32[]{:S(2)}, u32[]{:S(2)}) collective-permute-start(f32[3,13,16,128]{3,2,1,0:T(8,128)} %shard_map.46), channel_id=1, source_target_pairs={{0,752},{1,753},{2,754},{3,755},{4,756},{5,757},{6,758},{7,759},{8... | collective-permute-start | bytes 958472 | tf_op jit(solution)/shard_map/ppermute | solution.py:41
  30.7 0.0 collective-permute-done.1.refs_11_
  30.7 4.9 %collective-permute-done.2.refs_6_.refs_1_ = f32[3,13,16,128]{3,2,1,0:T(8,128)S(1)} collective-permute-done((f32[3,13,16,128]{3,2,1,0:T(8,128)}, f32[3,13,16,128]{3,2,1,0:T(8,128)S(1)}, u32[]{:S(2)}, u32[]{:S(2)}) %collective-permute-start.2) | collective-permute-done | bytes 319520 | tf_op jit(solution)/shard_map/ppermute | solution.py:41
  35.5 1.0 collective-permute-done.3.refs_8_.refs_2_
  36.5 1.2 pad_maximum_fusion.refs_2_.refs_3_
  37.8 2.3 %collective-permute-start.7 = (f32[2,3,13,16,128]{4,3,2,1,0:T(8,128)S(1)}, f32[2,3,13,16,128]{4,3,2,1,0:T(8,128)S(1)}, u32[]{:S(2)}, u32[]{:S(2)}) collective-permute-start(f32[2,3,13,16,128]{4,3,2,1,0:T(8,128)S(1)} %pad_maximum_fusion.refs_2_.refs_3_), channel_id=1, source_target_pairs={{0,2},{1,3},{2,0},{3,1},{4,6},{5,7},{6,4},{7,5},{8,10},{9,11},{10,... | collective-permute-start | bytes 1916936 | tf_op jit(solution)/shard_map/ppermute | solution.py:41
  40.1 1.9 %collective-permute-start.8 = (f32[3,13,16,128]{3,2,1,0:T(8,128)S(1)}, f32[3,13,16,128]{3,2,1,0:T(8,128)S(1)}, u32[]{:S(2)}, u32[]{:S(2)}) collective-permute-start(f32[3,13,16,128]{3,2,1,0:T(8,128)S(1)} %collective-permute-done.1.refs_11_), channel_id=1, source_target_pairs={{0,16},{1,17},{2,18},{3,19},{4,20},{5,21},{6,22},{7,23},{8,760},{9... | collective-permute-start | bytes 958472 | tf_op jit(solution)/shard_map/ppermute | solution.py:41
  42.0 8.5 %collective-permute-start.4 = (f32[3,13,16,128]{3,2,1,0:T(8,128)}, f32[3,13,16,128]{3,2,1,0:T(8,128)S(1)}, u32[]{:S(2)}, u32[]{:S(2)}) collective-permute-start(f32[3,13,16,128]{3,2,1,0:T(8,128)} %collective-permute-done), channel_id=1, source_target_pairs={{0,14},{1,15},{2,12},{3,13},{4,10},{5,11},{6,8},{7,9},{8,6},{9,7},... | collective-permute-start | bytes 958472 | tf_op jit(solution)/shard_map/ppermute | solution.py:41
  50.5 1.9 %collective-permute-start.5 = (f32[3,13,16,128]{3,2,1,0:T(8,128)}, f32[3,13,16,128]{3,2,1,0:T(8,128)S(1)}, u32[]{:S(2)}, u32[]{:S(2)}) collective-permute-start(f32[3,13,16,128]{3,2,1,0:T(8,128)} %collective-permute-done), channel_id=1, source_target_pairs={{0,16},{1,17},{2,18},{3,19},{4,20},{5,21},{6,22},{7,23},{8,24},{9,... | collective-permute-start | bytes 958472 | tf_op jit(solution)/shard_map/ppermute | solution.py:41
  52.5 6.7 %collective-permute-start.6 = (f32[3,13,16,128]{3,2,1,0:T(8,128)}, f32[3,13,16,128]{3,2,1,0:T(8,128)}, u32[]{:S(2)}, u32[]{:S(2)}) collective-permute-start(f32[3,13,16,128]{3,2,1,0:T(8,128)} %collective-permute-done), channel_id=1, source_target_pairs={{0,752},{1,753},{2,754},{3,755},{4,756},{5,757},{6,758},{7,759},{8... | collective-permute-start | bytes 958472 | tf_op jit(solution)/shard_map/ppermute | solution.py:41
  59.2 4.7 %collective-permute-start.9 = (f32[2,3,13,16,128]{4,3,2,1,0:T(8,128)S(1)}, f32[2,3,13,16,128]{4,3,2,1,0:T(8,128)}, u32[]{:S(2)}, u32[]{:S(2)}) collective-permute-start(f32[2,3,13,16,128]{4,3,2,1,0:T(8,128)S(1)} %pad_maximum_fusion.refs_2_.refs_3_), channel_id=1, source_target_pairs={{0,1},{1,0},{2,3},{3,2},{4,5},{5,4},{6,7},{7,6},{8,9},{9,8},{10,11... | collective-permute-start | bytes 1916936 | tf_op jit(solution)/shard_map/ppermute | solution.py:41
  63.9 1.9 %collective-permute-start.10 = (f32[2,3,13,16,128]{4,3,2,1,0:T(8,128)S(1)}, f32[2,3,13,16,128]{4,3,2,1,0:T(8,128)}, u32[]{:S(2)}, u32[]{:S(2)}) collective-permute-start(f32[2,3,13,16,128]{4,3,2,1,0:T(8,128)S(1)} %collective-permute-done.7.refs_3_), channel_id=1, source_target_pairs={{0,1},{1,0},{2,3},{3,2},{4,5},{5,4},{6,7},{7,6},{8,9},{9,8},{10,11... | collective-permute-start | bytes 1916936 | tf_op jit(solution)/shard_map/ppermute | solution.py:41
  65.9 0.0 collective-permute-done.4.refs_10_.refs_4_
  65.9 0.0 collective-permute-done.5.refs_7_
  65.9 0.8 copy-done.18
  66.7 0.0 collective-permute-done.6.refs_9_
  66.7 1.9 %collective-permute-start.11 = (f32[3,13,16,128]{3,2,1,0:T(8,128)S(1)}, f32[3,13,16,128]{3,2,1,0:T(8,128)S(1)}, u32[]{:S(2)}, u32[]{:S(2)}) collective-permute-start(f32[3,13,16,128]{3,2,1,0:T(8,128)S(1)} %collective-permute-done.4.refs_10_.refs_4_), channel_id=1, source_target_pairs={{0,16},{1,17},{2,18},{3,19},{4,20},{5,21},{6,22},{7,23},{8,760},{9... | collective-permute-start | bytes 958472 | tf_op jit(solution)/shard_map/ppermute | solution.py:41
  68.6 0.1 add_subtract_fusion
  68.7 0.7 concatenate.3.refs_0_
  69.4 10.6 %collective-permute-done.11.refs_2_.refs_5_ = f32[3,13,16,128]{3,2,1,0:T(8,128)S(1)} collective-permute-done((f32[3,13,16,128]{3,2,1,0:T(8,128)S(1)}, f32[3,13,16,128]{3,2,1,0:T(8,128)S(1)}, u32[]{:S(2)}, u32[]{:S(2)}) %collective-permute-start.11) | collective-permute-done | bytes 319520 | tf_op jit(solution)/shard_map/ppermute | solution.py:41
  80.0 0.0 collective-permute-done.9.refs_4_
  80.0 0.0 collective-permute-done.10.refs_5_
  80.1 8.0 %shard_map.47 = (f32[3,19,16,128]{3,2,1,0:T(8,128)}, f32[3,29,16,128]{3,2,1,0:T(8,128)}, bf16[3,384,384]{2,1,0:T(8,128)(2,1)}) custom-call(s32[13]{0:T(128)} %concatenate.3.refs_0_, s32[3,19]{1,0:T(4,128)} %refs_1_.4, f32[2,3,13,16,128]{4,3,2,1,0:T(8,128)} %copy-done, f32[2,3,13,16,128]{4,3,2,1,0:T(8,128)} %copy-done.15, ...), custom_call_target="tpu_custom_call" | custom-call | flops 1000000 | bytes 1000 | tf_op jit(solution)/shard_map/pallas_call | solution.py:244
  88.2 0.0 copy-start.11
  88.2 3.9 %collective-permute-start.12 = (f32[3,19,16,128]{3,2,1,0:T(8,128)}, f32[3,19,16,128]{3,2,1,0:T(8,128)S(1)}, u32[]{:S(2)}, u32[]{:S(2)}) collective-permute-start(f32[3,19,16,128]{3,2,1,0:T(8,128)} %get-tuple-element.35.refs_9_), channel_id=1, source_target_pairs={{0,1},{1,0},{2,3},{3,2},{4,5},{5,4},{6,7},{7,6},{8,9},{9,8},{10,11... | collective-permute-start | bytes 1400840 | tf_op jit(solution)/shard_map/ppermute | solution.py:41
  92.1 4.5 %collective-permute-start.17 = (f32[3,19,16,128]{3,2,1,0:T(8,128)}, f32[3,19,16,128]{3,2,1,0:T(8,128)S(1)}, u32[]{:S(2)}, u32[]{:S(2)}) collective-permute-start(f32[3,19,16,128]{3,2,1,0:T(8,128)} %get-tuple-element.35.refs_9_), channel_id=1, source_target_pairs={{0,2},{1,3},{2,0},{3,1},{4,6},{5,7},{6,4},{7,5},{8,10},{9,11},{10,... | collective-permute-start | bytes 1400840 | tf_op jit(solution)/shard_map/ppermute | solution.py:41
  96.6 0.0 collective-permute-done.12.refs_11_
  96.7 0.8 copy-done.12
  97.4 3.5 %shard_map.48.refs_8_.refs_4_ = f32[3,19,16,128]{3,2,1,0:T(8,128)} custom-call(s32[13]{0:T(128)} %concatenate.3.refs_0_, s32[3,19]{1,0:T(4,128)} %refs_1_.4, f32[3,13,16,128]{3,2,1,0:T(8,128)} %copy-done.9, bf16[3,384,384]{2,1,0:T(8,128)(2,1)} %get-tuple-element.38.refs_3_, f32[3,29,16,128]{3,2,1,0:T(8,128)} %get-tuple-element.39.refs_4_), custom_call_target="tpu_custom_call" | custom-call | flops 1000000 | bytes 1000 | tf_op jit(solution)/shard_map/pallas_call | solution.py:244
  101.0 0.0 copy-start.14
  101.0 2.2 %collective-permute-start.15 = (f32[3,19,16,128]{3,2,1,0:T(8,128)}, f32[3,19,16,128]{3,2,1,0:T(8,128)}, u32[]{:S(2)}, u32[]{:S(2)}) collective-permute-start(f32[3,19,16,128]{3,2,1,0:T(8,128)} %shard_map.48.refs_8_.refs_4_), channel_id=1, source_target_pairs={{0,1},{1,0},{2,3},{3,2},{4,5},{5,4},{6,7},{7,6},{8,9},{9,8},{10,11... | collective-permute-start | bytes 1400840 | tf_op jit(solution)/shard_map/ppermute | solution.py:41
  103.2 1.9 %collective-permute-start.16 = (f32[3,19,16,128]{3,2,1,0:T(8,128)}, f32[3,19,16,128]{3,2,1,0:T(8,128)S(1)}, u32[]{:S(2)}, u32[]{:S(2)}) collective-permute-start(f32[3,19,16,128]{3,2,1,0:T(8,128)} %shard_map.48.refs_8_.refs_4_), channel_id=1, source_target_pairs={{0,2},{1,3},{2,0},{3,1},{4,6},{5,7},{6,4},{7,5},{8,10},{9,11},{10,... | collective-permute-start | bytes 1400840 | tf_op jit(solution)/shard_map/ppermute | solution.py:41
  105.1 1.9 %collective-permute-start.13 = (f32[3,13,16,128]{3,2,1,0:T(8,128)S(1)}, f32[3,13,16,128]{3,2,1,0:T(8,128)}, u32[]{:S(2)}, u32[]{:S(2)}) collective-permute-start(f32[3,13,16,128]{3,2,1,0:T(8,128)S(1)} %copy-done.8), channel_id=1, source_target_pairs={{0,752},{1,753},{2,754},{3,755},{4,756},{5,757},{6,758},{7,759},{8... | collective-permute-start | bytes 958472 | tf_op jit(solution)/shard_map/ppermute | solution.py:41
  107.1 3.4 %collective-permute-start.14 = (f32[3,13,16,128]{3,2,1,0:T(8,128)S(1)}, f32[3,13,16,128]{3,2,1,0:T(8,128)}, u32[]{:S(2)}, u32[]{:S(2)}) collective-permute-start(f32[3,13,16,128]{3,2,1,0:T(8,128)S(1)} %copy-done.10), channel_id=1, source_target_pairs={{0,16},{1,17},{2,18},{3,19},{4,20},{5,21},{6,22},{7,23},{8,760},{9... | collective-permute-start | bytes 958472 | tf_op jit(solution)/shard_map/ppermute | solution.py:41
  110.4 0.1 stack.55.refs_0_
  110.5 3.0 %collective-permute-start.19 = (f32[3,19,16,128]{3,2,1,0:T(8,128)S(1)}, f32[3,19,16,128]{3,2,1,0:T(8,128)S(1)}, u32[]{:S(2)}, u32[]{:S(2)}) collective-permute-start(f32[3,19,16,128]{3,2,1,0:T(8,128)S(1)} %collective-permute-done.17.refs_6_), channel_id=1, source_target_pairs={{0,1},{1,0},{2,3},{3,2},{4,5},{5,4},{6,7},{7,6},{8,9},{9,8},{10,11... | collective-permute-start | bytes 1400840 | tf_op jit(solution)/shard_map/ppermute | solution.py:41
  113.5 2.2 %collective-permute-done.13.refs_6_ = f32[3,13,16,128]{3,2,1,0:T(8,128)} collective-permute-done((f32[3,13,16,128]{3,2,1,0:T(8,128)S(1)}, f32[3,13,16,128]{3,2,1,0:T(8,128)}, u32[]{:S(2)}, u32[]{:S(2)}) %collective-permute-start.13) | collective-permute-done | bytes 319520 | tf_op jit(solution)/shard_map/ppermute | solution.py:41
  115.7 5.3 %collective-permute-done.14.refs_7_ = f32[3,13,16,128]{3,2,1,0:T(8,128)} collective-permute-done((f32[3,13,16,128]{3,2,1,0:T(8,128)S(1)}, f32[3,13,16,128]{3,2,1,0:T(8,128)}, u32[]{:S(2)}, u32[]{:S(2)}) %collective-permute-start.14) | collective-permute-done | bytes 319520 | tf_op jit(solution)/shard_map/ppermute | solution.py:41
  121.0 1.0 copy-done.2
  122.0 1.0 copy-done.13
  123.1 4.3 %shard_map.49 = (f32[3,35,16,128]{3,2,1,0:T(8,128)S(1)}, bf16[21,13,16,256]{3,2,1,0:T(8,128)(2,1)S(1)}) custom-call(s32[9]{0:T(128)S(1)} %stack.55.refs_0_, f32[3,13,16,128]{3,2,1,0:T(8,128)S(1)} %copy-done.4, f32[3,13,16,128]{3,2,1,0:T(8,128)S(1)} %copy-done.6, f32[2,3,13,16,128]{4,3,2,1,0:T(8,128)S(1)} %copy-done.1, f32[3,13,16,128]{3,2,1,0:T(8,128)S(1)} %copy-done.8, ...), custom_call_target="tpu_custom_call" | custom-call | flops 1000000 | bytes 1000 | tf_op jit(solution)/shard_map/pallas_call | solution.py:244
  127.4 3.3 %collective-permute-start.18 = (f32[3,19,16,128]{3,2,1,0:T(8,128)S(1)}, f32[3,19,16,128]{3,2,1,0:T(8,128)S(1)}, u32[]{:S(2)}, u32[]{:S(2)}) collective-permute-start(f32[3,19,16,128]{3,2,1,0:T(8,128)S(1)} %collective-permute-done.16.refs_5_), channel_id=1, source_target_pairs={{0,1},{1,0},{2,3},{3,2},{4,5},{5,4},{6,7},{7,6},{8,9},{9,8},{10,11... | collective-permute-start | bytes 1400840 | tf_op jit(solution)/shard_map/ppermute | solution.py:41
  130.7 1.4 %collective-permute-done.18.refs_7_ = f32[3,19,16,128]{3,2,1,0:T(8,128)S(1)} collective-permute-done((f32[3,19,16,128]{3,2,1,0:T(8,128)S(1)}, f32[3,19,16,128]{3,2,1,0:T(8,128)S(1)}, u32[]{:S(2)}, u32[]{:S(2)}) %collective-permute-start.18) | collective-permute-done | bytes 466976 | tf_op jit(solution)/shard_map/ppermute | solution.py:41
  132.1 3.4 %shard_map.50 = f32[3,25,16,128]{3,2,1,0:T(8,128)} custom-call(s32[9]{0:T(128)S(1)} %stack.55.refs_0_, s32[3,25]{1,0:T(4,128)S(1)} %copy-done.14, f32[3,35,16,128]{3,2,1,0:T(8,128)S(1)} %get-tuple-element.42.refs_2_, bf16[21,13,16,256]{3,2,1,0:T(8,128)(2,1)S(1)} %get-tuple-element.43.refs_3_, f32[3,19,16,128]{3,2,1,0:T(8,128)S(1)} %copy-done.2, ...), custom_call_target="tpu_custom_call" | custom-call | flops 1000000 | bytes 1000 | tf_op jit(solution)/shard_map/pallas_call | solution.py:244
  (40 shorter events, 0.1 us)
Async XLA Ops:
  1.7 28.9 %collective-permute-start = (f32[3,13,16,128]{3,2,1,0:T(8,128)}, f32[3,13,16,128]{3,2,1,0:T(8,128)}, u32[]{:S(2)}, u32[]{:S(2)}) collective-permute-start(f32[3,13,16,128]{3,2,1,0:T(8,128)} %shard_map.46), channel_id=1, source_target_pairs={{0,6},{1,7},{2,4},{3,5},{4,2},{5,3},{6,0},{7,1},{8,14},{9,15},{10,... | collective-permute-start | bytes 958472 | tf_op jit(solution)/shard_map/ppermute | solution.py:41
  7.8 22.9 %collective-permute-start.1 = (f32[3,13,16,128]{3,2,1,0:T(8,128)}, f32[3,13,16,128]{3,2,1,0:T(8,128)S(1)}, u32[]{:S(2)}, u32[]{:S(2)}) collective-permute-start(f32[3,13,16,128]{3,2,1,0:T(8,128)} %shard_map.46), channel_id=1, source_target_pairs={{0,14},{1,15},{2,12},{3,13},{4,10},{5,11},{6,8},{7,9},{8,6},{9,7},... | collective-permute-start | bytes 958472 | tf_op jit(solution)/shard_map/ppermute | solution.py:41
  12.2 23.3 %collective-permute-start.2 = (f32[3,13,16,128]{3,2,1,0:T(8,128)}, f32[3,13,16,128]{3,2,1,0:T(8,128)S(1)}, u32[]{:S(2)}, u32[]{:S(2)}) collective-permute-start(f32[3,13,16,128]{3,2,1,0:T(8,128)} %shard_map.46), channel_id=1, source_target_pairs={{0,16},{1,17},{2,18},{3,19},{4,20},{5,21},{6,22},{7,23},{8,24},{9,... | collective-permute-start | bytes 958472 | tf_op jit(solution)/shard_map/ppermute | solution.py:41
  15.3 21.2 %collective-permute-start.3 = (f32[3,13,16,128]{3,2,1,0:T(8,128)}, f32[3,13,16,128]{3,2,1,0:T(8,128)S(1)}, u32[]{:S(2)}, u32[]{:S(2)}) collective-permute-start(f32[3,13,16,128]{3,2,1,0:T(8,128)} %shard_map.46), channel_id=1, source_target_pairs={{0,752},{1,753},{2,754},{3,755},{4,756},{5,757},{6,758},{7,759},{8... | collective-permute-start | bytes 958472 | tf_op jit(solution)/shard_map/ppermute | solution.py:41
  30.7 49.4 %copy-start.16 = (f32[3,13,16,128]{3,2,1,0:T(8,128)}, f32[3,13,16,128]{3,2,1,0:T(8,128)S(1)}, u32[]{:S(2)}) copy-start(f32[3,13,16,128]{3,2,1,0:T(8,128)S(1)} %collective-permute-done.1.refs_11_) | copy-start | bytes 958468
  35.5 44.5 %copy-start.3 = (f32[3,13,16,128]{3,2,1,0:T(8,128)}, f32[3,13,16,128]{3,2,1,0:T(8,128)S(1)}, u32[]{:S(2)}) copy-start(f32[3,13,16,128]{3,2,1,0:T(8,128)S(1)} %collective-permute-done.2.refs_6_.refs_1_) | copy-start | bytes 958468
  36.5 43.5 %copy-start.5 = (f32[3,13,16,128]{3,2,1,0:T(8,128)}, f32[3,13,16,128]{3,2,1,0:T(8,128)S(1)}, u32[]{:S(2)}) copy-start(f32[3,13,16,128]{3,2,1,0:T(8,128)S(1)} %collective-permute-done.3.refs_8_.refs_2_) | copy-start | bytes 958468
  37.8 42.3 %copy-start = (f32[2,3,13,16,128]{4,3,2,1,0:T(8,128)}, f32[2,3,13,16,128]{4,3,2,1,0:T(8,128)S(1)}, u32[]{:S(2)}) copy-start(f32[2,3,13,16,128]{4,3,2,1,0:T(8,128)S(1)} %pad_maximum_fusion.refs_2_.refs_3_) | copy-start | bytes 1916932
  37.8 26.2 %collective-permute-start.7 = (f32[2,3,13,16,128]{4,3,2,1,0:T(8,128)S(1)}, f32[2,3,13,16,128]{4,3,2,1,0:T(8,128)S(1)}, u32[]{:S(2)}, u32[]{:S(2)}) collective-permute-start(f32[2,3,13,16,128]{4,3,2,1,0:T(8,128)S(1)} %pad_maximum_fusion.refs_2_.refs_3_), channel_id=1, source_target_pairs={{0,2},{1,3},{2,0},{3,1},{4,6},{5,7},{6,4},{7,5},{8,10},{9,11},{10,... | collective-permute-start | bytes 1916936 | tf_op jit(solution)/shard_map/ppermute | solution.py:41
  40.1 19.1 %collective-permute-start.8 = (f32[3,13,16,128]{3,2,1,0:T(8,128)S(1)}, f32[3,13,16,128]{3,2,1,0:T(8,128)S(1)}, u32[]{:S(2)}, u32[]{:S(2)}) collective-permute-start(f32[3,13,16,128]{3,2,1,0:T(8,128)S(1)} %collective-permute-done.1.refs_11_), channel_id=1, source_target_pairs={{0,16},{1,17},{2,18},{3,19},{4,20},{5,21},{6,22},{7,23},{8,760},{9... | collective-permute-start | bytes 958472 | tf_op jit(solution)/shard_map/ppermute | solution.py:41
  42.0 23.9 %collective-permute-start.4 = (f32[3,13,16,128]{3,2,1,0:T(8,128)}, f32[3,13,16,128]{3,2,1,0:T(8,128)S(1)}, u32[]{:S(2)}, u32[]{:S(2)}) collective-permute-start(f32[3,13,16,128]{3,2,1,0:T(8,128)} %collective-permute-done), channel_id=1, source_target_pairs={{0,14},{1,15},{2,12},{3,13},{4,10},{5,11},{6,8},{7,9},{8,6},{9,7},... | collective-permute-start | bytes 958472 | tf_op jit(solution)/shard_map/ppermute | solution.py:41
  50.5 15.4 %collective-permute-start.5 = (f32[3,13,16,128]{3,2,1,0:T(8,128)}, f32[3,13,16,128]{3,2,1,0:T(8,128)S(1)}, u32[]{:S(2)}, u32[]{:S(2)}) collective-permute-start(f32[3,13,16,128]{3,2,1,0:T(8,128)} %collective-permute-done), channel_id=1, source_target_pairs={{0,16},{1,17},{2,18},{3,19},{4,20},{5,21},{6,22},{7,23},{8,24},{9,... | collective-permute-start | bytes 958472 | tf_op jit(solution)/shard_map/ppermute | solution.py:41
  52.5 14.3 %collective-permute-start.6 = (f32[3,13,16,128]{3,2,1,0:T(8,128)}, f32[3,13,16,128]{3,2,1,0:T(8,128)}, u32[]{:S(2)}, u32[]{:S(2)}) collective-permute-start(f32[3,13,16,128]{3,2,1,0:T(8,128)} %collective-permute-done), channel_id=1, source_target_pairs={{0,752},{1,753},{2,754},{3,755},{4,756},{5,757},{6,758},{7,759},{8... | collective-permute-start | bytes 958472 | tf_op jit(solution)/shard_map/ppermute | solution.py:41
  59.2 20.9 %copy-start.17 = (f32[3,13,16,128]{3,2,1,0:T(8,128)}, f32[3,13,16,128]{3,2,1,0:T(8,128)S(1)}, u32[]{:S(2)}) copy-start(f32[3,13,16,128]{3,2,1,0:T(8,128)S(1)} %collective-permute-done.8.refs_12_) | copy-start | bytes 958468
  59.2 20.8 %collective-permute-start.9 = (f32[2,3,13,16,128]{4,3,2,1,0:T(8,128)S(1)}, f32[2,3,13,16,128]{4,3,2,1,0:T(8,128)}, u32[]{:S(2)}, u32[]{:S(2)}) collective-permute-start(f32[2,3,13,16,128]{4,3,2,1,0:T(8,128)S(1)} %pad_maximum_fusion.refs_2_.refs_3_), channel_id=1, source_target_pairs={{0,1},{1,0},{2,3},{3,2},{4,5},{5,4},{6,7},{7,6},{8,9},{9,8},{10,11... | collective-permute-start | bytes 1916936 | tf_op jit(solution)/shard_map/ppermute | solution.py:41
  63.9 16.1 %copy-start.15 = (f32[2,3,13,16,128]{4,3,2,1,0:T(8,128)}, f32[2,3,13,16,128]{4,3,2,1,0:T(8,128)S(1)}, u32[]{:S(2)}) copy-start(f32[2,3,13,16,128]{4,3,2,1,0:T(8,128)S(1)} %collective-permute-done.7.refs_3_) | copy-start | bytes 1916932
  63.9 16.1 %collective-permute-start.10 = (f32[2,3,13,16,128]{4,3,2,1,0:T(8,128)S(1)}, f32[2,3,13,16,128]{4,3,2,1,0:T(8,128)}, u32[]{:S(2)}, u32[]{:S(2)}) collective-permute-start(f32[2,3,13,16,128]{4,3,2,1,0:T(8,128)S(1)} %collective-permute-done.7.refs_3_), channel_id=1, source_target_pairs={{0,1},{1,0},{2,3},{3,2},{4,5},{5,4},{6,7},{7,6},{8,9},{9,8},{10,11... | collective-permute-start | bytes 1916936 | tf_op jit(solution)/shard_map/ppermute | solution.py:41
  65.9 14.2 %copy-start.7 = (f32[3,13,16,128]{3,2,1,0:T(8,128)}, f32[3,13,16,128]{3,2,1,0:T(8,128)S(1)}, u32[]{:S(2)}) copy-start(f32[3,13,16,128]{3,2,1,0:T(8,128)S(1)} %collective-permute-done.4.refs_10_.refs_4_) | copy-start | bytes 958468
  65.9 0.8 copy-start.18
  66.7 13.3 %collective-permute-start.11 = (f32[3,13,16,128]{3,2,1,0:T(8,128)S(1)}, f32[3,13,16,128]{3,2,1,0:T(8,128)S(1)}, u32[]{:S(2)}, u32[]{:S(2)}) collective-permute-start(f32[3,13,16,128]{3,2,1,0:T(8,128)S(1)} %collective-permute-done.4.refs_10_.refs_4_), channel_id=1, source_target_pairs={{0,16},{1,17},{2,18},{3,19},{4,20},{5,21},{6,22},{7,23},{8,760},{9... | collective-permute-start | bytes 958472 | tf_op jit(solution)/shard_map/ppermute | solution.py:41
  80.0 8.1 %copy-start.9 = (f32[3,13,16,128]{3,2,1,0:T(8,128)}, f32[3,13,16,128]{3,2,1,0:T(8,128)S(1)}, u32[]{:S(2)}) copy-start(f32[3,13,16,128]{3,2,1,0:T(8,128)S(1)} %collective-permute-done.11.refs_2_.refs_5_) | copy-start | bytes 958468
  88.1 17.0 %copy-start.8 = (f32[3,13,16,128]{3,2,1,0:T(8,128)S(1)}, f32[3,13,16,128]{3,2,1,0:T(8,128)}, u32[]{:S(2)}) copy-start(f32[3,13,16,128]{3,2,1,0:T(8,128)} %copy-done.7) | copy-start | bytes 958468
  88.1 32.9 %copy-start.1 = (f32[2,3,13,16,128]{4,3,2,1,0:T(8,128)S(1)}, f32[2,3,13,16,128]{4,3,2,1,0:T(8,128)}, u32[]{:S(2)}) copy-start(f32[2,3,13,16,128]{4,3,2,1,0:T(8,128)} %copy-done) | copy-start | bytes 1916932
  88.1 32.9 %copy-start.4 = (f32[3,13,16,128]{3,2,1,0:T(8,128)S(1)}, f32[3,13,16,128]{3,2,1,0:T(8,128)}, u32[]{:S(2)}) copy-start(f32[3,13,16,128]{3,2,1,0:T(8,128)} %copy-done.3) | copy-start | bytes 958468
  88.1 32.9 %copy-start.6 = (f32[3,13,16,128]{3,2,1,0:T(8,128)S(1)}, f32[3,13,16,128]{3,2,1,0:T(8,128)}, u32[]{:S(2)}) copy-start(f32[3,13,16,128]{3,2,1,0:T(8,128)} %copy-done.5) | copy-start | bytes 958468
  88.2 32.9 %copy-start.11 = (f32[3,19,16,128]{3,2,1,0:T(8,128)S(1)}, f32[3,19,16,128]{3,2,1,0:T(8,128)}, u32[]{:S(2)}) copy-start(f32[3,19,16,128]{3,2,1,0:T(8,128)} %get-tuple-element.35.refs_9_) | copy-start | bytes 1400836
  88.2 18.9 %copy-start.10 = (f32[3,13,16,128]{3,2,1,0:T(8,128)S(1)}, f32[3,13,16,128]{3,2,1,0:T(8,128)}, u32[]{:S(2)}) copy-start(f32[3,13,16,128]{3,2,1,0:T(8,128)} %copy-done.9) | copy-start | bytes 958468
  88.2 8.5 %collective-permute-start.12 = (f32[3,19,16,128]{3,2,1,0:T(8,128)}, f32[3,19,16,128]{3,2,1,0:T(8,128)S(1)}, u32[]{:S(2)}, u32[]{:S(2)}) collective-permute-start(f32[3,19,16,128]{3,2,1,0:T(8,128)} %get-tuple-element.35.refs_9_), channel_id=1, source_target_pairs={{0,1},{1,0},{2,3},{3,2},{4,5},{5,4},{6,7},{7,6},{8,9},{9,8},{10,11... | collective-permute-start | bytes 1400840 | tf_op jit(solution)/shard_map/ppermute | solution.py:41
  92.1 18.5 %collective-permute-start.17 = (f32[3,19,16,128]{3,2,1,0:T(8,128)}, f32[3,19,16,128]{3,2,1,0:T(8,128)S(1)}, u32[]{:S(2)}, u32[]{:S(2)}) collective-permute-start(f32[3,19,16,128]{3,2,1,0:T(8,128)} %get-tuple-element.35.refs_9_), channel_id=1, source_target_pairs={{0,2},{1,3},{2,0},{3,1},{4,6},{5,7},{6,4},{7,5},{8,10},{9,11},{10,... | collective-permute-start | bytes 1400840 | tf_op jit(solution)/shard_map/ppermute | solution.py:41
  96.6 0.8 copy-start.12
  101.0 31.1 %copy-start.14 = (s32[3,25]{1,0:T(4,128)S(1)}, s32[3,25]{1,0:T(4,128)}, u32[]{:S(2)}) copy-start(s32[3,25]{1,0:T(4,128)} %refs_1_.5) | copy-start | bytes 904
  101.0 20.0 %collective-permute-start.15 = (f32[3,19,16,128]{3,2,1,0:T(8,128)}, f32[3,19,16,128]{3,2,1,0:T(8,128)}, u32[]{:S(2)}, u32[]{:S(2)}) collective-permute-start(f32[3,19,16,128]{3,2,1,0:T(8,128)} %shard_map.48.refs_8_.refs_4_), channel_id=1, source_target_pairs={{0,1},{1,0},{2,3},{3,2},{4,5},{5,4},{6,7},{7,6},{8,9},{9,8},{10,11... | collective-permute-start | bytes 1400840 | tf_op jit(solution)/shard_map/ppermute | solution.py:41
  103.2 24.2 %collective-permute-start.16 = (f32[3,19,16,128]{3,2,1,0:T(8,128)}, f32[3,19,16,128]{3,2,1,0:T(8,128)S(1)}, u32[]{:S(2)}, u32[]{:S(2)}) collective-permute-start(f32[3,19,16,128]{3,2,1,0:T(8,128)} %shard_map.48.refs_8_.refs_4_), channel_id=1, source_target_pairs={{0,2},{1,3},{2,0},{3,1},{4,6},{5,7},{6,4},{7,5},{8,10},{9,11},{10,... | collective-permute-start | bytes 1400840 | tf_op jit(solution)/shard_map/ppermute | solution.py:41
  105.1 10.6 %collective-permute-start.13 = (f32[3,13,16,128]{3,2,1,0:T(8,128)S(1)}, f32[3,13,16,128]{3,2,1,0:T(8,128)}, u32[]{:S(2)}, u32[]{:S(2)}) collective-permute-start(f32[3,13,16,128]{3,2,1,0:T(8,128)S(1)} %copy-done.8), channel_id=1, source_target_pairs={{0,752},{1,753},{2,754},{3,755},{4,756},{5,757},{6,758},{7,759},{8... | collective-permute-start | bytes 958472 | tf_op jit(solution)/shard_map/ppermute | solution.py:41
  107.1 13.9 %collective-permute-start.14 = (f32[3,13,16,128]{3,2,1,0:T(8,128)S(1)}, f32[3,13,16,128]{3,2,1,0:T(8,128)}, u32[]{:S(2)}, u32[]{:S(2)}) collective-permute-start(f32[3,13,16,128]{3,2,1,0:T(8,128)S(1)} %copy-done.10), channel_id=1, source_target_pairs={{0,16},{1,17},{2,18},{3,19},{4,20},{5,21},{6,22},{7,23},{8,760},{9... | collective-permute-start | bytes 958472 | tf_op jit(solution)/shard_map/ppermute | solution.py:41
  110.5 20.1 %collective-permute-start.19 = (f32[3,19,16,128]{3,2,1,0:T(8,128)S(1)}, f32[3,19,16,128]{3,2,1,0:T(8,128)S(1)}, u32[]{:S(2)}, u32[]{:S(2)}) collective-permute-start(f32[3,19,16,128]{3,2,1,0:T(8,128)S(1)} %collective-permute-done.17.refs_6_), channel_id=1, source_target_pairs={{0,1},{1,0},{2,3},{3,2},{4,5},{5,4},{6,7},{7,6},{8,9},{9,8},{10,11... | collective-permute-start | bytes 1400840 | tf_op jit(solution)/shard_map/ppermute | solution.py:41
  121.0 1.0 copy-start.2
  122.0 1.0 copy-start.13
  127.4 4.7 %collective-permute-start.18 = (f32[3,19,16,128]{3,2,1,0:T(8,128)S(1)}, f32[3,19,16,128]{3,2,1,0:T(8,128)S(1)}, u32[]{:S(2)}, u32[]{:S(2)}) collective-permute-start(f32[3,19,16,128]{3,2,1,0:T(8,128)S(1)} %collective-permute-done.16.refs_5_), channel_id=1, source_target_pairs={{0,1},{1,0},{2,3},{3,2},{4,5},{5,4},{6,7},{7,6},{8,9},{9,8},{10,11... | collective-permute-start | bytes 1400840 | tf_op jit(solution)/shard_map/ppermute | solution.py:41

commit v8 on v6

--- a/solution.py
+++ b/solution.py
@@ -139,12 +139,10 @@
     accumulate(pieces, total_ref, 32, firsts)
 
 
-def square_second_kernel(place_ref, mask_ref, given, out_ref, sent_ref, window_ref):
+def square_second_kernel(place_ref, mask_ref, given, out_ref, window_ref):
     before, rest, beside_o, beside_m = given
-    kept_o = beside_o()
-    put_left(window_ref, 0, 0, kept_o)
+    put_left(window_ref, 0, 0, beside_o())
     put_left(window_ref, 0, 1, beside_m())
-    sent_ref[...] = kept_o[...]
     total_ref, right_ref = before(), rest()
     firsts = [place_ref[4] * 3 + j for j in range(3)]
     pieces = ((window_ref[j].reshape(13 * 32, 384), right_ref[j]) for j in range(3))
@@ -263,9 +261,8 @@
     both = jnp.stack([own, own_m])
     pair_o = send(own_m, FLIP)
     after, twin = send(both, NEXT), send(both, SIBLING)
-    pair_o, below_m, above_m, beside_m = together(
-        pair_o, send(own_m, UP), send(own_m, DOWN), send(pair_m, ACROSS)
-    )
+    pair_o, below_m, above_m = together(pair_o, send(own_m, UP), send(own_m, DOWN))
+    after, beside_m = together(after, send(pair_m, ACROSS))
     beside_o, twin_after = send(pair_o, ACROSS), send(after, SIBLING)
 
     chips = jnp.stack([low_y, 3 - low_y, low_y ^ 1, (3 - low_y) ^ 1])
@@ -290,14 +287,11 @@
         LARGE,
         True,
     )
-    square, beside_late = call(
+    square = call(
         square_second_kernel,
         (square_places, sq_mask),
         [partial, rest, beside_o, beside_m],
-        (
-            jax.ShapeDtypeStruct((2, 3, 19, 16, 128), F32),
-            jax.ShapeDtypeStruct((3, 13, 16, 128), F32),
-        ),
+        jax.ShapeDtypeStruct((2, 3, 19, 16, 128), F32),
         [pltpu.VMEM((3, 13, 32, 384), BF16)],
         LARGE,
         True,

time: 129 us -> 127 us (0.984)
    unnamed x32 -> x30, local copies, waits for them, and re-layouts: 4.46 us -> 3.69 us
where the time goes in v8:
time: 127 us; the launch traced here: 126 us
  starting transfers between devices  77.3 us (61%)
  Pallas kernels  21.8 us (17%)
  waiting for transfers between devices  21.4 us (17%)
  local copies, waits for them, and re-layouts  4.42 us (3%)
    ppermute x17, starting transfers between devices, send(): return lax.ppermute(array, AXES, which)  77.3 us
    ppermute x17, waiting for transfers between devices, send(): return lax.ppermute(array, AXES, which)  21.4 us
    pallas_call x4, Pallas kernels, call(): pl.pallas_call(whole, out_shape=out_shape, in_specs=[SMEM] * first + [IN_...  20 us
    unnamed x30, local copies, waits for them, and re-layouts  3.69 us
  transfers between devices with their start and end apart: 17, of which 6 were waited for; matrix products, arithmetic and copies ran while one was open for 1% of the time, Pallas kernels for 10%

profile of v8, /device:TPU:1, one launch (start us, length us, event | category | flops | bytes accessed | tf_op | source)
XLA Modules:
  0.0 126.5 jit_solution(12003558874076966390)
XLA Ops:
  0.0 1.7 %shard_map.46 = f32[3,13,16,128]{3,2,1,0:T(8,128)} custom-call(s32[3,13]{1,0:T(4,128)} %mask_ref.1, f32[3,13,16,128]{3,2,1,0:T(8,128)} %x_ref.1), custom_call_target="tpu_custom_call" | custom-call | tf_op jit(solution)/shard_map/pallas_call | solution.py:251
  1.7 6.0 %collective-permute-start = (f32[3,13,16,128]{3,2,1,0:T(8,128)}, f32[3,13,16,128]{3,2,1,0:T(8,128)S(1)}, u32[]{:S(2)}, u32[]{:S(2)}) collective-permute-start(f32[3,13,16,128]{3,2,1,0:T(8,128)} %shard_map.46), channel_id=1, source_target_pairs={{0,6},{1,7},{2,4},{3,5},{4,2},{5,3},{6,0},{7,1},{8,14},{9,15},{10,... | collective-permute-start | bytes 958472 | tf_op jit(solution)/shard_map/ppermute | solution.py:41
  7.8 4.4 %collective-permute-start.1 = (f32[3,13,16,128]{3,2,1,0:T(8,128)}, f32[3,13,16,128]{3,2,1,0:T(8,128)S(1)}, u32[]{:S(2)}, u32[]{:S(2)}) collective-permute-start(f32[3,13,16,128]{3,2,1,0:T(8,128)} %shard_map.46), channel_id=1, source_target_pairs={{0,14},{1,15},{2,12},{3,13},{4,10},{5,11},{6,8},{7,9},{8,6},{9,7},... | collective-permute-start | bytes 958472 | tf_op jit(solution)/shard_map/ppermute | solution.py:41
  12.2 3.1 %collective-permute-start.2 = (f32[3,13,16,128]{3,2,1,0:T(8,128)}, f32[3,13,16,128]{3,2,1,0:T(8,128)S(1)}, u32[]{:S(2)}, u32[]{:S(2)}) collective-permute-start(f32[3,13,16,128]{3,2,1,0:T(8,128)} %shard_map.46), channel_id=1, source_target_pairs={{0,16},{1,17},{2,18},{3,19},{4,20},{5,21},{6,22},{7,23},{8,24},{9,... | collective-permute-start | bytes 958472 | tf_op jit(solution)/shard_map/ppermute | solution.py:41
  15.3 15.3 %collective-permute-start.3 = (f32[3,13,16,128]{3,2,1,0:T(8,128)}, f32[3,13,16,128]{3,2,1,0:T(8,128)S(1)}, u32[]{:S(2)}, u32[]{:S(2)}) collective-permute-start(f32[3,13,16,128]{3,2,1,0:T(8,128)} %shard_map.46), channel_id=1, source_target_pairs={{0,752},{1,753},{2,754},{3,755},{4,756},{5,757},{6,758},{7,759},{8... | collective-permute-start | bytes 958472 | tf_op jit(solution)/shard_map/ppermute | solution.py:41
  30.6 0.0 collective-permute-done
  30.6 0.0 collective-permute-done.1.refs_7_
  30.7 4.9 %collective-permute-done.2.refs_1_ = f32[3,13,16,128]{3,2,1,0:T(8,128)S(1)} collective-permute-done((f32[3,13,16,128]{3,2,1,0:T(8,128)}, f32[3,13,16,128]{3,2,1,0:T(8,128)S(1)}, u32[]{:S(2)}, u32[]{:S(2)}) %collective-permute-start.2) | collective-permute-done | bytes 319520 | tf_op jit(solution)/shard_map/ppermute | solution.py:41
  35.5 1.0 collective-permute-done.3.refs_3_.refs_2_
  36.5 1.1 pad_maximum_fusion.refs_5_.refs_3_
  37.7 2.3 %collective-permute-start.8 = (f32[2,3,13,16,128]{4,3,2,1,0:T(8,128)S(1)}, f32[2,3,13,16,128]{4,3,2,1,0:T(8,128)S(1)}, u32[]{:S(2)}, u32[]{:S(2)}) collective-permute-start(f32[2,3,13,16,128]{4,3,2,1,0:T(8,128)S(1)} %pad_maximum_fusion.refs_5_.refs_3_), channel_id=1, source_target_pairs={{0,2},{1,3},{2,0},{3,1},{4,6},{5,7},{6,4},{7,5},{8,10},{9,11},{10,... | collective-permute-start | bytes 1916936 | tf_op jit(solution)/shard_map/ppermute | solution.py:41
  40.0 1.9 %collective-permute-start.9 = (f32[3,13,16,128]{3,2,1,0:T(8,128)S(1)}, f32[3,13,16,128]{3,2,1,0:T(8,128)}, u32[]{:S(2)}, u32[]{:S(2)}) collective-permute-start(f32[3,13,16,128]{3,2,1,0:T(8,128)S(1)} %collective-permute-done.1.refs_7_), channel_id=1, source_target_pairs={{0,16},{1,17},{2,18},{3,19},{4,20},{5,21},{6,22},{7,23},{8,760},{9... | collective-permute-start | bytes 958472 | tf_op jit(solution)/shard_map/ppermute | solution.py:41
  41.9 8.4 %collective-permute-start.4 = (f32[3,13,16,128]{3,2,1,0:T(8,128)S(1)}, f32[3,13,16,128]{3,2,1,0:T(8,128)}, u32[]{:S(2)}, u32[]{:S(2)}) collective-permute-start(f32[3,13,16,128]{3,2,1,0:T(8,128)S(1)} %collective-permute-done), channel_id=1, source_target_pairs={{0,14},{1,15},{2,12},{3,13},{4,10},{5,11},{6,8},{7,9},{8,6},{9,7},... | collective-permute-start | bytes 958472 | tf_op jit(solution)/shard_map/ppermute | solution.py:41
  50.4 1.9 %collective-permute-start.5 = (f32[3,13,16,128]{3,2,1,0:T(8,128)S(1)}, f32[3,13,16,128]{3,2,1,0:T(8,128)S(1)}, u32[]{:S(2)}, u32[]{:S(2)}) collective-permute-start(f32[3,13,16,128]{3,2,1,0:T(8,128)S(1)} %collective-permute-done), channel_id=1, source_target_pairs={{0,16},{1,17},{2,18},{3,19},{4,20},{5,21},{6,22},{7,23},{8,24},{9,... | collective-permute-start | bytes 958472 | tf_op jit(solution)/shard_map/ppermute | solution.py:41
  52.3 6.7 %collective-permute-start.6 = (f32[3,13,16,128]{3,2,1,0:T(8,128)S(1)}, f32[3,13,16,128]{3,2,1,0:T(8,128)}, u32[]{:S(2)}, u32[]{:S(2)}) collective-permute-start(f32[3,13,16,128]{3,2,1,0:T(8,128)S(1)} %collective-permute-done), channel_id=1, source_target_pairs={{0,752},{1,753},{2,754},{3,755},{4,756},{5,757},{6,758},{7,759},{8... | collective-permute-start | bytes 958472 | tf_op jit(solution)/shard_map/ppermute | solution.py:41
  59.0 0.0 collective-permute-done.9.refs_5_
  59.0 4.7 %collective-permute-start.10 = (f32[2,3,13,16,128]{4,3,2,1,0:T(8,128)S(1)}, f32[2,3,13,16,128]{4,3,2,1,0:T(8,128)S(1)}, u32[]{:S(2)}, u32[]{:S(2)}) collective-permute-start(f32[2,3,13,16,128]{4,3,2,1,0:T(8,128)S(1)} %pad_maximum_fusion.refs_5_.refs_3_), channel_id=1, source_target_pairs={{0,1},{1,0},{2,3},{3,2},{4,5},{5,4},{6,7},{7,6},{8,9},{9,8},{10,11... | collective-permute-start | bytes 1916936 | tf_op jit(solution)/shard_map/ppermute | solution.py:41
  63.7 0.0 collective-permute-done.8.refs_8_
  63.8 1.9 %collective-permute-start.11 = (f32[2,3,13,16,128]{4,3,2,1,0:T(8,128)S(1)}, f32[2,3,13,16,128]{4,3,2,1,0:T(8,128)}, u32[]{:S(2)}, u32[]{:S(2)}) collective-permute-start(f32[2,3,13,16,128]{4,3,2,1,0:T(8,128)S(1)} %collective-permute-done.8.refs_8_), channel_id=1, source_target_pairs={{0,1},{1,0},{2,3},{3,2},{4,5},{5,4},{6,7},{7,6},{8,9},{9,8},{10,11... | collective-permute-start | bytes 1916936 | tf_op jit(solution)/shard_map/ppermute | solution.py:41
  65.7 0.0 collective-permute-done.4.refs_6_.refs_4_
  65.7 0.0 collective-permute-done.5.refs_2_
  65.7 0.0 copy-start.14
  65.8 0.0 collective-permute-done.6.refs_4_
  65.8 1.9 %collective-permute-start.7 = (f32[3,13,16,128]{3,2,1,0:T(8,128)}, f32[3,13,16,128]{3,2,1,0:T(8,128)S(1)}, u32[]{:S(2)}, u32[]{:S(2)}) collective-permute-start(f32[3,13,16,128]{3,2,1,0:T(8,128)} %collective-permute-done.4.refs_6_.refs_4_), channel_id=1, source_target_pairs={{0,16},{1,17},{2,18},{3,19},{4,20},{5,21},{6,22},{7,23},{8,760},{9... | collective-permute-start | bytes 958472 | tf_op jit(solution)/shard_map/ppermute | solution.py:41
  67.7 0.1 add_subtract_fusion
  67.8 0.6 concatenate.3.refs_0_
  68.4 0.0 collective-permute-done.10.refs_9_
  68.5 0.8 copy-done.12
  69.3 8.1 %shard_map.47 = (f32[3,29,32,128]{3,2,1,0:T(8,128)}, bf16[3,384,384]{2,1,0:T(8,128)(2,1)}) custom-call(s32[13]{0:T(128)} %concatenate.3.refs_0_, f32[3,13,16,128]{3,2,1,0:T(8,128)} %copy-done.4, f32[3,13,16,128]{3,2,1,0:T(8,128)} %copy-done.14, f32[3,13,16,128]{3,2,1,0:T(8,128)} %copy-done.6, f32[3,13,16,128]{3,2,1,0:T(8,128)} %collective-permute-done.6.refs_4_, ...), custom_call_target="tpu_custom_call" | custom-call | flops 1000000 | bytes 1000 | tf_op jit(solution)/shard_map/pallas_call | solution.py:236
  77.4 1.4 %collective-permute-done.7.refs_4_.refs_5_ = f32[3,13,16,128]{3,2,1,0:T(8,128)S(1)} collective-permute-done((f32[3,13,16,128]{3,2,1,0:T(8,128)}, f32[3,13,16,128]{3,2,1,0:T(8,128)S(1)}, u32[]{:S(2)}, u32[]{:S(2)}) %collective-permute-start.7) | collective-permute-done | bytes 319520 | tf_op jit(solution)/shard_map/ppermute | solution.py:41
  78.7 0.7 copy-done.8
  79.4 4.3 %shard_map.48.refs_8_.refs_4_ = f32[2,3,19,16,128]{4,3,2,1,0:T(8,128)} custom-call(s32[13]{0:T(128)} %concatenate.3.refs_0_, s32[3,19]{1,0:T(4,128)} %refs_1_.2, f32[3,29,32,128]{3,2,1,0:T(8,128)} %get-tuple-element.31.refs_2_, bf16[3,384,384]{2,1,0:T(8,128)(2,1)} %get-tuple-element.32.refs_3_, f32[3,13,16,128]{3,2,1,0:T(8,128)} %copy-done.8, ...), custom_call_target="tpu_custom_call" | custom-call | flops 1000000 | bytes 1000 | tf_op jit(solution)/shard_map/pallas_call | solution.py:236
  83.8 0.0 copy-start.10
  83.8 4.3 %collective-permute-start.12 = (f32[2,3,19,16,128]{4,3,2,1,0:T(8,128)}, f32[2,3,19,16,128]{4,3,2,1,0:T(8,128)S(1)}, u32[]{:S(2)}, u32[]{:S(2)}) collective-permute-start(f32[2,3,19,16,128]{4,3,2,1,0:T(8,128)} %shard_map.48.refs_8_.refs_4_), channel_id=1, source_target_pairs={{0,1},{1,0},{2,3},{3,2},{4,5},{5,4},{6,7},{7,6},{8,9},{9,8},{10,11... | collective-permute-start | bytes 2801672 | tf_op jit(solution)/shard_map/ppermute | solution.py:41
  88.1 4.5 %collective-permute-start.15 = (f32[2,3,19,16,128]{4,3,2,1,0:T(8,128)}, f32[2,3,19,16,128]{4,3,2,1,0:T(8,128)S(1)}, u32[]{:S(2)}, u32[]{:S(2)}) collective-permute-start(f32[2,3,19,16,128]{4,3,2,1,0:T(8,128)} %shard_map.48.refs_8_.refs_4_), channel_id=1, source_target_pairs={{0,2},{1,3},{2,0},{3,1},{4,6},{5,7},{6,4},{7,5},{8,10},{9,11},{10,... | collective-permute-start | bytes 2801672 | tf_op jit(solution)/shard_map/ppermute | solution.py:41
  92.7 0.0 collective-permute-done.12.refs_9_
  92.7 4.4 %collective-permute-start.13 = (f32[3,13,16,128]{3,2,1,0:T(8,128)}, f32[3,13,16,128]{3,2,1,0:T(8,128)S(1)}, u32[]{:S(2)}, u32[]{:S(2)}) collective-permute-start(f32[3,13,16,128]{3,2,1,0:T(8,128)} %collective-permute-done.4.refs_6_.refs_4_), channel_id=1, source_target_pairs={{0,752},{1,753},{2,754},{3,755},{4,756},{5,757},{6,758},{7,759},{8... | collective-permute-start | bytes 958472 | tf_op jit(solution)/shard_map/ppermute | solution.py:41
  97.1 1.9 %collective-permute-start.14 = (f32[3,13,16,128]{3,2,1,0:T(8,128)}, f32[3,13,16,128]{3,2,1,0:T(8,128)}, u32[]{:S(2)}, u32[]{:S(2)}) collective-permute-start(f32[3,13,16,128]{3,2,1,0:T(8,128)} %copy-done.8), channel_id=1, source_target_pairs={{0,16},{1,17},{2,18},{3,19},{4,20},{5,21},{6,22},{7,23},{8,760},{9... | collective-permute-start | bytes 958472 | tf_op jit(solution)/shard_map/ppermute | solution.py:41
  99.1 0.1 stack.55.refs_0_
  99.1 4.9 %collective-permute-done.13.refs_6_ = f32[3,13,16,128]{3,2,1,0:T(8,128)S(1)} collective-permute-done((f32[3,13,16,128]{3,2,1,0:T(8,128)}, f32[3,13,16,128]{3,2,1,0:T(8,128)S(1)}, u32[]{:S(2)}, u32[]{:S(2)}) %collective-permute-start.13) | collective-permute-done | bytes 319520 | tf_op jit(solution)/shard_map/ppermute | solution.py:41
  104.0 7.1 %collective-permute-done.14.refs_7_ = f32[3,13,16,128]{3,2,1,0:T(8,128)} collective-permute-done((f32[3,13,16,128]{3,2,1,0:T(8,128)}, f32[3,13,16,128]{3,2,1,0:T(8,128)}, u32[]{:S(2)}, u32[]{:S(2)}) %collective-permute-start.14) | collective-permute-done | bytes 319520 | tf_op jit(solution)/shard_map/ppermute | solution.py:41
  111.2 1.2 copy-done
  112.4 1.0 copy-done.9
  113.3 4.2 %shard_map.49 = (f32[3,35,16,128]{3,2,1,0:T(8,128)S(1)}, bf16[21,13,16,256]{3,2,1,0:T(8,128)(2,1)S(1)}) custom-call(s32[9]{0:T(128)S(1)} %stack.55.refs_0_, f32[3,13,16,128]{3,2,1,0:T(8,128)S(1)} %copy-done.5, f32[3,13,16,128]{3,2,1,0:T(8,128)S(1)} %copy-done.7, f32[2,3,13,16,128]{4,3,2,1,0:T(8,128)S(1)} %copy-done.3, ...), custom_call_target="tpu_custom_call" | custom-call | flops 1000000 | bytes 1000 | tf_op jit(solution)/shard_map/pallas_call | solution.py:236
  117.6 0.0 collective-permute-done.15.refs_5_
  117.6 3.4 %collective-permute-start.16 = (f32[2,3,19,16,128]{4,3,2,1,0:T(8,128)S(1)}, f32[2,3,19,16,128]{4,3,2,1,0:T(8,128)S(1)}, u32[]{:S(2)}, u32[]{:S(2)}) collective-permute-start(f32[2,3,19,16,128]{4,3,2,1,0:T(8,128)S(1)} %collective-permute-done.15.refs_5_), channel_id=1, source_target_pairs={{0,1},{1,0},{2,3},{3,2},{4,5},{5,4},{6,7},{7,6},{8,9},{9,8},{10,11... | collective-permute-start | bytes 2801672 | tf_op jit(solution)/shard_map/ppermute | solution.py:41
  121.0 2.1 %collective-permute-done.16.refs_6_ = f32[2,3,19,16,128]{4,3,2,1,0:T(8,128)S(1)} collective-permute-done((f32[2,3,19,16,128]{4,3,2,1,0:T(8,128)S(1)}, f32[2,3,19,16,128]{4,3,2,1,0:T(8,128)S(1)}, u32[]{:S(2)}, u32[]{:S(2)}) %collective-permute-start.16) | collective-permute-done | bytes 933920 | tf_op jit(solution)/shard_map/ppermute | solution.py:41
  123.1 3.4 %shard_map.50 = f32[3,25,16,128]{3,2,1,0:T(8,128)} custom-call(s32[9]{0:T(128)S(1)} %stack.55.refs_0_, s32[3,25]{1,0:T(4,128)S(1)} %copy-done.10, f32[3,35,16,128]{3,2,1,0:T(8,128)S(1)} %get-tuple-element.38.refs_2_, bf16[21,13,16,256]{3,2,1,0:T(8,128)(2,1)S(1)} %get-tuple-element.39.refs_3_, f32[2,3,19,16,128]{4,3,2,1,0:T(8,128)S(1)} %copy-done.1, ...), custom_call_target="tpu_custom_call" | custom-call | flops 1000000 | bytes 1000 | tf_op jit(solution)/shard_map/pallas_call | solution.py:236
  (26 shorter events, 0.1 us)
Async XLA Ops:
  1.7 28.9 %collective-permute-start = (f32[3,13,16,128]{3,2,1,0:T(8,128)}, f32[3,13,16,128]{3,2,1,0:T(8,128)S(1)}, u32[]{:S(2)}, u32[]{:S(2)}) collective-permute-start(f32[3,13,16,128]{3,2,1,0:T(8,128)} %shard_map.46), channel_id=1, source_target_pairs={{0,6},{1,7},{2,4},{3,5},{4,2},{5,3},{6,0},{7,1},{8,14},{9,15},{10,... | collective-permute-start | bytes 958472 | tf_op jit(solution)/shard_map/ppermute | solution.py:41
  7.8 22.9 %collective-permute-start.1 = (f32[3,13,16,128]{3,2,1,0:T(8,128)}, f32[3,13,16,128]{3,2,1,0:T(8,128)S(1)}, u32[]{:S(2)}, u32[]{:S(2)}) collective-permute-start(f32[3,13,16,128]{3,2,1,0:T(8,128)} %shard_map.46), channel_id=1, source_target_pairs={{0,14},{1,15},{2,12},{3,13},{4,10},{5,11},{6,8},{7,9},{8,6},{9,7},... | collective-permute-start | bytes 958472 | tf_op jit(solution)/shard_map/ppermute | solution.py:41
  12.2 23.3 %collective-permute-start.2 = (f32[3,13,16,128]{3,2,1,0:T(8,128)}, f32[3,13,16,128]{3,2,1,0:T(8,128)S(1)}, u32[]{:S(2)}, u32[]{:S(2)}) collective-permute-start(f32[3,13,16,128]{3,2,1,0:T(8,128)} %shard_map.46), channel_id=1, source_target_pairs={{0,16},{1,17},{2,18},{3,19},{4,20},{5,21},{6,22},{7,23},{8,24},{9,... | collective-permute-start | bytes 958472 | tf_op jit(solution)/shard_map/ppermute | solution.py:41
  15.3 21.2 %collective-permute-start.3 = (f32[3,13,16,128]{3,2,1,0:T(8,128)}, f32[3,13,16,128]{3,2,1,0:T(8,128)S(1)}, u32[]{:S(2)}, u32[]{:S(2)}) collective-permute-start(f32[3,13,16,128]{3,2,1,0:T(8,128)} %shard_map.46), channel_id=1, source_target_pairs={{0,752},{1,753},{2,754},{3,755},{4,756},{5,757},{6,758},{7,759},{8... | collective-permute-start | bytes 958472 | tf_op jit(solution)/shard_map/ppermute | solution.py:41
  30.7 37.8 %copy-start.13 = (f32[3,13,16,128]{3,2,1,0:T(8,128)}, f32[3,13,16,128]{3,2,1,0:T(8,128)S(1)}, u32[]{:S(2)}) copy-start(f32[3,13,16,128]{3,2,1,0:T(8,128)S(1)} %collective-permute-done.1.refs_7_) | copy-start | bytes 958468
  35.5 32.9 %copy-start.4 = (f32[3,13,16,128]{3,2,1,0:T(8,128)}, f32[3,13,16,128]{3,2,1,0:T(8,128)S(1)}, u32[]{:S(2)}) copy-start(f32[3,13,16,128]{3,2,1,0:T(8,128)S(1)} %collective-permute-done.2.refs_1_) | copy-start | bytes 958468
  36.5 31.9 %copy-start.6 = (f32[3,13,16,128]{3,2,1,0:T(8,128)}, f32[3,13,16,128]{3,2,1,0:T(8,128)S(1)}, u32[]{:S(2)}) copy-start(f32[3,13,16,128]{3,2,1,0:T(8,128)S(1)} %collective-permute-done.3.refs_3_.refs_2_) | copy-start | bytes 958468
  37.7 30.8 %copy-start.2 = (f32[2,3,13,16,128]{4,3,2,1,0:T(8,128)}, f32[2,3,13,16,128]{4,3,2,1,0:T(8,128)S(1)}, u32[]{:S(2)}) copy-start(f32[2,3,13,16,128]{4,3,2,1,0:T(8,128)S(1)} %pad_maximum_fusion.refs_5_.refs_3_) | copy-start | bytes 1916932
  37.7 26.1 %collective-permute-start.8 = (f32[2,3,13,16,128]{4,3,2,1,0:T(8,128)S(1)}, f32[2,3,13,16,128]{4,3,2,1,0:T(8,128)S(1)}, u32[]{:S(2)}, u32[]{:S(2)}) collective-permute-start(f32[2,3,13,16,128]{4,3,2,1,0:T(8,128)S(1)} %pad_maximum_fusion.refs_5_.refs_3_), channel_id=1, source_target_pairs={{0,2},{1,3},{2,0},{3,1},{4,6},{5,7},{6,4},{7,5},{8,10},{9,11},{10,... | collective-permute-start | bytes 1916936 | tf_op jit(solution)/shard_map/ppermute | solution.py:41
  40.0 19.0 %collective-permute-start.9 = (f32[3,13,16,128]{3,2,1,0:T(8,128)S(1)}, f32[3,13,16,128]{3,2,1,0:T(8,128)}, u32[]{:S(2)}, u32[]{:S(2)}) collective-permute-start(f32[3,13,16,128]{3,2,1,0:T(8,128)S(1)} %collective-permute-done.1.refs_7_), channel_id=1, source_target_pairs={{0,16},{1,17},{2,18},{3,19},{4,20},{5,21},{6,22},{7,23},{8,760},{9... | collective-permute-start | bytes 958472 | tf_op jit(solution)/shard_map/ppermute | solution.py:41
  41.9 23.8 %collective-permute-start.4 = (f32[3,13,16,128]{3,2,1,0:T(8,128)S(1)}, f32[3,13,16,128]{3,2,1,0:T(8,128)}, u32[]{:S(2)}, u32[]{:S(2)}) collective-permute-start(f32[3,13,16,128]{3,2,1,0:T(8,128)S(1)} %collective-permute-done), channel_id=1, source_target_pairs={{0,14},{1,15},{2,12},{3,13},{4,10},{5,11},{6,8},{7,9},{8,6},{9,7},... | collective-permute-start | bytes 958472 | tf_op jit(solution)/shard_map/ppermute | solution.py:41
  50.4 15.4 %collective-permute-start.5 = (f32[3,13,16,128]{3,2,1,0:T(8,128)S(1)}, f32[3,13,16,128]{3,2,1,0:T(8,128)S(1)}, u32[]{:S(2)}, u32[]{:S(2)}) collective-permute-start(f32[3,13,16,128]{3,2,1,0:T(8,128)S(1)} %collective-permute-done), channel_id=1, source_target_pairs={{0,16},{1,17},{2,18},{3,19},{4,20},{5,21},{6,22},{7,23},{8,24},{9,... | collective-permute-start | bytes 958472 | tf_op jit(solution)/shard_map/ppermute | solution.py:41
  52.3 13.5 %collective-permute-start.6 = (f32[3,13,16,128]{3,2,1,0:T(8,128)S(1)}, f32[3,13,16,128]{3,2,1,0:T(8,128)}, u32[]{:S(2)}, u32[]{:S(2)}) collective-permute-start(f32[3,13,16,128]{3,2,1,0:T(8,128)S(1)} %collective-permute-done), channel_id=1, source_target_pairs={{0,752},{1,753},{2,754},{3,755},{4,756},{5,757},{6,758},{7,759},{8... | collective-permute-start | bytes 958472 | tf_op jit(solution)/shard_map/ppermute | solution.py:41
  59.0 9.4 %collective-permute-start.10 = (f32[2,3,13,16,128]{4,3,2,1,0:T(8,128)S(1)}, f32[2,3,13,16,128]{4,3,2,1,0:T(8,128)S(1)}, u32[]{:S(2)}, u32[]{:S(2)}) collective-permute-start(f32[2,3,13,16,128]{4,3,2,1,0:T(8,128)S(1)} %pad_maximum_fusion.refs_5_.refs_3_), channel_id=1, source_target_pairs={{0,1},{1,0},{2,3},{3,2},{4,5},{5,4},{6,7},{7,6},{8,9},{9,8},{10,11... | collective-permute-start | bytes 1916936 | tf_op jit(solution)/shard_map/ppermute | solution.py:41
  63.7 4.7 %copy-start.11 = (f32[2,3,13,16,128]{4,3,2,1,0:T(8,128)}, f32[2,3,13,16,128]{4,3,2,1,0:T(8,128)S(1)}, u32[]{:S(2)}) copy-start(f32[2,3,13,16,128]{4,3,2,1,0:T(8,128)S(1)} %collective-permute-done.8.refs_8_) | copy-start | bytes 1916932
  63.8 4.7 %collective-permute-start.11 = (f32[2,3,13,16,128]{4,3,2,1,0:T(8,128)S(1)}, f32[2,3,13,16,128]{4,3,2,1,0:T(8,128)}, u32[]{:S(2)}, u32[]{:S(2)}) collective-permute-start(f32[2,3,13,16,128]{4,3,2,1,0:T(8,128)S(1)} %collective-permute-done.8.refs_8_), channel_id=1, source_target_pairs={{0,1},{1,0},{2,3},{3,2},{4,5},{5,4},{6,7},{7,6},{8,9},{9,8},{10,11... | collective-permute-start | bytes 1916936 | tf_op jit(solution)/shard_map/ppermute | solution.py:41
  65.7 2.7 %copy-start.14 = (f32[3,13,16,128]{3,2,1,0:T(8,128)}, f32[3,13,16,128]{3,2,1,0:T(8,128)S(1)}, u32[]{:S(2)}) copy-start(f32[3,13,16,128]{3,2,1,0:T(8,128)S(1)} %collective-permute-done.5.refs_2_) | copy-start | bytes 958468
  65.8 13.0 %collective-permute-start.7 = (f32[3,13,16,128]{3,2,1,0:T(8,128)}, f32[3,13,16,128]{3,2,1,0:T(8,128)S(1)}, u32[]{:S(2)}, u32[]{:S(2)}) collective-permute-start(f32[3,13,16,128]{3,2,1,0:T(8,128)} %collective-permute-done.4.refs_6_.refs_4_), channel_id=1, source_target_pairs={{0,16},{1,17},{2,18},{3,19},{4,20},{5,21},{6,22},{7,23},{8,760},{9... | collective-permute-start | bytes 958472 | tf_op jit(solution)/shard_map/ppermute | solution.py:41
  68.4 0.8 copy-start.12
  77.3 33.8 %copy-start.3 = (f32[2,3,13,16,128]{4,3,2,1,0:T(8,128)S(1)}, f32[2,3,13,16,128]{4,3,2,1,0:T(8,128)}, u32[]{:S(2)}) copy-start(f32[2,3,13,16,128]{4,3,2,1,0:T(8,128)} %copy-done.2) | copy-start | bytes 1916932
  77.3 33.8 %copy-start.5 = (f32[3,13,16,128]{3,2,1,0:T(8,128)S(1)}, f32[3,13,16,128]{3,2,1,0:T(8,128)}, u32[]{:S(2)}) copy-start(f32[3,13,16,128]{3,2,1,0:T(8,128)} %copy-done.4) | copy-start | bytes 958468
  77.4 33.8 %copy-start.7 = (f32[3,13,16,128]{3,2,1,0:T(8,128)S(1)}, f32[3,13,16,128]{3,2,1,0:T(8,128)}, u32[]{:S(2)}) copy-start(f32[3,13,16,128]{3,2,1,0:T(8,128)} %copy-done.6) | copy-start | bytes 958468
  78.7 0.7 copy-start.8
  83.8 39.3 %copy-start.10 = (s32[3,25]{1,0:T(4,128)S(1)}, s32[3,25]{1,0:T(4,128)}, u32[]{:S(2)}) copy-start(s32[3,25]{1,0:T(4,128)} %refs_1_.3) | copy-start | bytes 904
  83.8 8.9 %collective-permute-start.12 = (f32[2,3,19,16,128]{4,3,2,1,0:T(8,128)}, f32[2,3,19,16,128]{4,3,2,1,0:T(8,128)S(1)}, u32[]{:S(2)}, u32[]{:S(2)}) collective-permute-start(f32[2,3,19,16,128]{4,3,2,1,0:T(8,128)} %shard_map.48.refs_8_.refs_4_), channel_id=1, source_target_pairs={{0,1},{1,0},{2,3},{3,2},{4,5},{5,4},{6,7},{7,6},{8,9},{9,8},{10,11... | collective-permute-start | bytes 2801672 | tf_op jit(solution)/shard_map/ppermute | solution.py:41
  88.1 29.4 %collective-permute-start.15 = (f32[2,3,19,16,128]{4,3,2,1,0:T(8,128)}, f32[2,3,19,16,128]{4,3,2,1,0:T(8,128)S(1)}, u32[]{:S(2)}, u32[]{:S(2)}) collective-permute-start(f32[2,3,19,16,128]{4,3,2,1,0:T(8,128)} %shard_map.48.refs_8_.refs_4_), channel_id=1, source_target_pairs={{0,2},{1,3},{2,0},{3,1},{4,6},{5,7},{6,4},{7,5},{8,10},{9,11},{10,... | collective-permute-start | bytes 2801672 | tf_op jit(solution)/shard_map/ppermute | solution.py:41
  92.7 11.4 %collective-permute-start.13 = (f32[3,13,16,128]{3,2,1,0:T(8,128)}, f32[3,13,16,128]{3,2,1,0:T(8,128)S(1)}, u32[]{:S(2)}, u32[]{:S(2)}) collective-permute-start(f32[3,13,16,128]{3,2,1,0:T(8,128)} %collective-permute-done.4.refs_6_.refs_4_), channel_id=1, source_target_pairs={{0,752},{1,753},{2,754},{3,755},{4,756},{5,757},{6,758},{7,759},{8... | collective-permute-start | bytes 958472 | tf_op jit(solution)/shard_map/ppermute | solution.py:41
  97.1 14.0 %collective-permute-start.14 = (f32[3,13,16,128]{3,2,1,0:T(8,128)}, f32[3,13,16,128]{3,2,1,0:T(8,128)}, u32[]{:S(2)}, u32[]{:S(2)}) collective-permute-start(f32[3,13,16,128]{3,2,1,0:T(8,128)} %copy-done.8), channel_id=1, source_target_pairs={{0,16},{1,17},{2,18},{3,19},{4,20},{5,21},{6,22},{7,23},{8,760},{9... | collective-permute-start | bytes 958472 | tf_op jit(solution)/shard_map/ppermute | solution.py:41
  111.2 1.2 copy-start
  112.4 1.0 copy-start.9
  113.3 9.7 %copy-start.1 = (f32[2,3,19,16,128]{4,3,2,1,0:T(8,128)S(1)}, f32[2,3,19,16,128]{4,3,2,1,0:T(8,128)}, u32[]{:S(2)}) copy-start(f32[2,3,19,16,128]{4,3,2,1,0:T(8,128)} %shard_map.48.refs_8_.refs_4_) | copy-start | bytes 2801668
  117.6 5.5 %collective-permute-start.16 = (f32[2,3,19,16,128]{4,3,2,1,0:T(8,128)S(1)}, f32[2,3,19,16,128]{4,3,2,1,0:T(8,128)S(1)}, u32[]{:S(2)}, u32[]{:S(2)}) collective-permute-start(f32[2,3,19,16,128]{4,3,2,1,0:T(8,128)S(1)} %collective-permute-done.15.refs_5_), channel_id=1, source_target_pairs={{0,1},{1,0},{2,3},{3,2},{4,5},{5,4},{6,7},{7,6},{8,9},{9,8},{10,11... | collective-permute-start | bytes 2801672 | tf_op jit(solution)/shard_map/ppermute | solution.py:41

commit v9 on v8

--- a/solution.py
+++ b/solution.py
@@ -255,14 +255,12 @@
         out_specs=VMEM,
     )(x_mask, x_band)
 
-    own_m, pair_m, below_o, above_o = together(
-        send(own, MIRROR), send(own, FLIP), send(own, UP), send(own, DOWN)
-    )
+    own_m, pair_m = together(send(own, MIRROR), send(own, FLIP))
     both = jnp.stack([own, own_m])
     pair_o = send(own_m, FLIP)
     after, twin = send(both, NEXT), send(both, SIBLING)
-    pair_o, below_m, above_m = together(pair_o, send(own_m, UP), send(own_m, DOWN))
-    after, beside_m = together(after, send(pair_m, ACROSS))
+    after, pair_o, beside_m = together(after, pair_o, send(pair_m, ACROSS))
+    below, above = send(both, UP), send(both, DOWN)
     beside_o, twin_after = send(pair_o, ACROSS), send(after, SIBLING)
 
     chips = jnp.stack([low_y, 3 - low_y, low_y ^ 1, (3 - low_y) ^ 1])
@@ -278,7 +276,8 @@
     partial, rest = call(
         square_first_kernel,
         (square_places,),
-        [below_o, below_m, above_o, above_m, (both, 0), (both, 1), pair_o, pair_m] + left,
+        [(below, 0), (below, 1), (above, 0), (above, 1), (both, 0), (both, 1), pair_o, pair_m]
+        + left,
         (
             jax.ShapeDtypeStruct((3, 29, 32, 128), F32),
             jax.ShapeDtypeStruct((3, 384, 384), BF16),
@@ -302,7 +301,7 @@
     total, window = call(
         cube_first_kernel,
         (cube_places,),
-        [below_o, above_o, (both, 0), pair_o, beside_o, far_a, far_b]
+        [(below, 0), (above, 0), (both, 0), pair_o, beside_o, far_a, far_b]
         + [(square, 0), (square, 1), (square_twin, 0), (square_twin, 1)],
         (
             jax.ShapeDtypeStruct((3, 35, 16, 128), F32),

time: 127 us -> 130 us (1.024)
  waiting for transfers between devices: 21.4 us -> 32.5 us
  starting transfers between devices: 77.3 us -> 66.8 us
  local copies, waits for them, and re-layouts: 4.42 us -> 6.95 us
    ppermute x17 -> x15, waiting for transfers between devices: 21.4 us -> 32.5 us  [send(): return lax.ppermute(array, AXES, which)]
    ppermute x17 -> x15, starting transfers between devices: 77.3 us -> 66.8 us  [send(): return lax.ppermute(array, AXES, which)]
    unnamed x30 -> x34, local copies, waits for them, and re-layouts: 3.69 us -> 6.21 us
  transfers between devices with their start and end apart: 17 -> 15, of which waited for: 6 -> 6; matrix products, arithmetic and copies ran while one was open for 1% -> 1% of each run, Pallas kernels for 10% -> 9%
where the time goes in v9:
time: 130 us; the launch traced here: 129 us
  starting transfers between devices  66.8 us (51%)
  waiting for transfers between devices  32.5 us (25%)
  Pallas kernels  21.6 us (17%)
  local copies, waits for them, and re-layouts  6.95 us (5%)
    ppermute x15, starting transfers between devices, send(): return lax.ppermute(array, AXES, which)  66.8 us
    ppermute x15, waiting for transfers between devices, send(): return lax.ppermute(array, AXES, which)  32.5 us
    pallas_call x4, Pallas kernels, call(): pl.pallas_call(whole, out_shape=out_shape, in_specs=[SMEM] * first + [IN_...  19.9 us
    unnamed x34, local copies, waits for them, and re-layouts  6.21 us
  transfers between devices with their start and end apart: 15, of which 6 were waited for; matrix products, arithmetic and copies ran while one was open for 1% of the time, Pallas kernels for 9%

profile of v9, /device:TPU:1, one launch (start us, length us, event | category | flops | bytes accessed | tf_op | source)
XLA Modules:
  0.0 129.5 jit_solution(5555127905146025221)
XLA Ops:
  0.0 1.7 %shard_map.46 = f32[3,13,16,128]{3,2,1,0:T(8,128)} custom-call(s32[3,13]{1,0:T(4,128)} %mask_ref.1, f32[3,13,16,128]{3,2,1,0:T(8,128)} %x_ref.1), custom_call_target="tpu_custom_call" | custom-call | tf_op jit(solution)/shard_map/pallas_call | solution.py:251
  1.7 6.0 %collective-permute-start = (f32[3,13,16,128]{3,2,1,0:T(8,128)}, f32[3,13,16,128]{3,2,1,0:T(8,128)S(1)}, u32[]{:S(2)}, u32[]{:S(2)}) collective-permute-start(f32[3,13,16,128]{3,2,1,0:T(8,128)} %shard_map.46), channel_id=1, source_target_pairs={{0,6},{1,7},{2,4},{3,5},{4,2},{5,3},{6,0},{7,1},{8,14},{9,15},{10,... | collective-permute-start | bytes 958472 | tf_op jit(solution)/shard_map/ppermute | solution.py:41
  7.8 4.4 %collective-permute-start.1 = (f32[3,13,16,128]{3,2,1,0:T(8,128)}, f32[3,13,16,128]{3,2,1,0:T(8,128)S(1)}, u32[]{:S(2)}, u32[]{:S(2)}) collective-permute-start(f32[3,13,16,128]{3,2,1,0:T(8,128)} %shard_map.46), channel_id=1, source_target_pairs={{0,14},{1,15},{2,12},{3,13},{4,10},{5,11},{6,8},{7,9},{8,6},{9,7},... | collective-permute-start | bytes 958472 | tf_op jit(solution)/shard_map/ppermute | solution.py:41
  12.2 0.3 collective-permute-done
  12.5 14.0 %collective-permute-done.1.refs_5_ = f32[3,13,16,128]{3,2,1,0:T(8,128)S(1)} collective-permute-done((f32[3,13,16,128]{3,2,1,0:T(8,128)}, f32[3,13,16,128]{3,2,1,0:T(8,128)S(1)}, u32[]{:S(2)}, u32[]{:S(2)}) %collective-permute-start.1) | collective-permute-done | bytes 319520 | tf_op jit(solution)/shard_map/ppermute | solution.py:41
  26.5 1.1 pad_maximum_fusion.refs_3_
  27.6 2.4 %collective-permute-start.4 = (f32[2,3,13,16,128]{4,3,2,1,0:T(8,128)S(1)}, f32[2,3,13,16,128]{4,3,2,1,0:T(8,128)S(1)}, u32[]{:S(2)}, u32[]{:S(2)}) collective-permute-start(f32[2,3,13,16,128]{4,3,2,1,0:T(8,128)S(1)} %pad_maximum_fusion.refs_3_), channel_id=1, source_target_pairs={{0,2},{1,3},{2,0},{3,1},{4,6},{5,7},{6,4},{7,5},{8,10},{9,11},{10,... | collective-permute-start | bytes 1916936 | tf_op jit(solution)/shard_map/ppermute | solution.py:41
  30.0 4.8 %collective-permute-start.5 = (f32[3,13,16,128]{3,2,1,0:T(8,128)S(1)}, f32[3,13,16,128]{3,2,1,0:T(8,128)}, u32[]{:S(2)}, u32[]{:S(2)}) collective-permute-start(f32[3,13,16,128]{3,2,1,0:T(8,128)S(1)} %collective-permute-done), channel_id=1, source_target_pairs={{0,14},{1,15},{2,12},{3,13},{4,10},{5,11},{6,8},{7,9},{8,6},{9,7},... | collective-permute-start | bytes 958472 | tf_op jit(solution)/shard_map/ppermute | solution.py:41
  34.8 2.0 %collective-permute-start.6 = (f32[3,13,16,128]{3,2,1,0:T(8,128)S(1)}, f32[3,13,16,128]{3,2,1,0:T(8,128)S(1)}, u32[]{:S(2)}, u32[]{:S(2)}) collective-permute-start(f32[3,13,16,128]{3,2,1,0:T(8,128)S(1)} %collective-permute-done.1.refs_5_), channel_id=1, source_target_pairs={{0,16},{1,17},{2,18},{3,19},{4,20},{5,21},{6,22},{7,23},{8,760},{9... | collective-permute-start | bytes 958472 | tf_op jit(solution)/shard_map/ppermute | solution.py:41
  36.8 3.1 %collective-permute-start.2 = (f32[2,3,13,16,128]{4,3,2,1,0:T(8,128)S(1)}, f32[2,3,13,16,128]{4,3,2,1,0:T(8,128)S(1)}, u32[]{:S(2)}, u32[]{:S(2)}) collective-permute-start(f32[2,3,13,16,128]{4,3,2,1,0:T(8,128)S(1)} %pad_maximum_fusion.refs_3_), channel_id=1, source_target_pairs={{0,16},{1,17},{2,18},{3,19},{4,20},{5,21},{6,22},{7,23},{8,24},{9,... | collective-permute-start | bytes 1916936 | tf_op jit(solution)/shard_map/ppermute | solution.py:41
  39.9 14.1 %collective-permute-start.3 = (f32[2,3,13,16,128]{4,3,2,1,0:T(8,128)S(1)}, f32[2,3,13,16,128]{4,3,2,1,0:T(8,128)S(1)}, u32[]{:S(2)}, u32[]{:S(2)}) collective-permute-start(f32[2,3,13,16,128]{4,3,2,1,0:T(8,128)S(1)} %pad_maximum_fusion.refs_3_), channel_id=1, source_target_pairs={{0,752},{1,753},{2,754},{3,755},{4,756},{5,757},{6,758},{7,759},{8... | collective-permute-start | bytes 1916936 | tf_op jit(solution)/shard_map/ppermute | solution.py:41
  54.0 0.0 collective-permute-done.5.refs_4_
  54.0 4.2 %collective-permute-start.8 = (f32[2,3,13,16,128]{4,3,2,1,0:T(8,128)S(1)}, f32[2,3,13,16,128]{4,3,2,1,0:T(8,128)S(1)}, u32[]{:S(2)}, u32[]{:S(2)}) collective-permute-start(f32[2,3,13,16,128]{4,3,2,1,0:T(8,128)S(1)} %pad_maximum_fusion.refs_3_), channel_id=1, source_target_pairs={{0,1},{1,0},{2,3},{3,2},{4,5},{5,4},{6,7},{7,6},{8,9},{9,8},{10,11... | collective-permute-start | bytes 1916936 | tf_op jit(solution)/shard_map/ppermute | solution.py:41
  58.2 0.0 collective-permute-done.6.refs_5_
  58.3 0.0 collective-permute-done.4.refs_6_
  58.3 4.5 %collective-permute-start.9 = (f32[2,3,13,16,128]{4,3,2,1,0:T(8,128)S(1)}, f32[2,3,13,16,128]{4,3,2,1,0:T(8,128)}, u32[]{:S(2)}, u32[]{:S(2)}) collective-permute-start(f32[2,3,13,16,128]{4,3,2,1,0:T(8,128)S(1)} %collective-permute-done.4.refs_6_), channel_id=1, source_target_pairs={{0,1},{1,0},{2,3},{3,2},{4,5},{5,4},{6,7},{7,6},{8,9},{9,8},{10,11... | collective-permute-start | bytes 1916936 | tf_op jit(solution)/shard_map/ppermute | solution.py:41
  62.9 1.9 %collective-permute-start.7 = (f32[3,13,16,128]{3,2,1,0:T(8,128)}, f32[3,13,16,128]{3,2,1,0:T(8,128)S(1)}, u32[]{:S(2)}, u32[]{:S(2)}) collective-permute-start(f32[3,13,16,128]{3,2,1,0:T(8,128)} %collective-permute-done.5.refs_4_), channel_id=1, source_target_pairs={{0,16},{1,17},{2,18},{3,19},{4,20},{5,21},{6,22},{7,23},{8,760},{9... | collective-permute-start | bytes 958472 | tf_op jit(solution)/shard_map/ppermute | solution.py:41
  64.8 0.1 add_subtract_fusion
  64.9 0.7 concatenate.3.refs_0_
  65.5 4.2 %collective-permute-done.2.refs_1_ = f32[2,3,13,16,128]{4,3,2,1,0:T(8,128)S(1)} collective-permute-done((f32[2,3,13,16,128]{4,3,2,1,0:T(8,128)S(1)}, f32[2,3,13,16,128]{4,3,2,1,0:T(8,128)S(1)}, u32[]{:S(2)}, u32[]{:S(2)}) %collective-permute-start.2) | collective-permute-done | bytes 639008 | tf_op jit(solution)/shard_map/ppermute | solution.py:41
  69.7 0.0 collective-permute-done.3.refs_2_
  69.7 0.0 collective-permute-done.8.refs_7_
  69.7 0.0 collective-permute-done.9.refs_8_
  69.8 0.8 copy-done.4
  70.5 0.2 copy-done.6
  70.8 0.2 copy-done.14
  71.0 8.1 %shard_map.47 = (f32[3,29,32,128]{3,2,1,0:T(8,128)}, bf16[3,384,384]{2,1,0:T(8,128)(2,1)}) custom-call(s32[13]{0:T(128)} %concatenate.3.refs_0_, f32[2,3,13,16,128]{4,3,2,1,0:T(8,128)} %copy-done.4, f32[2,3,13,16,128]{4,3,2,1,0:T(8,128)} %copy-done.6, f32[2,3,13,16,128]{4,3,2,1,0:T(8,128)} %copy-done.2, f32[3,13,16,128]{3,2,1,0:T(8,128)} %collective-permute-done.5.refs_4_, ...), custom_call_target="tpu_custom_call" | custom-call | flops 1000000 | bytes 1000 | tf_op jit(solution)/shard_map/pallas_call | solution.py:236
  79.1 0.0 copy-start.8
  79.1 0.7 copy-done.8
  79.8 4.3 %shard_map.48.refs_8_.refs_4_ = f32[2,3,19,16,128]{4,3,2,1,0:T(8,128)} custom-call(s32[13]{0:T(128)} %concatenate.3.refs_0_, s32[3,19]{1,0:T(4,128)} %refs_1_.2, f32[3,29,32,128]{3,2,1,0:T(8,128)} %get-tuple-element.23.refs_2_, bf16[3,384,384]{2,1,0:T(8,128)(2,1)} %get-tuple-element.24.refs_3_, f32[3,13,16,128]{3,2,1,0:T(8,128)} %copy-done.8, ...), custom_call_target="tpu_custom_call" | custom-call | flops 1000000 | bytes 1000 | tf_op jit(solution)/shard_map/pallas_call | solution.py:236
  84.1 5.4 %collective-permute-start.10 = (f32[2,3,19,16,128]{4,3,2,1,0:T(8,128)}, f32[2,3,19,16,128]{4,3,2,1,0:T(8,128)S(1)}, u32[]{:S(2)}, u32[]{:S(2)}) collective-permute-start(f32[2,3,19,16,128]{4,3,2,1,0:T(8,128)} %shard_map.48.refs_8_.refs_4_), channel_id=1, source_target_pairs={{0,1},{1,0},{2,3},{3,2},{4,5},{5,4},{6,7},{7,6},{8,9},{9,8},{10,11... | collective-permute-start | bytes 2801672 | tf_op jit(solution)/shard_map/ppermute | solution.py:41
  89.5 4.8 %collective-permute-start.13 = (f32[2,3,19,16,128]{4,3,2,1,0:T(8,128)}, f32[2,3,19,16,128]{4,3,2,1,0:T(8,128)S(1)}, u32[]{:S(2)}, u32[]{:S(2)}) collective-permute-start(f32[2,3,19,16,128]{4,3,2,1,0:T(8,128)} %shard_map.48.refs_8_.refs_4_), channel_id=1, source_target_pairs={{0,2},{1,3},{2,0},{3,1},{4,6},{5,7},{6,4},{7,5},{8,10},{9,11},{10,... | collective-permute-start | bytes 2801672 | tf_op jit(solution)/shard_map/ppermute | solution.py:41
  94.4 0.0 collective-permute-done.10.refs_9_
  94.4 0.9 copy-done.10
  95.3 3.8 %collective-permute-start.11 = (f32[3,13,16,128]{3,2,1,0:T(8,128)}, f32[3,13,16,128]{3,2,1,0:T(8,128)S(1)}, u32[]{:S(2)}, u32[]{:S(2)}) collective-permute-start(f32[3,13,16,128]{3,2,1,0:T(8,128)} %collective-permute-done.5.refs_4_), channel_id=1, source_target_pairs={{0,752},{1,753},{2,754},{3,755},{4,756},{5,757},{6,758},{7,759},{8... | collective-permute-start | bytes 958472 | tf_op jit(solution)/shard_map/ppermute | solution.py:41
  99.1 1.9 %collective-permute-start.12 = (f32[3,13,16,128]{3,2,1,0:T(8,128)}, f32[3,13,16,128]{3,2,1,0:T(8,128)S(1)}, u32[]{:S(2)}, u32[]{:S(2)}) collective-permute-start(f32[3,13,16,128]{3,2,1,0:T(8,128)} %copy-done.8), channel_id=1, source_target_pairs={{0,16},{1,17},{2,18},{3,19},{4,20},{5,21},{6,22},{7,23},{8,760},{9... | collective-permute-start | bytes 958472 | tf_op jit(solution)/shard_map/ppermute | solution.py:41
  101.1 0.0 copy-start.12
  101.1 0.1 stack.55.refs_0_
  101.2 5.1 %collective-permute-done.11.refs_6_ = f32[3,13,16,128]{3,2,1,0:T(8,128)S(1)} collective-permute-done((f32[3,13,16,128]{3,2,1,0:T(8,128)}, f32[3,13,16,128]{3,2,1,0:T(8,128)S(1)}, u32[]{:S(2)}, u32[]{:S(2)}) %collective-permute-start.11) | collective-permute-done | bytes 319520 | tf_op jit(solution)/shard_map/ppermute | solution.py:41
  106.2 6.9 %collective-permute-done.12.refs_7_ = f32[3,13,16,128]{3,2,1,0:T(8,128)S(1)} collective-permute-done((f32[3,13,16,128]{3,2,1,0:T(8,128)}, f32[3,13,16,128]{3,2,1,0:T(8,128)S(1)}, u32[]{:S(2)}, u32[]{:S(2)}) %collective-permute-start.12) | collective-permute-done | bytes 319520 | tf_op jit(solution)/shard_map/ppermute | solution.py:41
  113.1 1.2 copy-done
  114.3 1.0 copy-done.9
  115.3 1.2 copy-done.11
  116.4 4.1 %shard_map.49 = (f32[3,35,16,128]{3,2,1,0:T(8,128)S(1)}, bf16[21,13,16,256]{3,2,1,0:T(8,128)(2,1)S(1)}) custom-call(s32[9]{0:T(128)S(1)} %stack.55.refs_0_, f32[2,3,13,16,128]{4,3,2,1,0:T(8,128)S(1)} %copy-done.5, f32[2,3,13,16,128]{4,3,2,1,0:T(8,128)S(1)} %copy-done.7, f32[2,3,13,16,128]{4,3,2,1,0:T(8,128)S(1)} %copy-done.3, ...), custom_call_target="tpu_custom_call" | custom-call | flops 1000000 | bytes 1000 | tf_op jit(solution)/shard_map/pallas_call | solution.py:236
  120.6 0.0 collective-permute-done.13.refs_5_
  120.6 3.3 %collective-permute-start.14 = (f32[2,3,19,16,128]{4,3,2,1,0:T(8,128)S(1)}, f32[2,3,19,16,128]{4,3,2,1,0:T(8,128)S(1)}, u32[]{:S(2)}, u32[]{:S(2)}) collective-permute-start(f32[2,3,19,16,128]{4,3,2,1,0:T(8,128)S(1)} %collective-permute-done.13.refs_5_), channel_id=1, source_target_pairs={{0,1},{1,0},{2,3},{3,2},{4,5},{5,4},{6,7},{7,6},{8,9},{9,8},{10,11... | collective-permute-start | bytes 2801672 | tf_op jit(solution)/shard_map/ppermute | solution.py:41
  124.0 2.1 %collective-permute-done.14.refs_6_ = f32[2,3,19,16,128]{4,3,2,1,0:T(8,128)S(1)} collective-permute-done((f32[2,3,19,16,128]{4,3,2,1,0:T(8,128)S(1)}, f32[2,3,19,16,128]{4,3,2,1,0:T(8,128)S(1)}, u32[]{:S(2)}, u32[]{:S(2)}) %collective-permute-start.14) | collective-permute-done | bytes 933920 | tf_op jit(solution)/shard_map/ppermute | solution.py:41
  126.1 3.4 %shard_map.50 = f32[3,25,16,128]{3,2,1,0:T(8,128)} custom-call(s32[9]{0:T(128)S(1)} %stack.55.refs_0_, s32[3,25]{1,0:T(4,128)S(1)} %copy-done.12, f32[3,35,16,128]{3,2,1,0:T(8,128)S(1)} %get-tuple-element.30.refs_2_, bf16[21,13,16,256]{3,2,1,0:T(8,128)(2,1)S(1)} %get-tuple-element.31.refs_3_, f32[2,3,19,16,128]{4,3,2,1,0:T(8,128)S(1)} %copy-done.1, ...), custom_call_target="tpu_custom_call" | custom-call | flops 1000000 | bytes 1000 | tf_op jit(solution)/shard_map/pallas_call | solution.py:236
  (26 shorter events, 0.1 us)
Async XLA Ops:
  1.7 10.7 %collective-permute-start = (f32[3,13,16,128]{3,2,1,0:T(8,128)}, f32[3,13,16,128]{3,2,1,0:T(8,128)S(1)}, u32[]{:S(2)}, u32[]{:S(2)}) collective-permute-start(f32[3,13,16,128]{3,2,1,0:T(8,128)} %shard_map.46), channel_id=1, source_target_pairs={{0,6},{1,7},{2,4},{3,5},{4,2},{5,3},{6,0},{7,1},{8,14},{9,15},{10,... | collective-permute-start | bytes 958472 | tf_op jit(solution)/shard_map/ppermute | solution.py:41
  7.8 18.7 %collective-permute-start.1 = (f32[3,13,16,128]{3,2,1,0:T(8,128)}, f32[3,13,16,128]{3,2,1,0:T(8,128)S(1)}, u32[]{:S(2)}, u32[]{:S(2)}) collective-permute-start(f32[3,13,16,128]{3,2,1,0:T(8,128)} %shard_map.46), channel_id=1, source_target_pairs={{0,14},{1,15},{2,12},{3,13},{4,10},{5,11},{6,8},{7,9},{8,6},{9,7},... | collective-permute-start | bytes 958472 | tf_op jit(solution)/shard_map/ppermute | solution.py:41
  26.5 31.8 %copy-start.15 = (f32[3,13,16,128]{3,2,1,0:T(8,128)}, f32[3,13,16,128]{3,2,1,0:T(8,128)S(1)}, u32[]{:S(2)}) copy-start(f32[3,13,16,128]{3,2,1,0:T(8,128)S(1)} %collective-permute-done.1.refs_5_) | copy-start | bytes 958468
  27.6 42.1 %copy-start.2 = (f32[2,3,13,16,128]{4,3,2,1,0:T(8,128)}, f32[2,3,13,16,128]{4,3,2,1,0:T(8,128)S(1)}, u32[]{:S(2)}) copy-start(f32[2,3,13,16,128]{4,3,2,1,0:T(8,128)S(1)} %pad_maximum_fusion.refs_3_) | copy-start | bytes 1916932
  27.6 30.6 %collective-permute-start.4 = (f32[2,3,13,16,128]{4,3,2,1,0:T(8,128)S(1)}, f32[2,3,13,16,128]{4,3,2,1,0:T(8,128)S(1)}, u32[]{:S(2)}, u32[]{:S(2)}) collective-permute-start(f32[2,3,13,16,128]{4,3,2,1,0:T(8,128)S(1)} %pad_maximum_fusion.refs_3_), channel_id=1, source_target_pairs={{0,2},{1,3},{2,0},{3,1},{4,6},{5,7},{6,4},{7,5},{8,10},{9,11},{10,... | collective-permute-start | bytes 1916936 | tf_op jit(solution)/shard_map/ppermute | solution.py:41
  30.0 24.0 %collective-permute-start.5 = (f32[3,13,16,128]{3,2,1,0:T(8,128)S(1)}, f32[3,13,16,128]{3,2,1,0:T(8,128)}, u32[]{:S(2)}, u32[]{:S(2)}) collective-permute-start(f32[3,13,16,128]{3,2,1,0:T(8,128)S(1)} %collective-permute-done), channel_id=1, source_target_pairs={{0,14},{1,15},{2,12},{3,13},{4,10},{5,11},{6,8},{7,9},{8,6},{9,7},... | collective-permute-start | bytes 958472 | tf_op jit(solution)/shard_map/ppermute | solution.py:41
  34.8 23.5 %collective-permute-start.6 = (f32[3,13,16,128]{3,2,1,0:T(8,128)S(1)}, f32[3,13,16,128]{3,2,1,0:T(8,128)S(1)}, u32[]{:S(2)}, u32[]{:S(2)}) collective-permute-start(f32[3,13,16,128]{3,2,1,0:T(8,128)S(1)} %collective-permute-done.1.refs_5_), channel_id=1, source_target_pairs={{0,16},{1,17},{2,18},{3,19},{4,20},{5,21},{6,22},{7,23},{8,760},{9... | collective-permute-start | bytes 958472 | tf_op jit(solution)/shard_map/ppermute | solution.py:41
  36.8 32.9 %collective-permute-start.2 = (f32[2,3,13,16,128]{4,3,2,1,0:T(8,128)S(1)}, f32[2,3,13,16,128]{4,3,2,1,0:T(8,128)S(1)}, u32[]{:S(2)}, u32[]{:S(2)}) collective-permute-start(f32[2,3,13,16,128]{4,3,2,1,0:T(8,128)S(1)} %pad_maximum_fusion.refs_3_), channel_id=1, source_target_pairs={{0,16},{1,17},{2,18},{3,19},{4,20},{5,21},{6,22},{7,23},{8,24},{9,... | collective-permute-start | bytes 1916936 | tf_op jit(solution)/shard_map/ppermute | solution.py:41
  39.9 29.8 %collective-permute-start.3 = (f32[2,3,13,16,128]{4,3,2,1,0:T(8,128)S(1)}, f32[2,3,13,16,128]{4,3,2,1,0:T(8,128)S(1)}, u32[]{:S(2)}, u32[]{:S(2)}) collective-permute-start(f32[2,3,13,16,128]{4,3,2,1,0:T(8,128)S(1)} %pad_maximum_fusion.refs_3_), channel_id=1, source_target_pairs={{0,752},{1,753},{2,754},{3,755},{4,756},{5,757},{6,758},{7,759},{8... | collective-permute-start | bytes 1916936 | tf_op jit(solution)/shard_map/ppermute | solution.py:41
  54.0 15.7 %collective-permute-start.8 = (f32[2,3,13,16,128]{4,3,2,1,0:T(8,128)S(1)}, f32[2,3,13,16,128]{4,3,2,1,0:T(8,128)S(1)}, u32[]{:S(2)}, u32[]{:S(2)}) collective-permute-start(f32[2,3,13,16,128]{4,3,2,1,0:T(8,128)S(1)} %pad_maximum_fusion.refs_3_), channel_id=1, source_target_pairs={{0,1},{1,0},{2,3},{3,2},{4,5},{5,4},{6,7},{7,6},{8,9},{9,8},{10,11... | collective-permute-start | bytes 1916936 | tf_op jit(solution)/shard_map/ppermute | solution.py:41
  58.2 4.6 %copy-start.16 = (f32[3,13,16,128]{3,2,1,0:T(8,128)}, f32[3,13,16,128]{3,2,1,0:T(8,128)S(1)}, u32[]{:S(2)}) copy-start(f32[3,13,16,128]{3,2,1,0:T(8,128)S(1)} %collective-permute-done.6.refs_5_) | copy-start | bytes 958468
  58.3 11.5 %copy-start.13 = (f32[2,3,13,16,128]{4,3,2,1,0:T(8,128)}, f32[2,3,13,16,128]{4,3,2,1,0:T(8,128)S(1)}, u32[]{:S(2)}) copy-start(f32[2,3,13,16,128]{4,3,2,1,0:T(8,128)S(1)} %collective-permute-done.4.refs_6_) | copy-start | bytes 1916932
  58.3 11.4 %collective-permute-start.9 = (f32[2,3,13,16,128]{4,3,2,1,0:T(8,128)S(1)}, f32[2,3,13,16,128]{4,3,2,1,0:T(8,128)}, u32[]{:S(2)}, u32[]{:S(2)}) collective-permute-start(f32[2,3,13,16,128]{4,3,2,1,0:T(8,128)S(1)} %collective-permute-done.4.refs_6_), channel_id=1, source_target_pairs={{0,1},{1,0},{2,3},{3,2},{4,5},{5,4},{6,7},{7,6},{8,9},{9,8},{10,11... | collective-permute-start | bytes 1916936 | tf_op jit(solution)/shard_map/ppermute | solution.py:41
  62.9 16.2 %collective-permute-start.7 = (f32[3,13,16,128]{3,2,1,0:T(8,128)}, f32[3,13,16,128]{3,2,1,0:T(8,128)S(1)}, u32[]{:S(2)}, u32[]{:S(2)}) collective-permute-start(f32[3,13,16,128]{3,2,1,0:T(8,128)} %collective-permute-done.5.refs_4_), channel_id=1, source_target_pairs={{0,16},{1,17},{2,18},{3,19},{4,20},{5,21},{6,22},{7,23},{8,760},{9... | collective-permute-start | bytes 958472 | tf_op jit(solution)/shard_map/ppermute | solution.py:41
  69.7 0.8 copy-start.4
  69.7 1.0 copy-start.6
  69.7 1.2 copy-start.14
  79.0 34.1 %copy-start.3 = (f32[2,3,13,16,128]{4,3,2,1,0:T(8,128)S(1)}, f32[2,3,13,16,128]{4,3,2,1,0:T(8,128)}, u32[]{:S(2)}) copy-start(f32[2,3,13,16,128]{4,3,2,1,0:T(8,128)} %copy-done.2) | copy-start | bytes 1916932
  79.0 34.1 %copy-start.5 = (f32[2,3,13,16,128]{4,3,2,1,0:T(8,128)S(1)}, f32[2,3,13,16,128]{4,3,2,1,0:T(8,128)}, u32[]{:S(2)}) copy-start(f32[2,3,13,16,128]{4,3,2,1,0:T(8,128)} %copy-done.4) | copy-start | bytes 1916932
  79.0 34.0 %copy-start.7 = (f32[2,3,13,16,128]{4,3,2,1,0:T(8,128)S(1)}, f32[2,3,13,16,128]{4,3,2,1,0:T(8,128)}, u32[]{:S(2)}) copy-start(f32[2,3,13,16,128]{4,3,2,1,0:T(8,128)} %copy-done.6) | copy-start | bytes 1916932
  79.1 0.7 copy-start.8
  84.1 10.3 %collective-permute-start.10 = (f32[2,3,19,16,128]{4,3,2,1,0:T(8,128)}, f32[2,3,19,16,128]{4,3,2,1,0:T(8,128)S(1)}, u32[]{:S(2)}, u32[]{:S(2)}) collective-permute-start(f32[2,3,19,16,128]{4,3,2,1,0:T(8,128)} %shard_map.48.refs_8_.refs_4_), channel_id=1, source_target_pairs={{0,1},{1,0},{2,3},{3,2},{4,5},{5,4},{6,7},{7,6},{8,9},{9,8},{10,11... | collective-permute-start | bytes 2801672 | tf_op jit(solution)/shard_map/ppermute | solution.py:41
  89.5 31.1 %collective-permute-start.13 = (f32[2,3,19,16,128]{4,3,2,1,0:T(8,128)}, f32[2,3,19,16,128]{4,3,2,1,0:T(8,128)S(1)}, u32[]{:S(2)}, u32[]{:S(2)}) collective-permute-start(f32[2,3,19,16,128]{4,3,2,1,0:T(8,128)} %shard_map.48.refs_8_.refs_4_), channel_id=1, source_target_pairs={{0,2},{1,3},{2,0},{3,1},{4,6},{5,7},{6,4},{7,5},{8,10},{9,11},{10,... | collective-permute-start | bytes 2801672 | tf_op jit(solution)/shard_map/ppermute | solution.py:41
  94.4 0.9 copy-start.10
  95.3 10.9 %collective-permute-start.11 = (f32[3,13,16,128]{3,2,1,0:T(8,128)}, f32[3,13,16,128]{3,2,1,0:T(8,128)S(1)}, u32[]{:S(2)}, u32[]{:S(2)}) collective-permute-start(f32[3,13,16,128]{3,2,1,0:T(8,128)} %collective-permute-done.5.refs_4_), channel_id=1, source_target_pairs={{0,752},{1,753},{2,754},{3,755},{4,756},{5,757},{6,758},{7,759},{8... | collective-permute-start | bytes 958472 | tf_op jit(solution)/shard_map/ppermute | solution.py:41
  99.1 13.9 %collective-permute-start.12 = (f32[3,13,16,128]{3,2,1,0:T(8,128)}, f32[3,13,16,128]{3,2,1,0:T(8,128)S(1)}, u32[]{:S(2)}, u32[]{:S(2)}) collective-permute-start(f32[3,13,16,128]{3,2,1,0:T(8,128)} %copy-done.8), channel_id=1, source_target_pairs={{0,16},{1,17},{2,18},{3,19},{4,20},{5,21},{6,22},{7,23},{8,760},{9... | collective-permute-start | bytes 958472 | tf_op jit(solution)/shard_map/ppermute | solution.py:41
  101.1 25.0 %copy-start.12 = (s32[3,25]{1,0:T(4,128)S(1)}, s32[3,25]{1,0:T(4,128)}, u32[]{:S(2)}) copy-start(s32[3,25]{1,0:T(4,128)} %refs_1_.3) | copy-start | bytes 904
  113.1 1.2 copy-start
  114.3 1.0 copy-start.9
  115.3 1.2 copy-start.11
  116.4 9.6 %copy-start.1 = (f32[2,3,19,16,128]{4,3,2,1,0:T(8,128)S(1)}, f32[2,3,19,16,128]{4,3,2,1,0:T(8,128)}, u32[]{:S(2)}) copy-start(f32[2,3,19,16,128]{4,3,2,1,0:T(8,128)} %shard_map.48.refs_8_.refs_4_) | copy-start | bytes 2801668
  120.6 5.5 %collective-permute-start.14 = (f32[2,3,19,16,128]{4,3,2,1,0:T(8,128)S(1)}, f32[2,3,19,16,128]{4,3,2,1,0:T(8,128)S(1)}, u32[]{:S(2)}, u32[]{:S(2)}) collective-permute-start(f32[2,3,19,16,128]{4,3,2,1,0:T(8,128)S(1)} %collective-permute-done.13.refs_5_), channel_id=1, source_target_pairs={{0,1},{1,0},{2,3},{3,2},{4,5},{5,4},{6,7},{7,6},{8,9},{9,8},{10,11... | collective-permute-start | bytes 2801672 | tf_op jit(solution)/shard_map/ppermute | solution.py:41

commit v10 on v8

--- a/solution.py
+++ b/solution.py
@@ -121,7 +121,7 @@
 def square_first_kernel(
     place_ref, given, total_ref, rest_ref, window_ref, right_ref
 ):
-    rows, slabs = given[:8], given[8:]
+    slabs, rows = given[:8], given[8:]
     blank_corners(right_ref, 13)
     total_ref[...] = jnp.zeros_like(total_ref)
     for n, wait in enumerate(slabs):
@@ -130,13 +130,14 @@
     for n in range(4):
         for side in range(2):
             put_left(window_ref, 3 * n, side, rows[2 * n + side]())
+        firsts = [place_ref[n] * 3 + j for j in range(3)]
+        pieces = (
+            (window_ref[3 * n + j].reshape(13 * 32, 384), right_ref[r])
+            for j, r in enumerate(firsts)
+        )
+        accumulate(pieces, total_ref, 32, firsts)
     for j in range(3):
         rest_ref[j] = right_ref[place_ref[4] * 3 + j]
-    firsts = [place_ref[n] * 3 + j for n in range(4) for j in range(3)]
-    pieces = (
-        (window_ref[n].reshape(13 * 32, 384), right_ref[r]) for n, r in enumerate(firsts)
-    )
-    accumulate(pieces, total_ref, 32, firsts)
 
 
 def square_second_kernel(place_ref, mask_ref, given, out_ref, window_ref):
@@ -154,25 +155,26 @@
                 out_ref[side, g, e] = total_ref[g, e + 5, 16 * side : 16 * side + 16] * kept
 
 
+def quartet(low_y):
+    return low_y, 3 - low_y, low_y ^ 1, (3 - low_y) ^ 1
+
+
 def fill_half(right_ref, chips, slabs, core):
     blank_corners(right_ref, 19)
     zero = jnp.zeros((21, 16, 384), BF16)
-    for n, chip in enumerate(chips):
-        other = lax.rem(chip + 2, 4)
-        for k in range(2):
-            right_ref[:, pl.ds(pl.multiple_of(128 + 32 * other + 16 * k, 16), 16), :] = zero
-        for k, slab in ((core, slabs[n]), (1 - core, slabs[2 + n])):
-            place = 32 * chip + 16 * k
-            again = 32 * other + 16 * k
-            put_right(right_ref, ((place, True), (again, True), (128 + place, False)), slab())
+    for chip, slab in zip(chips, slabs):
+        place = 32 * chip + 16 * core
+        idle = 128 + 32 * chip + 16 * (1 - core)
+        right_ref[:, pl.ds(pl.multiple_of(idle, 16), 16), :] = zero
+        again = lax.rem(place + 16, 128)
+        put_right(right_ref, ((place, True), (again, True), (128 + place, False)), slab())
 
 
 def cube_first_kernel(place_ref, given, total_ref, next_ref, window_ref, right_ref):
     rows, slabs = given[:7], given[7:]
     low_y, core = place_ref[7], place_ref[8]
-    fill_half(right_ref, (low_y, 3 - low_y), slabs, core)
-    chip = lax.broadcasted_iota(jnp.int32, (208, 128), 1) // 32
-    mine = (chip == low_y) | (chip == 3 - low_y)
+    fill_half(right_ref, quartet(low_y), slabs, core)
+    mine = lax.broadcasted_iota(jnp.int32, (208, 128), 1) // 16 % 2 == core
     blocks = window_ref.shape[1:3] + (128,)
     for n, wait in enumerate(rows):
         base = place_ref[n] * 3
@@ -181,7 +183,7 @@
             values = ref[j].reshape(208, 128)
             rounded = values.astype(BF16)
             high = rounded.astype(F32)
-            low = pltpu.roll(values - high, 64, 1)
+            low = pltpu.roll(values - high, 16, 1)
             first = jnp.where(mine, high, low).astype(BF16)
             second = jnp.where(mine, low, high).astype(BF16)
             window_ref[base + j, :, :, lanes(0)] = first.reshape(blocks)
@@ -195,7 +197,7 @@
 def cube_second_kernel(place_ref, mask_ref, given, out_ref, right_ref, total_ref):
     before, window, own, slabs = given[0], given[1], given[2], given[3:]
     low_y, core = place_ref[7], place_ref[8]
-    fill_half(right_ref, (low_y ^ 1, (3 - low_y) ^ 1), slabs, core)
+    fill_half(right_ref, quartet(low_y), slabs, 1 - core)
     total_ref[...] = before()[...]
     window_ref, own_ref = window(), own()
     all_rows(window_ref, right_ref, total_ref)
@@ -278,7 +280,7 @@
     partial, rest = call(
         square_first_kernel,
         (square_places,),
-        [below_o, below_m, above_o, above_m, (both, 0), (both, 1), pair_o, pair_m] + left,
+        left + [below_o, below_m, above_o, above_m, (both, 0), (both, 1), pair_o, pair_m],
         (
             jax.ShapeDtypeStruct((3, 29, 32, 128), F32),
             jax.ShapeDtypeStruct((3, 384, 384), BF16),
@@ -296,14 +298,15 @@
         LARGE,
         True,
     )
-    square_after = send(square, NEXT)
-    square_twin, pair_late, beside_late = together(send(square, SIBLING), pair_o, beside_o)
-    far_a, far_b = send(pair_late, AGAINST), send(beside_late, ACROSS)
+    square_twin = send(square, SIBLING)
+    square_after, far_a, far_b = together(
+        send(square, NEXT), send(pair_o, AGAINST), send(beside_o, ACROSS)
+    )
     total, window = call(
         cube_first_kernel,
         (cube_places,),
         [below_o, above_o, (both, 0), pair_o, beside_o, far_a, far_b]
-        + [(square, 0), (square, 1), (square_twin, 0), (square_twin, 1)],
+        + [(square, 0), (square, 1), (square_after, 0), (square_after, 1)],
         (
             jax.ShapeDtypeStruct((3, 35, 16, 128), F32),
             jax.ShapeDtypeStruct((21, 13, 16, 256), BF16),
@@ -312,12 +315,11 @@
         SMALL,
         False,
     )
-    total, square_after = together(total, square_after)
     after_twin = send(square_after, SIBLING)
     return call(
         cube_second_kernel,
         (cube_places, cube_mask),
-        [total, window, (square, 0), (square_after, 0), (square_after, 1)]
+        [total, window, (square, 0), (square_twin, 0), (square_twin, 1)]
         + [(after_twin, 0), (after_twin, 1)],
         jax.ShapeDtypeStruct((3, 25, 16, 128), F32),
         [pltpu.VMEM((21, 256, 384), BF16), pltpu.VMEM((3, 35, 16, 128), F32)],

time: 127 us -> 125 us (0.984)
  waiting for transfers between devices: 21.4 us -> 12.6 us
  starting transfers between devices: 77.3 us -> 80.8 us
  local copies, waits for them, and re-layouts: 4.42 us -> 7.01 us
    ppermute x17, waiting for transfers between devices: 21.4 us -> 12.6 us  [send(): return lax.ppermute(array, AXES, which)]
    ppermute x17, starting transfers between devices: 77.3 us -> 80.8 us  [send(): return lax.ppermute(array, AXES, which)]
    unnamed x30 -> x36, local copies, waits for them, and re-layouts: 3.69 us -> 6.24 us
  transfers between devices with their start and end apart: 17 -> 17, of which waited for: 6 -> 5; matrix products, arithmetic and copies ran while one was open for 1% -> 1% of each run, Pallas kernels for 10% -> 10%
where the time goes in v10:
time: 125 us; the launch traced here: 124 us
  starting transfers between devices  80.8 us (65%)
  Pallas kernels  22 us (18%)
  waiting for transfers between devices  12.6 us (10%)
  local copies, waits for them, and re-layouts  7.01 us (6%)
  other arithmetic  1.31 us (1%)
    ppermute x17, starting transfers between devices, send(): return lax.ppermute(array, AXES, which)  80.8 us
    pallas_call x4, Pallas kernels, call(): pl.pallas_call(whole, out_shape=out_shape, in_specs=[SMEM] * first + [IN_...  20.3 us
    ppermute x17, waiting for transfers between devices, send(): return lax.ppermute(array, AXES, which)  12.6 us
    unnamed x36, local copies, waits for them, and re-layouts  6.24 us
  transfers between devices with their start and end apart: 17, of which 5 were waited for; matrix products, arithmetic and copies ran while one was open for 1% of the time, Pallas kernels for 10%

profile of v10, /device:TPU:1, one launch (start us, length us, event | category | flops | bytes accessed | tf_op | source)
XLA Modules:
  0.0 124.1 jit_solution(3109431145099476818)
XLA Ops:
  0.0 1.7 %shard_map.46 = f32[3,13,16,128]{3,2,1,0:T(8,128)} custom-call(s32[3,13]{1,0:T(4,128)} %mask_ref.1, f32[3,13,16,128]{3,2,1,0:T(8,128)} %x_ref.1), custom_call_target="tpu_custom_call" | custom-call | tf_op jit(solution)/shard_map/pallas_call | solution.py:253
  1.7 6.0 %collective-permute-start = (f32[3,13,16,128]{3,2,1,0:T(8,128)}, f32[3,13,16,128]{3,2,1,0:T(8,128)}, u32[]{:S(2)}, u32[]{:S(2)}) collective-permute-start(f32[3,13,16,128]{3,2,1,0:T(8,128)} %shard_map.46), channel_id=1, source_target_pairs={{0,6},{1,7},{2,4},{3,5},{4,2},{5,3},{6,0},{7,1},{8,14},{9,15},{10,... | collective-permute-start | bytes 958472 | tf_op jit(solution)/shard_map/ppermute | solution.py:41
  7.8 4.4 %collective-permute-start.1 = (f32[3,13,16,128]{3,2,1,0:T(8,128)}, f32[3,13,16,128]{3,2,1,0:T(8,128)S(1)}, u32[]{:S(2)}, u32[]{:S(2)}) collective-permute-start(f32[3,13,16,128]{3,2,1,0:T(8,128)} %shard_map.46), channel_id=1, source_target_pairs={{0,14},{1,15},{2,12},{3,13},{4,10},{5,11},{6,8},{7,9},{8,6},{9,7},... | collective-permute-start | bytes 958472 | tf_op jit(solution)/shard_map/ppermute | solution.py:41
  12.2 3.1 %collective-permute-start.2 = (f32[3,13,16,128]{3,2,1,0:T(8,128)}, f32[3,13,16,128]{3,2,1,0:T(8,128)S(1)}, u32[]{:S(2)}, u32[]{:S(2)}) collective-permute-start(f32[3,13,16,128]{3,2,1,0:T(8,128)} %shard_map.46), channel_id=1, source_target_pairs={{0,16},{1,17},{2,18},{3,19},{4,20},{5,21},{6,22},{7,23},{8,24},{9,... | collective-permute-start | bytes 958472 | tf_op jit(solution)/shard_map/ppermute | solution.py:41
  15.3 15.3 %collective-permute-start.3 = (f32[3,13,16,128]{3,2,1,0:T(8,128)}, f32[3,13,16,128]{3,2,1,0:T(8,128)S(1)}, u32[]{:S(2)}, u32[]{:S(2)}) collective-permute-start(f32[3,13,16,128]{3,2,1,0:T(8,128)} %shard_map.46), channel_id=1, source_target_pairs={{0,752},{1,753},{2,754},{3,755},{4,756},{5,757},{6,758},{7,759},{8... | collective-permute-start | bytes 958472 | tf_op jit(solution)/shard_map/ppermute | solution.py:41
  30.6 0.0 collective-permute-done
  30.7 0.0 collective-permute-done.1.refs_10_
  30.7 4.9 %collective-permute-done.2.refs_5_.refs_1_ = f32[3,13,16,128]{3,2,1,0:T(8,128)S(1)} collective-permute-done((f32[3,13,16,128]{3,2,1,0:T(8,128)}, f32[3,13,16,128]{3,2,1,0:T(8,128)S(1)}, u32[]{:S(2)}, u32[]{:S(2)}) %collective-permute-start.2) | collective-permute-done | bytes 319520 | tf_op jit(solution)/shard_map/ppermute | solution.py:41
  35.5 1.0 collective-permute-done.3.refs_7_.refs_2_
  36.5 1.2 pad_maximum_fusion.refs_1_.refs_3_
  37.8 2.3 %collective-permute-start.8 = (f32[2,3,13,16,128]{4,3,2,1,0:T(8,128)S(1)}, f32[2,3,13,16,128]{4,3,2,1,0:T(8,128)S(1)}, u32[]{:S(2)}, u32[]{:S(2)}) collective-permute-start(f32[2,3,13,16,128]{4,3,2,1,0:T(8,128)S(1)} %pad_maximum_fusion.refs_1_.refs_3_), channel_id=1, source_target_pairs={{0,2},{1,3},{2,0},{3,1},{4,6},{5,7},{6,4},{7,5},{8,10},{9,11},{10,... | collective-permute-start | bytes 1916936 | tf_op jit(solution)/shard_map/ppermute | solution.py:41
  40.1 1.9 %collective-permute-start.9 = (f32[3,13,16,128]{3,2,1,0:T(8,128)S(1)}, f32[3,13,16,128]{3,2,1,0:T(8,128)S(1)}, u32[]{:S(2)}, u32[]{:S(2)}) collective-permute-start(f32[3,13,16,128]{3,2,1,0:T(8,128)S(1)} %collective-permute-done.1.refs_10_), channel_id=1, source_target_pairs={{0,16},{1,17},{2,18},{3,19},{4,20},{5,21},{6,22},{7,23},{8,760},{9... | collective-permute-start | bytes 958472 | tf_op jit(solution)/shard_map/ppermute | solution.py:41
  42.0 8.5 %collective-permute-start.4 = (f32[3,13,16,128]{3,2,1,0:T(8,128)}, f32[3,13,16,128]{3,2,1,0:T(8,128)}, u32[]{:S(2)}, u32[]{:S(2)}) collective-permute-start(f32[3,13,16,128]{3,2,1,0:T(8,128)} %collective-permute-done), channel_id=1, source_target_pairs={{0,14},{1,15},{2,12},{3,13},{4,10},{5,11},{6,8},{7,9},{8,6},{9,7},... | collective-permute-start | bytes 958472 | tf_op jit(solution)/shard_map/ppermute | solution.py:41
  50.5 1.9 %collective-permute-start.5 = (f32[3,13,16,128]{3,2,1,0:T(8,128)}, f32[3,13,16,128]{3,2,1,0:T(8,128)}, u32[]{:S(2)}, u32[]{:S(2)}) collective-permute-start(f32[3,13,16,128]{3,2,1,0:T(8,128)} %collective-permute-done), channel_id=1, source_target_pairs={{0,16},{1,17},{2,18},{3,19},{4,20},{5,21},{6,22},{7,23},{8,24},{9,... | collective-permute-start | bytes 958472 | tf_op jit(solution)/shard_map/ppermute | solution.py:41
  52.5 6.7 %collective-permute-start.6 = (f32[3,13,16,128]{3,2,1,0:T(8,128)}, f32[3,13,16,128]{3,2,1,0:T(8,128)}, u32[]{:S(2)}, u32[]{:S(2)}) collective-permute-start(f32[3,13,16,128]{3,2,1,0:T(8,128)} %collective-permute-done), channel_id=1, source_target_pairs={{0,752},{1,753},{2,754},{3,755},{4,756},{5,757},{6,758},{7,759},{8... | collective-permute-start | bytes 958472 | tf_op jit(solution)/shard_map/ppermute | solution.py:41
  59.1 0.0 collective-permute-done.9.refs_5_
  59.2 4.7 %collective-permute-start.10 = (f32[2,3,13,16,128]{4,3,2,1,0:T(8,128)S(1)}, f32[2,3,13,16,128]{4,3,2,1,0:T(8,128)S(1)}, u32[]{:S(2)}, u32[]{:S(2)}) collective-permute-start(f32[2,3,13,16,128]{4,3,2,1,0:T(8,128)S(1)} %pad_maximum_fusion.refs_1_.refs_3_), channel_id=1, source_target_pairs={{0,1},{1,0},{2,3},{3,2},{4,5},{5,4},{6,7},{7,6},{8,9},{9,8},{10,11... | collective-permute-start | bytes 1916936 | tf_op jit(solution)/shard_map/ppermute | solution.py:41
  63.9 0.0 collective-permute-done.8.refs_2_
  64.0 1.9 %collective-permute-start.11 = (f32[2,3,13,16,128]{4,3,2,1,0:T(8,128)S(1)}, f32[2,3,13,16,128]{4,3,2,1,0:T(8,128)S(1)}, u32[]{:S(2)}, u32[]{:S(2)}) collective-permute-start(f32[2,3,13,16,128]{4,3,2,1,0:T(8,128)S(1)} %collective-permute-done.8.refs_2_), channel_id=1, source_target_pairs={{0,1},{1,0},{2,3},{3,2},{4,5},{5,4},{6,7},{7,6},{8,9},{9,8},{10,11... | collective-permute-start | bytes 1916936 | tf_op jit(solution)/shard_map/ppermute | solution.py:41
  65.9 0.0 collective-permute-done.4.refs_9_.refs_4_
  65.9 0.0 collective-permute-done.6.refs_8_
  66.0 1.9 %collective-permute-start.7 = (f32[3,13,16,128]{3,2,1,0:T(8,128)}, f32[3,13,16,128]{3,2,1,0:T(8,128)S(1)}, u32[]{:S(2)}, u32[]{:S(2)}) collective-permute-start(f32[3,13,16,128]{3,2,1,0:T(8,128)} %collective-permute-done.4.refs_9_.refs_4_), channel_id=1, source_target_pairs={{0,16},{1,17},{2,18},{3,19},{4,20},{5,21},{6,22},{7,23},{8,760},{9... | collective-permute-start | bytes 958472 | tf_op jit(solution)/shard_map/ppermute | solution.py:41
  67.9 0.1 add_subtract_fusion
  68.0 0.7 concatenate.3.refs_0_
  68.7 0.0 collective-permute-done.10.refs_3_
  68.7 0.0 collective-permute-done.11.refs_4_
  68.7 0.8 copy-done.14
  69.5 0.8 copy-done.15
  70.3 7.8 %shard_map.47 = (f32[3,29,32,128]{3,2,1,0:T(8,128)}, bf16[3,384,384]{2,1,0:T(8,128)(2,1)}) custom-call(s32[13]{0:T(128)} %concatenate.3.refs_0_, f32[2,3,13,16,128]{4,3,2,1,0:T(8,128)} %copy-done.2, f32[2,3,13,16,128]{4,3,2,1,0:T(8,128)} %copy-done.13, f32[2,3,13,16,128]{4,3,2,1,0:T(8,128)} %copy-done.14, f32[2,3,13,16,128]{4,3,2,1,0:T(8,128)} %copy-done.15, ...), custom_call_target="tpu_custom_call" | custom-call | flops 1000000 | bytes 1000 | tf_op jit(solution)/shard_map/pallas_call | solution.py:238
  78.2 0.5 collective-permute-done.7.refs_4_.refs_5_
  78.7 0.7 copy-done.8
  79.4 4.3 %shard_map.48.refs_8_.refs_4_ = f32[2,3,19,16,128]{4,3,2,1,0:T(8,128)} custom-call(s32[13]{0:T(128)} %concatenate.3.refs_0_, s32[3,19]{1,0:T(4,128)} %refs_1_.2, f32[3,29,32,128]{3,2,1,0:T(8,128)} %get-tuple-element.29.refs_2_, bf16[3,384,384]{2,1,0:T(8,128)(2,1)} %get-tuple-element.30.refs_3_, f32[3,13,16,128]{3,2,1,0:T(8,128)} %copy-done.8, ...), custom_call_target="tpu_custom_call" | custom-call | flops 1000000 | bytes 1000 | tf_op jit(solution)/shard_map/pallas_call | solution.py:238
  83.8 0.0 copy-start.12
  83.8 4.8 %collective-permute-start.12 = (f32[2,3,19,16,128]{4,3,2,1,0:T(8,128)}, f32[2,3,19,16,128]{4,3,2,1,0:T(8,128)S(1)}, u32[]{:S(2)}, u32[]{:S(2)}) collective-permute-start(f32[2,3,19,16,128]{4,3,2,1,0:T(8,128)} %shard_map.48.refs_8_.refs_4_), channel_id=1, source_target_pairs={{0,2},{1,3},{2,0},{3,1},{4,6},{5,7},{6,4},{7,5},{8,10},{9,11},{10,... | collective-permute-start | bytes 2801672 | tf_op jit(solution)/shard_map/ppermute | solution.py:41
  88.6 5.9 %collective-permute-start.13 = (f32[3,13,16,128]{3,2,1,0:T(8,128)}, f32[3,13,16,128]{3,2,1,0:T(8,128)S(1)}, u32[]{:S(2)}, u32[]{:S(2)}) collective-permute-start(f32[3,13,16,128]{3,2,1,0:T(8,128)} %collective-permute-done.4.refs_9_.refs_4_), channel_id=1, source_target_pairs={{0,752},{1,753},{2,754},{3,755},{4,756},{5,757},{6,758},{7,759},{8... | collective-permute-start | bytes 958472 | tf_op jit(solution)/shard_map/ppermute | solution.py:41
  94.5 1.9 %collective-permute-start.14 = (f32[3,13,16,128]{3,2,1,0:T(8,128)}, f32[3,13,16,128]{3,2,1,0:T(8,128)S(1)}, u32[]{:S(2)}, u32[]{:S(2)}) collective-permute-start(f32[3,13,16,128]{3,2,1,0:T(8,128)} %copy-done.8), channel_id=1, source_target_pairs={{0,16},{1,17},{2,18},{3,19},{4,20},{5,21},{6,22},{7,23},{8,760},{9... | collective-permute-start | bytes 958472 | tf_op jit(solution)/shard_map/ppermute | solution.py:41
  96.4 4.2 %collective-permute-start.15 = (f32[2,3,19,16,128]{4,3,2,1,0:T(8,128)}, f32[2,3,19,16,128]{4,3,2,1,0:T(8,128)S(1)}, u32[]{:S(2)}, u32[]{:S(2)}) collective-permute-start(f32[2,3,19,16,128]{4,3,2,1,0:T(8,128)} %shard_map.48.refs_8_.refs_4_), channel_id=1, source_target_pairs={{0,1},{1,0},{2,3},{3,2},{4,5},{5,4},{6,7},{7,6},{8,9},{9,8},{10,11... | collective-permute-start | bytes 2801672 | tf_op jit(solution)/shard_map/ppermute | solution.py:41
  100.6 6.1 %collective-permute-done.14.refs_7_ = f32[3,13,16,128]{3,2,1,0:T(8,128)S(1)} collective-permute-done((f32[3,13,16,128]{3,2,1,0:T(8,128)}, f32[3,13,16,128]{3,2,1,0:T(8,128)S(1)}, u32[]{:S(2)}, u32[]{:S(2)}) %collective-permute-start.14) | collective-permute-done | bytes 319520 | tf_op jit(solution)/shard_map/ppermute | solution.py:41
  106.7 0.7 copy-done.10
  107.4 0.1 collective-permute-done.12.refs_9_
  107.5 5.2 %collective-permute-start.16 = (f32[2,3,19,16,128]{4,3,2,1,0:T(8,128)S(1)}, f32[2,3,19,16,128]{4,3,2,1,0:T(8,128)}, u32[]{:S(2)}, u32[]{:S(2)}) collective-permute-start(f32[2,3,19,16,128]{4,3,2,1,0:T(8,128)S(1)} %collective-permute-done.12.refs_9_), channel_id=1, source_target_pairs={{0,1},{1,0},{2,3},{3,2},{4,5},{5,4},{6,7},{7,6},{8,9},{9,8},{10,11... | collective-permute-start | bytes 2801672 | tf_op jit(solution)/shard_map/ppermute | solution.py:41
  112.7 0.1 stack.55.refs_0_
  112.8 1.2 copy-done
  114.0 1.0 copy-done.9
  115.0 1.0 copy-done.11
  115.9 4.1 %shard_map.49 = (f32[3,35,16,128]{3,2,1,0:T(8,128)S(1)}, bf16[21,13,16,256]{3,2,1,0:T(8,128)(2,1)S(1)}) custom-call(s32[9]{0:T(128)S(1)} %stack.55.refs_0_, f32[3,13,16,128]{3,2,1,0:T(8,128)S(1)} %copy-done.5, f32[3,13,16,128]{3,2,1,0:T(8,128)S(1)} %copy-done.7, f32[2,3,13,16,128]{4,3,2,1,0:T(8,128)S(1)} %copy-done.3, ...), custom_call_target="tpu_custom_call" | custom-call | flops 1000000 | bytes 1000 | tf_op jit(solution)/shard_map/pallas_call | solution.py:238
  120.1 0.0 collective-permute-done.15.refs_5_
  120.1 4.0 %shard_map.50 = f32[3,25,16,128]{3,2,1,0:T(8,128)} custom-call(s32[9]{0:T(128)S(1)} %stack.55.refs_0_, s32[3,25]{1,0:T(4,128)S(1)} %copy-done.12, f32[3,35,16,128]{3,2,1,0:T(8,128)S(1)} %get-tuple-element.35.refs_2_, bf16[21,13,16,256]{3,2,1,0:T(8,128)(2,1)S(1)} %get-tuple-element.36.refs_3_, f32[2,3,19,16,128]{4,3,2,1,0:T(8,128)S(1)} %copy-done.1, ...), custom_call_target="tpu_custom_call" | custom-call | flops 1000000 | bytes 1000 | tf_op jit(solution)/shard_map/pallas_call | solution.py:238
  (32 shorter events, 0.1 us)
Async XLA Ops:
  1.7 28.9 %collective-permute-start = (f32[3,13,16,128]{3,2,1,0:T(8,128)}, f32[3,13,16,128]{3,2,1,0:T(8,128)}, u32[]{:S(2)}, u32[]{:S(2)}) collective-permute-start(f32[3,13,16,128]{3,2,1,0:T(8,128)} %shard_map.46), channel_id=1, source_target_pairs={{0,6},{1,7},{2,4},{3,5},{4,2},{5,3},{6,0},{7,1},{8,14},{9,15},{10,... | collective-permute-start | bytes 958472 | tf_op jit(solution)/shard_map/ppermute | solution.py:41
  7.8 22.9 %collective-permute-start.1 = (f32[3,13,16,128]{3,2,1,0:T(8,128)}, f32[3,13,16,128]{3,2,1,0:T(8,128)S(1)}, u32[]{:S(2)}, u32[]{:S(2)}) collective-permute-start(f32[3,13,16,128]{3,2,1,0:T(8,128)} %shard_map.46), channel_id=1, source_target_pairs={{0,14},{1,15},{2,12},{3,13},{4,10},{5,11},{6,8},{7,9},{8,6},{9,7},... | collective-permute-start | bytes 958472 | tf_op jit(solution)/shard_map/ppermute | solution.py:41
  12.2 23.3 %collective-permute-start.2 = (f32[3,13,16,128]{3,2,1,0:T(8,128)}, f32[3,13,16,128]{3,2,1,0:T(8,128)S(1)}, u32[]{:S(2)}, u32[]{:S(2)}) collective-permute-start(f32[3,13,16,128]{3,2,1,0:T(8,128)} %shard_map.46), channel_id=1, source_target_pairs={{0,16},{1,17},{2,18},{3,19},{4,20},{5,21},{6,22},{7,23},{8,24},{9,... | collective-permute-start | bytes 958472 | tf_op jit(solution)/shard_map/ppermute | solution.py:41
  15.3 21.2 %collective-permute-start.3 = (f32[3,13,16,128]{3,2,1,0:T(8,128)}, f32[3,13,16,128]{3,2,1,0:T(8,128)S(1)}, u32[]{:S(2)}, u32[]{:S(2)}) collective-permute-start(f32[3,13,16,128]{3,2,1,0:T(8,128)} %shard_map.46), channel_id=1, source_target_pairs={{0,752},{1,753},{2,754},{3,755},{4,756},{5,757},{6,758},{7,759},{8... | collective-permute-start | bytes 958472 | tf_op jit(solution)/shard_map/ppermute | solution.py:41
  30.7 35.3 %copy-start.16 = (f32[3,13,16,128]{3,2,1,0:T(8,128)}, f32[3,13,16,128]{3,2,1,0:T(8,128)S(1)}, u32[]{:S(2)}) copy-start(f32[3,13,16,128]{3,2,1,0:T(8,128)S(1)} %collective-permute-done.1.refs_10_) | copy-start | bytes 958468
  35.5 33.1 %copy-start.4 = (f32[3,13,16,128]{3,2,1,0:T(8,128)}, f32[3,13,16,128]{3,2,1,0:T(8,128)S(1)}, u32[]{:S(2)}) copy-start(f32[3,13,16,128]{3,2,1,0:T(8,128)S(1)} %collective-permute-done.2.refs_5_.refs_1_) | copy-start | bytes 958468
  36.5 32.2 %copy-start.6 = (f32[3,13,16,128]{3,2,1,0:T(8,128)}, f32[3,13,16,128]{3,2,1,0:T(8,128)S(1)}, u32[]{:S(2)}) copy-start(f32[3,13,16,128]{3,2,1,0:T(8,128)S(1)} %collective-permute-done.3.refs_7_.refs_2_) | copy-start | bytes 958468
  37.8 30.9 %copy-start.2 = (f32[2,3,13,16,128]{4,3,2,1,0:T(8,128)}, f32[2,3,13,16,128]{4,3,2,1,0:T(8,128)S(1)}, u32[]{:S(2)}) copy-start(f32[2,3,13,16,128]{4,3,2,1,0:T(8,128)S(1)} %pad_maximum_fusion.refs_1_.refs_3_) | copy-start | bytes 1916932
  37.8 26.2 %collective-permute-start.8 = (f32[2,3,13,16,128]{4,3,2,1,0:T(8,128)S(1)}, f32[2,3,13,16,128]{4,3,2,1,0:T(8,128)S(1)}, u32[]{:S(2)}, u32[]{:S(2)}) collective-permute-start(f32[2,3,13,16,128]{4,3,2,1,0:T(8,128)S(1)} %pad_maximum_fusion.refs_1_.refs_3_), channel_id=1, source_target_pairs={{0,2},{1,3},{2,0},{3,1},{4,6},{5,7},{6,4},{7,5},{8,10},{9,11},{10,... | collective-permute-start | bytes 1916936 | tf_op jit(solution)/shard_map/ppermute | solution.py:41
  40.1 19.1 %collective-permute-start.9 = (f32[3,13,16,128]{3,2,1,0:T(8,128)S(1)}, f32[3,13,16,128]{3,2,1,0:T(8,128)S(1)}, u32[]{:S(2)}, u32[]{:S(2)}) collective-permute-start(f32[3,13,16,128]{3,2,1,0:T(8,128)S(1)} %collective-permute-done.1.refs_10_), channel_id=1, source_target_pairs={{0,16},{1,17},{2,18},{3,19},{4,20},{5,21},{6,22},{7,23},{8,760},{9... | collective-permute-start | bytes 958472 | tf_op jit(solution)/shard_map/ppermute | solution.py:41
  42.0 23.9 %collective-permute-start.4 = (f32[3,13,16,128]{3,2,1,0:T(8,128)}, f32[3,13,16,128]{3,2,1,0:T(8,128)}, u32[]{:S(2)}, u32[]{:S(2)}) collective-permute-start(f32[3,13,16,128]{3,2,1,0:T(8,128)} %collective-permute-done), channel_id=1, source_target_pairs={{0,14},{1,15},{2,12},{3,13},{4,10},{5,11},{6,8},{7,9},{8,6},{9,7},... | collective-permute-start | bytes 958472 | tf_op jit(solution)/shard_map/ppermute | solution.py:41
  50.5 15.4 %collective-permute-start.5 = (f32[3,13,16,128]{3,2,1,0:T(8,128)}, f32[3,13,16,128]{3,2,1,0:T(8,128)}, u32[]{:S(2)}, u32[]{:S(2)}) collective-permute-start(f32[3,13,16,128]{3,2,1,0:T(8,128)} %collective-permute-done), channel_id=1, source_target_pairs={{0,16},{1,17},{2,18},{3,19},{4,20},{5,21},{6,22},{7,23},{8,24},{9,... | collective-permute-start | bytes 958472 | tf_op jit(solution)/shard_map/ppermute | solution.py:41
  52.5 13.5 %collective-permute-start.6 = (f32[3,13,16,128]{3,2,1,0:T(8,128)}, f32[3,13,16,128]{3,2,1,0:T(8,128)}, u32[]{:S(2)}, u32[]{:S(2)}) collective-permute-start(f32[3,13,16,128]{3,2,1,0:T(8,128)} %collective-permute-done), channel_id=1, source_target_pairs={{0,752},{1,753},{2,754},{3,755},{4,756},{5,757},{6,758},{7,759},{8... | collective-permute-start | bytes 958472 | tf_op jit(solution)/shard_map/ppermute | solution.py:41
  59.2 4.8 %copy-start.17 = (f32[3,13,16,128]{3,2,1,0:T(8,128)}, f32[3,13,16,128]{3,2,1,0:T(8,128)S(1)}, u32[]{:S(2)}) copy-start(f32[3,13,16,128]{3,2,1,0:T(8,128)S(1)} %collective-permute-done.9.refs_5_) | copy-start | bytes 958468
  59.2 9.5 %collective-permute-start.10 = (f32[2,3,13,16,128]{4,3,2,1,0:T(8,128)S(1)}, f32[2,3,13,16,128]{4,3,2,1,0:T(8,128)S(1)}, u32[]{:S(2)}, u32[]{:S(2)}) collective-permute-start(f32[2,3,13,16,128]{4,3,2,1,0:T(8,128)S(1)} %pad_maximum_fusion.refs_1_.refs_3_), channel_id=1, source_target_pairs={{0,1},{1,0},{2,3},{3,2},{4,5},{5,4},{6,7},{7,6},{8,9},{9,8},{10,11... | collective-permute-start | bytes 1916936 | tf_op jit(solution)/shard_map/ppermute | solution.py:41
  63.9 4.8 %copy-start.13 = (f32[2,3,13,16,128]{4,3,2,1,0:T(8,128)}, f32[2,3,13,16,128]{4,3,2,1,0:T(8,128)S(1)}, u32[]{:S(2)}) copy-start(f32[2,3,13,16,128]{4,3,2,1,0:T(8,128)S(1)} %collective-permute-done.8.refs_2_) | copy-start | bytes 1916932
  64.0 4.7 %collective-permute-start.11 = (f32[2,3,13,16,128]{4,3,2,1,0:T(8,128)S(1)}, f32[2,3,13,16,128]{4,3,2,1,0:T(8,128)S(1)}, u32[]{:S(2)}, u32[]{:S(2)}) collective-permute-start(f32[2,3,13,16,128]{4,3,2,1,0:T(8,128)S(1)} %collective-permute-done.8.refs_2_), channel_id=1, source_target_pairs={{0,1},{1,0},{2,3},{3,2},{4,5},{5,4},{6,7},{7,6},{8,9},{9,8},{10,11... | collective-permute-start | bytes 1916936 | tf_op jit(solution)/shard_map/ppermute | solution.py:41
  66.0 12.8 %collective-permute-start.7 = (f32[3,13,16,128]{3,2,1,0:T(8,128)}, f32[3,13,16,128]{3,2,1,0:T(8,128)S(1)}, u32[]{:S(2)}, u32[]{:S(2)}) collective-permute-start(f32[3,13,16,128]{3,2,1,0:T(8,128)} %collective-permute-done.4.refs_9_.refs_4_), channel_id=1, source_target_pairs={{0,16},{1,17},{2,18},{3,19},{4,20},{5,21},{6,22},{7,23},{8,760},{9... | collective-permute-start | bytes 958472 | tf_op jit(solution)/shard_map/ppermute | solution.py:41
  68.7 0.8 copy-start.14
  69.5 0.8 copy-start.15
  78.1 34.6 %copy-start.3 = (f32[2,3,13,16,128]{4,3,2,1,0:T(8,128)S(1)}, f32[2,3,13,16,128]{4,3,2,1,0:T(8,128)}, u32[]{:S(2)}) copy-start(f32[2,3,13,16,128]{4,3,2,1,0:T(8,128)} %copy-done.2) | copy-start | bytes 1916932
  78.2 34.6 %copy-start.5 = (f32[3,13,16,128]{3,2,1,0:T(8,128)S(1)}, f32[3,13,16,128]{3,2,1,0:T(8,128)}, u32[]{:S(2)}) copy-start(f32[3,13,16,128]{3,2,1,0:T(8,128)} %copy-done.4) | copy-start | bytes 958468
  78.2 34.6 %copy-start.7 = (f32[3,13,16,128]{3,2,1,0:T(8,128)S(1)}, f32[3,13,16,128]{3,2,1,0:T(8,128)}, u32[]{:S(2)}) copy-start(f32[3,13,16,128]{3,2,1,0:T(8,128)} %copy-done.6) | copy-start | bytes 958468
  78.7 0.7 copy-start.8
  83.8 36.3 %copy-start.12 = (s32[3,25]{1,0:T(4,128)S(1)}, s32[3,25]{1,0:T(4,128)}, u32[]{:S(2)}) copy-start(s32[3,25]{1,0:T(4,128)} %refs_1_.3) | copy-start | bytes 904
  83.8 23.7 %collective-permute-start.12 = (f32[2,3,19,16,128]{4,3,2,1,0:T(8,128)}, f32[2,3,19,16,128]{4,3,2,1,0:T(8,128)S(1)}, u32[]{:S(2)}, u32[]{:S(2)}) collective-permute-start(f32[2,3,19,16,128]{4,3,2,1,0:T(8,128)} %shard_map.48.refs_8_.refs_4_), channel_id=1, source_target_pairs={{0,2},{1,3},{2,0},{3,1},{4,6},{5,7},{6,4},{7,5},{8,10},{9,11},{10,... | collective-permute-start | bytes 2801672 | tf_op jit(solution)/shard_map/ppermute | solution.py:41
  88.6 12.0 %collective-permute-start.13 = (f32[3,13,16,128]{3,2,1,0:T(8,128)}, f32[3,13,16,128]{3,2,1,0:T(8,128)S(1)}, u32[]{:S(2)}, u32[]{:S(2)}) collective-permute-start(f32[3,13,16,128]{3,2,1,0:T(8,128)} %collective-permute-done.4.refs_9_.refs_4_), channel_id=1, source_target_pairs={{0,752},{1,753},{2,754},{3,755},{4,756},{5,757},{6,758},{7,759},{8... | collective-permute-start | bytes 958472 | tf_op jit(solution)/shard_map/ppermute | solution.py:41
  94.5 12.2 %collective-permute-start.14 = (f32[3,13,16,128]{3,2,1,0:T(8,128)}, f32[3,13,16,128]{3,2,1,0:T(8,128)S(1)}, u32[]{:S(2)}, u32[]{:S(2)}) collective-permute-start(f32[3,13,16,128]{3,2,1,0:T(8,128)} %copy-done.8), channel_id=1, source_target_pairs={{0,16},{1,17},{2,18},{3,19},{4,20},{5,21},{6,22},{7,23},{8,760},{9... | collective-permute-start | bytes 958472 | tf_op jit(solution)/shard_map/ppermute | solution.py:41
  96.4 23.6 %collective-permute-start.15 = (f32[2,3,19,16,128]{4,3,2,1,0:T(8,128)}, f32[2,3,19,16,128]{4,3,2,1,0:T(8,128)S(1)}, u32[]{:S(2)}, u32[]{:S(2)}) collective-permute-start(f32[2,3,19,16,128]{4,3,2,1,0:T(8,128)} %shard_map.48.refs_8_.refs_4_), channel_id=1, source_target_pairs={{0,1},{1,0},{2,3},{3,2},{4,5},{5,4},{6,7},{7,6},{8,9},{9,8},{10,11... | collective-permute-start | bytes 2801672 | tf_op jit(solution)/shard_map/ppermute | solution.py:41
  106.7 0.7 copy-start.10
  107.5 12.6 %collective-permute-start.16 = (f32[2,3,19,16,128]{4,3,2,1,0:T(8,128)S(1)}, f32[2,3,19,16,128]{4,3,2,1,0:T(8,128)}, u32[]{:S(2)}, u32[]{:S(2)}) collective-permute-start(f32[2,3,19,16,128]{4,3,2,1,0:T(8,128)S(1)} %collective-permute-done.12.refs_9_), channel_id=1, source_target_pairs={{0,1},{1,0},{2,3},{3,2},{4,5},{5,4},{6,7},{7,6},{8,9},{9,8},{10,11... | collective-permute-start | bytes 2801672 | tf_op jit(solution)/shard_map/ppermute | solution.py:41
  112.8 1.2 copy-start
  114.0 1.0 copy-start.9
  115.0 1.0 copy-start.11
  115.9 4.2 %copy-start.1 = (f32[2,3,19,16,128]{4,3,2,1,0:T(8,128)S(1)}, f32[2,3,19,16,128]{4,3,2,1,0:T(8,128)}, u32[]{:S(2)}) copy-start(f32[2,3,19,16,128]{4,3,2,1,0:T(8,128)} %shard_map.48.refs_8_.refs_4_) | copy-start | bytes 2801668

commit v11 on v10

--- a/solution.py
+++ b/solution.py
@@ -140,11 +140,12 @@
         rest_ref[j] = right_ref[place_ref[4] * 3 + j]
 
 
-def square_second_kernel(place_ref, mask_ref, given, out_ref, window_ref):
+def square_second_kernel(place_ref, mask_ref, given, out_ref, window_ref, total_ref):
     before, rest, beside_o, beside_m = given
     put_left(window_ref, 0, 0, beside_o())
     put_left(window_ref, 0, 1, beside_m())
-    total_ref, right_ref = before(), rest()
+    right_ref = rest()
+    total_ref[...] = before()[...]
     firsts = [place_ref[4] * 3 + j for j in range(3)]
     pieces = ((window_ref[j].reshape(13 * 32, 384), right_ref[j]) for j in range(3))
     accumulate(pieces, total_ref, 32, firsts)
@@ -294,9 +295,9 @@
         (square_places, sq_mask),
         [partial, rest, beside_o, beside_m],
         jax.ShapeDtypeStruct((2, 3, 19, 16, 128), F32),
-        [pltpu.VMEM((3, 13, 32, 384), BF16)],
-        LARGE,
-        True,
+        [pltpu.VMEM((3, 13, 32, 384), BF16), pltpu.VMEM((3, 29, 32, 128), F32)],
+        SMALL,
+        False,
     )
     square_twin = send(square, SIBLING)
     square_after, far_a, far_b = together(

time: 125 us -> 122 us (0.976)
  waiting for transfers between devices: 12.6 us -> 17.4 us
  starting transfers between devices: 80.8 us -> 77.6 us
  Pallas kernels: 22 us -> 19.5 us
  local copies, waits for them, and re-layouts: 7.01 us -> 4.9 us
    ppermute x17, waiting for transfers between devices: 12.6 us -> 17.4 us  [send(): return lax.ppermute(array, AXES, which)]
    ppermute x17, starting transfers between devices: 80.8 us -> 77.6 us  [send(): return lax.ppermute(array, AXES, which)]
    pallas_call x4, Pallas kernels: 20.3 us -> 17.8 us  [call(): pl.pallas_call(whole, out_shape=out_shape, in_specs=[SMEM] * first + [IN_...]
    unnamed x36 -> x34, local copies, waits for them, and re-layouts: 6.24 us -> 4.14 us
  transfers between devices with their start and end apart: 17 -> 17, of which waited for: 5 -> 6; matrix products, arithmetic and copies ran while one was open for 1% -> 1% of each run, Pallas kernels for 10% -> 10%
where the time goes in v11:
time: 122 us; the launch traced here: 121 us
  starting transfers between devices  77.6 us (64%)
  Pallas kernels  19.5 us (16%)
  waiting for transfers between devices  17.4 us (14%)
  local copies, waits for them, and re-layouts  4.9 us (4%)
  other arithmetic  1.32 us (1%)
    ppermute x17, starting transfers between devices, send(): return lax.ppermute(array, AXES, which)  77.6 us
    pallas_call x4, Pallas kernels, call(): pl.pallas_call(whole, out_shape=out_shape, in_specs=[SMEM] * first + [IN_...  17.8 us
    ppermute x17, waiting for transfers between devices, send(): return lax.ppermute(array, AXES, which)  17.4 us
    unnamed x34, local copies, waits for them, and re-layouts  4.14 us
  transfers between devices with their start and end apart: 17, of which 6 were waited for; matrix products, arithmetic and copies ran while one was open for 1% of the time, Pallas kernels for 10%

profile of v11, /device:TPU:1, one launch (start us, length us, event | category | flops | bytes accessed | tf_op | source)
XLA Modules:
  0.0 121.2 jit_solution(10141169220676744041)
XLA Ops:
  0.0 1.7 %shard_map.46 = f32[3,13,16,128]{3,2,1,0:T(8,128)} custom-call(s32[3,13]{1,0:T(4,128)} %mask_ref.1, f32[3,13,16,128]{3,2,1,0:T(8,128)} %x_ref.1), custom_call_target="tpu_custom_call" | custom-call | tf_op jit(solution)/shard_map/pallas_call | solution.py:254
  1.7 6.0 %collective-permute-start = (f32[3,13,16,128]{3,2,1,0:T(8,128)}, f32[3,13,16,128]{3,2,1,0:T(8,128)}, u32[]{:S(2)}, u32[]{:S(2)}) collective-permute-start(f32[3,13,16,128]{3,2,1,0:T(8,128)} %shard_map.46), channel_id=1, source_target_pairs={{0,6},{1,7},{2,4},{3,5},{4,2},{5,3},{6,0},{7,1},{8,14},{9,15},{10,... | collective-permute-start | bytes 958472 | tf_op jit(solution)/shard_map/ppermute | solution.py:41
  7.8 4.4 %collective-permute-start.1 = (f32[3,13,16,128]{3,2,1,0:T(8,128)}, f32[3,13,16,128]{3,2,1,0:T(8,128)S(1)}, u32[]{:S(2)}, u32[]{:S(2)}) collective-permute-start(f32[3,13,16,128]{3,2,1,0:T(8,128)} %shard_map.46), channel_id=1, source_target_pairs={{0,14},{1,15},{2,12},{3,13},{4,10},{5,11},{6,8},{7,9},{8,6},{9,7},... | collective-permute-start | bytes 958472 | tf_op jit(solution)/shard_map/ppermute | solution.py:41
  12.2 3.1 %collective-permute-start.2 = (f32[3,13,16,128]{3,2,1,0:T(8,128)}, f32[3,13,16,128]{3,2,1,0:T(8,128)S(1)}, u32[]{:S(2)}, u32[]{:S(2)}) collective-permute-start(f32[3,13,16,128]{3,2,1,0:T(8,128)} %shard_map.46), channel_id=1, source_target_pairs={{0,16},{1,17},{2,18},{3,19},{4,20},{5,21},{6,22},{7,23},{8,24},{9,... | collective-permute-start | bytes 958472 | tf_op jit(solution)/shard_map/ppermute | solution.py:41
  15.3 15.3 %collective-permute-start.3 = (f32[3,13,16,128]{3,2,1,0:T(8,128)}, f32[3,13,16,128]{3,2,1,0:T(8,128)S(1)}, u32[]{:S(2)}, u32[]{:S(2)}) collective-permute-start(f32[3,13,16,128]{3,2,1,0:T(8,128)} %shard_map.46), channel_id=1, source_target_pairs={{0,752},{1,753},{2,754},{3,755},{4,756},{5,757},{6,758},{7,759},{8... | collective-permute-start | bytes 958472 | tf_op jit(solution)/shard_map/ppermute | solution.py:41
  30.6 0.0 collective-permute-done
  30.7 0.0 collective-permute-done.1.refs_10_
  30.7 4.9 %collective-permute-done.2.refs_5_.refs_1_ = f32[3,13,16,128]{3,2,1,0:T(8,128)S(1)} collective-permute-done((f32[3,13,16,128]{3,2,1,0:T(8,128)}, f32[3,13,16,128]{3,2,1,0:T(8,128)S(1)}, u32[]{:S(2)}, u32[]{:S(2)}) %collective-permute-start.2) | collective-permute-done | bytes 319520 | tf_op jit(solution)/shard_map/ppermute | solution.py:41
  35.5 1.0 collective-permute-done.3.refs_7_.refs_2_
  36.5 1.2 %pad_maximum_fusion.refs_1_.refs_3_ = f32[2,3,13,16,128]{4,3,2,1,0:T(8,128)S(1)} fusion(f32[1,3,13,16,128]{4,3,2,1,0:T(8,128)} %bitcast.7, f32[1,3,13,16,128]{4,3,2,1,0:T(8,128)} %bitcast.13), kind=kLoop, calls=%fused_computation | loop fusion | flops 159744 | bytes 1277952 | tf_op jit(solution)/shard_map/stack | solution.py:264
  37.8 2.3 %collective-permute-start.8 = (f32[2,3,13,16,128]{4,3,2,1,0:T(8,128)S(1)}, f32[2,3,13,16,128]{4,3,2,1,0:T(8,128)S(1)}, u32[]{:S(2)}, u32[]{:S(2)}) collective-permute-start(f32[2,3,13,16,128]{4,3,2,1,0:T(8,128)S(1)} %pad_maximum_fusion.refs_1_.refs_3_), channel_id=1, source_target_pairs={{0,2},{1,3},{2,0},{3,1},{4,6},{5,7},{6,4},{7,5},{8,10},{9,11},{10,... | collective-permute-start | bytes 1916936 | tf_op jit(solution)/shard_map/ppermute | solution.py:41
  40.1 1.9 %collective-permute-start.9 = (f32[3,13,16,128]{3,2,1,0:T(8,128)S(1)}, f32[3,13,16,128]{3,2,1,0:T(8,128)S(1)}, u32[]{:S(2)}, u32[]{:S(2)}) collective-permute-start(f32[3,13,16,128]{3,2,1,0:T(8,128)S(1)} %collective-permute-done.1.refs_10_), channel_id=1, source_target_pairs={{0,16},{1,17},{2,18},{3,19},{4,20},{5,21},{6,22},{7,23},{8,760},{9... | collective-permute-start | bytes 958472 | tf_op jit(solution)/shard_map/ppermute | solution.py:41
  42.0 8.5 %collective-permute-start.4 = (f32[3,13,16,128]{3,2,1,0:T(8,128)}, f32[3,13,16,128]{3,2,1,0:T(8,128)S(1)}, u32[]{:S(2)}, u32[]{:S(2)}) collective-permute-start(f32[3,13,16,128]{3,2,1,0:T(8,128)} %collective-permute-done), channel_id=1, source_target_pairs={{0,14},{1,15},{2,12},{3,13},{4,10},{5,11},{6,8},{7,9},{8,6},{9,7},... | collective-permute-start | bytes 958472 | tf_op jit(solution)/shard_map/ppermute | solution.py:41
  50.5 1.9 %collective-permute-start.5 = (f32[3,13,16,128]{3,2,1,0:T(8,128)}, f32[3,13,16,128]{3,2,1,0:T(8,128)S(1)}, u32[]{:S(2)}, u32[]{:S(2)}) collective-permute-start(f32[3,13,16,128]{3,2,1,0:T(8,128)} %collective-permute-done), channel_id=1, source_target_pairs={{0,16},{1,17},{2,18},{3,19},{4,20},{5,21},{6,22},{7,23},{8,24},{9,... | collective-permute-start | bytes 958472 | tf_op jit(solution)/shard_map/ppermute | solution.py:41
  52.5 6.7 %collective-permute-start.6 = (f32[3,13,16,128]{3,2,1,0:T(8,128)}, f32[3,13,16,128]{3,2,1,0:T(8,128)}, u32[]{:S(2)}, u32[]{:S(2)}) collective-permute-start(f32[3,13,16,128]{3,2,1,0:T(8,128)} %collective-permute-done), channel_id=1, source_target_pairs={{0,752},{1,753},{2,754},{3,755},{4,756},{5,757},{6,758},{7,759},{8... | collective-permute-start | bytes 958472 | tf_op jit(solution)/shard_map/ppermute | solution.py:41
  59.2 0.0 collective-permute-done.9.refs_5_
  59.2 4.7 %collective-permute-start.10 = (f32[2,3,13,16,128]{4,3,2,1,0:T(8,128)S(1)}, f32[2,3,13,16,128]{4,3,2,1,0:T(8,128)S(1)}, u32[]{:S(2)}, u32[]{:S(2)}) collective-permute-start(f32[2,3,13,16,128]{4,3,2,1,0:T(8,128)S(1)} %pad_maximum_fusion.refs_1_.refs_3_), channel_id=1, source_target_pairs={{0,1},{1,0},{2,3},{3,2},{4,5},{5,4},{6,7},{7,6},{8,9},{9,8},{10,11... | collective-permute-start | bytes 1916936 | tf_op jit(solution)/shard_map/ppermute | solution.py:41
  63.9 0.0 collective-permute-done.8.refs_2_
  63.9 1.9 %collective-permute-start.11 = (f32[2,3,13,16,128]{4,3,2,1,0:T(8,128)S(1)}, f32[2,3,13,16,128]{4,3,2,1,0:T(8,128)}, u32[]{:S(2)}, u32[]{:S(2)}) collective-permute-start(f32[2,3,13,16,128]{4,3,2,1,0:T(8,128)S(1)} %collective-permute-done.8.refs_2_), channel_id=1, source_target_pairs={{0,1},{1,0},{2,3},{3,2},{4,5},{5,4},{6,7},{7,6},{8,9},{9,8},{10,11... | collective-permute-start | bytes 1916936 | tf_op jit(solution)/shard_map/ppermute | solution.py:41
  65.9 0.0 collective-permute-done.4.refs_9_.refs_4_
  65.9 0.0 copy-start.7
  65.9 0.0 collective-permute-done.5.refs_6_
  66.0 0.8 copy-done.16
  66.7 0.0 collective-permute-done.6.refs_8_
  66.7 1.9 %collective-permute-start.7 = (f32[3,13,16,128]{3,2,1,0:T(8,128)S(1)}, f32[3,13,16,128]{3,2,1,0:T(8,128)S(1)}, u32[]{:S(2)}, u32[]{:S(2)}) collective-permute-start(f32[3,13,16,128]{3,2,1,0:T(8,128)S(1)} %collective-permute-done.4.refs_9_.refs_4_), channel_id=1, source_target_pairs={{0,16},{1,17},{2,18},{3,19},{4,20},{5,21},{6,22},{7,23},{8,760},{9... | collective-permute-start | bytes 958472 | tf_op jit(solution)/shard_map/ppermute | solution.py:41
  68.6 0.1 add_subtract_fusion
  68.7 0.7 concatenate.3.refs_0_
  69.4 0.0 collective-permute-done.10.refs_3_
  69.4 0.0 collective-permute-done.11.refs_4_
  69.5 0.8 copy-done.14
  70.3 7.8 %shard_map.47 = (f32[3,29,32,128]{3,2,1,0:T(8,128)}, bf16[3,384,384]{2,1,0:T(8,128)(2,1)}) custom-call(s32[13]{0:T(128)} %concatenate.3.refs_0_, f32[2,3,13,16,128]{4,3,2,1,0:T(8,128)} %copy-done, f32[2,3,13,16,128]{4,3,2,1,0:T(8,128)} %copy-done.13, f32[2,3,13,16,128]{4,3,2,1,0:T(8,128)} %copy-done.14, ...), custom_call_target="tpu_custom_call" | custom-call | flops 1000000 | bytes 1000 | tf_op jit(solution)/shard_map/pallas_call | solution.py:239
  78.1 1.9 %collective-permute-done.7.refs_4_.refs_5_ = f32[3,13,16,128]{3,2,1,0:T(8,128)S(1)} collective-permute-done((f32[3,13,16,128]{3,2,1,0:T(8,128)S(1)}, f32[3,13,16,128]{3,2,1,0:T(8,128)S(1)}, u32[]{:S(2)}, u32[]{:S(2)}) %collective-permute-start.7) | collective-permute-done | bytes 319520 | tf_op jit(solution)/shard_map/ppermute | solution.py:41
  80.0 1.4 %copy-done.2 = f32[3,29,32,128]{3,2,1,0:T(8,128)S(1)} copy-done((f32[3,29,32,128]{3,2,1,0:T(8,128)S(1)}, f32[3,29,32,128]{3,2,1,0:T(8,128)}, u32[]{:S(2)}) %copy-start.2) | copy-done | bytes 1425432
  81.4 1.2 copy-done.9
  82.6 1.4 %shard_map.48.refs_8_.refs_4_ = f32[2,3,19,16,128]{4,3,2,1,0:T(8,128)S(1)} custom-call(s32[13]{0:T(128)S(1)} %copy-done.10, s32[3,19]{1,0:T(4,128)S(1)} %copy-done.11, f32[3,29,32,128]{3,2,1,0:T(8,128)S(1)} %copy-done.2, bf16[3,384,384]{2,1,0:T(8,128)(2,1)S(1)} %copy-done.9, f32[3,13,16,128]{3,2,1,0:T(8,128)S(1)} %collective-permute-done.7.refs_4_.refs_5_, ...), custom_call_target="tpu_custom_call" | custom-call | flops 1000000 | bytes 1000 | tf_op jit(solution)/shard_map/pallas_call | solution.py:239
  84.0 0.0 copy-start.12
  84.0 4.9 %collective-permute-start.12 = (f32[2,3,19,16,128]{4,3,2,1,0:T(8,128)S(1)}, f32[2,3,19,16,128]{4,3,2,1,0:T(8,128)}, u32[]{:S(2)}, u32[]{:S(2)}) collective-permute-start(f32[2,3,19,16,128]{4,3,2,1,0:T(8,128)S(1)} %shard_map.48.refs_8_.refs_4_), channel_id=1, source_target_pairs={{0,2},{1,3},{2,0},{3,1},{4,6},{5,7},{6,4},{7,5},{8,10},{9,11},{10,... | collective-permute-start | bytes 2801672 | tf_op jit(solution)/shard_map/ppermute | solution.py:41
  88.9 4.5 %collective-permute-start.13 = (f32[3,13,16,128]{3,2,1,0:T(8,128)S(1)}, f32[3,13,16,128]{3,2,1,0:T(8,128)S(1)}, u32[]{:S(2)}, u32[]{:S(2)}) collective-permute-start(f32[3,13,16,128]{3,2,1,0:T(8,128)S(1)} %copy-done.8), channel_id=1, source_target_pairs={{0,752},{1,753},{2,754},{3,755},{4,756},{5,757},{6,758},{7,759},{8... | collective-permute-start | bytes 958472 | tf_op jit(solution)/shard_map/ppermute | solution.py:41
  93.4 1.9 %collective-permute-start.14 = (f32[3,13,16,128]{3,2,1,0:T(8,128)S(1)}, f32[3,13,16,128]{3,2,1,0:T(8,128)S(1)}, u32[]{:S(2)}, u32[]{:S(2)}) collective-permute-start(f32[3,13,16,128]{3,2,1,0:T(8,128)S(1)} %collective-permute-done.7.refs_4_.refs_5_), channel_id=1, source_target_pairs={{0,16},{1,17},{2,18},{3,19},{4,20},{5,21},{6,22},{7,23},{8,760},{9... | collective-permute-start | bytes 958472 | tf_op jit(solution)/shard_map/ppermute | solution.py:41
  95.4 3.4 %collective-permute-start.15 = (f32[2,3,19,16,128]{4,3,2,1,0:T(8,128)S(1)}, f32[2,3,19,16,128]{4,3,2,1,0:T(8,128)}, u32[]{:S(2)}, u32[]{:S(2)}) collective-permute-start(f32[2,3,19,16,128]{4,3,2,1,0:T(8,128)S(1)} %shard_map.48.refs_8_.refs_4_), channel_id=1, source_target_pairs={{0,1},{1,0},{2,3},{3,2},{4,5},{5,4},{6,7},{7,6},{8,9},{9,8},{10,11... | collective-permute-start | bytes 2801672 | tf_op jit(solution)/shard_map/ppermute | solution.py:41
  98.8 0.2 collective-permute-done.13.refs_6_
  99.0 7.2 %collective-permute-done.14.refs_7_ = f32[3,13,16,128]{3,2,1,0:T(8,128)S(1)} collective-permute-done((f32[3,13,16,128]{3,2,1,0:T(8,128)S(1)}, f32[3,13,16,128]{3,2,1,0:T(8,128)S(1)}, u32[]{:S(2)}, u32[]{:S(2)}) %collective-permute-start.14) | collective-permute-done | bytes 319520 | tf_op jit(solution)/shard_map/ppermute | solution.py:41
  106.2 2.3 %collective-permute-done.12.refs_9_ = f32[2,3,19,16,128]{4,3,2,1,0:T(8,128)} collective-permute-done((f32[2,3,19,16,128]{4,3,2,1,0:T(8,128)S(1)}, f32[2,3,19,16,128]{4,3,2,1,0:T(8,128)}, u32[]{:S(2)}, u32[]{:S(2)}) %collective-permute-start.12) | collective-permute-done | bytes 933920 | tf_op jit(solution)/shard_map/ppermute | solution.py:41
  108.4 4.1 %collective-permute-start.16 = (f32[2,3,19,16,128]{4,3,2,1,0:T(8,128)}, f32[2,3,19,16,128]{4,3,2,1,0:T(8,128)}, u32[]{:S(2)}, u32[]{:S(2)}) collective-permute-start(f32[2,3,19,16,128]{4,3,2,1,0:T(8,128)} %collective-permute-done.12.refs_9_), channel_id=1, source_target_pairs={{0,1},{1,0},{2,3},{3,2},{4,5},{5,4},{6,7},{7,6},{8,9},{9,8},{10,11... | collective-permute-start | bytes 2801672 | tf_op jit(solution)/shard_map/ppermute | solution.py:41
  112.5 0.1 stack.55.refs_0_
  112.6 4.3 %shard_map.49 = (f32[3,35,16,128]{3,2,1,0:T(8,128)S(1)}, bf16[21,13,16,256]{3,2,1,0:T(8,128)(2,1)S(1)}) custom-call(s32[9]{0:T(128)S(1)} %stack.55.refs_0_, f32[3,13,16,128]{3,2,1,0:T(8,128)S(1)} %copy-done.4, f32[3,13,16,128]{3,2,1,0:T(8,128)S(1)} %copy-done.6, f32[2,3,13,16,128]{4,3,2,1,0:T(8,128)S(1)} %copy-done.1, f32[3,13,16,128]{3,2,1,0:T(8,128)S(1)} %copy-done.8, ...), custom_call_target="tpu_custom_call" | custom-call | flops 1000000 | bytes 1000 | tf_op jit(solution)/shard_map/pallas_call | solution.py:239
  116.9 0.0 collective-permute-done.15.refs_5_
  116.9 4.3 %shard_map.50 = f32[3,25,16,128]{3,2,1,0:T(8,128)} custom-call(s32[9]{0:T(128)S(1)} %stack.55.refs_0_, s32[3,25]{1,0:T(4,128)S(1)} %copy-done.12, f32[3,35,16,128]{3,2,1,0:T(8,128)S(1)} %get-tuple-element.35.refs_2_, bf16[21,13,16,256]{3,2,1,0:T(8,128)(2,1)S(1)} %get-tuple-element.36.refs_3_, f32[2,3,19,16,128]{4,3,2,1,0:T(8,128)S(1)} %shard_map.48.refs_8_.refs_4_, ...), custom_call_target="tpu_custom_call" | custom-call | flops 1000000 | bytes 1000 | tf_op jit(solution)/shard_map/pallas_call | solution.py:239
  (30 shorter events, 0.1 us)
Async XLA Ops:
  1.7 28.9 %collective-permute-start = (f32[3,13,16,128]{3,2,1,0:T(8,128)}, f32[3,13,16,128]{3,2,1,0:T(8,128)}, u32[]{:S(2)}, u32[]{:S(2)}) collective-permute-start(f32[3,13,16,128]{3,2,1,0:T(8,128)} %shard_map.46), channel_id=1, source_target_pairs={{0,6},{1,7},{2,4},{3,5},{4,2},{5,3},{6,0},{7,1},{8,14},{9,15},{10,... | collective-permute-start | bytes 958472 | tf_op jit(solution)/shard_map/ppermute | solution.py:41
  7.8 22.9 %collective-permute-start.1 = (f32[3,13,16,128]{3,2,1,0:T(8,128)}, f32[3,13,16,128]{3,2,1,0:T(8,128)S(1)}, u32[]{:S(2)}, u32[]{:S(2)}) collective-permute-start(f32[3,13,16,128]{3,2,1,0:T(8,128)} %shard_map.46), channel_id=1, source_target_pairs={{0,14},{1,15},{2,12},{3,13},{4,10},{5,11},{6,8},{7,9},{8,6},{9,7},... | collective-permute-start | bytes 958472 | tf_op jit(solution)/shard_map/ppermute | solution.py:41
  12.2 23.3 %collective-permute-start.2 = (f32[3,13,16,128]{3,2,1,0:T(8,128)}, f32[3,13,16,128]{3,2,1,0:T(8,128)S(1)}, u32[]{:S(2)}, u32[]{:S(2)}) collective-permute-start(f32[3,13,16,128]{3,2,1,0:T(8,128)} %shard_map.46), channel_id=1, source_target_pairs={{0,16},{1,17},{2,18},{3,19},{4,20},{5,21},{6,22},{7,23},{8,24},{9,... | collective-permute-start | bytes 958472 | tf_op jit(solution)/shard_map/ppermute | solution.py:41
  15.3 21.2 %collective-permute-start.3 = (f32[3,13,16,128]{3,2,1,0:T(8,128)}, f32[3,13,16,128]{3,2,1,0:T(8,128)S(1)}, u32[]{:S(2)}, u32[]{:S(2)}) collective-permute-start(f32[3,13,16,128]{3,2,1,0:T(8,128)} %shard_map.46), channel_id=1, source_target_pairs={{0,752},{1,753},{2,754},{3,755},{4,756},{5,757},{6,758},{7,759},{8... | collective-permute-start | bytes 958472 | tf_op jit(solution)/shard_map/ppermute | solution.py:41
  30.7 33.3 %copy-start.15 = (f32[3,13,16,128]{3,2,1,0:T(8,128)}, f32[3,13,16,128]{3,2,1,0:T(8,128)S(1)}, u32[]{:S(2)}) copy-start(f32[3,13,16,128]{3,2,1,0:T(8,128)S(1)} %collective-permute-done.1.refs_10_) | copy-start | bytes 958468
  35.5 33.9 %copy-start.3 = (f32[3,13,16,128]{3,2,1,0:T(8,128)}, f32[3,13,16,128]{3,2,1,0:T(8,128)S(1)}, u32[]{:S(2)}) copy-start(f32[3,13,16,128]{3,2,1,0:T(8,128)S(1)} %collective-permute-done.2.refs_5_.refs_1_) | copy-start | bytes 958468
  36.5 32.9 %copy-start.5 = (f32[3,13,16,128]{3,2,1,0:T(8,128)}, f32[3,13,16,128]{3,2,1,0:T(8,128)S(1)}, u32[]{:S(2)}) copy-start(f32[3,13,16,128]{3,2,1,0:T(8,128)S(1)} %collective-permute-done.3.refs_7_.refs_2_) | copy-start | bytes 958468
  37.8 31.7 %copy-start = (f32[2,3,13,16,128]{4,3,2,1,0:T(8,128)}, f32[2,3,13,16,128]{4,3,2,1,0:T(8,128)S(1)}, u32[]{:S(2)}) copy-start(f32[2,3,13,16,128]{4,3,2,1,0:T(8,128)S(1)} %pad_maximum_fusion.refs_1_.refs_3_) | copy-start | bytes 1916932
  37.8 26.1 %collective-permute-start.8 = (f32[2,3,13,16,128]{4,3,2,1,0:T(8,128)S(1)}, f32[2,3,13,16,128]{4,3,2,1,0:T(8,128)S(1)}, u32[]{:S(2)}, u32[]{:S(2)}) collective-permute-start(f32[2,3,13,16,128]{4,3,2,1,0:T(8,128)S(1)} %pad_maximum_fusion.refs_1_.refs_3_), channel_id=1, source_target_pairs={{0,2},{1,3},{2,0},{3,1},{4,6},{5,7},{6,4},{7,5},{8,10},{9,11},{10,... | collective-permute-start | bytes 1916936 | tf_op jit(solution)/shard_map/ppermute | solution.py:41
  40.1 19.1 %collective-permute-start.9 = (f32[3,13,16,128]{3,2,1,0:T(8,128)S(1)}, f32[3,13,16,128]{3,2,1,0:T(8,128)S(1)}, u32[]{:S(2)}, u32[]{:S(2)}) collective-permute-start(f32[3,13,16,128]{3,2,1,0:T(8,128)S(1)} %collective-permute-done.1.refs_10_), channel_id=1, source_target_pairs={{0,16},{1,17},{2,18},{3,19},{4,20},{5,21},{6,22},{7,23},{8,760},{9... | collective-permute-start | bytes 958472 | tf_op jit(solution)/shard_map/ppermute | solution.py:41
  42.0 23.9 %collective-permute-start.4 = (f32[3,13,16,128]{3,2,1,0:T(8,128)}, f32[3,13,16,128]{3,2,1,0:T(8,128)S(1)}, u32[]{:S(2)}, u32[]{:S(2)}) collective-permute-start(f32[3,13,16,128]{3,2,1,0:T(8,128)} %collective-permute-done), channel_id=1, source_target_pairs={{0,14},{1,15},{2,12},{3,13},{4,10},{5,11},{6,8},{7,9},{8,6},{9,7},... | collective-permute-start | bytes 958472 | tf_op jit(solution)/shard_map/ppermute | solution.py:41
  50.5 15.4 %collective-permute-start.5 = (f32[3,13,16,128]{3,2,1,0:T(8,128)}, f32[3,13,16,128]{3,2,1,0:T(8,128)S(1)}, u32[]{:S(2)}, u32[]{:S(2)}) collective-permute-start(f32[3,13,16,128]{3,2,1,0:T(8,128)} %collective-permute-done), channel_id=1, source_target_pairs={{0,16},{1,17},{2,18},{3,19},{4,20},{5,21},{6,22},{7,23},{8,24},{9,... | collective-permute-start | bytes 958472 | tf_op jit(solution)/shard_map/ppermute | solution.py:41
  52.5 14.3 %collective-permute-start.6 = (f32[3,13,16,128]{3,2,1,0:T(8,128)}, f32[3,13,16,128]{3,2,1,0:T(8,128)}, u32[]{:S(2)}, u32[]{:S(2)}) collective-permute-start(f32[3,13,16,128]{3,2,1,0:T(8,128)} %collective-permute-done), channel_id=1, source_target_pairs={{0,752},{1,753},{2,754},{3,755},{4,756},{5,757},{6,758},{7,759},{8... | collective-permute-start | bytes 958472 | tf_op jit(solution)/shard_map/ppermute | solution.py:41
  59.2 10.2 %collective-permute-start.10 = (f32[2,3,13,16,128]{4,3,2,1,0:T(8,128)S(1)}, f32[2,3,13,16,128]{4,3,2,1,0:T(8,128)S(1)}, u32[]{:S(2)}, u32[]{:S(2)}) collective-permute-start(f32[2,3,13,16,128]{4,3,2,1,0:T(8,128)S(1)} %pad_maximum_fusion.refs_1_.refs_3_), channel_id=1, source_target_pairs={{0,1},{1,0},{2,3},{3,2},{4,5},{5,4},{6,7},{7,6},{8,9},{9,8},{10,11... | collective-permute-start | bytes 1916936 | tf_op jit(solution)/shard_map/ppermute | solution.py:41
  63.9 5.5 %copy-start.13 = (f32[2,3,13,16,128]{4,3,2,1,0:T(8,128)}, f32[2,3,13,16,128]{4,3,2,1,0:T(8,128)S(1)}, u32[]{:S(2)}) copy-start(f32[2,3,13,16,128]{4,3,2,1,0:T(8,128)S(1)} %collective-permute-done.8.refs_2_) | copy-start | bytes 1916932
  63.9 5.5 %collective-permute-start.11 = (f32[2,3,13,16,128]{4,3,2,1,0:T(8,128)S(1)}, f32[2,3,13,16,128]{4,3,2,1,0:T(8,128)}, u32[]{:S(2)}, u32[]{:S(2)}) collective-permute-start(f32[2,3,13,16,128]{4,3,2,1,0:T(8,128)S(1)} %collective-permute-done.8.refs_2_), channel_id=1, source_target_pairs={{0,1},{1,0},{2,3},{3,2},{4,5},{5,4},{6,7},{7,6},{8,9},{9,8},{10,11... | collective-permute-start | bytes 1916936 | tf_op jit(solution)/shard_map/ppermute | solution.py:41
  65.9 3.5 %copy-start.7 = (f32[3,13,16,128]{3,2,1,0:T(8,128)}, f32[3,13,16,128]{3,2,1,0:T(8,128)S(1)}, u32[]{:S(2)}) copy-start(f32[3,13,16,128]{3,2,1,0:T(8,128)S(1)} %collective-permute-done.4.refs_9_.refs_4_) | copy-start | bytes 958468
  65.9 0.8 copy-start.16
  66.7 13.3 %collective-permute-start.7 = (f32[3,13,16,128]{3,2,1,0:T(8,128)S(1)}, f32[3,13,16,128]{3,2,1,0:T(8,128)S(1)}, u32[]{:S(2)}, u32[]{:S(2)}) collective-permute-start(f32[3,13,16,128]{3,2,1,0:T(8,128)S(1)} %collective-permute-done.4.refs_9_.refs_4_), channel_id=1, source_target_pairs={{0,16},{1,17},{2,18},{3,19},{4,20},{5,21},{6,22},{7,23},{8,760},{9... | collective-permute-start | bytes 958472 | tf_op jit(solution)/shard_map/ppermute | solution.py:41
  69.4 10.6 %copy-start.10 = (s32[13]{0:T(128)S(1)}, s32[13]{0:T(128)}, u32[]{:S(2)}) copy-start(s32[13]{0:T(128)} %concatenate.3.refs_0_) | copy-start | bytes 160
  69.4 10.6 %copy-start.11 = (s32[3,19]{1,0:T(4,128)S(1)}, s32[3,19]{1,0:T(4,128)}, u32[]{:S(2)}) copy-start(s32[3,19]{1,0:T(4,128)} %refs_1_.2) | copy-start | bytes 688
  69.4 0.9 copy-start.14
  78.1 34.5 %copy-start.1 = (f32[2,3,13,16,128]{4,3,2,1,0:T(8,128)S(1)}, f32[2,3,13,16,128]{4,3,2,1,0:T(8,128)}, u32[]{:S(2)}) copy-start(f32[2,3,13,16,128]{4,3,2,1,0:T(8,128)} %copy-done) | copy-start | bytes 1916932
  80.0 1.4 %copy-start.2 = (f32[3,29,32,128]{3,2,1,0:T(8,128)S(1)}, f32[3,29,32,128]{3,2,1,0:T(8,128)}, u32[]{:S(2)}) copy-start(f32[3,29,32,128]{3,2,1,0:T(8,128)} %get-tuple-element.29.refs_2_) | copy-start | bytes 4276228
  81.4 1.2 copy-start.9
  82.5 6.3 %copy-start.8 = (f32[3,13,16,128]{3,2,1,0:T(8,128)S(1)}, f32[3,13,16,128]{3,2,1,0:T(8,128)}, u32[]{:S(2)}) copy-start(f32[3,13,16,128]{3,2,1,0:T(8,128)} %copy-done.7) | copy-start | bytes 958468
  82.5 30.1 %copy-start.4 = (f32[3,13,16,128]{3,2,1,0:T(8,128)S(1)}, f32[3,13,16,128]{3,2,1,0:T(8,128)}, u32[]{:S(2)}) copy-start(f32[3,13,16,128]{3,2,1,0:T(8,128)} %copy-done.3) | copy-start | bytes 958468
  82.5 30.1 %copy-start.6 = (f32[3,13,16,128]{3,2,1,0:T(8,128)S(1)}, f32[3,13,16,128]{3,2,1,0:T(8,128)}, u32[]{:S(2)}) copy-start(f32[3,13,16,128]{3,2,1,0:T(8,128)} %copy-done.5) | copy-start | bytes 958468
  84.0 32.9 %copy-start.12 = (s32[3,25]{1,0:T(4,128)S(1)}, s32[3,25]{1,0:T(4,128)}, u32[]{:S(2)}) copy-start(s32[3,25]{1,0:T(4,128)} %refs_1_.3) | copy-start | bytes 904
  84.0 24.4 %collective-permute-start.12 = (f32[2,3,19,16,128]{4,3,2,1,0:T(8,128)S(1)}, f32[2,3,19,16,128]{4,3,2,1,0:T(8,128)}, u32[]{:S(2)}, u32[]{:S(2)}) collective-permute-start(f32[2,3,19,16,128]{4,3,2,1,0:T(8,128)S(1)} %shard_map.48.refs_8_.refs_4_), channel_id=1, source_target_pairs={{0,2},{1,3},{2,0},{3,1},{4,6},{5,7},{6,4},{7,5},{8,10},{9,11},{10,... | collective-permute-start | bytes 2801672 | tf_op jit(solution)/shard_map/ppermute | solution.py:41
  88.9 10.1 %collective-permute-start.13 = (f32[3,13,16,128]{3,2,1,0:T(8,128)S(1)}, f32[3,13,16,128]{3,2,1,0:T(8,128)S(1)}, u32[]{:S(2)}, u32[]{:S(2)}) collective-permute-start(f32[3,13,16,128]{3,2,1,0:T(8,128)S(1)} %copy-done.8), channel_id=1, source_target_pairs={{0,752},{1,753},{2,754},{3,755},{4,756},{5,757},{6,758},{7,759},{8... | collective-permute-start | bytes 958472 | tf_op jit(solution)/shard_map/ppermute | solution.py:41
  93.4 12.7 %collective-permute-start.14 = (f32[3,13,16,128]{3,2,1,0:T(8,128)S(1)}, f32[3,13,16,128]{3,2,1,0:T(8,128)S(1)}, u32[]{:S(2)}, u32[]{:S(2)}) collective-permute-start(f32[3,13,16,128]{3,2,1,0:T(8,128)S(1)} %collective-permute-done.7.refs_4_.refs_5_), channel_id=1, source_target_pairs={{0,16},{1,17},{2,18},{3,19},{4,20},{5,21},{6,22},{7,23},{8,760},{9... | collective-permute-start | bytes 958472 | tf_op jit(solution)/shard_map/ppermute | solution.py:41
  95.4 21.5 %collective-permute-start.15 = (f32[2,3,19,16,128]{4,3,2,1,0:T(8,128)S(1)}, f32[2,3,19,16,128]{4,3,2,1,0:T(8,128)}, u32[]{:S(2)}, u32[]{:S(2)}) collective-permute-start(f32[2,3,19,16,128]{4,3,2,1,0:T(8,128)S(1)} %shard_map.48.refs_8_.refs_4_), channel_id=1, source_target_pairs={{0,1},{1,0},{2,3},{3,2},{4,5},{5,4},{6,7},{7,6},{8,9},{9,8},{10,11... | collective-permute-start | bytes 2801672 | tf_op jit(solution)/shard_map/ppermute | solution.py:41
  108.4 8.5 %collective-permute-start.16 = (f32[2,3,19,16,128]{4,3,2,1,0:T(8,128)}, f32[2,3,19,16,128]{4,3,2,1,0:T(8,128)}, u32[]{:S(2)}, u32[]{:S(2)}) collective-permute-start(f32[2,3,19,16,128]{4,3,2,1,0:T(8,128)} %collective-permute-done.12.refs_9_), channel_id=1, source_target_pairs={{0,1},{1,0},{2,3},{3,2},{4,5},{5,4},{6,7},{7,6},{8,9},{9,8},{10,11... | collective-permute-start | bytes 2801672 | tf_op jit(solution)/shard_map/ppermute | solution.py:41
